TPU v7x, 256 devices: a whole 4x4x8 slice. The times are simulated.
256 devices in a mesh: gx: 8 (over x, core), gy: 4 (over y), gz: 8 (over z).
Axes of the slice: x: 4, y: 4, z: 8, core: 2. Of those that a mesh axis runs over, the one named last changes fastest.
Arguments:
- velocity: float32 [3, 128, 64, 1024], P(None, 'gx', 'gy', 'gz'), may hold values from -6 to 6
- gradients: bfloat16 [2, 3, 128, 64, 1024], P(None, None, 'gx', 'gy', 'gz'), may hold values from -6 to 6
- shift_x: int32 [2, 16, 8, 8], P(None, 'gx', 'gy', 'gz'), may hold values from -6 to 6
- shift_y: int32 [2, 16, 8, 8], P(None, 'gx', 'gy', 'gz'), may hold values from -6 to 6
- shift_z: int32 [2, 16, 8, 8], P(None, 'gx', 'gy', 'gz'), may hold values from -14 to 14
- fractions: int32 [2, 3, 16, 8, 8], P(None, None, 'gx', 'gy', 'gz'), may hold values from 0 to 7
Outputs:
- hess_vec: float32 [3, 128, 64, 1024], P(None, 'gx', 'gy', 'gz')
All inputs are finite; a program needn't handle non-finite values.
Results may differ from a plain program's by a relative error of at most 0.0003.
Values sent between devices are 32-bit elements; how exact they have to be, the bound alone decides.
No kernel may reach another device: no remote copies, remote signals or barrier semaphores. Data moves between devices by JAX's collectives and lax.ppermute only.
A program may use at most 64 MiB of HBM per device.

v0:
```python
import jax
import jax.numpy as jnp
from jax import lax
from jax.sharding import PartitionSpec as P

BX = 8
BY = 8
BZ = 128
RX = 6
RY = 6
RZ = 14
STEPS = 2


STEP_SIZE = 0.5
REG_WEIGHT = 0.1
LAPLACE_TAPS = (-205.0 / 72.0, 8.0 / 5.0, -1.0 / 5.0, 8.0 / 315.0, -1.0 / 560.0)


def with_halo(shard, sides, width):
    for axis, dim in sides:
        count, length = (lax.axis_size(axis), shard.shape[dim])
        up = [(i, (i + 1) % count) for i in range(count - 1)]
        down = [(j, i) for i, j in up]
        last = lax.slice_in_dim(shard, length - width, length, axis=dim)
        initial = lax.slice_in_dim(shard, 0, width, axis=dim)
        before = lax.ppermute(last, axis, up)
        after = lax.ppermute(initial, axis, down)
        shard = jnp.concatenate([before, shard, after], axis=dim)
    return shard


def with_halo_2(shard, sides, width):
    edges = {}
    for axis, dim in sides:
        count, length = (lax.axis_size(axis), shard.shape[dim])
        up = [(i, (i + 1) % count) for i in range(count - 1)]
        last = lax.slice_in_dim(shard, length - width, length, axis=dim)
        initial = lax.slice_in_dim(shard, 0, width, axis=dim)
        edges[dim] = (
            lax.ppermute(last, axis, up),
            lax.ppermute(initial, axis, [(b, a) for a, b in up]),
        )
    done = []
    for _, dim in sides:
        low, high = edges[dim]
        around = [(width, width) if d in done else (0, 0) for d in range(shard.ndim)]
        shard = jnp.concatenate([jnp.pad(low, around), shard, jnp.pad(high, around)], axis=dim)
        done.append(dim)
    return shard


def cubic_weights(fractions):
    fraction = fractions.astype(jnp.float32) / 8.0
    squared = fraction * fraction
    cubed = squared * fraction
    taps = jnp.stack(
        [
            0.5 * (2.0 * squared - cubed - fraction),
            0.5 * (3.0 * cubed - 5.0 * squared + 2.0),
            0.5 * (4.0 * squared - 3.0 * cubed + fraction),
            0.5 * (cubed - squared),
        ],
        axis=-1,
    )
    return taps.reshape(3, -1, 4)


def block_starts(shift_x, shift_y, shift_z):
    count_x, count_y, count_z = shift_x.shape
    base_x = jnp.arange(count_x, dtype=jnp.int32)[:, None, None] * BX
    base_y = jnp.arange(count_y, dtype=jnp.int32)[None, :, None] * BY
    base_z = jnp.arange(count_z, dtype=jnp.int32)[None, None, :] * BZ
    start_x = (base_x + shift_x + (RX + 1)).reshape(-1)
    start_y = (base_y + shift_y + (RY + 1)).reshape(-1)
    start_z = (base_z + shift_z + (RZ + 1)).reshape(-1)
    return (start_x, start_y, start_z)


def to_blocks(field):
    tile_x, tile_y, tile_z = field.shape
    split = field.reshape(tile_x // BX, BX, tile_y // BY, BY, tile_z // BZ, BZ)
    return split.transpose(0, 2, 4, 1, 3, 5).reshape(-1, BX, BY, BZ)


def from_blocks(blocks, tile_x, tile_y, tile_z):
    split = blocks.reshape(tile_x // BX, tile_y // BY, tile_z // BZ, BX, BY, BZ)
    return split.transpose(0, 3, 1, 4, 2, 5).reshape(tile_x, tile_y, tile_z)


def spread_blocks(field, start_x, start_y, start_z, weights):
    values = to_blocks(field)
    accumulated = jnp.zeros(
        (
            field.shape[0] + 2 * (RX + 2),
            field.shape[1] + 2 * (RY + 2),
            field.shape[2] + 2 * (RZ + 2),
        ),
        jnp.float32,
    )

    def add_block(b, accumulated):
        weight_x = weights[0, b]
        weight_y = weights[1, b]
        weight_z = weights[2, b]
        block_vals = values[b]
        along_x = sum(
            (weight_x[a] * jnp.pad(block_vals, ((a, 3 - a), (0, 0), (0, 0))) for a in range(4))
        )
        along_y = sum(
            (weight_y[a] * jnp.pad(along_x, ((0, 0), (a, 3 - a), (0, 0))) for a in range(4))
        )
        for a in range(4):
            corner = (start_x[b], start_y[b], start_z[b] + a)
            current = lax.dynamic_slice(accumulated, corner, along_y.shape)
            accumulated = lax.dynamic_update_slice(
                accumulated, current + weight_z[a] * along_y, corner
            )
        return accumulated

    return lax.fori_loop(0, values.shape[0], add_block, accumulated)


def neg_laplacian(padded):
    tile_x = padded.shape[1] - 8
    tile_y = padded.shape[2] - 8
    tile_z = padded.shape[3] - 8

    def shifted(off_x, off_y, off_z):
        return padded[
            :,
            4 + off_x : 4 + off_x + tile_x,
            4 + off_y : 4 + off_y + tile_y,
            4 + off_z : 4 + off_z + tile_z,
        ]

    result = 3.0 * LAPLACE_TAPS[0] * shifted(0, 0, 0)
    for k in range(1, 5):
        result = result + LAPLACE_TAPS[k] * (
            shifted(k, 0, 0)
            + shifted(-k, 0, 0)
            + shifted(0, k, 0)
            + shifted(0, -k, 0)
            + shifted(0, 0, k)
            + shifted(0, 0, -k)
        )
    return -result


def departure(source, widths):
    wide_x, wide_y, wide_z = widths
    padded = with_halo(source, (("gx", 0),), wide_x)
    padded = with_halo(padded, (("gy", 1),), wide_y)
    return with_halo(padded, (("gz", 2),), wide_z)


def rim_pair(accumulated, dim, width):
    extent = accumulated.shape[dim]
    low_rim = lax.slice_in_dim(accumulated, 0, width, axis=dim)
    high_rim = lax.slice_in_dim(accumulated, extent - width, extent, axis=dim)
    return jnp.concatenate([low_rim, high_rim], axis=dim)


def fold_rim(accumulated, dim, width, outer_rims):
    extent = accumulated.shape[dim]
    interior = lax.slice_in_dim(accumulated, width, extent - width, axis=dim)
    inner_len = extent - 2 * width
    from_below = lax.slice_in_dim(outer_rims, 0, width, axis=dim)
    from_above = lax.slice_in_dim(outer_rims, 3 * width, 4 * width, axis=dim)
    padding = [(0, 0), (0, 0), (0, 0)]
    padding[dim] = (0, inner_len - width)
    low_part = jnp.pad(from_below, padding)
    padding[dim] = (inner_len - width, 0)
    return interior + low_part + jnp.pad(from_above, padding)


def return_rims(accumulated, widths):
    wide_x, wide_y, wide_z = widths
    accumulated = fold_rim(
        accumulated, 0, wide_x, with_halo(rim_pair(accumulated, 0, wide_x), (("gx", 0),), wide_x)
    )
    accumulated = fold_rim(
        accumulated, 1, wide_y, with_halo(rim_pair(accumulated, 1, wide_y), (("gy", 1),), wide_y)
    )
    return fold_rim(
        accumulated, 2, wide_z, with_halo(rim_pair(accumulated, 2, wide_z), (("gz", 2),), wide_z)
    )


def body(velocity, gradients, shift_x, shift_y, shift_z, fractions):
    widths = (RX + 2, RY + 2, RZ + 2)
    tile_x, tile_y, tile_z = (velocity.shape[1], velocity.shape[2], velocity.shape[3])
    faces = with_halo_2(velocity, (("gx", 1), ("gy", 2), ("gz", 3)), 4)
    regular = REG_WEIGHT * neg_laplacian(faces)
    state = jnp.zeros((tile_x, tile_y, tile_z), jnp.float32)
    for k in range(STEPS):
        source = state + STEP_SIZE * jnp.sum(gradients[k].astype(jnp.float32) * velocity, axis=0)
        padded = departure(source, widths)
        start_x, start_y, start_z = block_starts(shift_x[k], shift_y[k], shift_z[k])
        weights = cubic_weights(fractions[k])

        def one_block(corner_x, corner_y, corner_z, weight_x, weight_y, weight_z):
            along_z = sum(
                (
                    weight_z[a]
                    * lax.dynamic_slice(
                        padded, (corner_x, corner_y, corner_z + a), (BX + 3, BY + 3, BZ)
                    )
                    for a in range(4)
                )
            )
            along_y = sum((weight_y[a] * along_z[:, a : a + BY, :] for a in range(4)))
            return sum((weight_x[a] * along_y[a : a + BX] for a in range(4)))

        blocks = jax.vmap(one_block)(start_x, start_y, start_z, weights[0], weights[1], weights[2])
        state = from_blocks(blocks, tile_x, tile_y, tile_z)
    adjoint = state
    gauss_term = jnp.zeros_like(velocity)
    for k in reversed(range(STEPS)):
        start_x, start_y, start_z = block_starts(shift_x[k], shift_y[k], shift_z[k])
        weights = cubic_weights(fractions[k])
        accumulated = spread_blocks(adjoint, start_x, start_y, start_z, weights)
        adjoint = return_rims(accumulated, widths)
        gauss_term = gauss_term + STEP_SIZE * gradients[k].astype(jnp.float32) * adjoint[None]
    return regular + gauss_term


def solution(mesh):
    in_specs = (
        P(None, "gx", "gy", "gz"),
        P(None, None, "gx", "gy", "gz"),
        P(None, "gx", "gy", "gz"),
        P(None, "gx", "gy", "gz"),
        P(None, "gx", "gy", "gz"),
        P(None, None, "gx", "gy", "gz"),
    )
    out_specs = P(None, "gx", "gy", "gz")
    return jax.shard_map(body, mesh=mesh, in_specs=in_specs, out_specs=out_specs, check_vma=False)
```

profile of v0, /device:TPU:1, one launch (start us, length us, event | category | flops | bytes accessed | tf_op | source)
XLA Modules:
  0.0 618.6 jit_solution(15213875508925458048)
XLA Ops:
  1.6 4.5 collective-permute-start.1
  20.7 3.6 collective-permute-start.6
  39.2 3.6 collective-permute-start.10
  44.9 9.1 %collective-permute-done.10 = f32[32,32,16]{2,1,0:T(8,128)S(1)} collective-permute-done((f32[32,32,16]{2,1,0:T(8,128)S(1)}, f32[32,32,16]{2,1,0:T(8,128)S(1)}, u32[]{:S(2)}, u32[]{:S(2)}) %collective-permute-start.10) | collective-permute-done | bytes 65568 | tf_op jit(solution)/shard_map/ppermute | solution.py:27
  53.9 4.1 collective-permute-done.11
  58.6 10.6 %while.40 = (s32[]{:T(128)}, f32[32,32,160]{2,1,0:T(8,128)S(1)}, s32[4,3]{1,0:T(4,128)S(1)}, f32[4,11,11,128]{3,2,1,0:T(8,128)S(1)}, s32[]{:T(128)}) while((s32[]{:T(128)}, f32[32,32,160]{2,1,0:T(8,128)S(1)}, s32[4,3]{1,0:T(4,128)S(1)}, f32[4,11,11,128]{3,2,1,0:T(8,128)S(1)}, s32[]{:T(128)}) %tuple.353), condition=%wide.while_cond, body=%wide.while_body.sunk | while | flops 2 | bytes 180353 | solution.py:206
  69.2 13.3 %while.41 = (s32[]{:T(128)}, f32[32,32,160]{2,1,0:T(8,128)S(1)}, s32[4,3]{1,0:T(4,128)}, f32[4,11,11,128]{3,2,1,0:T(8,128)S(1)}, s32[]{:T(128)}) while((s32[]{:T(128)}, f32[32,32,160]{2,1,0:T(8,128)S(1)}, s32[4,3]{1,0:T(4,128)}, f32[4,11,11,128]{3,2,1,0:T(8,128)S(1)}, s32[]{:T(128)}) %tuple.374), condition=%wide.while_cond.1, body=%wide.while_body.1.sunk | while | flops 2 | bytes 180353 | solution.py:206
  83.3 12.9 %while.42 = (s32[]{:T(128)}, f32[32,32,160]{2,1,0:T(8,128)S(1)}, s32[4,3]{1,0:T(4,128)S(1)}, f32[4,11,11,128]{3,2,1,0:T(8,128)}, s32[]{:T(128)}) while((s32[]{:T(128)}, f32[32,32,160]{2,1,0:T(8,128)S(1)}, s32[4,3]{1,0:T(4,128)S(1)}, f32[4,11,11,128]{3,2,1,0:T(8,128)}, s32[]{:T(128)}) %tuple.375), condition=%wide.while_cond.2, body=%wide.while_body.2.sunk | while | flops 2 | bytes 154225 | solution.py:206
  97.0 15.7 %while.43 = (s32[]{:T(128)}, f32[32,32,160]{2,1,0:T(8,128)S(1)}, s32[4,3]{1,0:T(4,128)}, f32[4,11,11,128]{3,2,1,0:T(8,128)}, s32[]{:T(128)}) while((s32[]{:T(128)}, f32[32,32,160]{2,1,0:T(8,128)S(1)}, s32[4,3]{1,0:T(4,128)}, f32[4,11,11,128]{3,2,1,0:T(8,128)}, s32[]{:T(128)}) %tuple.376), condition=%wide.while_cond.3, body=%wide.while_body.3.sunk | while | flops 2 | bytes 154225 | solution.py:206
  114.4 5.1 collective-permute-start.12
  121.5 3.6 collective-permute-done.13
  130.7 3.3 collective-permute-done.15
  134.3 3.6 collective-permute-start.16
  139.4 9.6 %collective-permute-done.16 = f32[32,32,16]{2,1,0:T(8,128)S(1)} collective-permute-done((f32[32,32,16]{2,1,0:T(8,128)S(1)}, f32[32,32,16]{2,1,0:T(8,128)S(1)}, u32[]{:S(2)}, u32[]{:S(2)}) %collective-permute-start.16) | collective-permute-done | bytes 65568 | tf_op jit(solution)/shard_map/ppermute | solution.py:27
  149.1 5.2 collective-permute-done.17
  154.8 10.4 %while.44 = (s32[]{:T(128)}, f32[32,32,160]{2,1,0:T(8,128)S(1)}, s32[4,3]{1,0:T(4,128)S(1)}, f32[4,11,11,128]{3,2,1,0:T(8,128)S(1)}, s32[]{:T(128)}) while((s32[]{:T(128)}, f32[32,32,160]{2,1,0:T(8,128)S(1)}, s32[4,3]{1,0:T(4,128)S(1)}, f32[4,11,11,128]{3,2,1,0:T(8,128)S(1)}, s32[]{:T(128)}) %tuple.365), condition=%wide.while_cond.4, body=%wide.while_body.4.sunk | while | flops 2 | bytes 180353 | solution.py:206
  165.3 10.0 %while.45 = (s32[]{:T(128)}, f32[32,32,160]{2,1,0:T(8,128)S(1)}, s32[4,3]{1,0:T(4,128)S(1)}, f32[4,11,11,128]{3,2,1,0:T(8,128)S(1)}, s32[]{:T(128)}) while((s32[]{:T(128)}, f32[32,32,160]{2,1,0:T(8,128)S(1)}, s32[4,3]{1,0:T(4,128)S(1)}, f32[4,11,11,128]{3,2,1,0:T(8,128)S(1)}, s32[]{:T(128)}) %tuple.377), condition=%wide.while_cond.5, body=%wide.while_body.5.sunk | while | flops 2 | bytes 180353 | solution.py:206
  176.0 12.4 %while.46 = (s32[]{:T(128)}, f32[32,32,160]{2,1,0:T(8,128)S(1)}, s32[4,3]{1,0:T(4,128)S(1)}, f32[4,11,11,128]{3,2,1,0:T(8,128)}, s32[]{:T(128)}) while((s32[]{:T(128)}, f32[32,32,160]{2,1,0:T(8,128)S(1)}, s32[4,3]{1,0:T(4,128)S(1)}, f32[4,11,11,128]{3,2,1,0:T(8,128)}, s32[]{:T(128)}) %tuple.378), condition=%wide.while_cond.6, body=%wide.while_body.6.sunk | while | flops 2 | bytes 154225 | solution.py:206
  189.2 12.7 %while.47 = (s32[]{:T(128)}, f32[32,32,160]{2,1,0:T(8,128)S(1)}, s32[4,3]{1,0:T(4,128)S(1)}, f32[4,11,11,128]{3,2,1,0:T(8,128)}, s32[]{:T(128)}) while((s32[]{:T(128)}, f32[32,32,160]{2,1,0:T(8,128)S(1)}, s32[4,3]{1,0:T(4,128)S(1)}, f32[4,11,11,128]{3,2,1,0:T(8,128)}, s32[]{:T(128)}) %tuple.379), condition=%wide.while_cond.7, body=%wide.while_body.7.sunk | while | flops 2 | bytes 154225 | solution.py:206
  203.6 172.9 %while.38 = (s32[]{:T(128)}, f32[32,32,160]{2,1,0:T(8,128)S(1)}, s32[4]{0:T(128)S(1)}, s32[4]{0:T(128)S(1)}, s32[4]{0:T(128)S(1)}, /*index=5*/f32[3,4,4]{2,1,0:T...) while((s32[]{:T(128)}, f32[32,32,160]{2,1,0:T(8,128)S(1)}, ...), condition=%wide.region_3.4_spmd, body=%wide.region_2.3_spmd.sunk | while | flops 636439 | bytes 1315601 | solution.py:121
  218.0 3.9 dynamic_update_slice.88
  226.3 3.9 dynamic_update_slice.89
  234.6 3.9 dynamic_update_slice.90
  242.9 3.9 dynamic_update_slice.91
  261.2 3.9 dynamic_update_slice.88
  269.5 3.9 dynamic_update_slice.89
  277.8 3.9 dynamic_update_slice.90
  286.1 3.9 dynamic_update_slice.91
  304.5 3.9 dynamic_update_slice.88
  312.8 3.9 dynamic_update_slice.89
  321.0 3.9 dynamic_update_slice.90
  329.4 3.9 dynamic_update_slice.91
  347.7 3.9 dynamic_update_slice.88
  356.0 3.9 dynamic_update_slice.89
  364.3 3.9 dynamic_update_slice.90
  372.6 3.9 dynamic_update_slice.91
  376.6 4.2 collective-permute-start.18
  384.9 4.1 collective-permute-start.3
  389.1 3.4 collective-permute-start.20
  394.4 3.8 collective-permute-done.21
  398.4 4.4 collective-permute-start.22
  406.0 4.2 collective-permute-done.23
  410.5 174.7 %while.39 = (s32[]{:T(128)}, f32[32,32,160]{2,1,0:T(8,128)S(1)}, s32[4]{0:T(128)S(1)}, s32[4]{0:T(128)S(1)}, s32[4]{0:T(128)S(1)}, /*index=5*/f32[3,4,4]{2,1,0:T...) while((s32[]{:T(128)}, f32[32,32,160]{2,1,0:T(8,128)S(1)}, ...), condition=%wide.region_5.6_spmd, body=%wide.region_4.5_spmd.sunk | while | flops 636439 | bytes 1315601 | solution.py:121
  425.1 3.9 dynamic_update_slice.92
  433.5 3.9 dynamic_update_slice.93
  441.8 3.9 dynamic_update_slice.94
  450.2 3.9 dynamic_update_slice.95
  468.7 3.9 dynamic_update_slice.92
  477.2 3.9 dynamic_update_slice.93
  485.5 3.9 dynamic_update_slice.94
  493.8 3.9 dynamic_update_slice.95
  512.4 4.0 dynamic_update_slice.92
  520.8 4.0 dynamic_update_slice.93
  529.2 4.0 dynamic_update_slice.94
  537.6 4.0 dynamic_update_slice.95
  556.1 3.9 dynamic_update_slice.92
  564.6 3.9 dynamic_update_slice.93
  572.9 3.9 dynamic_update_slice.94
  581.2 3.9 dynamic_update_slice.95
  585.2 5.8 collective-permute-start.24
  595.4 4.0 collective-permute-start.5
  603.9 3.5 collective-permute-done.27
  607.5 3.3 collective-permute-start.28
  613.2 3.4 collective-permute-done.29
  (416 shorter events, 317.4 us)
Async XLA Ops:
  1.6 17.7 %collective-permute-start.1 = (f32[3,4,16,128]{3,2,1,0:T(8,128)S(1)}, f32[3,4,16,128]{3,2,1,0:T(8,128)S(1)}, u32[]{:S(2)}, u32[]{:S(2)}) collective-permute-start(f32[3,4,16,128]{3,2,1,0:T(8,128)S(1)} %get-tuple-element.745), channel_id=1, source_target_pairs={{0,32},{32,64},{64,96},{96,128},{128,160},{160,192},{192,224},{1,3... | collective-permute-start | bytes 294920 | tf_op jit(solution)/shard_map/ppermute | solution.py:41
  6.1 596.9 %collective-permute-start = (f32[3,4,16,128]{3,2,1,0:T(8,128)}, f32[3,4,16,128]{3,2,1,0:T(8,128)}, u32[]{:S(2)}, u32[]{:S(2)}) collective-permute-start(f32[3,4,16,128]{3,2,1,0:T(8,128)} %get-tuple-element.744), channel_id=1, source_target_pairs={{32,0},{64,32},{96,64},{128,96},{160,128},{192,160},{224,192},{33,... | collective-permute-start | bytes 294920 | tf_op jit(solution)/shard_map/ppermute | solution.py:42
  20.7 6.3 %collective-permute-start.6 = (f32[8,16,128]{2,1,0:T(8,128)S(1)}, f32[8,16,128]{2,1,0:T(8,128)S(1)}, u32[]{:S(2)}, u32[]{:S(2)}) collective-permute-start(f32[8,16,128]{2,1,0:T(8,128)S(1)} %get-tuple-element.756), channel_id=1, source_target_pairs={{0,32},{32,64},{64,96},{96,128},{128,160},{160,192},{192,224},{1,3... | collective-permute-start | bytes 196616 | tf_op jit(solution)/shard_map/ppermute | solution.py:27
  24.4 5.6 collective-permute-start.7
  30.0 7.0 %collective-permute-start.8 = (f32[32,8,128]{2,1,0:T(8,128)S(1)}, f32[32,8,128]{2,1,0:T(8,128)S(1)}, u32[]{:S(2)}, u32[]{:S(2)}) collective-permute-start(f32[32,8,128]{2,1,0:T(8,128)S(1)} %get-tuple-element.752), channel_id=1, source_target_pairs={{0,8},{8,16},{16,24},{1,9},{9,17},{17,25},{2,10},{10,18},{18,26},{... | collective-permute-start | bytes 393224 | tf_op jit(solution)/shard_map/ppermute | solution.py:27
  33.2 5.7 collective-permute-start.9
  39.2 14.7 %collective-permute-start.10 = (f32[32,32,16]{2,1,0:T(8,128)S(1)}, f32[32,32,16]{2,1,0:T(8,128)S(1)}, u32[]{:S(2)}, u32[]{:S(2)}) collective-permute-start(f32[32,32,16]{2,1,0:T(8,128)S(1)} %get-tuple-element.735), channel_id=1, source_target_pairs={{0,1},{1,2},{2,3},{3,4},{4,5},{5,6},{6,7},{8,9},{9,10},{10,11},{11... | collective-permute-start | bytes 196616 | tf_op jit(solution)/shard_map/ppermute | solution.py:27
  42.8 15.3 %collective-permute-start.11 = (f32[32,32,16]{2,1,0:T(8,128)S(1)}, f32[32,32,16]{2,1,0:T(8,128)S(1)}, u32[]{:S(2)}, u32[]{:S(2)}) collective-permute-start(f32[32,32,16]{2,1,0:T(8,128)S(1)} %get-tuple-element.736), channel_id=1, source_target_pairs={{1,0},{2,1},{3,2},{4,3},{5,4},{6,5},{7,6},{9,8},{10,9},{11,10},{12... | collective-permute-start | bytes 196616 | tf_op jit(solution)/shard_map/ppermute | solution.py:28
  69.2 43.5 %copy-start.7 = (f32[4]{0:T(128)S(1)}, f32[4]{0:T(128)}, u32[]{:S(2)}) copy-start(f32[4]{0:T(128)} %get-tuple-element.559) | copy-start | bytes 52
  69.2 43.4 %copy-start.8 = (f32[4]{0:T(128)S(1)}, f32[4]{0:T(128)}, u32[]{:S(2)}) copy-start(f32[4]{0:T(128)} %get-tuple-element.560) | copy-start | bytes 52
  69.2 43.4 %copy-start.9 = (f32[4]{0:T(128)S(1)}, f32[4]{0:T(128)}, u32[]{:S(2)}) copy-start(f32[4]{0:T(128)} %get-tuple-element.561) | copy-start | bytes 52
  69.2 43.4 %copy-start.10 = (f32[4]{0:T(128)S(1)}, f32[4]{0:T(128)}, u32[]{:S(2)}) copy-start(f32[4]{0:T(128)} %get-tuple-element.562) | copy-start | bytes 52
  96.2 17.7 %copy-start.2 = (f32[4]{0:T(128)S(1)}, f32[4]{0:T(128)}, u32[]{:S(2)}) copy-start(f32[4]{0:T(128)} %get-tuple-element.558) | copy-start | bytes 52
  112.6 1.5 copy-start.11
  112.6 1.6 copy-start.12
  113.9 15.7 %copy-start.13 = (s32[4,1]{0,1:T(1,128)S(1)}, s32[4,1]{0,1:T(1,128)}, u32[]{:S(2)}) copy-start(s32[4,1]{0,1:T(1,128)} %get-tuple-element.802) | copy-start | bytes 52
  113.9 15.7 %copy-start.14 = (s32[4,1]{0,1:T(1,128)S(1)}, s32[4,1]{0,1:T(1,128)}, u32[]{:S(2)}) copy-start(s32[4,1]{0,1:T(1,128)} %get-tuple-element.800) | copy-start | bytes 52
  114.0 15.7 %copy-start.21 = (s32[4,1]{0,1:T(1,128)S(1)}, s32[4,1]{0,1:T(1,128)}, u32[]{:S(2)}) copy-start(s32[4,1]{0,1:T(1,128)} %compare_select_fusion) | copy-start | bytes 52
  114.0 15.7 %copy-start.22 = (s32[4,1]{0,1:T(1,128)S(1)}, s32[4,1]{0,1:T(1,128)}, u32[]{:S(2)}) copy-start(s32[4,1]{0,1:T(1,128)} %compare_select_fusion.1) | copy-start | bytes 52
  114.0 15.7 %copy-start.23 = (s32[4,1]{0,1:T(1,128)S(1)}, s32[4,1]{0,1:T(1,128)}, u32[]{:S(2)}) copy-start(s32[4,1]{0,1:T(1,128)} %compare_select_fusion.2) | copy-start | bytes 52
  114.0 15.7 %copy-start.24 = (s32[4,1]{0,1:T(1,128)S(1)}, s32[4,1]{0,1:T(1,128)}, u32[]{:S(2)}) copy-start(s32[4,1]{0,1:T(1,128)} %compare_select_fusion.3) | copy-start | bytes 52
  114.0 16.3 %copy-start.16 = (s32[2,2]{1,0:T(2,128)S(1)}, s32[2,2]{1,0:T(2,128)}, u32[]{:S(2)}) copy-start(s32[2,2]{1,0:T(2,128)} %get-tuple-element.542) | copy-start | bytes 52
  114.4 7.1 %collective-permute-start.12 = (f32[8,16,128]{2,1,0:T(8,128)S(1)}, f32[8,16,128]{2,1,0:T(8,128)S(1)}, u32[]{:S(2)}, u32[]{:S(2)}) collective-permute-start(f32[8,16,128]{2,1,0:T(8,128)S(1)} %get-tuple-element.754), channel_id=1, source_target_pairs={{0,32},{32,64},{64,96},{96,128},{128,160},{160,192},{192,224},{1,3... | collective-permute-start | bytes 196616 | tf_op jit(solution)/shard_map/ppermute | solution.py:27
  119.5 5.6 collective-permute-start.13
  125.1 5.6 collective-permute-start.14
  128.3 5.7 collective-permute-start.15
  134.3 14.7 %collective-permute-start.16 = (f32[32,32,16]{2,1,0:T(8,128)S(1)}, f32[32,32,16]{2,1,0:T(8,128)S(1)}, u32[]{:S(2)}, u32[]{:S(2)}) collective-permute-start(f32[32,32,16]{2,1,0:T(8,128)S(1)} %get-tuple-element.733), channel_id=1, source_target_pairs={{0,1},{1,2},{2,3},{3,4},{4,5},{5,6},{6,7},{8,9},{9,10},{10,11},{11... | collective-permute-start | bytes 196616 | tf_op jit(solution)/shard_map/ppermute | solution.py:27
  137.9 16.4 %collective-permute-start.17 = (f32[32,32,16]{2,1,0:T(8,128)S(1)}, f32[32,32,16]{2,1,0:T(8,128)S(1)}, u32[]{:S(2)}, u32[]{:S(2)}) collective-permute-start(f32[32,32,16]{2,1,0:T(8,128)S(1)} %get-tuple-element.734), channel_id=1, source_target_pairs={{1,0},{2,1},{3,2},{4,3},{5,4},{6,5},{7,6},{9,8},{10,9},{11,10},{12... | collective-permute-start | bytes 196616 | tf_op jit(solution)/shard_map/ppermute | solution.py:28
  165.2 36.7 %copy-start.3 = (f32[4]{0:T(128)S(1)}, f32[4]{0:T(128)}, u32[]{:S(2)}) copy-start(f32[4]{0:T(128)} %get-tuple-element.531) | copy-start | bytes 52
  165.3 36.6 %copy-start.4 = (f32[4]{0:T(128)S(1)}, f32[4]{0:T(128)}, u32[]{:S(2)}) copy-start(f32[4]{0:T(128)} %get-tuple-element.532) | copy-start | bytes 52
  165.3 36.6 %copy-start.5 = (f32[4]{0:T(128)S(1)}, f32[4]{0:T(128)}, u32[]{:S(2)}) copy-start(f32[4]{0:T(128)} %get-tuple-element.533) | copy-start | bytes 52
  165.3 36.6 %copy-start.6 = (f32[4]{0:T(128)S(1)}, f32[4]{0:T(128)}, u32[]{:S(2)}) copy-start(f32[4]{0:T(128)} %get-tuple-element.534) | copy-start | bytes 52
  201.9 1.7 copy-start.19
  201.9 1.7 copy-start.20
  203.6 179.1 %copy-start = (f32[3,16,16,128]{3,2,1,0:T(8,128)S(1)}, f32[3,16,16,128]{3,2,1,0:T(8,128)}, u32[]{:S(2)}) copy-start(f32[3,16,16,128]{3,2,1,0:T(8,128)} %param.10) | copy-start | bytes 1179652
  376.6 12.4 %collective-permute-start.18 = (f32[8,32,160]{2,1,0:T(8,128)S(1)}, f32[8,32,160]{2,1,0:T(8,128)S(1)}, u32[]{:S(2)}, u32[]{:S(2)}) collective-permute-start(f32[8,32,160]{2,1,0:T(8,128)S(1)} %get-tuple-element.725), channel_id=1, source_target_pairs={{0,32},{32,64},{64,96},{96,128},{128,160},{160,192},{192,224},{1,3... | collective-permute-start | bytes 491528 | tf_op jit(solution)/shard_map/ppermute | solution.py:27
  380.8 8.2 %collective-permute-start.19 = (f32[8,32,160]{2,1,0:T(8,128)S(1)}, f32[8,32,160]{2,1,0:T(8,128)S(1)}, u32[]{:S(2)}, u32[]{:S(2)}) collective-permute-start(f32[8,32,160]{2,1,0:T(8,128)S(1)} %get-tuple-element.726), channel_id=1, source_target_pairs={{32,0},{64,32},{96,64},{128,96},{160,128},{192,160},{224,192},{33,... | collective-permute-start | bytes 491528 | tf_op jit(solution)/shard_map/ppermute | solution.py:28
  383.4 20.8 %copy-start.15 = (s32[1,2,2,1]{2,3,1,0:T(1,128)S(1)}, s32[1,2,2,1]{2,3,1,0:T(1,128)}, u32[]{:S(2)}) copy-start(s32[1,2,2,1]{2,3,1,0:T(1,128)} %get-tuple-element.785) | copy-start | bytes 52
  383.4 209.7 %collective-permute-start.2 = (f32[3,16,4,128]{3,2,1,0:T(4,128)}, f32[3,16,4,128]{3,2,1,0:T(4,128)}, u32[]{:S(2)}, u32[]{:S(2)}) collective-permute-start(f32[3,16,4,128]{3,2,1,0:T(4,128)} %get-tuple-element.742), channel_id=1, source_target_pairs={{8,0},{16,8},{24,16},{9,1},{17,9},{25,17},{10,2},{18,10},{26,18},{... | collective-permute-start | bytes 294920 | tf_op jit(solution)/shard_map/ppermute | solution.py:42
  384.9 210.5 %collective-permute-start.3 = (f32[3,16,4,128]{3,2,1,0:T(4,128)}, f32[3,16,4,128]{3,2,1,0:T(4,128)S(1)}, u32[]{:S(2)}, u32[]{:S(2)}) collective-permute-start(f32[3,16,4,128]{3,2,1,0:T(4,128)} %get-tuple-element.743), channel_id=1, source_target_pairs={{0,8},{8,16},{16,24},{1,9},{9,17},{17,25},{2,10},{10,18},{18,26},{... | collective-permute-start | bytes 294920 | tf_op jit(solution)/shard_map/ppermute | solution.py:41
  389.1 21.4 %copy-start.17 = (s32[4]{0:T(128)S(1)}, s32[4]{0:T(128)}, u32[]{:S(2)}) copy-start(s32[4]{0:T(128)} %get-tuple-element.1377) | copy-start | bytes 52
  389.1 21.4 %copy-start.18 = (s32[4]{0:T(128)S(1)}, s32[4]{0:T(128)}, u32[]{:S(2)}) copy-start(s32[4]{0:T(128)} %get-tuple-element.1376) | copy-start | bytes 52
  389.1 5.3 collective-permute-start.20
  392.5 5.7 collective-permute-start.21
  398.4 7.7 %collective-permute-start.22 = (f32[16,16,16]{2,1,0:T(8,128)S(1)}, f32[16,16,16]{2,1,0:T(8,128)S(1)}, u32[]{:S(2)}, u32[]{:S(2)}) collective-permute-start(f32[16,16,16]{2,1,0:T(8,128)S(1)} %get-tuple-element.748), channel_id=1, source_target_pairs={{0,1},{1,2},{2,3},{3,4},{4,5},{5,6},{6,7},{8,9},{9,10},{10,11},{11... | collective-permute-start | bytes 49160 | tf_op jit(solution)/shard_map/ppermute | solution.py:27
  402.8 7.4 %collective-permute-start.23 = (f32[16,16,16]{2,1,0:T(8,128)S(1)}, f32[16,16,16]{2,1,0:T(8,128)S(1)}, u32[]{:S(2)}, u32[]{:S(2)}) collective-permute-start(f32[16,16,16]{2,1,0:T(8,128)S(1)} %get-tuple-element.749), channel_id=1, source_target_pairs={{1,0},{2,1},{3,2},{4,3},{5,4},{6,5},{7,6},{9,8},{10,9},{11,10},{12... | collective-permute-start | bytes 49160 | tf_op jit(solution)/shard_map/ppermute | solution.py:28
  585.2 14.2 %collective-permute-start.24 = (f32[8,32,160]{2,1,0:T(8,128)S(1)}, f32[8,32,160]{2,1,0:T(8,128)S(1)}, u32[]{:S(2)}, u32[]{:S(2)}) collective-permute-start(f32[8,32,160]{2,1,0:T(8,128)S(1)} %get-tuple-element.723), channel_id=1, source_target_pairs={{0,32},{32,64},{64,96},{96,128},{128,160},{160,192},{192,224},{1,3... | collective-permute-start | bytes 491528 | tf_op jit(solution)/shard_map/ppermute | solution.py:27
  591.0 8.4 %collective-permute-start.25 = (f32[8,32,160]{2,1,0:T(8,128)S(1)}, f32[8,32,160]{2,1,0:T(8,128)S(1)}, u32[]{:S(2)}, u32[]{:S(2)}) collective-permute-start(f32[8,32,160]{2,1,0:T(8,128)S(1)} %get-tuple-element.724), channel_id=1, source_target_pairs={{32,0},{64,32},{96,64},{128,96},{160,128},{192,160},{224,192},{33,... | collective-permute-start | bytes 491528 | tf_op jit(solution)/shard_map/ppermute | solution.py:28
  593.2 19.0 %collective-permute-start.4 = (f32[3,16,16,4]{3,2,1,0:T(8,128)S(1)}, f32[3,16,16,4]{3,2,1,0:T(8,128)S(1)}, u32[]{:S(2)}, u32[]{:S(2)}) collective-permute-start(f32[3,16,16,4]{3,2,1,0:T(8,128)S(1)} %get-tuple-element.740), channel_id=1, source_target_pairs={{1,0},{2,1},{3,2},{4,3},{5,4},{6,5},{7,6},{9,8},{10,9},{11,10},{12... | collective-permute-start | bytes 36872 | tf_op jit(solution)/shard_map/ppermute | solution.py:42
  595.4 16.8 %collective-permute-start.5 = (f32[3,16,16,4]{3,2,1,0:T(8,128)S(1)}, f32[3,16,16,4]{3,2,1,0:T(8,128)S(1)}, u32[]{:S(2)}, u32[]{:S(2)}) collective-permute-start(f32[3,16,16,4]{3,2,1,0:T(8,128)S(1)} %get-tuple-element.741), channel_id=1, source_target_pairs={{0,1},{1,2},{2,3},{3,4},{4,5},{5,6},{6,7},{8,9},{9,10},{10,11},{11... | collective-permute-start | bytes 36872 | tf_op jit(solution)/shard_map/ppermute | solution.py:41
  599.6 4.3 collective-permute-start.26
  601.7 5.7 collective-permute-start.27
  607.5 5.7 collective-permute-start.28
  610.9 5.7 collective-permute-start.29
  612.2 4.5 copy-start.1
where the time goes:
time: 626 us; the launch traced here: 619 us
  local copies, waits for them, and re-layouts  267 us (43%)
  other arithmetic  138 us (22%)
  starting transfers between devices  81 us (13%)
  loops' own time  74.4 us (12%)
  waiting for transfers between devices  56.8 us (9%)
    dynamic_update_slice x32, local copies, waits for them, and re-layouts, add_block(): lax.dynamic_update_slice(accumulated, current + weight_z[a] * along_y, co...  126 us
    add x32, other arithmetic, add_block(): current + weight_z[a] * along_y  103 us
    gather x96, local copies, waits for them, and re-layouts  97.5 us
    another operation x2, loops' own time, spread_blocks(): return lax.fori_loop(0, values.shape[0], add_block, accumulated)  74 us
    ppermute x12, starting transfers between devices, with_halo(): before = lax.ppermute(last, axis, up)  45.5 us
    ppermute x12, waiting for transfers between devices, with_halo(): after = lax.ppermute(initial, axis, down)  35.9 us
    ppermute x12, waiting for transfers between devices, with_halo(): before = lax.ppermute(last, axis, up)  20.9 us
    add x8, other arithmetic, add_block(): sum((weight_x[a] * jnp.pad(block_vals, ((a, 3 - a), (0, 0), (0, 0))) for...  19.7 us
  transfers between devices with their start and end apart: 30, of which 14 were waited for; matrix products, arithmetic and copies ran while one was open for 65% of the time, Pallas kernels for 0%

commit v1 on v0

v1 whole, which is shorter than its diff:
```python
import jax
import jax.numpy as jnp
from jax import lax
from jax.experimental import pallas as pl
from jax.experimental.pallas import tpu as pltpu
from jax.sharding import PartitionSpec as P

F32 = jnp.float32
LAPLACE_TAPS = (-205.0 / 72.0, 8.0 / 5.0, -1.0 / 5.0, 8.0 / 315.0, -1.0 / 560.0)
STEP_SIZE = 0.5
REG_WEIGHT = 0.1
T = 16
L = 128
META = 48

Z_S0, Z_S1, Z_V, Z_META, Z_ROWS = 0, 64, 96, 144, 152
Y_S0, Y_M0, Y_S1, Y_M1, Y_V, Y_META, Y_ROWS = 0, 256, 384, 512, 544, 736, 744
X_S0, X_M0, X_S1, X_M1, X_V, X_META, X_ROWS = 0, 768, 1152, 1408, 1472, 1664, 1688
R_E, R_ROWS = 512, 640


def lanes(rows=8):
    return lax.broadcasted_iota(jnp.int32, (rows, L), 1)


def subs():
    return lax.broadcasted_iota(jnp.int32, (8, L), 0)


def roll(x, amount):
    amount = amount % L
    return x if amount == 0 else pltpu.roll(x, amount, 1)


def tap_weights(f):
    e = f * 0.125
    e2 = e * e
    e3 = e2 * e
    return [
        0.5 * (2.0 * e2 - e3 - e),
        0.5 * (3.0 * e3 - 5.0 * e2 + 2.0),
        0.5 * (4.0 * e2 - 3.0 * e3 + e),
        0.5 * (e3 - e2),
    ]


def block_numbers(meta, row, step, ix, iy):
    at = ((step * 2 + ix) * 2 + iy) * 6
    shift = [meta[row, at + d].astype(jnp.int32) for d in range(3)]
    weights = [tap_weights(meta[row, at + 3 + d]) for d in range(3)]
    return shift, weights


def sources_kernel(v, g, sx, sy, sz, fr, s0, s1, up, down):
    lane = lanes(T)
    for x in range(T):
        vel = [v[c, x] for c in range(3)]
        for k, s in ((0, s0), (1, s1)):
            total = g[k, 0, x].astype(F32) * vel[0]
            for c in (1, 2):
                total = total + g[k, c, x].astype(F32) * vel[c]
            s[x] = STEP_SIZE * total
    quarter = lane // 32
    for j in range(4):
        a, b, c, d = s0[j], roll(s0[j + 4], 32), roll(s0[j + 8], 64), roll(s0[j + 12], 96)
        rows = pl.ds(Z_S0 + j * T, T)
        up[rows] = jnp.where(quarter == 3, a, jnp.where(quarter == 1, c, jnp.where(quarter == 0, b, d)))
        down[rows] = jnp.where(quarter == 0, a, jnp.where(quarter == 2, c, jnp.where(quarter == 1, b, d)))
    eighth = lane // 16
    for h in range(2):
        u, d = s1[8 * h], s1[8 * h]
        for i in range(1, 8):
            r = roll(s1[8 * h + i], 16 * i)
            u = jnp.where(eighth == (7 + i) % 8, r, u)
            d = jnp.where(eighth == i, r, d)
        up[pl.ds(Z_S1 + h * T, T)] = u
        down[pl.ds(Z_S1 + h * T, T)] = d
    piece = lane // 8
    for c in range(3):
        u, d = v[c, 0], v[c, 0]
        for x in range(1, T):
            r = roll(v[c, x], 8 * x)
            u = jnp.where(piece == (15 + x) % 16, r, u)
            d = jnp.where(piece == x, r, d)
        up[pl.ds(Z_V + c * T, T)] = u
        down[pl.ds(Z_V + c * T, T)] = d
    lane = lanes()
    row = jnp.zeros((8, L), jnp.int32)
    for k in range(2):
        for ix in range(2):
            for iy in range(2):
                at = ((k * 2 + ix) * 2 + iy) * 6
                numbers = [sx[k, ix, iy, 0], sy[k, ix, iy, 0], sz[k, ix, iy, 0]]
                numbers += [fr[k, d, ix, iy, 0] for d in range(3)]
                for n, number in enumerate(numbers):
                    row = jnp.where(lane == at + n, number, row)
    up[pl.ds(Z_META, 8)] = row.astype(F32)
    down[pl.ds(Z_META, 8)] = row.astype(F32)


def y_message_kernel(s0, s1, v, own, low, high, up, down):
    lane = lanes(T)
    even = (lane // 32) % 2 == 0
    for x in range(T):
        for out in (up, down):
            out[pl.ds(Y_S0 + x * T, T)] = s0[x]
        up[pl.ds(Y_S1 + x * 8, 8)] = s1[x, 8:16]
        down[pl.ds(Y_S1 + x * 8, 8)] = s1[x, 0:8]
    for j in range(4):
        a, b = low[pl.ds(Z_S0 + j * T, T)], high[pl.ds(Z_S0 + j * T, T)]
        first = jnp.where(even, b, a)
        second = roll(jnp.where(even, a, b), -32)
        for out in (up, down):
            out[pl.ds(Y_M0 + j * T, T)] = first
            out[pl.ds(Y_M0 + (j + 4) * T, T)] = second
    even = (lane // 16) % 2 == 0
    for h in range(2):
        a, b = low[pl.ds(Z_S1 + h * T, T)], high[pl.ds(Z_S1 + h * T, T)]
        for j, value in enumerate((jnp.where(even, b, a), roll(jnp.where(even, a, b), -16))):
            up[pl.ds(Y_M1 + (h * 2 + j) * 8, 8)] = value[8:16]
            down[pl.ds(Y_M1 + (h * 2 + j) * 8, 8)] = value[0:8]
    first_half = subs() < 4
    for c in range(3):
        for x in range(8):
            rows = pl.ds(Y_V + (c * 8 + x) * 8, 8)
            up[rows] = jnp.where(first_half, pltpu.roll(v[c, x + 8, 8:16], 4, 0), v[c, x, 8:16])
            down[rows] = jnp.where(first_half, v[c, x, 0:8], pltpu.roll(v[c, x + 8, 0:8], 4, 0))
    sub = subs()
    meta = [ref[pl.ds(Z_META, 8)] for ref in (low, own, high)]
    row = jnp.where(sub == 0, meta[0], jnp.where(sub == 1, meta[1], meta[2]))
    up[pl.ds(Y_META, 8)] = row
    down[pl.ds(Y_META, 8)] = row


def x_message_kernel(own_up, own_down, low, high, v, up, down):
    for n, (start, planes, to) in enumerate(((Y_S0, T, X_S0), (Y_M0, 8, X_M0))):
        for x in range(planes):
            for at, ref in enumerate((low, own_up, high)):
                value = ref[pl.ds(start + x * T, T)]
                for out in (up, down):
                    out[pl.ds(to + x * 48 + at * T, T)] = value
    for h, out in ((1, up), (0, down)):
        for x in range(8):
            for at, ref in enumerate((low, own_down, own_up, high)):
                out[pl.ds(X_S1 + x * 32 + at * 8, 8)] = ref[pl.ds(Y_S1 + (8 * h + x) * 8, 8)]
        for j in range(2):
            for at, ref in enumerate((low, own_down, own_up, high)):
                out[pl.ds(X_M1 + j * 32 + at * 8, 8)] = ref[pl.ds(Y_M1 + (h * 2 + j) * 8, 8)]
        for c in range(3):
            for i in range(4):
                out[pl.ds(X_V + (c * 4 + i) * T, T)] = v[c, 12 * h + i]
        for at, ref in enumerate((low, own_up, high)):
            out[pl.ds(X_META + at * 8, 8)] = ref[pl.ds(Y_META, 8)]


def gather_xy(ref, x0, y0, wx, wy):
    planes = []
    for i in range(11):
        plane = wy[0] * ref[x0 + i, pl.ds(y0, 8), :]
        for t in range(1, 4):
            plane = plane + wy[t] * ref[x0 + i, pl.ds(y0 + t, 8), :]
        planes.append(plane)
    out = []
    for i in range(8):
        value = wx[0] * planes[i]
        for t in range(1, 4):
            value = value + wx[t] * planes[i + t]
        out.append(value)
    return out


def scatter_xy(ref, vals, x0, y0, wx, wy):
    sub = subs()
    low_w = [jnp.where(sub >= t, wy[t], 0.0) for t in range(4)]
    high_w = [jnp.where(sub < t, wy[t], 0.0) for t in range(4)]
    pairs = []
    for value in vals:
        first, second = wy[0] * value, None
        for t in range(1, 4):
            turned = pltpu.roll(value, t, 0)
            first = first + low_w[t] * turned
            second = high_w[t] * turned if second is None else second + high_w[t] * turned
        pairs.append((first, second))
    for p in range(11):
        for half in range(2):
            total = None
            for t in range(4):
                if 0 <= p - t < 8:
                    term = wx[t] * pairs[p - t][half]
                    total = term if total is None else total + term
            rows = pl.ds(y0 + 8 * half, 8)
            ref[x0 + p, rows, :] = ref[x0 + p, rows, :] + total


def block_of(b):
    return (b + 1) // 2, (b + 1) % 2


def steps_kernel(own_up, own_down, low, high, ra, up, down, clo, chi, a1, e1, re, meta, sem):
    lane = lanes()
    upper = lane >= 64
    copies = []
    for n, ref in enumerate((low, own_up, high)):
        copy = pltpu.make_async_copy(ref.at[pl.ds(X_META, 24)], meta.at[pl.ds(n * 24, 24)], sem.at[n])
        copy.start()
        copies.append(copy)
    upper48 = lanes(48) >= 64
    for n, ref in enumerate((low, own_up, high)):

        def assemble(x, _, n=n, ref=ref):
            m = ref[pl.ds(pl.multiple_of(X_M0 + x * 48, 8), 48)]
            for half, e in ((0, m), (1, roll(m, 64))):
                a = ref[pl.ds(pl.multiple_of(X_S0 + (x + 8 * half) * 48, 8), 48)]
                clo[n * T + 8 * half + x] = jnp.where(upper48, e, a)
                chi[n * T + 8 * half + x] = jnp.where(upper48, a, e)
            return 0

        lax.fori_loop(0, 8, assemble, 0)
    for n, ref in enumerate((low, own_down, own_up, high)):
        for x in range(8):
            a1[n * 8 + x] = ref[pl.ds(X_S1 + x * 32, 32)]
            e1[n * 8 + x] = roll(ref[pl.ds(X_M1 + (x % 2) * 32, 32)], -32 * (x // 2))
    ra[...] = jnp.zeros(ra.shape, F32)
    re[...] = jnp.zeros(re.shape, F32)
    for copy in copies:
        copy.wait()

    def first_step(i, _):
        bx, by = i // 4, i % 4
        (slot_x, ix), (slot_y, iy) = block_of(bx), block_of(by)
        row = slot_x * 24 + slot_y * 8
        edges = []
        for n, ref in ((0, clo), (2, chi)):
            (a, b, c), (wx, wy, wz) = block_numbers(meta, row + n, 0, ix, iy)
            values = gather_xy(ref, bx * 8 + 7 + a, by * 8 + 7 + b, wx, wy)
            turns = [(1 - c - t) & 127 for t in range(4)]
            edges.append([sum(wz[t] * pltpu.roll(value, turns[t], 1) for t in range(4)) for value in values])
        (a, b, c), (wx, wy, wz) = block_numbers(meta, row + 1, 0, ix, iy)
        x0, y0 = bx * 8 + 7 + a, by * 8 + 7 + b
        lows = gather_xy(clo, x0, y0, wx, wy)
        highs = gather_xy(chi, x0, y0, wx, wy)
        masks = [jnp.logical_xor(((lane - (c + t - 1)) & -128) == 0, upper) for t in range(4)]
        turns = [(1 - c - t) & 127 for t in range(4)]
        rows = pl.ds(pl.multiple_of(by * 8, 8), 8)
        for p in range(8):
            value = sum(wz[t] * pltpu.roll(jnp.where(masks[t], lows[p], highs[p]), turns[t], 1) for t in range(4))
            x = bx * 8 + p
            a1[x, rows, :] = a1[x, rows, :] + value
            e1[x, rows, :] = e1[x, rows, :] + jnp.where(upper, edges[0][p], edges[1][p])
        return 0

    lax.fori_loop(0, 16, first_step, 0)

    def second_step(i, _):
        ix, iy = i // 2, i % 2
        (a, b, c), (wx, wy, wz) = block_numbers(meta, 24 + 8 + 1, 1, ix, iy)
        x0, y0 = ix * 8 + 7 + a, iy * 8 + 7 + b
        inner = gather_xy(a1, x0, y0, wx, wy)
        outer = gather_xy(e1, x0, y0, wx, wy)
        masks = [((lane - (c + t - 1)) & -128) == 0 for t in range(4)]
        turns = [(1 - c - t) & 127 for t in range(4)]
        back = [(c + t - 1) & 127 for t in range(4)]
        in_w = [jnp.where(masks[t], wz[t], 0.0) for t in range(4)]
        out_w = [jnp.where(masks[t], 0.0, wz[t]) for t in range(4)]
        to_a, to_e = [], []
        for p in range(8):
            state = sum(wz[t] * pltpu.roll(jnp.where(masks[t], inner[p], outer[p]), turns[t], 1) for t in range(4))
            turned = [pltpu.roll(state, back[t], 1) for t in range(4)]
            to_a.append(sum(in_w[t] * turned[t] for t in range(4)))
            to_e.append(sum(out_w[t] * turned[t] for t in range(4)))
        scatter_xy(ra, to_a, x0, y0, wx, wy)
        scatter_xy(re, to_e, x0, y0, wx, wy)
        return 0

    lax.fori_loop(0, 4, second_step, 0)

    wide = lanes(32)
    quarter = ((wide + 16) & 127) // 32
    for h in range(2):
        for x in range(4):
            u, d = None, None
            for g in range(4):
                a, e = ra[16 * h + 4 * g + x, 0:32], re[16 * h + 4 * g + x, 0:32]
                rise = roll(jnp.where(wide >= 64, a, e), 32 * g)
                fall = roll(jnp.where(wide >= 64, e, a), 32 * g)
                u = rise if g == 0 else jnp.where(quarter == g, rise, u)
                d = fall if g == 0 else jnp.where(quarter == g, fall, d)
            up[h * 4 + x] = u
            down[h * 4 + x] = d


def sum_z_kernel(ra, own_up, own_down, low, high, up, down):
    wide = lanes(32)
    even = (wide // 16) % 2 == 0
    valid = (wide < 16) | (wide >= 112)
    for h in range(2):
        for x in range(4):
            a, b = low[h * 4 + x], high[h * 4 + x]
            inner = jnp.where(even, a, b)
            outer = jnp.where(even, own_up[h * 4 + x], own_down[h * 4 + x]) + jnp.where(even, b, a)
            down[pl.ds(R_E + (h * 4 + x) * T, T)] = outer[0:16]
            up[pl.ds(R_E + (h * 4 + x) * T, T)] = outer[16:32]
            for g in range(4):
                at = 16 * h + 4 * g + x
                value = ra[at, 0:32] + jnp.where(valid, roll(inner, -32 * g), 0.0)
                down[pl.ds(at * T, T)] = value[0:16]
                up[pl.ds(at * T, T)] = value[16:32]


def sum_y_kernel(own_up, own_down, low, high, up, down):
    for h, out in ((0, down), (1, up)):
        for start, planes in ((0, 16), (R_E, 4)):
            for x in range(planes):
                rows = pl.ds(start + (h * planes + x) * T, T)
                out[pl.ds(start + x * 32, T)] = own_down[rows] + low[rows]
                out[pl.ds(start + x * 32 + T, T)] = own_up[rows] + high[rows]


def last_step_kernel(own_up, own_down, low, high, meta_low, meta_own, meta_high, g, reg, out, a1, e1, acc, meta, sem):
    copies = []
    for n, ref in enumerate((meta_low, meta_own, meta_high)):
        copy = pltpu.make_async_copy(ref.at[pl.ds(X_META, 24)], meta.at[pl.ds(n * 24, 24)], sem.at[n])
        copy.start()
        copies.append(copy)
    wide = lanes(32)
    valid = (wide < 16) | (wide >= 112)
    for h, (mine, other) in enumerate(((own_down, low), (own_up, high))):
        for x in range(16):
            rows = pl.ds(x * 32, 32)
            a1[16 * h + x] = mine[rows] + other[rows]
        for x in range(4):
            rows = pl.ds(R_E + x * 32, 32)
            packed = mine[rows] + other[rows]
            for q in range(4):
                e1[16 * h + 4 * q + x] = jnp.where(valid, roll(packed, -32 * q), 0.0)
    acc[...] = jnp.zeros(acc.shape, F32)
    for copy in copies:
        copy.wait()
    lane = lanes()
    upper = lane >= 64

    def step(i, _):
        bx, by = i // 4, i % 4
        (slot_x, ix), (slot_y, iy) = block_of(bx), block_of(by)
        row = slot_x * 24 + slot_y * 8
        rows = pl.ds(pl.multiple_of(by * 8, 8), 8)
        inner = [a1[bx * 8 + p, rows, :] for p in range(8)]
        outer = [e1[bx * 8 + p, rows, :] for p in range(8)]
        for n in range(3):
            (a, b, c), (wx, wy, wz) = block_numbers(meta, row + n, 0, ix, iy)
            back = [(c + t - 1) & 127 for t in range(4)]
            if n == 1:
                w = [jnp.where(((lane - (c + t - 1)) & -128) == 0, wz[t], 0.0) for t in range(4)]
                values = inner
            else:
                keep = upper if n == 2 else jnp.logical_not(upper)
                w = [jnp.where(keep, wz[t], 0.0) for t in range(4)]
                values = [jnp.where(upper if n == 0 else jnp.logical_not(upper), value, 0.0) for value in outer]
            moved = [sum(w[t] * pltpu.roll(value, back[t], 1) for t in range(4)) for value in values]
            scatter_xy(acc, moved, bx * 8 + 7 + a, by * 8 + 7 + b, wx, wy)
        return 0

    lax.fori_loop(0, 16, step, 0)
    for x in range(T):
        first, second = acc[16 + x, 16:32], a1[8 + x, 8:24]
        for c in range(3):
            out[c, x] = reg[c, x] + STEP_SIZE * (g[1, c, x].astype(F32) * second + g[0, c, x].astype(F32) * first)


def laplace_kernel(v, zlow, zhigh, ylow, yhigh, xlow, xhigh, out, w):
    lane = lanes(T)
    half = (lane & 4) == 0
    sides = [-REG_WEIGHT * t for t in LAPLACE_TAPS]
    for c in range(3):
        rows = pl.ds(Z_V + c * T, T)
        faces = jnp.where(half, zhigh[rows], zlow[rows])
        for i in range(4):
            rows = pl.ds(X_V + (c * 4 + i) * T, T)
            w[i, 8:24] = xlow[rows]
            w[20 + i, 8:24] = xhigh[rows]
        for x in range(8):
            rows = pl.ds(Y_V + (c * 8 + x) * 8, 8)
            a, b = ylow[rows], yhigh[rows]
            w[4 + x, 0:8] = a
            w[12 + x, 0:8] = pltpu.roll(a, 4, 0)
            w[4 + x, 24:32] = b
            w[12 + x, 24:32] = pltpu.roll(b, 4, 0)
        for x in range(T):
            w[4 + x, 8:24] = v[c, x]
        for x in range(T):
            here = v[c, x]
            edge = roll(faces, -8 * x)
            total = 3.0 * sides[0] * here
            for k in range(1, 5):
                near = roll(jnp.where(lane < k, edge, here), -k) + roll(jnp.where(lane >= L - k, edge, here), k)
                near = near + w[4 + x - k, 8:24] + w[4 + x + k, 8:24]
                near = near + w[4 + x, 8 - k : 24 - k] + w[4 + x, 8 + k : 24 + k]
                total = total + sides[k] * near
            out[c, x] = total


VMEM = pl.BlockSpec(memory_space=pltpu.VMEM)
SMEM = pl.BlockSpec(memory_space=pltpu.SMEM)


def call(kernel, args, outs, scratch=(), smem=(), cost=20000):
    specs = [SMEM if i in smem else VMEM for i in range(len(args))]
    shapes = [jax.ShapeDtypeStruct(s, F32) for s in outs]
    return pl.pallas_call(
        kernel,
        out_shape=shapes,
        in_specs=specs,
        out_specs=[VMEM] * len(shapes),
        scratch_shapes=list(scratch),
        compiler_params=pltpu.CompilerParams(vmem_limit_bytes=24 * 1024 * 1024),
        cost_estimate=pl.CostEstimate(flops=cost, bytes_accessed=cost, transcendentals=0),
    )(*args)


def exchange(up, down, axis):
    n = lax.axis_size(axis)
    rise = [(i, i + 1) for i in range(n - 1)]
    fall = [(j, i) for i, j in rise]
    return lax.ppermute(up, axis, rise), lax.ppermute(down, axis, fall)


def body(velocity, gradients, shift_x, shift_y, shift_z, fractions):
    v, g = velocity, gradients
    tile = (T, T, L)
    s0, s1, zup, zdown = call(
        sources_kernel,
        (v, g, shift_x, shift_y, shift_z, fractions),
        [tile, tile, (Z_ROWS, L), (Z_ROWS, L)],
        smem=(2, 3, 4, 5),
    )
    zlow, zhigh = exchange(zup, zdown, "gz")
    yup, ydown = call(y_message_kernel, (s0, s1, v, zup, zlow, zhigh), [(Y_ROWS, L)] * 2)
    ylow, yhigh = exchange(yup, ydown, "gy")
    xup, xdown = call(x_message_kernel, (yup, ydown, ylow, yhigh, v), [(X_ROWS, L)] * 2)
    xlow, xhigh = exchange(xup, xdown, "gx")
    meta = [pltpu.SMEM((72, L), F32), pltpu.SemaphoreType.DMA((3,))]
    vm = lambda *s: pltpu.VMEM(s, F32)
    ra, zup, zdown = call(
        steps_kernel,
        (xup, xdown, xlow, xhigh),
        [(32, 40, L), (8, 32, L), (8, 32, L)],
        scratch=[vm(48, 48, L), vm(48, 48, L), vm(32, 32, L), vm(32, 32, L), vm(32, 40, L)] + meta,
    )
    (reg,) = call(
        laplace_kernel, (v, zlow, zhigh, ylow, yhigh, xlow, xhigh), [v.shape], scratch=[vm(24, 32, L)], cost=4000000
    )
    low, high = exchange(zup, zdown, "gz")
    up, down = call(sum_z_kernel, (ra, zup, zdown, low, high), [(R_ROWS, L)] * 2)
    low, high = exchange(up, down, "gy")
    up, down = call(sum_y_kernel, (up, down, low, high), [(R_ROWS, L)] * 2)
    low, high = exchange(up, down, "gx")
    (out,) = call(
        last_step_kernel,
        (up, down, low, high, xlow, xup, xhigh, g, reg),
        [v.shape],
        scratch=[vm(32, 32, L), vm(32, 32, L), vm(48, 56, L)] + meta,
    )
    return out


def solution(mesh):
    in_specs = (
        P(None, "gx", "gy", "gz"),
        P(None, None, "gx", "gy", "gz"),
        P(None, "gx", "gy", "gz"),
        P(None, "gx", "gy", "gz"),
        P(None, "gx", "gy", "gz"),
        P(None, None, "gx", "gy", "gz"),
    )
    out_specs = P(None, "gx", "gy", "gz")
    return jax.shard_map(body, mesh=mesh, in_specs=in_specs, out_specs=out_specs, check_vma=False)
```

time: 626 us -> 97.7 us (0.16)
  the two profiles are of different devices: /device:TPU:1 before, /device:TPU:97 now
where the time goes in v1:
time: 97.7 us; the launch traced here: 97.2 us
  starting transfers between devices  39.7 us (41%)
  waiting for transfers between devices  34.5 us (35%)
  Pallas kernels  18.5 us (19%)
  local copies, waits for them, and re-layouts  4.31 us (4%)
    ppermute x12, starting transfers between devices, exchange(): return (lax.ppermute(up, axis, rise), lax.ppermute(down, axis, fall))  39.7 us
    ppermute x12, waiting for transfers between devices, exchange(): return (lax.ppermute(up, axis, rise), lax.ppermute(down, axis, fall))  34.5 us
    pallas_call x8, Pallas kernels, call(): pl.pallas_call(kernel, out_shape=shapes, in_specs=specs, out_specs=[VMEM]...  18.5 us
    unnamed x18, local copies, waits for them, and re-layouts  4.31 us
  transfers between devices with their start and end apart: 12, of which 9 were waited for; matrix products, arithmetic and copies ran while one was open for 0% of the time, Pallas kernels for 4%

profile of v1, /device:TPU:97, one launch (start us, length us, event | category | flops | bytes accessed | tf_op | source)
XLA Modules:
  0.0 97.2 jit_solution(3807221624648029493)
XLA Ops:
  0.0 0.0 copy-start.5
  0.0 0.8 copy.7.sx
  0.8 0.0 copy-done.5
  0.8 0.0 copy-start.6
  0.8 0.1 copy.8.sy
  0.9 0.6 copy-done.6
  1.5 0.0 copy-start.4
  1.5 0.1 copy.9.sz
  1.6 0.6 copy-done.4
  2.2 0.1 copy.10.fr
  2.3 0.0 copy-start
  2.3 1.0 %copy-done = f32[3,16,16,128]{3,2,1,0:T(8,128)S(1)} copy-done((f32[3,16,16,128]{3,2,1,0:T(8,128)S(1)}, f32[3,16,16,128]{3,2,1,0:T(8,128)}, u32[]{:S(2)}) %copy-start) | copy-done | bytes 393240
  3.3 0.0 copy-start.2
  3.3 1.0 %copy-done.2 = bf16[2,3,16,16,128]{4,3,2,1,0:T(8,128)(2,1)S(1)} copy-done((bf16[2,3,16,16,128]{4,3,2,1,0:T(8,128)(2,1)S(1)}, bf16[2,3,16,16,128]{4,3,2,1,0:T(8,128)(2,1)}, u32[]{:S(2)}) %copy-start.2) | copy-done | bytes 393240
  4.3 1.2 %shard_map.64 = (f32[16,16,128]{2,1,0:T(8,128)S(1)}, f32[16,16,128]{2,1,0:T(8,128)S(1)}, f32[152,128]{1,0:T(8,128)S(1)}, f32[152,128]{1,0:T(8,128)S(1)}) custom-call(f32[3,16,16,128]{3,2,1,0:T(8,128)S(1)} %copy-done, bf16[2,3,16,16,128]{4,3,2,1,0:T(8,128)(2,1)S(1)} %copy-done.2, s32[2,2,2,1]{3,2,1,0:T(2,128)S(1)} %copy.7.sx, s32[2,2,2,1]{3,2,1,0:T(2,128)S(1)} %copy.8.sy, ...), custom_call_target="tpu_custom_call" | custom-call | flops 20000 | bytes 20000 | tf_op jit(solution)/shard_map/pallas_call | solution.py:409
  5.5 1.9 %collective-permute-start.1 = (f32[152,128]{1,0:T(8,128)S(1)}, f32[152,128]{1,0:T(8,128)S(1)}, u32[]{:S(2)}, u32[]{:S(2)}) collective-permute-start(f32[152,128]{1,0:T(8,128)S(1)} %get-tuple-element.23), channel_id=1, source_target_pairs={{1,0},{2,1},{3,2},{4,3},{5,4},{6,5},{7,6},{9,8},{10,9},{11,10},{12... | collective-permute-start | bytes 233480 | tf_op jit(solution)/shard_map/ppermute | solution.py:424
  7.4 4.8 %collective-permute-start = (f32[152,128]{1,0:T(8,128)S(1)}, f32[152,128]{1,0:T(8,128)S(1)}, u32[]{:S(2)}, u32[]{:S(2)}) collective-permute-start(f32[152,128]{1,0:T(8,128)S(1)} %get-tuple-element.22.own), channel_id=1, source_target_pairs={{0,1},{1,2},{2,3},{3,4},{4,5},{5,6},{6,7},{8,9},{9,10},{10,11},{11... | collective-permute-start | bytes 233480 | tf_op jit(solution)/shard_map/ppermute | solution.py:424
  12.2 0.0 collective-permute-done.1.high.zhigh
  12.2 1.4 %collective-permute-done.low.zlow = f32[152,128]{1,0:T(8,128)S(1)} collective-permute-done((f32[152,128]{1,0:T(8,128)S(1)}, f32[152,128]{1,0:T(8,128)S(1)}, u32[]{:S(2)}, u32[]{:S(2)}) %collective-permute-start) | collective-permute-done | bytes 77856 | tf_op jit(solution)/shard_map/ppermute | solution.py:424
  13.6 0.1 shard_map.65
  13.7 3.2 %collective-permute-start.2 = (f32[744,128]{1,0:T(8,128)S(1)}, f32[744,128]{1,0:T(8,128)S(1)}, u32[]{:S(2)}, u32[]{:S(2)}) collective-permute-start(f32[744,128]{1,0:T(8,128)S(1)} %get-tuple-element.24.own_up), channel_id=1, source_target_pairs={{0,8},{8,16},{16,24},{1,9},{9,17},{17,25},{2,10},{10,18},{18,26},{... | collective-permute-start | bytes 1142792 | tf_op jit(solution)/shard_map/ppermute | solution.py:424
  16.9 1.3 %collective-permute-start.3 = (f32[744,128]{1,0:T(8,128)S(1)}, f32[744,128]{1,0:T(8,128)S(1)}, u32[]{:S(2)}, u32[]{:S(2)}) collective-permute-start(f32[744,128]{1,0:T(8,128)S(1)} %get-tuple-element.25.own_down), channel_id=1, source_target_pairs={{8,0},{16,8},{24,16},{9,1},{17,9},{25,17},{10,2},{18,10},{26,18},{... | collective-permute-start | bytes 1142792 | tf_op jit(solution)/shard_map/ppermute | solution.py:424
  18.2 5.2 %collective-permute-done.2.low.ylow = f32[744,128]{1,0:T(8,128)S(1)} collective-permute-done((f32[744,128]{1,0:T(8,128)S(1)}, f32[744,128]{1,0:T(8,128)S(1)}, u32[]{:S(2)}, u32[]{:S(2)}) %collective-permute-start.2) | collective-permute-done | bytes 380960 | tf_op jit(solution)/shard_map/ppermute | solution.py:424
  23.4 3.9 %collective-permute-done.3.high.yhigh = f32[744,128]{1,0:T(8,128)S(1)} collective-permute-done((f32[744,128]{1,0:T(8,128)S(1)}, f32[744,128]{1,0:T(8,128)S(1)}, u32[]{:S(2)}, u32[]{:S(2)}) %collective-permute-start.3) | collective-permute-done | bytes 380960 | tf_op jit(solution)/shard_map/ppermute | solution.py:424
  27.3 0.1 shard_map.66
  27.4 4.7 %collective-permute-start.5 = (f32[1688,128]{1,0:T(8,128)S(1)}, f32[1688,128]{1,0:T(8,128)S(1)}, u32[]{:S(2)}, u32[]{:S(2)}) collective-permute-start(f32[1688,128]{1,0:T(8,128)S(1)} %get-tuple-element.27.own_down), channel_id=1, source_target_pairs={{32,0},{64,32},{96,64},{128,96},{160,128},{192,160},{224,192},{33,... | collective-permute-start | bytes 2592776 | tf_op jit(solution)/shard_map/ppermute | solution.py:424
  32.1 3.0 %collective-permute-start.4 = (f32[1688,128]{1,0:T(8,128)S(1)}, f32[1688,128]{1,0:T(8,128)S(1)}, u32[]{:S(2)}, u32[]{:S(2)}) collective-permute-start(f32[1688,128]{1,0:T(8,128)S(1)} %get-tuple-element.26.own_up.meta_own), channel_id=1, source_target_pairs={{0,32},{32,64},{64,96},{96,128},{128,160},{160,192},{192,224},{1,3... | collective-permute-start | bytes 2592776 | tf_op jit(solution)/shard_map/ppermute | solution.py:424
  35.1 8.6 %collective-permute-done.5.high.xhigh.meta_high = f32[1688,128]{1,0:T(8,128)S(1)} collective-permute-done((f32[1688,128]{1,0:T(8,128)S(1)}, f32[1688,128]{1,0:T(8,128)S(1)}, u32[]{:S(2)}, u32[]{:S(2)}) %collective-permute-start.5) | collective-permute-done | bytes 864288 | tf_op jit(solution)/shard_map/ppermute | solution.py:424
  43.7 1.2 %collective-permute-done.4.low.xlow.meta_low = f32[1688,128]{1,0:T(8,128)S(1)} collective-permute-done((f32[1688,128]{1,0:T(8,128)S(1)}, f32[1688,128]{1,0:T(8,128)S(1)}, u32[]{:S(2)}, u32[]{:S(2)}) %collective-permute-start.4) | collective-permute-done | bytes 864288 | tf_op jit(solution)/shard_map/ppermute | solution.py:424
  44.9 7.2 %shard_map.67 = (f32[32,40,128]{2,1,0:T(8,128)S(1)}, f32[8,32,128]{2,1,0:T(8,128)S(1)}, f32[8,32,128]{2,1,0:T(8,128)S(1)}) custom-call(f32[1688,128]{1,0:T(8,128)S(1)} %get-tuple-element.26.own_up.meta_own, f32[1688,128]{1,0:T(8,128)S(1)} %get-tuple-element.27.own_down, f32[1688,128]{1,0:T(8,128)S(1)} %collective-permute-done.4.low.xlow.meta_low, ...), custom_call_target="tpu_custom_call" | custom-call | flops 20000 | bytes 20000 | tf_op jit(solution)/shard_map/pallas_call | solution.py:409
  52.1 4.9 %collective-permute-start.6 = (f32[8,32,128]{2,1,0:T(8,128)S(1)}, f32[8,32,128]{2,1,0:T(8,128)S(1)}, u32[]{:S(2)}, u32[]{:S(2)}) collective-permute-start(f32[8,32,128]{2,1,0:T(8,128)S(1)} %get-tuple-element.29.own_up), channel_id=1, source_target_pairs={{0,1},{1,2},{2,3},{3,4},{4,5},{5,6},{6,7},{8,9},{9,10},{10,11},{11... | collective-permute-start | bytes 393224 | tf_op jit(solution)/shard_map/ppermute | solution.py:424
  57.0 1.9 %collective-permute-start.7 = (f32[8,32,128]{2,1,0:T(8,128)S(1)}, f32[8,32,128]{2,1,0:T(8,128)S(1)}, u32[]{:S(2)}, u32[]{:S(2)}) collective-permute-start(f32[8,32,128]{2,1,0:T(8,128)S(1)} %get-tuple-element.30.own_down), channel_id=1, source_target_pairs={{1,0},{2,1},{3,2},{4,3},{5,4},{6,5},{7,6},{9,8},{10,9},{11,10},{12... | collective-permute-start | bytes 393224 | tf_op jit(solution)/shard_map/ppermute | solution.py:424
  59.0 0.0 collective-permute-done.6.low
  59.0 5.0 %collective-permute-done.7.high = f32[8,32,128]{2,1,0:T(8,128)S(1)} collective-permute-done((f32[8,32,128]{2,1,0:T(8,128)S(1)}, f32[8,32,128]{2,1,0:T(8,128)S(1)}, u32[]{:S(2)}, u32[]{:S(2)}) %collective-permute-start.7) | collective-permute-done | bytes 131104 | tf_op jit(solution)/shard_map/ppermute | solution.py:424
  64.0 0.2 shard_map.68
  64.2 3.2 %collective-permute-start.8 = (f32[640,128]{1,0:T(8,128)S(1)}, f32[640,128]{1,0:T(8,128)S(1)}, u32[]{:S(2)}, u32[]{:S(2)}) collective-permute-start(f32[640,128]{1,0:T(8,128)S(1)} %get-tuple-element.31.own_up), channel_id=1, source_target_pairs={{0,8},{8,16},{16,24},{1,9},{9,17},{17,25},{2,10},{10,18},{18,26},{... | collective-permute-start | bytes 983048 | tf_op jit(solution)/shard_map/ppermute | solution.py:424
  67.4 0.0 copy-start.1
  67.4 1.4 %collective-permute-start.9 = (f32[640,128]{1,0:T(8,128)S(1)}, f32[640,128]{1,0:T(8,128)S(1)}, u32[]{:S(2)}, u32[]{:S(2)}) collective-permute-start(f32[640,128]{1,0:T(8,128)S(1)} %get-tuple-element.32.own_down), channel_id=1, source_target_pairs={{8,0},{16,8},{24,16},{9,1},{17,9},{25,17},{10,2},{18,10},{26,18},{... | collective-permute-start | bytes 983048 | tf_op jit(solution)/shard_map/ppermute | solution.py:424
  68.8 2.5 %collective-permute-done.8.low = f32[640,128]{1,0:T(8,128)S(1)} collective-permute-done((f32[640,128]{1,0:T(8,128)S(1)}, f32[640,128]{1,0:T(8,128)S(1)}, u32[]{:S(2)}, u32[]{:S(2)}) %collective-permute-start.8) | collective-permute-done | bytes 327712 | tf_op jit(solution)/shard_map/ppermute | solution.py:424
  71.4 4.0 %collective-permute-done.9.high = f32[640,128]{1,0:T(8,128)S(1)} collective-permute-done((f32[640,128]{1,0:T(8,128)S(1)}, f32[640,128]{1,0:T(8,128)S(1)}, u32[]{:S(2)}, u32[]{:S(2)}) %collective-permute-start.9) | collective-permute-done | bytes 327712 | tf_op jit(solution)/shard_map/ppermute | solution.py:424
  75.3 0.1 shard_map.69
  75.4 7.3 %collective-permute-start.10 = (f32[640,128]{1,0:T(8,128)S(1)}, f32[640,128]{1,0:T(8,128)S(1)}, u32[]{:S(2)}, u32[]{:S(2)}) collective-permute-start(f32[640,128]{1,0:T(8,128)S(1)} %get-tuple-element.33.own_up), channel_id=1, source_target_pairs={{0,32},{32,64},{64,96},{96,128},{128,160},{160,192},{192,224},{1,3... | collective-permute-start | bytes 983048 | tf_op jit(solution)/shard_map/ppermute | solution.py:424
  82.7 0.0 copy-start.3
  82.7 2.1 %collective-permute-start.11 = (f32[640,128]{1,0:T(8,128)S(1)}, f32[640,128]{1,0:T(8,128)S(1)}, u32[]{:S(2)}, u32[]{:S(2)}) collective-permute-start(f32[640,128]{1,0:T(8,128)S(1)} %get-tuple-element.34.own_down), channel_id=1, source_target_pairs={{32,0},{64,32},{96,64},{128,96},{160,128},{192,160},{224,192},{33,... | collective-permute-start | bytes 983048 | tf_op jit(solution)/shard_map/ppermute | solution.py:424
  84.8 0.0 copy-done.1
  84.8 3.6 %shard_map.70.reg = f32[3,16,16,128]{3,2,1,0:T(8,128)S(1)} custom-call(f32[3,16,16,128]{3,2,1,0:T(8,128)S(1)} %copy-done.1, f32[152,128]{1,0:T(8,128)S(1)} %collective-permute-done.low.zlow, f32[152,128]{1,0:T(8,128)S(1)} %collective-permute-done.1.high.zhigh, f32[744,128]{1,0:T(8,128)S(1)} %collective-permute-done.2.low.ylow, ...), custom_call_target="tpu_custom_call" | custom-call | flops 4000000 | bytes 4000000 | tf_op jit(solution)/shard_map/pallas_call | solution.py:409
  88.4 0.0 collective-permute-done.10.low
  88.4 2.8 %collective-permute-done.11.high = f32[640,128]{1,0:T(8,128)S(1)} collective-permute-done((f32[640,128]{1,0:T(8,128)S(1)}, f32[640,128]{1,0:T(8,128)S(1)}, u32[]{:S(2)}, u32[]{:S(2)}) %collective-permute-start.11) | collective-permute-done | bytes 327712 | tf_op jit(solution)/shard_map/ppermute | solution.py:424
  91.2 0.0 copy-done.3
  91.2 5.9 %shard_map.71 = f32[3,16,16,128]{3,2,1,0:T(8,128)} custom-call(f32[640,128]{1,0:T(8,128)S(1)} %get-tuple-element.33.own_up, f32[640,128]{1,0:T(8,128)S(1)} %get-tuple-element.34.own_down, f32[640,128]{1,0:T(8,128)S(1)} %collective-permute-done.10.low, f32[640,128]{1,0:T(8,128)S(1)} %collective-permute-done.11.high, ...), custom_call_target="tpu_custom_call" | custom-call | flops 20000 | bytes 20000 | tf_op jit(solution)/shard_map/pallas_call | solution.py:409
Async XLA Ops:
  0.0 0.8 copy-start.5
  0.8 0.7 copy-start.6
  1.5 0.7 copy-start.4
  2.3 1.0 %copy-start = (f32[3,16,16,128]{3,2,1,0:T(8,128)S(1)}, f32[3,16,16,128]{3,2,1,0:T(8,128)}, u32[]{:S(2)}) copy-start(f32[3,16,16,128]{3,2,1,0:T(8,128)} %v.7) | copy-start | bytes 1179652
  3.3 1.0 %copy-start.2 = (bf16[2,3,16,16,128]{4,3,2,1,0:T(8,128)(2,1)S(1)}, bf16[2,3,16,16,128]{4,3,2,1,0:T(8,128)(2,1)}, u32[]{:S(2)}) copy-start(bf16[2,3,16,16,128]{4,3,2,1,0:T(8,128)(2,1)} %g.3) | copy-start | bytes 1179652
  5.5 6.7 %collective-permute-start.1 = (f32[152,128]{1,0:T(8,128)S(1)}, f32[152,128]{1,0:T(8,128)S(1)}, u32[]{:S(2)}, u32[]{:S(2)}) collective-permute-start(f32[152,128]{1,0:T(8,128)S(1)} %get-tuple-element.23), channel_id=1, source_target_pairs={{1,0},{2,1},{3,2},{4,3},{5,4},{6,5},{7,6},{9,8},{10,9},{11,10},{12... | collective-permute-start | bytes 233480 | tf_op jit(solution)/shard_map/ppermute | solution.py:424
  7.4 6.2 %collective-permute-start = (f32[152,128]{1,0:T(8,128)S(1)}, f32[152,128]{1,0:T(8,128)S(1)}, u32[]{:S(2)}, u32[]{:S(2)}) collective-permute-start(f32[152,128]{1,0:T(8,128)S(1)} %get-tuple-element.22.own), channel_id=1, source_target_pairs={{0,1},{1,2},{2,3},{3,4},{4,5},{5,6},{6,7},{8,9},{9,10},{10,11},{11... | collective-permute-start | bytes 233480 | tf_op jit(solution)/shard_map/ppermute | solution.py:424
  13.7 9.7 %collective-permute-start.2 = (f32[744,128]{1,0:T(8,128)S(1)}, f32[744,128]{1,0:T(8,128)S(1)}, u32[]{:S(2)}, u32[]{:S(2)}) collective-permute-start(f32[744,128]{1,0:T(8,128)S(1)} %get-tuple-element.24.own_up), channel_id=1, source_target_pairs={{0,8},{8,16},{16,24},{1,9},{9,17},{17,25},{2,10},{10,18},{18,26},{... | collective-permute-start | bytes 1142792 | tf_op jit(solution)/shard_map/ppermute | solution.py:424
  16.9 10.3 %collective-permute-start.3 = (f32[744,128]{1,0:T(8,128)S(1)}, f32[744,128]{1,0:T(8,128)S(1)}, u32[]{:S(2)}, u32[]{:S(2)}) collective-permute-start(f32[744,128]{1,0:T(8,128)S(1)} %get-tuple-element.25.own_down), channel_id=1, source_target_pairs={{8,0},{16,8},{24,16},{9,1},{17,9},{25,17},{10,2},{18,10},{26,18},{... | collective-permute-start | bytes 1142792 | tf_op jit(solution)/shard_map/ppermute | solution.py:424
  27.4 16.3 %collective-permute-start.5 = (f32[1688,128]{1,0:T(8,128)S(1)}, f32[1688,128]{1,0:T(8,128)S(1)}, u32[]{:S(2)}, u32[]{:S(2)}) collective-permute-start(f32[1688,128]{1,0:T(8,128)S(1)} %get-tuple-element.27.own_down), channel_id=1, source_target_pairs={{32,0},{64,32},{96,64},{128,96},{160,128},{192,160},{224,192},{33,... | collective-permute-start | bytes 2592776 | tf_op jit(solution)/shard_map/ppermute | solution.py:424
  32.1 12.8 %collective-permute-start.4 = (f32[1688,128]{1,0:T(8,128)S(1)}, f32[1688,128]{1,0:T(8,128)S(1)}, u32[]{:S(2)}, u32[]{:S(2)}) collective-permute-start(f32[1688,128]{1,0:T(8,128)S(1)} %get-tuple-element.26.own_up.meta_own), channel_id=1, source_target_pairs={{0,32},{32,64},{64,96},{96,128},{128,160},{160,192},{192,224},{1,3... | collective-permute-start | bytes 2592776 | tf_op jit(solution)/shard_map/ppermute | solution.py:424
  52.1 6.9 %collective-permute-start.6 = (f32[8,32,128]{2,1,0:T(8,128)S(1)}, f32[8,32,128]{2,1,0:T(8,128)S(1)}, u32[]{:S(2)}, u32[]{:S(2)}) collective-permute-start(f32[8,32,128]{2,1,0:T(8,128)S(1)} %get-tuple-element.29.own_up), channel_id=1, source_target_pairs={{0,1},{1,2},{2,3},{3,4},{4,5},{5,6},{6,7},{8,9},{9,10},{10,11},{11... | collective-permute-start | bytes 393224 | tf_op jit(solution)/shard_map/ppermute | solution.py:424
  57.0 6.9 %collective-permute-start.7 = (f32[8,32,128]{2,1,0:T(8,128)S(1)}, f32[8,32,128]{2,1,0:T(8,128)S(1)}, u32[]{:S(2)}, u32[]{:S(2)}) collective-permute-start(f32[8,32,128]{2,1,0:T(8,128)S(1)} %get-tuple-element.30.own_down), channel_id=1, source_target_pairs={{1,0},{2,1},{3,2},{4,3},{5,4},{6,5},{7,6},{9,8},{10,9},{11,10},{12... | collective-permute-start | bytes 393224 | tf_op jit(solution)/shard_map/ppermute | solution.py:424
  64.2 7.2 %collective-permute-start.8 = (f32[640,128]{1,0:T(8,128)S(1)}, f32[640,128]{1,0:T(8,128)S(1)}, u32[]{:S(2)}, u32[]{:S(2)}) collective-permute-start(f32[640,128]{1,0:T(8,128)S(1)} %get-tuple-element.31.own_up), channel_id=1, source_target_pairs={{0,8},{8,16},{16,24},{1,9},{9,17},{17,25},{2,10},{10,18},{18,26},{... | collective-permute-start | bytes 983048 | tf_op jit(solution)/shard_map/ppermute | solution.py:424
  67.4 17.4 %copy-start.1 = (f32[3,16,16,128]{3,2,1,0:T(8,128)S(1)}, f32[3,16,16,128]{3,2,1,0:T(8,128)}, u32[]{:S(2)}) copy-start(f32[3,16,16,128]{3,2,1,0:T(8,128)} %v.7) | copy-start | bytes 1179652
  67.4 8.0 %collective-permute-start.9 = (f32[640,128]{1,0:T(8,128)S(1)}, f32[640,128]{1,0:T(8,128)S(1)}, u32[]{:S(2)}, u32[]{:S(2)}) collective-permute-start(f32[640,128]{1,0:T(8,128)S(1)} %get-tuple-element.32.own_down), channel_id=1, source_target_pairs={{8,0},{16,8},{24,16},{9,1},{17,9},{25,17},{10,2},{18,10},{26,18},{... | collective-permute-start | bytes 983048 | tf_op jit(solution)/shard_map/ppermute | solution.py:424
  75.4 13.0 %collective-permute-start.10 = (f32[640,128]{1,0:T(8,128)S(1)}, f32[640,128]{1,0:T(8,128)S(1)}, u32[]{:S(2)}, u32[]{:S(2)}) collective-permute-start(f32[640,128]{1,0:T(8,128)S(1)} %get-tuple-element.33.own_up), channel_id=1, source_target_pairs={{0,32},{32,64},{64,96},{96,128},{128,160},{160,192},{192,224},{1,3... | collective-permute-start | bytes 983048 | tf_op jit(solution)/shard_map/ppermute | solution.py:424
  82.7 8.5 %copy-start.3 = (bf16[2,3,16,16,128]{4,3,2,1,0:T(8,128)(2,1)S(1)}, bf16[2,3,16,16,128]{4,3,2,1,0:T(8,128)(2,1)}, u32[]{:S(2)}) copy-start(bf16[2,3,16,16,128]{4,3,2,1,0:T(8,128)(2,1)} %g.3) | copy-start | bytes 1179652
  82.7 8.5 %collective-permute-start.11 = (f32[640,128]{1,0:T(8,128)S(1)}, f32[640,128]{1,0:T(8,128)S(1)}, u32[]{:S(2)}, u32[]{:S(2)}) collective-permute-start(f32[640,128]{1,0:T(8,128)S(1)} %get-tuple-element.34.own_down), channel_id=1, source_target_pairs={{32,0},{64,32},{96,64},{128,96},{160,128},{192,160},{224,192},{33,... | collective-permute-start | bytes 983048 | tf_op jit(solution)/shard_map/ppermute | solution.py:424

commit v2 on v1

--- a/solution.py
+++ b/solution.py
@@ -44,16 +44,36 @@
     ]
 
 
-def block_numbers(meta, row, step, ix, iy):
+def block_numbers(meta, row, step, ix, iy, keep=None):
     at = ((step * 2 + ix) * 2 + iy) * 6
-    shift = [meta[row, at + d].astype(jnp.int32) for d in range(3)]
-    weights = [tap_weights(meta[row, at + 3 + d]) for d in range(3)]
-    return shift, weights
-
-
-def sources_kernel(v, g, sx, sy, sz, fr, s0, s1, up, down):
+    numbers = [meta[row, at + d] for d in range(6)]
+    if keep is not None:
+        numbers = [number * keep for number in numbers]
+    return [n.astype(jnp.int32) for n in numbers[:3]], [tap_weights(n) for n in numbers[3:]]
+
+
+def inside(axis):
+    i, n = lax.axis_index(axis), lax.axis_size(axis)
+    return jnp.where(i > 0, 1.0, 0.0).astype(F32), jnp.where(i < n - 1, 1.0, 0.0).astype(F32)
+
+
+def sources_kernel(v_hbm, g_hbm, sx_hbm, sy_hbm, sz_hbm, fr_hbm, s0, s1, up, down, v, g, sx, sy, sz, fr, sem, small_sem):
+    copies = []
+    for q in range(4):
+        part = pl.ds(4 * q, 4)
+        copies.append(pltpu.make_async_copy(v_hbm.at[:, part], v.at[:, part], sem.at[2 * q]))
+        copies.append(pltpu.make_async_copy(g_hbm.at[:, :, part], g.at[:, :, part], sem.at[2 * q + 1]))
+    small = [
+        pltpu.make_async_copy(a, b, small_sem.at[n])
+        for n, (a, b) in enumerate(((sx_hbm, sx), (sy_hbm, sy), (sz_hbm, sz), (fr_hbm, fr)))
+    ]
+    for copy in copies + small:
+        copy.start()
     lane = lanes(T)
     for x in range(T):
+        if x % 4 == 0:
+            copies[x // 2].wait()
+            copies[x // 2 + 1].wait()
         vel = [v[c, x] for c in range(3)]
         for k, s in ((0, s0), (1, s1)):
             total = g[k, 0, x].astype(F32) * vel[0]
@@ -85,13 +105,15 @@
         up[pl.ds(Z_V + c * T, T)] = u
         down[pl.ds(Z_V + c * T, T)] = d
     lane = lanes()
+    for copy in small:
+        copy.wait()
     row = jnp.zeros((8, L), jnp.int32)
     for k in range(2):
         for ix in range(2):
             for iy in range(2):
                 at = ((k * 2 + ix) * 2 + iy) * 6
-                numbers = [sx[k, ix, iy, 0], sy[k, ix, iy, 0], sz[k, ix, iy, 0]]
-                numbers += [fr[k, d, ix, iy, 0] for d in range(3)]
+                numbers = [sx[k, ix, 0, iy], sy[k, ix, 0, iy], sz[k, ix, 0, iy]]
+                numbers += [fr[k, ix, iy, 0, d] for d in range(3)]
                 for n, number in enumerate(numbers):
                     row = jnp.where(lane == at + n, number, row)
     up[pl.ds(Z_META, 8)] = row.astype(F32)
@@ -99,6 +121,7 @@
 
 
 def y_message_kernel(s0, s1, v, own, low, high, up, down):
+    low_in, high_in = inside("gz")
     lane = lanes(T)
     even = (lane // 32) % 2 == 0
     for x in range(T):
@@ -107,7 +130,7 @@
         up[pl.ds(Y_S1 + x * 8, 8)] = s1[x, 8:16]
         down[pl.ds(Y_S1 + x * 8, 8)] = s1[x, 0:8]
     for j in range(4):
-        a, b = low[pl.ds(Z_S0 + j * T, T)], high[pl.ds(Z_S0 + j * T, T)]
+        a, b = low_in * low[pl.ds(Z_S0 + j * T, T)], high_in * high[pl.ds(Z_S0 + j * T, T)]
         first = jnp.where(even, b, a)
         second = roll(jnp.where(even, a, b), -32)
         for out in (up, down):
@@ -115,7 +138,7 @@
             out[pl.ds(Y_M0 + (j + 4) * T, T)] = second
     even = (lane // 16) % 2 == 0
     for h in range(2):
-        a, b = low[pl.ds(Z_S1 + h * T, T)], high[pl.ds(Z_S1 + h * T, T)]
+        a, b = low_in * low[pl.ds(Z_S1 + h * T, T)], high_in * high[pl.ds(Z_S1 + h * T, T)]
         for j, value in enumerate((jnp.where(even, b, a), roll(jnp.where(even, a, b), -16))):
             up[pl.ds(Y_M1 + (h * 2 + j) * 8, 8)] = value[8:16]
             down[pl.ds(Y_M1 + (h * 2 + j) * 8, 8)] = value[0:8]
@@ -127,30 +150,36 @@
             down[rows] = jnp.where(first_half, v[c, x, 0:8], pltpu.roll(v[c, x + 8, 0:8], 4, 0))
     sub = subs()
     meta = [ref[pl.ds(Z_META, 8)] for ref in (low, own, high)]
-    row = jnp.where(sub == 0, meta[0], jnp.where(sub == 1, meta[1], meta[2]))
+    row = jnp.where(sub == 0, low_in * meta[0], jnp.where(sub == 1, meta[1], high_in * meta[2]))
     up[pl.ds(Y_META, 8)] = row
     down[pl.ds(Y_META, 8)] = row
 
 
 def x_message_kernel(own_up, own_down, low, high, v, up, down):
+    low_in, high_in = inside("gy")
+
+    def take(ref, rows):
+        value = ref[rows]
+        return low_in * value if ref is low else high_in * value if ref is high else value
+
     for n, (start, planes, to) in enumerate(((Y_S0, T, X_S0), (Y_M0, 8, X_M0))):
         for x in range(planes):
             for at, ref in enumerate((low, own_up, high)):
-                value = ref[pl.ds(start + x * T, T)]
+                value = take(ref, pl.ds(start + x * T, T))
                 for out in (up, down):
                     out[pl.ds(to + x * 48 + at * T, T)] = value
     for h, out in ((1, up), (0, down)):
         for x in range(8):
             for at, ref in enumerate((low, own_down, own_up, high)):
-                out[pl.ds(X_S1 + x * 32 + at * 8, 8)] = ref[pl.ds(Y_S1 + (8 * h + x) * 8, 8)]
+                out[pl.ds(X_S1 + x * 32 + at * 8, 8)] = take(ref, pl.ds(Y_S1 + (8 * h + x) * 8, 8))
         for j in range(2):
             for at, ref in enumerate((low, own_down, own_up, high)):
-                out[pl.ds(X_M1 + j * 32 + at * 8, 8)] = ref[pl.ds(Y_M1 + (h * 2 + j) * 8, 8)]
+                out[pl.ds(X_M1 + j * 32 + at * 8, 8)] = take(ref, pl.ds(Y_M1 + (h * 2 + j) * 8, 8))
         for c in range(3):
             for i in range(4):
                 out[pl.ds(X_V + (c * 4 + i) * T, T)] = v[c, 12 * h + i]
         for at, ref in enumerate((low, own_up, high)):
-            out[pl.ds(X_META + at * 8, 8)] = ref[pl.ds(Y_META, 8)]
+            out[pl.ds(X_META + at * 8, 8)] = take(ref, pl.ds(Y_META, 8))
 
 
 def gather_xy(ref, x0, y0, wx, wy):
@@ -197,6 +226,7 @@
 
 
 def steps_kernel(own_up, own_down, low, high, ra, up, down, clo, chi, a1, e1, re, meta, sem):
+    low_in, high_in = inside("gx")
     lane = lanes()
     upper = lane >= 64
     copies = []
@@ -205,21 +235,25 @@
         copy.start()
         copies.append(copy)
     upper48 = lanes(48) >= 64
-    for n, ref in enumerate((low, own_up, high)):
-
-        def assemble(x, _, n=n, ref=ref):
+    for n, (ref, keep) in enumerate(((low, low_in), (own_up, None), (high, high_in))):
+
+        def assemble(x, _, n=n, ref=ref, keep=keep):
             m = ref[pl.ds(pl.multiple_of(X_M0 + x * 48, 8), 48)]
+            m = m if keep is None else keep * m
             for half, e in ((0, m), (1, roll(m, 64))):
                 a = ref[pl.ds(pl.multiple_of(X_S0 + (x + 8 * half) * 48, 8), 48)]
+                a = a if keep is None else keep * a
                 clo[n * T + 8 * half + x] = jnp.where(upper48, e, a)
                 chi[n * T + 8 * half + x] = jnp.where(upper48, a, e)
             return 0
 
         lax.fori_loop(0, 8, assemble, 0)
-    for n, ref in enumerate((low, own_down, own_up, high)):
+    for n, (ref, keep) in enumerate(((low, low_in), (own_down, None), (own_up, None), (high, high_in))):
         for x in range(8):
-            a1[n * 8 + x] = ref[pl.ds(X_S1 + x * 32, 32)]
-            e1[n * 8 + x] = roll(ref[pl.ds(X_M1 + (x % 2) * 32, 32)], -32 * (x // 2))
+            a = ref[pl.ds(X_S1 + x * 32, 32)]
+            e = roll(ref[pl.ds(X_M1 + (x % 2) * 32, 32)], -32 * (x // 2))
+            a1[n * 8 + x] = a if keep is None else keep * a
+            e1[n * 8 + x] = e if keep is None else keep * e
     ra[...] = jnp.zeros(ra.shape, F32)
     re[...] = jnp.zeros(re.shape, F32)
     for copy in copies:
@@ -229,13 +263,14 @@
         bx, by = i // 4, i % 4
         (slot_x, ix), (slot_y, iy) = block_of(bx), block_of(by)
         row = slot_x * 24 + slot_y * 8
+        keep = jnp.where(slot_x == 0, low_in, jnp.where(slot_x == 2, high_in, 1.0))
         edges = []
         for n, ref in ((0, clo), (2, chi)):
-            (a, b, c), (wx, wy, wz) = block_numbers(meta, row + n, 0, ix, iy)
+            (a, b, c), (wx, wy, wz) = block_numbers(meta, row + n, 0, ix, iy, keep)
             values = gather_xy(ref, bx * 8 + 7 + a, by * 8 + 7 + b, wx, wy)
             turns = [(1 - c - t) & 127 for t in range(4)]
             edges.append([sum(wz[t] * pltpu.roll(value, turns[t], 1) for t in range(4)) for value in values])
-        (a, b, c), (wx, wy, wz) = block_numbers(meta, row + 1, 0, ix, iy)
+        (a, b, c), (wx, wy, wz) = block_numbers(meta, row + 1, 0, ix, iy, keep)
         x0, y0 = bx * 8 + 7 + a, by * 8 + 7 + b
         lows = gather_xy(clo, x0, y0, wx, wy)
         highs = gather_xy(chi, x0, y0, wx, wy)
@@ -290,12 +325,13 @@
 
 
 def sum_z_kernel(ra, own_up, own_down, low, high, up, down):
+    low_in, high_in = inside("gz")
     wide = lanes(32)
     even = (wide // 16) % 2 == 0
     valid = (wide < 16) | (wide >= 112)
     for h in range(2):
         for x in range(4):
-            a, b = low[h * 4 + x], high[h * 4 + x]
+            a, b = low_in * low[h * 4 + x], high_in * high[h * 4 + x]
             inner = jnp.where(even, a, b)
             outer = jnp.where(even, own_up[h * 4 + x], own_down[h * 4 + x]) + jnp.where(even, b, a)
             down[pl.ds(R_E + (h * 4 + x) * T, T)] = outer[0:16]
@@ -308,12 +344,13 @@
 
 
 def sum_y_kernel(own_up, own_down, low, high, up, down):
+    low_in, high_in = inside("gy")
     for h, out in ((0, down), (1, up)):
         for start, planes in ((0, 16), (R_E, 4)):
             for x in range(planes):
                 rows = pl.ds(start + (h * planes + x) * T, T)
-                out[pl.ds(start + x * 32, T)] = own_down[rows] + low[rows]
-                out[pl.ds(start + x * 32 + T, T)] = own_up[rows] + high[rows]
+                out[pl.ds(start + x * 32, T)] = own_down[rows] + low_in * low[rows]
+                out[pl.ds(start + x * 32 + T, T)] = own_up[rows] + high_in * high[rows]
 
 
 def last_step_kernel(own_up, own_down, low, high, meta_low, meta_own, meta_high, g, reg, out, a1, e1, acc, meta, sem):
@@ -322,15 +359,16 @@
         copy = pltpu.make_async_copy(ref.at[pl.ds(X_META, 24)], meta.at[pl.ds(n * 24, 24)], sem.at[n])
         copy.start()
         copies.append(copy)
+    low_in, high_in = inside("gx")
     wide = lanes(32)
     valid = (wide < 16) | (wide >= 112)
-    for h, (mine, other) in enumerate(((own_down, low), (own_up, high))):
+    for h, (mine, other, keep) in enumerate(((own_down, low, low_in), (own_up, high, high_in))):
         for x in range(16):
             rows = pl.ds(x * 32, 32)
-            a1[16 * h + x] = mine[rows] + other[rows]
+            a1[16 * h + x] = mine[rows] + keep * other[rows]
         for x in range(4):
             rows = pl.ds(R_E + x * 32, 32)
-            packed = mine[rows] + other[rows]
+            packed = mine[rows] + keep * other[rows]
             for q in range(4):
                 e1[16 * h + 4 * q + x] = jnp.where(valid, roll(packed, -32 * q), 0.0)
     acc[...] = jnp.zeros(acc.shape, F32)
@@ -343,18 +381,19 @@
         bx, by = i // 4, i % 4
         (slot_x, ix), (slot_y, iy) = block_of(bx), block_of(by)
         row = slot_x * 24 + slot_y * 8
+        keep = jnp.where(slot_x == 0, low_in, jnp.where(slot_x == 2, high_in, 1.0))
         rows = pl.ds(pl.multiple_of(by * 8, 8), 8)
         inner = [a1[bx * 8 + p, rows, :] for p in range(8)]
         outer = [e1[bx * 8 + p, rows, :] for p in range(8)]
         for n in range(3):
-            (a, b, c), (wx, wy, wz) = block_numbers(meta, row + n, 0, ix, iy)
+            (a, b, c), (wx, wy, wz) = block_numbers(meta, row + n, 0, ix, iy, keep)
             back = [(c + t - 1) & 127 for t in range(4)]
             if n == 1:
                 w = [jnp.where(((lane - (c + t - 1)) & -128) == 0, wz[t], 0.0) for t in range(4)]
                 values = inner
             else:
-                keep = upper if n == 2 else jnp.logical_not(upper)
-                w = [jnp.where(keep, wz[t], 0.0) for t in range(4)]
+                lands = upper if n == 2 else jnp.logical_not(upper)
+                w = [jnp.where(lands, wz[t], 0.0) for t in range(4)]
                 values = [jnp.where(upper if n == 0 else jnp.logical_not(upper), value, 0.0) for value in outer]
             moved = [sum(w[t] * pltpu.roll(value, back[t], 1) for t in range(4)) for value in values]
             scatter_xy(acc, moved, bx * 8 + 7 + a, by * 8 + 7 + b, wx, wy)
@@ -370,17 +409,18 @@
 def laplace_kernel(v, zlow, zhigh, ylow, yhigh, xlow, xhigh, out, w):
     lane = lanes(T)
     half = (lane & 4) == 0
+    (x_low, x_high), (y_low, y_high), (z_low, z_high) = inside("gx"), inside("gy"), inside("gz")
     sides = [-REG_WEIGHT * t for t in LAPLACE_TAPS]
     for c in range(3):
         rows = pl.ds(Z_V + c * T, T)
-        faces = jnp.where(half, zhigh[rows], zlow[rows])
+        faces = jnp.where(half, z_high * zhigh[rows], z_low * zlow[rows])
         for i in range(4):
             rows = pl.ds(X_V + (c * 4 + i) * T, T)
-            w[i, 8:24] = xlow[rows]
-            w[20 + i, 8:24] = xhigh[rows]
+            w[i, 8:24] = x_low * xlow[rows]
+            w[20 + i, 8:24] = x_high * xhigh[rows]
         for x in range(8):
             rows = pl.ds(Y_V + (c * 8 + x) * 8, 8)
-            a, b = ylow[rows], yhigh[rows]
+            a, b = y_low * ylow[rows], y_high * yhigh[rows]
             w[4 + x, 0:8] = a
             w[12 + x, 0:8] = pltpu.roll(a, 4, 0)
             w[4 + x, 24:32] = b
@@ -400,11 +440,11 @@
 
 
 VMEM = pl.BlockSpec(memory_space=pltpu.VMEM)
-SMEM = pl.BlockSpec(memory_space=pltpu.SMEM)
-
-
-def call(kernel, args, outs, scratch=(), smem=(), cost=20000):
-    specs = [SMEM if i in smem else VMEM for i in range(len(args))]
+HBM = pl.BlockSpec(memory_space=pltpu.HBM)
+
+
+def call(kernel, args, outs, scratch=(), hbm=(), cost=20000):
+    specs = [HBM if i in hbm else VMEM for i in range(len(args))]
     shapes = [jax.ShapeDtypeStruct(s, F32) for s in outs]
     return pl.pallas_call(
         kernel,
@@ -419,7 +459,7 @@
 
 def exchange(up, down, axis):
     n = lax.axis_size(axis)
-    rise = [(i, i + 1) for i in range(n - 1)]
+    rise = [(i, (i + 1) % n) for i in range(n)]
     fall = [(j, i) for i, j in rise]
     return lax.ppermute(up, axis, rise), lax.ppermute(down, axis, fall)
 
@@ -427,11 +467,16 @@
 def body(velocity, gradients, shift_x, shift_y, shift_z, fractions):
     v, g = velocity, gradients
     tile = (T, T, L)
+    vm = lambda *s: pltpu.VMEM(s, F32)
+    shifts = [s.transpose(0, 1, 3, 2) for s in (shift_x, shift_y, shift_z)]
     s0, s1, zup, zdown = call(
         sources_kernel,
-        (v, g, shift_x, shift_y, shift_z, fractions),
+        [pltpu.with_memory_space_constraint(a, pltpu.HBM) for a in (v, g, *shifts, fractions.transpose(0, 2, 3, 4, 1))],
         [tile, tile, (Z_ROWS, L), (Z_ROWS, L)],
-        smem=(2, 3, 4, 5),
+        scratch=[vm(*v.shape), pltpu.VMEM(g.shape, g.dtype)]
+        + [pltpu.SMEM((2, 2, 1, 2), jnp.int32)] * 3
+        + [pltpu.SMEM((2, 2, 2, 1, 3), jnp.int32), pltpu.SemaphoreType.DMA((8,)), pltpu.SemaphoreType.DMA((4,))],
+        hbm=range(6),
     )
     zlow, zhigh = exchange(zup, zdown, "gz")
     yup, ydown = call(y_message_kernel, (s0, s1, v, zup, zlow, zhigh), [(Y_ROWS, L)] * 2)
@@ -439,7 +484,6 @@
     xup, xdown = call(x_message_kernel, (yup, ydown, ylow, yhigh, v), [(X_ROWS, L)] * 2)
     xlow, xhigh = exchange(xup, xdown, "gx")
     meta = [pltpu.SMEM((72, L), F32), pltpu.SemaphoreType.DMA((3,))]
-    vm = lambda *s: pltpu.VMEM(s, F32)
     ra, zup, zdown = call(
         steps_kernel,
         (xup, xdown, xlow, xhigh),

time: 97.7 us -> 76.4 us (0.78)
  the two profiles are of different devices: /device:TPU:97 before, /device:TPU:1 now
where the time goes in v2:
time: 76.4 us; the launch traced here: 76.3 us
  waiting for transfers between devices  32.3 us (42%)
  starting transfers between devices  24.7 us (32%)
  Pallas kernels  19.2 us (25%)
    ppermute x12, waiting for transfers between devices, exchange(): return (lax.ppermute(up, axis, rise), lax.ppermute(down, axis, fall))  32.3 us
    ppermute x12, starting transfers between devices, exchange(): return (lax.ppermute(up, axis, rise), lax.ppermute(down, axis, fall))  24.7 us
    pallas_call x8, Pallas kernels, call(): pl.pallas_call(kernel, out_shape=shapes, in_specs=specs, out_specs=[VMEM]...  19.2 us
  transfers between devices with their start and end apart: 12, of which 8 were waited for; matrix products, arithmetic and copies ran while one was open for 0% of the time, Pallas kernels for 5%

profile of v2, /device:TPU:1, one launch (start us, length us, event | category | flops | bytes accessed | tf_op | source)
XLA Modules:
  0.0 76.3 jit_solution(13154094850635911303)
XLA Ops:
  0.0 0.0 copy-start
  0.0 1.6 %shard_map.64 = (f32[16,16,128]{2,1,0:T(8,128)S(1)}, f32[16,16,128]{2,1,0:T(8,128)S(1)}, f32[152,128]{1,0:T(8,128)S(1)}, f32[152,128]{1,0:T(8,128)S(1)}) custom-call(f32[3,16,16,128]{3,2,1,0:T(8,128)} %v.5, bf16[2,3,16,16,128]{4,3,2,1,0:T(8,128)(2,1)} %g.1, s32[2,2,1,2]{3,2,1,0:T(1,128)} %bitcast.11, s32[2,2,1,2]{3,2,1,0:T(1,128)} %bitcast.12, ...), custom_call_target="tpu_custom_call" | custom-call | flops 20000 | bytes 20000 | tf_op jit(solution)/shard_map/pallas_call | solution.py:449
  1.7 6.5 %collective-permute-start.1 = (f32[152,128]{1,0:T(8,128)S(1)}, f32[152,128]{1,0:T(8,128)S(1)}, u32[]{:S(2)}, u32[]{:S(2)}) collective-permute-start(f32[152,128]{1,0:T(8,128)S(1)} %get-tuple-element.23), channel_id=1, source_target_pairs={{1,0},{2,1},{3,2},{4,3},{5,4},{6,5},{7,6},{0,7},{9,8},{10,9},{11,1... | collective-permute-start | bytes 233480 | tf_op jit(solution)/shard_map/ppermute | solution.py:464
  8.1 0.0 collective-permute-start
  8.1 1.4 %collective-permute-done.1.high.zhigh = f32[152,128]{1,0:T(8,128)S(1)} collective-permute-done((f32[152,128]{1,0:T(8,128)S(1)}, f32[152,128]{1,0:T(8,128)S(1)}, u32[]{:S(2)}, u32[]{:S(2)}) %collective-permute-start.1) | collective-permute-done | bytes 77856 | tf_op jit(solution)/shard_map/ppermute | solution.py:464
  9.6 3.0 %collective-permute-done.low.zlow = f32[152,128]{1,0:T(8,128)S(1)} collective-permute-done((f32[152,128]{1,0:T(8,128)S(1)}, f32[152,128]{1,0:T(8,128)S(1)}, u32[]{:S(2)}, u32[]{:S(2)}) %collective-permute-start) | collective-permute-done | bytes 77856 | tf_op jit(solution)/shard_map/ppermute | solution.py:464
  12.6 0.0 copy-done
  12.6 0.1 shard_map.65
  12.7 1.4 %collective-permute-start.2 = (f32[744,128]{1,0:T(8,128)S(1)}, f32[744,128]{1,0:T(8,128)S(1)}, u32[]{:S(2)}, u32[]{:S(2)}) collective-permute-start(f32[744,128]{1,0:T(8,128)S(1)} %get-tuple-element.24.own_up), channel_id=1, source_target_pairs={{0,8},{8,16},{16,24},{24,0},{1,9},{9,17},{17,25},{25,1},{2,10},{10... | collective-permute-start | bytes 1142792 | tf_op jit(solution)/shard_map/ppermute | solution.py:464
  14.1 1.5 %collective-permute-start.3 = (f32[744,128]{1,0:T(8,128)S(1)}, f32[744,128]{1,0:T(8,128)S(1)}, u32[]{:S(2)}, u32[]{:S(2)}) collective-permute-start(f32[744,128]{1,0:T(8,128)S(1)} %get-tuple-element.25.own_down), channel_id=1, source_target_pairs={{8,0},{16,8},{24,16},{0,24},{9,1},{17,9},{25,17},{1,25},{10,2},{18... | collective-permute-start | bytes 1142792 | tf_op jit(solution)/shard_map/ppermute | solution.py:464
  15.6 6.8 %collective-permute-done.2.low.ylow = f32[744,128]{1,0:T(8,128)S(1)} collective-permute-done((f32[744,128]{1,0:T(8,128)S(1)}, f32[744,128]{1,0:T(8,128)S(1)}, u32[]{:S(2)}, u32[]{:S(2)}) %collective-permute-start.2) | collective-permute-done | bytes 380960 | tf_op jit(solution)/shard_map/ppermute | solution.py:464
  22.4 0.0 collective-permute-done.3.high.yhigh
  22.4 0.1 shard_map.66
  22.5 3.0 %collective-permute-start.5 = (f32[1688,128]{1,0:T(8,128)S(1)}, f32[1688,128]{1,0:T(8,128)S(1)}, u32[]{:S(2)}, u32[]{:S(2)}) collective-permute-start(f32[1688,128]{1,0:T(8,128)S(1)} %get-tuple-element.27.own_down), channel_id=1, source_target_pairs={{32,0},{64,32},{96,64},{128,96},{160,128},{192,160},{224,192},{0,2... | collective-permute-start | bytes 2592776 | tf_op jit(solution)/shard_map/ppermute | solution.py:464
  25.5 1.1 %collective-permute-start.4 = (f32[1688,128]{1,0:T(8,128)S(1)}, f32[1688,128]{1,0:T(8,128)S(1)}, u32[]{:S(2)}, u32[]{:S(2)}) collective-permute-start(f32[1688,128]{1,0:T(8,128)S(1)} %get-tuple-element.26.own_up.meta_own), channel_id=1, source_target_pairs={{0,32},{32,64},{64,96},{96,128},{128,160},{160,192},{192,224},{224... | collective-permute-start | bytes 2592776 | tf_op jit(solution)/shard_map/ppermute | solution.py:464
  26.6 10.8 %collective-permute-done.5.high.xhigh.meta_high = f32[1688,128]{1,0:T(8,128)S(1)} collective-permute-done((f32[1688,128]{1,0:T(8,128)S(1)}, f32[1688,128]{1,0:T(8,128)S(1)}, u32[]{:S(2)}, u32[]{:S(2)}) %collective-permute-start.5) | collective-permute-done | bytes 864288 | tf_op jit(solution)/shard_map/ppermute | solution.py:464
  37.4 0.0 collective-permute-done.4.low.xlow.meta_low
  37.4 7.5 %shard_map.67 = (f32[32,40,128]{2,1,0:T(8,128)S(1)}, f32[8,32,128]{2,1,0:T(8,128)S(1)}, f32[8,32,128]{2,1,0:T(8,128)S(1)}) custom-call(f32[1688,128]{1,0:T(8,128)S(1)} %get-tuple-element.26.own_up.meta_own, f32[1688,128]{1,0:T(8,128)S(1)} %get-tuple-element.27.own_down, f32[1688,128]{1,0:T(8,128)S(1)} %collective-permute-done.4.low.xlow.meta_low, ...), custom_call_target="tpu_custom_call" | custom-call | flops 20000 | bytes 20000 | tf_op jit(solution)/shard_map/pallas_call | solution.py:449
  44.9 0.1 collective-permute-start.6
  45.0 2.7 %collective-permute-start.7 = (f32[8,32,128]{2,1,0:T(8,128)S(1)}, f32[8,32,128]{2,1,0:T(8,128)S(1)}, u32[]{:S(2)}, u32[]{:S(2)}) collective-permute-start(f32[8,32,128]{2,1,0:T(8,128)S(1)} %get-tuple-element.30.own_down), channel_id=1, source_target_pairs={{1,0},{2,1},{3,2},{4,3},{5,4},{6,5},{7,6},{0,7},{9,8},{10,9},{11,1... | collective-permute-start | bytes 393224 | tf_op jit(solution)/shard_map/ppermute | solution.py:464
  47.6 2.4 %collective-permute-done.6.low = f32[8,32,128]{2,1,0:T(8,128)S(1)} collective-permute-done((f32[8,32,128]{2,1,0:T(8,128)S(1)}, f32[8,32,128]{2,1,0:T(8,128)S(1)}, u32[]{:S(2)}, u32[]{:S(2)}) %collective-permute-start.6) | collective-permute-done | bytes 131104 | tf_op jit(solution)/shard_map/ppermute | solution.py:464
  50.0 0.0 collective-permute-done.7.high
  50.0 0.2 shard_map.68
  50.2 1.4 %collective-permute-start.8 = (f32[640,128]{1,0:T(8,128)S(1)}, f32[640,128]{1,0:T(8,128)S(1)}, u32[]{:S(2)}, u32[]{:S(2)}) collective-permute-start(f32[640,128]{1,0:T(8,128)S(1)} %get-tuple-element.31.own_up), channel_id=1, source_target_pairs={{0,8},{8,16},{16,24},{24,0},{1,9},{9,17},{17,25},{25,1},{2,10},{10... | collective-permute-start | bytes 983048 | tf_op jit(solution)/shard_map/ppermute | solution.py:464
  51.6 1.5 %collective-permute-start.9 = (f32[640,128]{1,0:T(8,128)S(1)}, f32[640,128]{1,0:T(8,128)S(1)}, u32[]{:S(2)}, u32[]{:S(2)}) collective-permute-start(f32[640,128]{1,0:T(8,128)S(1)} %get-tuple-element.32.own_down), channel_id=1, source_target_pairs={{8,0},{16,8},{24,16},{0,24},{9,1},{17,9},{25,17},{1,25},{10,2},{18... | collective-permute-start | bytes 983048 | tf_op jit(solution)/shard_map/ppermute | solution.py:464
  53.1 5.0 %collective-permute-done.8.low = f32[640,128]{1,0:T(8,128)S(1)} collective-permute-done((f32[640,128]{1,0:T(8,128)S(1)}, f32[640,128]{1,0:T(8,128)S(1)}, u32[]{:S(2)}, u32[]{:S(2)}) %collective-permute-start.8) | collective-permute-done | bytes 327712 | tf_op jit(solution)/shard_map/ppermute | solution.py:464
  58.1 0.0 collective-permute-done.9.high
  58.1 0.1 shard_map.69
  58.2 5.5 %collective-permute-start.10 = (f32[640,128]{1,0:T(8,128)S(1)}, f32[640,128]{1,0:T(8,128)S(1)}, u32[]{:S(2)}, u32[]{:S(2)}) collective-permute-start(f32[640,128]{1,0:T(8,128)S(1)} %get-tuple-element.33.own_up), channel_id=1, source_target_pairs={{0,32},{32,64},{64,96},{96,128},{128,160},{160,192},{192,224},{224... | collective-permute-start | bytes 983048 | tf_op jit(solution)/shard_map/ppermute | solution.py:464
  63.7 0.0 copy-start.1
  63.7 0.0 collective-permute-start.11
  63.7 3.6 %shard_map.70.reg = f32[3,16,16,128]{3,2,1,0:T(8,128)S(1)} custom-call(f32[3,16,16,128]{3,2,1,0:T(8,128)S(1)} %copy-done, f32[152,128]{1,0:T(8,128)S(1)} %collective-permute-done.low.zlow, f32[152,128]{1,0:T(8,128)S(1)} %collective-permute-done.1.high.zhigh, f32[744,128]{1,0:T(8,128)S(1)} %collective-permute-done.2.low.ylow, ...), custom_call_target="tpu_custom_call" | custom-call | flops 4000000 | bytes 4000000 | tf_op jit(solution)/shard_map/pallas_call | solution.py:449
  67.3 0.4 collective-permute-done.10.low
  67.7 2.5 %collective-permute-done.11.high = f32[640,128]{1,0:T(8,128)S(1)} collective-permute-done((f32[640,128]{1,0:T(8,128)S(1)}, f32[640,128]{1,0:T(8,128)S(1)}, u32[]{:S(2)}, u32[]{:S(2)}) %collective-permute-start.11) | collective-permute-done | bytes 327712 | tf_op jit(solution)/shard_map/ppermute | solution.py:464
  70.2 0.0 copy-done.1
  70.2 6.0 %shard_map.71 = f32[3,16,16,128]{3,2,1,0:T(8,128)} custom-call(f32[640,128]{1,0:T(8,128)S(1)} %get-tuple-element.33.own_up, f32[640,128]{1,0:T(8,128)S(1)} %get-tuple-element.34.own_down, f32[640,128]{1,0:T(8,128)S(1)} %collective-permute-done.10.low, f32[640,128]{1,0:T(8,128)S(1)} %collective-permute-done.11.high, ...), custom_call_target="tpu_custom_call" | custom-call | flops 20000 | bytes 20000 | tf_op jit(solution)/shard_map/pallas_call | solution.py:449
Async XLA Ops:
  0.0 12.6 %copy-start = (f32[3,16,16,128]{3,2,1,0:T(8,128)S(1)}, f32[3,16,16,128]{3,2,1,0:T(8,128)}, u32[]{:S(2)}) copy-start(f32[3,16,16,128]{3,2,1,0:T(8,128)} %v.5) | copy-start | bytes 1179652
  1.7 7.9 %collective-permute-start.1 = (f32[152,128]{1,0:T(8,128)S(1)}, f32[152,128]{1,0:T(8,128)S(1)}, u32[]{:S(2)}, u32[]{:S(2)}) collective-permute-start(f32[152,128]{1,0:T(8,128)S(1)} %get-tuple-element.23), channel_id=1, source_target_pairs={{1,0},{2,1},{3,2},{4,3},{5,4},{6,5},{7,6},{0,7},{9,8},{10,9},{11,1... | collective-permute-start | bytes 233480 | tf_op jit(solution)/shard_map/ppermute | solution.py:464
  8.1 4.5 %collective-permute-start = (f32[152,128]{1,0:T(8,128)S(1)}, f32[152,128]{1,0:T(8,128)S(1)}, u32[]{:S(2)}, u32[]{:S(2)}) collective-permute-start(f32[152,128]{1,0:T(8,128)S(1)} %get-tuple-element.22.own), channel_id=1, source_target_pairs={{0,1},{1,2},{2,3},{3,4},{4,5},{5,6},{6,7},{7,0},{8,9},{9,10},{10,1... | collective-permute-start | bytes 233480 | tf_op jit(solution)/shard_map/ppermute | solution.py:464
  12.7 9.6 %collective-permute-start.2 = (f32[744,128]{1,0:T(8,128)S(1)}, f32[744,128]{1,0:T(8,128)S(1)}, u32[]{:S(2)}, u32[]{:S(2)}) collective-permute-start(f32[744,128]{1,0:T(8,128)S(1)} %get-tuple-element.24.own_up), channel_id=1, source_target_pairs={{0,8},{8,16},{16,24},{24,0},{1,9},{9,17},{17,25},{25,1},{2,10},{10... | collective-permute-start | bytes 1142792 | tf_op jit(solution)/shard_map/ppermute | solution.py:464
  14.1 8.3 %collective-permute-start.3 = (f32[744,128]{1,0:T(8,128)S(1)}, f32[744,128]{1,0:T(8,128)S(1)}, u32[]{:S(2)}, u32[]{:S(2)}) collective-permute-start(f32[744,128]{1,0:T(8,128)S(1)} %get-tuple-element.25.own_down), channel_id=1, source_target_pairs={{8,0},{16,8},{24,16},{0,24},{9,1},{17,9},{25,17},{1,25},{10,2},{18... | collective-permute-start | bytes 1142792 | tf_op jit(solution)/shard_map/ppermute | solution.py:464
  22.5 14.9 %collective-permute-start.5 = (f32[1688,128]{1,0:T(8,128)S(1)}, f32[1688,128]{1,0:T(8,128)S(1)}, u32[]{:S(2)}, u32[]{:S(2)}) collective-permute-start(f32[1688,128]{1,0:T(8,128)S(1)} %get-tuple-element.27.own_down), channel_id=1, source_target_pairs={{32,0},{64,32},{96,64},{128,96},{160,128},{192,160},{224,192},{0,2... | collective-permute-start | bytes 2592776 | tf_op jit(solution)/shard_map/ppermute | solution.py:464
  25.5 11.9 %collective-permute-start.4 = (f32[1688,128]{1,0:T(8,128)S(1)}, f32[1688,128]{1,0:T(8,128)S(1)}, u32[]{:S(2)}, u32[]{:S(2)}) collective-permute-start(f32[1688,128]{1,0:T(8,128)S(1)} %get-tuple-element.26.own_up.meta_own), channel_id=1, source_target_pairs={{0,32},{32,64},{64,96},{96,128},{128,160},{160,192},{192,224},{224... | collective-permute-start | bytes 2592776 | tf_op jit(solution)/shard_map/ppermute | solution.py:464
  44.9 5.1 %collective-permute-start.6 = (f32[8,32,128]{2,1,0:T(8,128)S(1)}, f32[8,32,128]{2,1,0:T(8,128)S(1)}, u32[]{:S(2)}, u32[]{:S(2)}) collective-permute-start(f32[8,32,128]{2,1,0:T(8,128)S(1)} %get-tuple-element.29.own_up), channel_id=1, source_target_pairs={{0,1},{1,2},{2,3},{3,4},{4,5},{5,6},{6,7},{7,0},{8,9},{9,10},{10,1... | collective-permute-start | bytes 393224 | tf_op jit(solution)/shard_map/ppermute | solution.py:464
  45.0 5.0 %collective-permute-start.7 = (f32[8,32,128]{2,1,0:T(8,128)S(1)}, f32[8,32,128]{2,1,0:T(8,128)S(1)}, u32[]{:S(2)}, u32[]{:S(2)}) collective-permute-start(f32[8,32,128]{2,1,0:T(8,128)S(1)} %get-tuple-element.30.own_down), channel_id=1, source_target_pairs={{1,0},{2,1},{3,2},{4,3},{5,4},{6,5},{7,6},{0,7},{9,8},{10,9},{11,1... | collective-permute-start | bytes 393224 | tf_op jit(solution)/shard_map/ppermute | solution.py:464
  50.2 7.9 %collective-permute-start.8 = (f32[640,128]{1,0:T(8,128)S(1)}, f32[640,128]{1,0:T(8,128)S(1)}, u32[]{:S(2)}, u32[]{:S(2)}) collective-permute-start(f32[640,128]{1,0:T(8,128)S(1)} %get-tuple-element.31.own_up), channel_id=1, source_target_pairs={{0,8},{8,16},{16,24},{24,0},{1,9},{9,17},{17,25},{25,1},{2,10},{10... | collective-permute-start | bytes 983048 | tf_op jit(solution)/shard_map/ppermute | solution.py:464
  51.6 6.5 %collective-permute-start.9 = (f32[640,128]{1,0:T(8,128)S(1)}, f32[640,128]{1,0:T(8,128)S(1)}, u32[]{:S(2)}, u32[]{:S(2)}) collective-permute-start(f32[640,128]{1,0:T(8,128)S(1)} %get-tuple-element.32.own_down), channel_id=1, source_target_pairs={{8,0},{16,8},{24,16},{0,24},{9,1},{17,9},{25,17},{1,25},{10,2},{18... | collective-permute-start | bytes 983048 | tf_op jit(solution)/shard_map/ppermute | solution.py:464
  58.2 9.6 %collective-permute-start.10 = (f32[640,128]{1,0:T(8,128)S(1)}, f32[640,128]{1,0:T(8,128)S(1)}, u32[]{:S(2)}, u32[]{:S(2)}) collective-permute-start(f32[640,128]{1,0:T(8,128)S(1)} %get-tuple-element.33.own_up), channel_id=1, source_target_pairs={{0,32},{32,64},{64,96},{96,128},{128,160},{160,192},{192,224},{224... | collective-permute-start | bytes 983048 | tf_op jit(solution)/shard_map/ppermute | solution.py:464
  63.7 6.5 %copy-start.1 = (bf16[2,3,16,16,128]{4,3,2,1,0:T(8,128)(2,1)S(1)}, bf16[2,3,16,16,128]{4,3,2,1,0:T(8,128)(2,1)}, u32[]{:S(2)}) copy-start(bf16[2,3,16,16,128]{4,3,2,1,0:T(8,128)(2,1)} %g.1) | copy-start | bytes 1179652
  63.7 6.5 %collective-permute-start.11 = (f32[640,128]{1,0:T(8,128)S(1)}, f32[640,128]{1,0:T(8,128)S(1)}, u32[]{:S(2)}, u32[]{:S(2)}) collective-permute-start(f32[640,128]{1,0:T(8,128)S(1)} %get-tuple-element.34.own_down), channel_id=1, source_target_pairs={{32,0},{64,32},{96,64},{128,96},{160,128},{192,160},{224,192},{0,2... | collective-permute-start | bytes 983048 | tf_op jit(solution)/shard_map/ppermute | solution.py:464

commit v3 on v2

--- a/solution.py
+++ b/solution.py
@@ -11,7 +11,8 @@
 REG_WEIGHT = 0.1
 T = 16
 L = 128
-META = 48
+UN_ASM, UN_SEC, UN_FIRST, UN_SECOND, UN_PACK, UN_UNPACK, UN_STEP, UN_FIN = 8, 4, 16, 1, 8, 4, 16, 16
+META = 15
 
 Z_S0, Z_S1, Z_V, Z_META, Z_ROWS = 0, 64, 96, 144, 152
 Y_S0, Y_M0, Y_S1, Y_M1, Y_V, Y_META, Y_ROWS = 0, 256, 384, 512, 544, 736, 744
@@ -32,24 +33,21 @@
     return x if amount == 0 else pltpu.roll(x, amount, 1)
 
 
-def tap_weights(f):
-    e = f * 0.125
-    e2 = e * e
-    e3 = e2 * e
-    return [
-        0.5 * (2.0 * e2 - e3 - e),
-        0.5 * (3.0 * e3 - 5.0 * e2 + 2.0),
-        0.5 * (4.0 * e2 - 3.0 * e3 + e),
-        0.5 * (e3 - e2),
-    ]
-
-
 def block_numbers(meta, row, step, ix, iy, keep=None):
-    at = ((step * 2 + ix) * 2 + iy) * 6
-    numbers = [meta[row, at + d] for d in range(6)]
+    at = ((step * 2 + ix) * 2 + iy) * META
+    shift = [meta[row, at + d].astype(jnp.int32) for d in range(3)]
+    weights = [[meta[row, at + 3 + 4 * d + t] for t in range(4)] for d in range(3)]
     if keep is not None:
-        numbers = [number * keep for number in numbers]
-    return [n.astype(jnp.int32) for n in numbers[:3]], [tap_weights(n) for n in numbers[3:]]
+        weights[0] = [w * keep for w in weights[0]]
+    return shift, weights
+
+
+def loop(count, body, unroll=1):
+    def step(i, _):
+        body(i)
+        return 0
+
+    lax.fori_loop(0, count, step, 0, unroll=unroll)
 
 
 def inside(axis):
@@ -107,17 +105,30 @@
     lane = lanes()
     for copy in small:
         copy.wait()
-    row = jnp.zeros((8, L), jnp.int32)
+    shifts, eighths = jnp.zeros((8, L), jnp.int32), jnp.zeros((8, L), jnp.int32)
     for k in range(2):
         for ix in range(2):
             for iy in range(2):
-                at = ((k * 2 + ix) * 2 + iy) * 6
-                numbers = [sx[k, ix, 0, iy], sy[k, ix, 0, iy], sz[k, ix, 0, iy]]
-                numbers += [fr[k, ix, iy, 0, d] for d in range(3)]
-                for n, number in enumerate(numbers):
-                    row = jnp.where(lane == at + n, number, row)
-    up[pl.ds(Z_META, 8)] = row.astype(F32)
-    down[pl.ds(Z_META, 8)] = row.astype(F32)
+                at = ((k * 2 + ix) * 2 + iy) * META
+                for n, ref in enumerate((sx, sy, sz)):
+                    shifts = jnp.where(lane == at + n, ref[k, ix, 0, iy], shifts)
+                    first = at + 3 + 4 * n
+                    eighths = jnp.where((lane >= first) & (lane < first + 4), fr[k, ix, iy, 0, n], eighths)
+    e = eighths.astype(F32) / 8.0
+    e2 = e * e
+    e3 = e2 * e
+    weights = [
+        0.5 * (2.0 * e2 - e3 - e),
+        0.5 * (3.0 * e3 - 5.0 * e2 + 2.0),
+        0.5 * (4.0 * e2 - 3.0 * e3 + e),
+        0.5 * (e3 - e2),
+    ]
+    place = lane % META
+    tap = (place - 3) % 4
+    row = jnp.where(tap == 0, weights[0], jnp.where(tap == 1, weights[1], jnp.where(tap == 2, weights[2], weights[3])))
+    row = jnp.where(place < 3, shifts.astype(F32), row)
+    up[pl.ds(Z_META, 8)] = row
+    down[pl.ds(Z_META, 8)] = row
 
 
 def y_message_kernel(s0, s1, v, own, low, high, up, down):
@@ -182,12 +193,13 @@
             out[pl.ds(X_META + at * 8, 8)] = take(ref, pl.ds(Y_META, 8))
 
 
-def gather_xy(ref, x0, y0, wx, wy):
+def gather_xy(ref, width, x0, y0, wx, wy):
+    base = x0 * width + y0
     planes = []
     for i in range(11):
-        plane = wy[0] * ref[x0 + i, pl.ds(y0, 8), :]
+        plane = wy[0] * ref[pl.ds(base + i * width, 8), :]
         for t in range(1, 4):
-            plane = plane + wy[t] * ref[x0 + i, pl.ds(y0 + t, 8), :]
+            plane = plane + wy[t] * ref[pl.ds(base + (i * width + t), 8), :]
         planes.append(plane)
     out = []
     for i in range(8):
@@ -198,8 +210,10 @@
     return out
 
 
-def scatter_xy(ref, vals, x0, y0, wx, wy):
+def scatter_xy(ref, width, vals, x0, y0, wx, wy):
     sub = subs()
+    base = x0 * width + y0
+    places = [pl.ds(base + (p * width + 8 * half), 8) for p in range(11) for half in range(2)]
     low_w = [jnp.where(sub >= t, wy[t], 0.0) for t in range(4)]
     high_w = [jnp.where(sub < t, wy[t], 0.0) for t in range(4)]
     pairs = []
@@ -210,15 +224,16 @@
             first = first + low_w[t] * turned
             second = high_w[t] * turned if second is None else second + high_w[t] * turned
         pairs.append((first, second))
+    sums = []
     for p in range(11):
         for half in range(2):
-            total = None
+            total = ref[places[len(sums)], :]
             for t in range(4):
                 if 0 <= p - t < 8:
-                    term = wx[t] * pairs[p - t][half]
-                    total = term if total is None else total + term
-            rows = pl.ds(y0 + 8 * half, 8)
-            ref[x0 + p, rows, :] = ref[x0 + p, rows, :] + total
+                    total = total + wx[t] * pairs[p - t][half]
+            sums.append(total)
+    for place, total in zip(places, sums):
+        ref[place, :] = total
 
 
 def block_of(b):
@@ -237,61 +252,75 @@
     upper48 = lanes(48) >= 64
     for n, (ref, keep) in enumerate(((low, low_in), (own_up, None), (high, high_in))):
 
-        def assemble(x, _, n=n, ref=ref, keep=keep):
+        def assemble(x, n=n, ref=ref, keep=keep):
             m = ref[pl.ds(pl.multiple_of(X_M0 + x * 48, 8), 48)]
             m = m if keep is None else keep * m
             for half, e in ((0, m), (1, roll(m, 64))):
                 a = ref[pl.ds(pl.multiple_of(X_S0 + (x + 8 * half) * 48, 8), 48)]
                 a = a if keep is None else keep * a
-                clo[n * T + 8 * half + x] = jnp.where(upper48, e, a)
-                chi[n * T + 8 * half + x] = jnp.where(upper48, a, e)
-            return 0
-
-        lax.fori_loop(0, 8, assemble, 0)
+                rows = pl.ds(pl.multiple_of((n * T + 8 * half + x) * 48, 8), 48)
+                clo[rows] = jnp.where(upper48, e, a)
+                chi[rows] = jnp.where(upper48, a, e)
+
+        loop(8, assemble, UN_ASM)
     for n, (ref, keep) in enumerate(((low, low_in), (own_down, None), (own_up, None), (high, high_in))):
-        for x in range(8):
-            a = ref[pl.ds(X_S1 + x * 32, 32)]
-            e = roll(ref[pl.ds(X_M1 + (x % 2) * 32, 32)], -32 * (x // 2))
-            a1[n * 8 + x] = a if keep is None else keep * a
-            e1[n * 8 + x] = e if keep is None else keep * e
-    ra[...] = jnp.zeros(ra.shape, F32)
-    re[...] = jnp.zeros(re.shape, F32)
+
+        def assemble_second(q, n=n, ref=ref, keep=keep):
+            for j in range(2):
+                x = 2 * q + j
+                a = ref[pl.ds(pl.multiple_of(X_S1 + x * 32, 8), 32)]
+                e = pltpu.roll(ref[pl.ds(X_M1 + j * 32, 32)], (L - 32 * q) & 127, 1)
+                rows = pl.ds(pl.multiple_of((n * 8 + x) * 32, 8), 32)
+                a1[rows] = a if keep is None else keep * a
+                e1[rows] = e if keep is None else keep * e
+
+        loop(4, assemble_second, UN_SEC)
+
+    def clear(i):
+        rows = pl.ds(pl.multiple_of(i * 128, 8), 128)
+        ra[rows] = jnp.zeros((128, L), F32)
+        re[rows] = jnp.zeros((128, L), F32)
+
+    loop(10, clear)
     for copy in copies:
         copy.wait()
 
-    def first_step(i, _):
+    def first_step(i):
         bx, by = i // 4, i % 4
         (slot_x, ix), (slot_y, iy) = block_of(bx), block_of(by)
         row = slot_x * 24 + slot_y * 8
         keep = jnp.where(slot_x == 0, low_in, jnp.where(slot_x == 2, high_in, 1.0))
+        rows = [pl.ds(pl.multiple_of(bx * 256 + by * 8, 8) + p * 32, 8) for p in range(8)]
+
+        def numbers(n):
+            (a, b, c), (wx, wy, wz) = block_numbers(meta, row + n, 0, ix, iy, keep)
+            return bx * 8 + 7 + a, by * 8 + 7 + b, c, wx, wy, wz
+
+        x0, y0, c, wx, wy, wz = numbers(1)
+        lows = gather_xy(clo, 48, x0, y0, wx, wy)
+        highs = gather_xy(chi, 48, x0, y0, wx, wy)
+        masks = [jnp.logical_xor(((lane - (c + t - 1)) & -128) == 0, upper) for t in range(4)]
+        turns = [(1 - c - t) & 127 for t in range(4)]
+        for p in range(8):
+            value = sum(wz[t] * pltpu.roll(jnp.where(masks[t], lows[p], highs[p]), turns[t], 1) for t in range(4))
+            a1[rows[p], :] = a1[rows[p], :] + value
         edges = []
         for n, ref in ((0, clo), (2, chi)):
-            (a, b, c), (wx, wy, wz) = block_numbers(meta, row + n, 0, ix, iy, keep)
-            values = gather_xy(ref, bx * 8 + 7 + a, by * 8 + 7 + b, wx, wy)
+            x0, y0, c, wx, wy, wz = numbers(n)
+            values = gather_xy(ref, 48, x0, y0, wx, wy)
             turns = [(1 - c - t) & 127 for t in range(4)]
             edges.append([sum(wz[t] * pltpu.roll(value, turns[t], 1) for t in range(4)) for value in values])
-        (a, b, c), (wx, wy, wz) = block_numbers(meta, row + 1, 0, ix, iy, keep)
-        x0, y0 = bx * 8 + 7 + a, by * 8 + 7 + b
-        lows = gather_xy(clo, x0, y0, wx, wy)
-        highs = gather_xy(chi, x0, y0, wx, wy)
-        masks = [jnp.logical_xor(((lane - (c + t - 1)) & -128) == 0, upper) for t in range(4)]
-        turns = [(1 - c - t) & 127 for t in range(4)]
-        rows = pl.ds(pl.multiple_of(by * 8, 8), 8)
         for p in range(8):
-            value = sum(wz[t] * pltpu.roll(jnp.where(masks[t], lows[p], highs[p]), turns[t], 1) for t in range(4))
-            x = bx * 8 + p
-            a1[x, rows, :] = a1[x, rows, :] + value
-            e1[x, rows, :] = e1[x, rows, :] + jnp.where(upper, edges[0][p], edges[1][p])
-        return 0
-
-    lax.fori_loop(0, 16, first_step, 0)
-
-    def second_step(i, _):
+            e1[rows[p], :] = e1[rows[p], :] + jnp.where(upper, edges[0][p], edges[1][p])
+
+    loop(16, first_step, UN_FIRST)
+
+    def second_step(i):
         ix, iy = i // 2, i % 2
         (a, b, c), (wx, wy, wz) = block_numbers(meta, 24 + 8 + 1, 1, ix, iy)
         x0, y0 = ix * 8 + 7 + a, iy * 8 + 7 + b
-        inner = gather_xy(a1, x0, y0, wx, wy)
-        outer = gather_xy(e1, x0, y0, wx, wy)
+        inner = gather_xy(a1, 32, x0, y0, wx, wy)
+        outer = gather_xy(e1, 32, x0, y0, wx, wy)
         masks = [((lane - (c + t - 1)) & -128) == 0 for t in range(4)]
         turns = [(1 - c - t) & 127 for t in range(4)]
         back = [(c + t - 1) & 127 for t in range(4)]
@@ -303,25 +332,27 @@
             turned = [pltpu.roll(state, back[t], 1) for t in range(4)]
             to_a.append(sum(in_w[t] * turned[t] for t in range(4)))
             to_e.append(sum(out_w[t] * turned[t] for t in range(4)))
-        scatter_xy(ra, to_a, x0, y0, wx, wy)
-        scatter_xy(re, to_e, x0, y0, wx, wy)
-        return 0
-
-    lax.fori_loop(0, 4, second_step, 0)
+        scatter_xy(ra, 40, to_a, x0, y0, wx, wy)
+        scatter_xy(re, 40, to_e, x0, y0, wx, wy)
+
+    loop(4, second_step, UN_SECOND)
 
     wide = lanes(32)
     quarter = ((wide + 16) & 127) // 32
-    for h in range(2):
-        for x in range(4):
-            u, d = None, None
-            for g in range(4):
-                a, e = ra[16 * h + 4 * g + x, 0:32], re[16 * h + 4 * g + x, 0:32]
-                rise = roll(jnp.where(wide >= 64, a, e), 32 * g)
-                fall = roll(jnp.where(wide >= 64, e, a), 32 * g)
-                u = rise if g == 0 else jnp.where(quarter == g, rise, u)
-                d = fall if g == 0 else jnp.where(quarter == g, fall, d)
-            up[h * 4 + x] = u
-            down[h * 4 + x] = d
+
+    def pack(i):
+        u, d = None, None
+        for g in range(4):
+            rows = pl.ds(pl.multiple_of((16 * (i // 4) + 4 * g + i % 4) * 40, 8), 32)
+            a, e = ra[rows], re[rows]
+            rise = roll(jnp.where(wide >= 64, a, e), 32 * g)
+            fall = roll(jnp.where(wide >= 64, e, a), 32 * g)
+            u = rise if g == 0 else jnp.where(quarter == g, rise, u)
+            d = fall if g == 0 else jnp.where(quarter == g, fall, d)
+        up[i] = u
+        down[i] = d
+
+    loop(8, pack, UN_PACK)
 
 
 def sum_z_kernel(ra, own_up, own_down, low, high, up, down):
@@ -338,7 +369,7 @@
             up[pl.ds(R_E + (h * 4 + x) * T, T)] = outer[16:32]
             for g in range(4):
                 at = 16 * h + 4 * g + x
-                value = ra[at, 0:32] + jnp.where(valid, roll(inner, -32 * g), 0.0)
+                value = ra[pl.ds(at * 40, 32)] + jnp.where(valid, roll(inner, -32 * g), 0.0)
                 down[pl.ds(at * T, T)] = value[0:16]
                 up[pl.ds(at * T, T)] = value[16:32]
 
@@ -363,28 +394,34 @@
     wide = lanes(32)
     valid = (wide < 16) | (wide >= 112)
     for h, (mine, other, keep) in enumerate(((own_down, low, low_in), (own_up, high, high_in))):
-        for x in range(16):
-            rows = pl.ds(x * 32, 32)
-            a1[16 * h + x] = mine[rows] + keep * other[rows]
-        for x in range(4):
-            rows = pl.ds(R_E + x * 32, 32)
+
+        def unpack(x, h=h, mine=mine, other=other, keep=keep):
+            rows = pl.ds(pl.multiple_of(R_E + x * 32, 8), 32)
             packed = mine[rows] + keep * other[rows]
             for q in range(4):
-                e1[16 * h + 4 * q + x] = jnp.where(valid, roll(packed, -32 * q), 0.0)
-    acc[...] = jnp.zeros(acc.shape, F32)
+                at = pl.multiple_of((4 * q + x) * 32, 8)
+                e1[pl.ds(512 * h + at, 32)] = jnp.where(valid, roll(packed, -32 * q), 0.0)
+                a1[pl.ds(512 * h + at, 32)] = mine[pl.ds(at, 32)] + keep * other[pl.ds(at, 32)]
+
+        loop(4, unpack, UN_UNPACK)
+
+    def clear(i):
+        acc[pl.ds(pl.multiple_of(i * 168, 8), 168)] = jnp.zeros((168, L), F32)
+
+    loop(16, clear)
     for copy in copies:
         copy.wait()
     lane = lanes()
     upper = lane >= 64
 
-    def step(i, _):
+    def step(i):
         bx, by = i // 4, i % 4
         (slot_x, ix), (slot_y, iy) = block_of(bx), block_of(by)
         row = slot_x * 24 + slot_y * 8
         keep = jnp.where(slot_x == 0, low_in, jnp.where(slot_x == 2, high_in, 1.0))
-        rows = pl.ds(pl.multiple_of(by * 8, 8), 8)
-        inner = [a1[bx * 8 + p, rows, :] for p in range(8)]
-        outer = [e1[bx * 8 + p, rows, :] for p in range(8)]
+        rows = [pl.ds(pl.multiple_of(bx * 256 + by * 8, 8) + p * 32, 8) for p in range(8)]
+        inner = [a1[r, :] for r in rows]
+        outer = [e1[r, :] for r in rows]
         for n in range(3):
             (a, b, c), (wx, wy, wz) = block_numbers(meta, row + n, 0, ix, iy, keep)
             back = [(c + t - 1) & 127 for t in range(4)]
@@ -396,14 +433,16 @@
                 w = [jnp.where(lands, wz[t], 0.0) for t in range(4)]
                 values = [jnp.where(upper if n == 0 else jnp.logical_not(upper), value, 0.0) for value in outer]
             moved = [sum(w[t] * pltpu.roll(value, back[t], 1) for t in range(4)) for value in values]
-            scatter_xy(acc, moved, bx * 8 + 7 + a, by * 8 + 7 + b, wx, wy)
-        return 0
-
-    lax.fori_loop(0, 16, step, 0)
-    for x in range(T):
-        first, second = acc[16 + x, 16:32], a1[8 + x, 8:24]
+            scatter_xy(acc, 56, moved, bx * 8 + 7 + a, by * 8 + 7 + b, wx, wy)
+
+    loop(16, step, UN_STEP)
+
+    def finish(x):
+        first, second = acc[pl.ds(pl.multiple_of((16 + x) * 56 + 16, 8), 16)], a1[pl.ds(pl.multiple_of((8 + x) * 32 + 8, 8), 16)]
         for c in range(3):
             out[c, x] = reg[c, x] + STEP_SIZE * (g[1, c, x].astype(F32) * second + g[0, c, x].astype(F32) * first)
+
+    loop(T, finish, UN_FIN)
 
 
 def laplace_kernel(v, zlow, zhigh, ylow, yhigh, xlow, xhigh, out, w):
@@ -487,8 +526,8 @@
     ra, zup, zdown = call(
         steps_kernel,
         (xup, xdown, xlow, xhigh),
-        [(32, 40, L), (8, 32, L), (8, 32, L)],
-        scratch=[vm(48, 48, L), vm(48, 48, L), vm(32, 32, L), vm(32, 32, L), vm(32, 40, L)] + meta,
+        [(32 * 40, L), (8, 32, L), (8, 32, L)],
+        scratch=[vm(48 * 48, L), vm(48 * 48, L), vm(32 * 32, L), vm(32 * 32, L), vm(32 * 40, L)] + meta,
     )
     (reg,) = call(
         laplace_kernel, (v, zlow, zhigh, ylow, yhigh, xlow, xhigh), [v.shape], scratch=[vm(24, 32, L)], cost=4000000
@@ -502,7 +541,7 @@
         last_step_kernel,
         (up, down, low, high, xlow, xup, xhigh, g, reg),
         [v.shape],
-        scratch=[vm(32, 32, L), vm(32, 32, L), vm(48, 56, L)] + meta,
+        scratch=[vm(32 * 32, L), vm(32 * 32, L), vm(48 * 56, L)] + meta,
     )
     return out
 

time: 76.4 us -> 72 us (0.942)
  Pallas kernels: 19.2 us -> 14.7 us
    pallas_call x8, Pallas kernels: 19.2 us -> 14.7 us  [call(): pl.pallas_call(kernel, out_shape=shapes, in_specs=specs, out_specs=[VMEM]...]
where the time goes in v3:
time: 72 us; the launch traced here: 71.9 us
  waiting for transfers between devices  32.1 us (45%)
  starting transfers between devices  24.9 us (35%)
  Pallas kernels  14.7 us (20%)
    ppermute x12, waiting for transfers between devices, exchange(): return (lax.ppermute(up, axis, rise), lax.ppermute(down, axis, fall))  32.1 us
    ppermute x12, starting transfers between devices, exchange(): return (lax.ppermute(up, axis, rise), lax.ppermute(down, axis, fall))  24.9 us
    pallas_call x8, Pallas kernels, call(): pl.pallas_call(kernel, out_shape=shapes, in_specs=specs, out_specs=[VMEM]...  14.7 us
  transfers between devices with their start and end apart: 12, of which 8 were waited for; matrix products, arithmetic and copies ran while one was open for 0% of the time, Pallas kernels for 5%

profile of v3, /device:TPU:1, one launch (start us, length us, event | category | flops | bytes accessed | tf_op | source)
XLA Modules:
  0.0 71.9 jit_solution(9047991568245875102)
XLA Ops:
  0.0 0.0 copy-start
  0.0 1.7 %shard_map.64 = (f32[16,16,128]{2,1,0:T(8,128)S(1)}, f32[16,16,128]{2,1,0:T(8,128)S(1)}, f32[152,128]{1,0:T(8,128)S(1)}, f32[152,128]{1,0:T(8,128)S(1)}) custom-call(f32[3,16,16,128]{3,2,1,0:T(8,128)} %v.5, bf16[2,3,16,16,128]{4,3,2,1,0:T(8,128)(2,1)} %g.1, s32[2,2,1,2]{3,2,1,0:T(1,128)} %bitcast.11, s32[2,2,1,2]{3,2,1,0:T(1,128)} %bitcast.12, ...), custom_call_target="tpu_custom_call" | custom-call | flops 20000 | bytes 20000 | tf_op jit(solution)/shard_map/pallas_call | solution.py:488
  1.7 6.5 %collective-permute-start.1 = (f32[152,128]{1,0:T(8,128)S(1)}, f32[152,128]{1,0:T(8,128)S(1)}, u32[]{:S(2)}, u32[]{:S(2)}) collective-permute-start(f32[152,128]{1,0:T(8,128)S(1)} %get-tuple-element.23), channel_id=1, source_target_pairs={{1,0},{2,1},{3,2},{4,3},{5,4},{6,5},{7,6},{0,7},{9,8},{10,9},{11,1... | collective-permute-start | bytes 233480 | tf_op jit(solution)/shard_map/ppermute | solution.py:503
  8.2 0.0 collective-permute-start
  8.2 1.4 %collective-permute-done.1.high.zhigh = f32[152,128]{1,0:T(8,128)S(1)} collective-permute-done((f32[152,128]{1,0:T(8,128)S(1)}, f32[152,128]{1,0:T(8,128)S(1)}, u32[]{:S(2)}, u32[]{:S(2)}) %collective-permute-start.1) | collective-permute-done | bytes 77856 | tf_op jit(solution)/shard_map/ppermute | solution.py:503
  9.6 3.0 %collective-permute-done.low.zlow = f32[152,128]{1,0:T(8,128)S(1)} collective-permute-done((f32[152,128]{1,0:T(8,128)S(1)}, f32[152,128]{1,0:T(8,128)S(1)}, u32[]{:S(2)}, u32[]{:S(2)}) %collective-permute-start) | collective-permute-done | bytes 77856 | tf_op jit(solution)/shard_map/ppermute | solution.py:503
  12.6 0.0 copy-done
  12.6 0.1 shard_map.65
  12.7 1.4 %collective-permute-start.2 = (f32[744,128]{1,0:T(8,128)S(1)}, f32[744,128]{1,0:T(8,128)S(1)}, u32[]{:S(2)}, u32[]{:S(2)}) collective-permute-start(f32[744,128]{1,0:T(8,128)S(1)} %get-tuple-element.24.own_up), channel_id=1, source_target_pairs={{0,8},{8,16},{16,24},{24,0},{1,9},{9,17},{17,25},{25,1},{2,10},{10... | collective-permute-start | bytes 1142792 | tf_op jit(solution)/shard_map/ppermute | solution.py:503
  14.1 1.5 %collective-permute-start.3 = (f32[744,128]{1,0:T(8,128)S(1)}, f32[744,128]{1,0:T(8,128)S(1)}, u32[]{:S(2)}, u32[]{:S(2)}) collective-permute-start(f32[744,128]{1,0:T(8,128)S(1)} %get-tuple-element.25.own_down), channel_id=1, source_target_pairs={{8,0},{16,8},{24,16},{0,24},{9,1},{17,9},{25,17},{1,25},{10,2},{18... | collective-permute-start | bytes 1142792 | tf_op jit(solution)/shard_map/ppermute | solution.py:503
  15.6 6.8 %collective-permute-done.2.low.ylow = f32[744,128]{1,0:T(8,128)S(1)} collective-permute-done((f32[744,128]{1,0:T(8,128)S(1)}, f32[744,128]{1,0:T(8,128)S(1)}, u32[]{:S(2)}, u32[]{:S(2)}) %collective-permute-start.2) | collective-permute-done | bytes 380960 | tf_op jit(solution)/shard_map/ppermute | solution.py:503
  22.4 0.0 collective-permute-done.3.high.yhigh
  22.4 0.1 shard_map.66
  22.5 3.0 %collective-permute-start.5 = (f32[1688,128]{1,0:T(8,128)S(1)}, f32[1688,128]{1,0:T(8,128)S(1)}, u32[]{:S(2)}, u32[]{:S(2)}) collective-permute-start(f32[1688,128]{1,0:T(8,128)S(1)} %get-tuple-element.27.own_down), channel_id=1, source_target_pairs={{32,0},{64,32},{96,64},{128,96},{160,128},{192,160},{224,192},{0,2... | collective-permute-start | bytes 2592776 | tf_op jit(solution)/shard_map/ppermute | solution.py:503
  25.5 1.1 %collective-permute-start.4 = (f32[1688,128]{1,0:T(8,128)S(1)}, f32[1688,128]{1,0:T(8,128)S(1)}, u32[]{:S(2)}, u32[]{:S(2)}) collective-permute-start(f32[1688,128]{1,0:T(8,128)S(1)} %get-tuple-element.26.own_up.meta_own), channel_id=1, source_target_pairs={{0,32},{32,64},{64,96},{96,128},{128,160},{160,192},{192,224},{224... | collective-permute-start | bytes 2592776 | tf_op jit(solution)/shard_map/ppermute | solution.py:503
  26.6 10.8 %collective-permute-done.5.high.xhigh.meta_high = f32[1688,128]{1,0:T(8,128)S(1)} collective-permute-done((f32[1688,128]{1,0:T(8,128)S(1)}, f32[1688,128]{1,0:T(8,128)S(1)}, u32[]{:S(2)}, u32[]{:S(2)}) %collective-permute-start.5) | collective-permute-done | bytes 864288 | tf_op jit(solution)/shard_map/ppermute | solution.py:503
  37.4 0.0 collective-permute-done.4.low.xlow.meta_low
  37.4 4.6 %shard_map.67 = (f32[1280,128]{1,0:T(8,128)S(1)}, f32[8,32,128]{2,1,0:T(8,128)S(1)}, f32[8,32,128]{2,1,0:T(8,128)S(1)}) custom-call(f32[1688,128]{1,0:T(8,128)S(1)} %get-tuple-element.26.own_up.meta_own, f32[1688,128]{1,0:T(8,128)S(1)} %get-tuple-element.27.own_down, f32[1688,128]{1,0:T(8,128)S(1)} %collective-permute-done.4.low.xlow.meta_low, ...), custom_call_target="tpu_custom_call" | custom-call | flops 20000 | bytes 20000 | tf_op jit(solution)/shard_map/pallas_call | solution.py:488
  42.0 0.1 collective-permute-start.6
  42.1 2.7 %collective-permute-start.7 = (f32[8,32,128]{2,1,0:T(8,128)S(1)}, f32[8,32,128]{2,1,0:T(8,128)S(1)}, u32[]{:S(2)}, u32[]{:S(2)}) collective-permute-start(f32[8,32,128]{2,1,0:T(8,128)S(1)} %get-tuple-element.30.own_down), channel_id=1, source_target_pairs={{1,0},{2,1},{3,2},{4,3},{5,4},{6,5},{7,6},{0,7},{9,8},{10,9},{11,1... | collective-permute-start | bytes 393224 | tf_op jit(solution)/shard_map/ppermute | solution.py:503
  44.7 2.4 %collective-permute-done.6.low = f32[8,32,128]{2,1,0:T(8,128)S(1)} collective-permute-done((f32[8,32,128]{2,1,0:T(8,128)S(1)}, f32[8,32,128]{2,1,0:T(8,128)S(1)}, u32[]{:S(2)}, u32[]{:S(2)}) %collective-permute-start.6) | collective-permute-done | bytes 131104 | tf_op jit(solution)/shard_map/ppermute | solution.py:503
  47.1 0.0 collective-permute-done.7.high
  47.1 0.2 shard_map.68
  47.3 1.4 %collective-permute-start.8 = (f32[640,128]{1,0:T(8,128)S(1)}, f32[640,128]{1,0:T(8,128)S(1)}, u32[]{:S(2)}, u32[]{:S(2)}) collective-permute-start(f32[640,128]{1,0:T(8,128)S(1)} %get-tuple-element.31.own_up), channel_id=1, source_target_pairs={{0,8},{8,16},{16,24},{24,0},{1,9},{9,17},{17,25},{25,1},{2,10},{10... | collective-permute-start | bytes 983048 | tf_op jit(solution)/shard_map/ppermute | solution.py:503
  48.6 1.7 %collective-permute-start.9 = (f32[640,128]{1,0:T(8,128)S(1)}, f32[640,128]{1,0:T(8,128)S(1)}, u32[]{:S(2)}, u32[]{:S(2)}) collective-permute-start(f32[640,128]{1,0:T(8,128)S(1)} %get-tuple-element.32.own_down), channel_id=1, source_target_pairs={{8,0},{16,8},{24,16},{0,24},{9,1},{17,9},{25,17},{1,25},{10,2},{18... | collective-permute-start | bytes 983048 | tf_op jit(solution)/shard_map/ppermute | solution.py:503
  50.3 4.8 %collective-permute-done.8.low = f32[640,128]{1,0:T(8,128)S(1)} collective-permute-done((f32[640,128]{1,0:T(8,128)S(1)}, f32[640,128]{1,0:T(8,128)S(1)}, u32[]{:S(2)}, u32[]{:S(2)}) %collective-permute-start.8) | collective-permute-done | bytes 327712 | tf_op jit(solution)/shard_map/ppermute | solution.py:503
  55.1 0.0 collective-permute-done.9.high
  55.1 0.1 shard_map.69
  55.2 5.6 %collective-permute-start.10 = (f32[640,128]{1,0:T(8,128)S(1)}, f32[640,128]{1,0:T(8,128)S(1)}, u32[]{:S(2)}, u32[]{:S(2)}) collective-permute-start(f32[640,128]{1,0:T(8,128)S(1)} %get-tuple-element.33.own_up), channel_id=1, source_target_pairs={{0,32},{32,64},{64,96},{96,128},{128,160},{160,192},{192,224},{224... | collective-permute-start | bytes 983048 | tf_op jit(solution)/shard_map/ppermute | solution.py:503
  60.8 0.0 copy-start.1
  60.8 0.0 collective-permute-start.11
  60.8 3.6 %shard_map.70.reg = f32[3,16,16,128]{3,2,1,0:T(8,128)S(1)} custom-call(f32[3,16,16,128]{3,2,1,0:T(8,128)S(1)} %copy-done, f32[152,128]{1,0:T(8,128)S(1)} %collective-permute-done.low.zlow, f32[152,128]{1,0:T(8,128)S(1)} %collective-permute-done.1.high.zhigh, f32[744,128]{1,0:T(8,128)S(1)} %collective-permute-done.2.low.ylow, ...), custom_call_target="tpu_custom_call" | custom-call | flops 4000000 | bytes 4000000 | tf_op jit(solution)/shard_map/pallas_call | solution.py:488
  64.4 0.4 collective-permute-done.10.low
  64.8 2.5 %collective-permute-done.11.high = f32[640,128]{1,0:T(8,128)S(1)} collective-permute-done((f32[640,128]{1,0:T(8,128)S(1)}, f32[640,128]{1,0:T(8,128)S(1)}, u32[]{:S(2)}, u32[]{:S(2)}) %collective-permute-start.11) | collective-permute-done | bytes 327712 | tf_op jit(solution)/shard_map/ppermute | solution.py:503
  67.3 0.0 copy-done.1
  67.3 4.4 %shard_map.71 = f32[3,16,16,128]{3,2,1,0:T(8,128)} custom-call(f32[640,128]{1,0:T(8,128)S(1)} %get-tuple-element.33.own_up, f32[640,128]{1,0:T(8,128)S(1)} %get-tuple-element.34.own_down, f32[640,128]{1,0:T(8,128)S(1)} %collective-permute-done.10.low, f32[640,128]{1,0:T(8,128)S(1)} %collective-permute-done.11.high, ...), custom_call_target="tpu_custom_call" | custom-call | flops 20000 | bytes 20000 | tf_op jit(solution)/shard_map/pallas_call | solution.py:488
Async XLA Ops:
  0.0 12.6 %copy-start = (f32[3,16,16,128]{3,2,1,0:T(8,128)S(1)}, f32[3,16,16,128]{3,2,1,0:T(8,128)}, u32[]{:S(2)}) copy-start(f32[3,16,16,128]{3,2,1,0:T(8,128)} %v.5) | copy-start | bytes 1179652
  1.7 7.9 %collective-permute-start.1 = (f32[152,128]{1,0:T(8,128)S(1)}, f32[152,128]{1,0:T(8,128)S(1)}, u32[]{:S(2)}, u32[]{:S(2)}) collective-permute-start(f32[152,128]{1,0:T(8,128)S(1)} %get-tuple-element.23), channel_id=1, source_target_pairs={{1,0},{2,1},{3,2},{4,3},{5,4},{6,5},{7,6},{0,7},{9,8},{10,9},{11,1... | collective-permute-start | bytes 233480 | tf_op jit(solution)/shard_map/ppermute | solution.py:503
  8.2 4.5 %collective-permute-start = (f32[152,128]{1,0:T(8,128)S(1)}, f32[152,128]{1,0:T(8,128)S(1)}, u32[]{:S(2)}, u32[]{:S(2)}) collective-permute-start(f32[152,128]{1,0:T(8,128)S(1)} %get-tuple-element.22.own), channel_id=1, source_target_pairs={{0,1},{1,2},{2,3},{3,4},{4,5},{5,6},{6,7},{7,0},{8,9},{9,10},{10,1... | collective-permute-start | bytes 233480 | tf_op jit(solution)/shard_map/ppermute | solution.py:503
  12.7 9.6 %collective-permute-start.2 = (f32[744,128]{1,0:T(8,128)S(1)}, f32[744,128]{1,0:T(8,128)S(1)}, u32[]{:S(2)}, u32[]{:S(2)}) collective-permute-start(f32[744,128]{1,0:T(8,128)S(1)} %get-tuple-element.24.own_up), channel_id=1, source_target_pairs={{0,8},{8,16},{16,24},{24,0},{1,9},{9,17},{17,25},{25,1},{2,10},{10... | collective-permute-start | bytes 1142792 | tf_op jit(solution)/shard_map/ppermute | solution.py:503
  14.1 8.3 %collective-permute-start.3 = (f32[744,128]{1,0:T(8,128)S(1)}, f32[744,128]{1,0:T(8,128)S(1)}, u32[]{:S(2)}, u32[]{:S(2)}) collective-permute-start(f32[744,128]{1,0:T(8,128)S(1)} %get-tuple-element.25.own_down), channel_id=1, source_target_pairs={{8,0},{16,8},{24,16},{0,24},{9,1},{17,9},{25,17},{1,25},{10,2},{18... | collective-permute-start | bytes 1142792 | tf_op jit(solution)/shard_map/ppermute | solution.py:503
  22.5 14.9 %collective-permute-start.5 = (f32[1688,128]{1,0:T(8,128)S(1)}, f32[1688,128]{1,0:T(8,128)S(1)}, u32[]{:S(2)}, u32[]{:S(2)}) collective-permute-start(f32[1688,128]{1,0:T(8,128)S(1)} %get-tuple-element.27.own_down), channel_id=1, source_target_pairs={{32,0},{64,32},{96,64},{128,96},{160,128},{192,160},{224,192},{0,2... | collective-permute-start | bytes 2592776 | tf_op jit(solution)/shard_map/ppermute | solution.py:503
  25.5 11.9 %collective-permute-start.4 = (f32[1688,128]{1,0:T(8,128)S(1)}, f32[1688,128]{1,0:T(8,128)S(1)}, u32[]{:S(2)}, u32[]{:S(2)}) collective-permute-start(f32[1688,128]{1,0:T(8,128)S(1)} %get-tuple-element.26.own_up.meta_own), channel_id=1, source_target_pairs={{0,32},{32,64},{64,96},{96,128},{128,160},{160,192},{192,224},{224... | collective-permute-start | bytes 2592776 | tf_op jit(solution)/shard_map/ppermute | solution.py:503
  42.0 5.1 %collective-permute-start.6 = (f32[8,32,128]{2,1,0:T(8,128)S(1)}, f32[8,32,128]{2,1,0:T(8,128)S(1)}, u32[]{:S(2)}, u32[]{:S(2)}) collective-permute-start(f32[8,32,128]{2,1,0:T(8,128)S(1)} %get-tuple-element.29.own_up), channel_id=1, source_target_pairs={{0,1},{1,2},{2,3},{3,4},{4,5},{5,6},{6,7},{7,0},{8,9},{9,10},{10,1... | collective-permute-start | bytes 393224 | tf_op jit(solution)/shard_map/ppermute | solution.py:503
  42.1 5.0 %collective-permute-start.7 = (f32[8,32,128]{2,1,0:T(8,128)S(1)}, f32[8,32,128]{2,1,0:T(8,128)S(1)}, u32[]{:S(2)}, u32[]{:S(2)}) collective-permute-start(f32[8,32,128]{2,1,0:T(8,128)S(1)} %get-tuple-element.30.own_down), channel_id=1, source_target_pairs={{1,0},{2,1},{3,2},{4,3},{5,4},{6,5},{7,6},{0,7},{9,8},{10,9},{11,1... | collective-permute-start | bytes 393224 | tf_op jit(solution)/shard_map/ppermute | solution.py:503
  47.3 7.9 %collective-permute-start.8 = (f32[640,128]{1,0:T(8,128)S(1)}, f32[640,128]{1,0:T(8,128)S(1)}, u32[]{:S(2)}, u32[]{:S(2)}) collective-permute-start(f32[640,128]{1,0:T(8,128)S(1)} %get-tuple-element.31.own_up), channel_id=1, source_target_pairs={{0,8},{8,16},{16,24},{24,0},{1,9},{9,17},{17,25},{25,1},{2,10},{10... | collective-permute-start | bytes 983048 | tf_op jit(solution)/shard_map/ppermute | solution.py:503
  48.6 6.5 %collective-permute-start.9 = (f32[640,128]{1,0:T(8,128)S(1)}, f32[640,128]{1,0:T(8,128)S(1)}, u32[]{:S(2)}, u32[]{:S(2)}) collective-permute-start(f32[640,128]{1,0:T(8,128)S(1)} %get-tuple-element.32.own_down), channel_id=1, source_target_pairs={{8,0},{16,8},{24,16},{0,24},{9,1},{17,9},{25,17},{1,25},{10,2},{18... | collective-permute-start | bytes 983048 | tf_op jit(solution)/shard_map/ppermute | solution.py:503
  55.2 9.6 %collective-permute-start.10 = (f32[640,128]{1,0:T(8,128)S(1)}, f32[640,128]{1,0:T(8,128)S(1)}, u32[]{:S(2)}, u32[]{:S(2)}) collective-permute-start(f32[640,128]{1,0:T(8,128)S(1)} %get-tuple-element.33.own_up), channel_id=1, source_target_pairs={{0,32},{32,64},{64,96},{96,128},{128,160},{160,192},{192,224},{224... | collective-permute-start | bytes 983048 | tf_op jit(solution)/shard_map/ppermute | solution.py:503
  60.8 6.5 %copy-start.1 = (bf16[2,3,16,16,128]{4,3,2,1,0:T(8,128)(2,1)S(1)}, bf16[2,3,16,16,128]{4,3,2,1,0:T(8,128)(2,1)}, u32[]{:S(2)}) copy-start(bf16[2,3,16,16,128]{4,3,2,1,0:T(8,128)(2,1)} %g.1) | copy-start | bytes 1179652
  60.8 6.5 %collective-permute-start.11 = (f32[640,128]{1,0:T(8,128)S(1)}, f32[640,128]{1,0:T(8,128)S(1)}, u32[]{:S(2)}, u32[]{:S(2)}) collective-permute-start(f32[640,128]{1,0:T(8,128)S(1)} %get-tuple-element.34.own_down), channel_id=1, source_target_pairs={{32,0},{64,32},{96,64},{128,96},{160,128},{192,160},{224,192},{0,2... | collective-permute-start | bytes 983048 | tf_op jit(solution)/shard_map/ppermute | solution.py:503

commit v4 on v3

v4 whole, which is shorter than its diff:
```python
import jax
import jax.numpy as jnp
from jax import lax
from jax.experimental import pallas as pl
from jax.experimental.pallas import tpu as pltpu
from jax.sharding import PartitionSpec as P

F32 = jnp.float32
LAPLACE_TAPS = (-205.0 / 72.0, 8.0 / 5.0, -1.0 / 5.0, 8.0 / 315.0, -1.0 / 560.0)
STEP_SIZE = 0.5
REG_WEIGHT = 0.1
T = 16
L = 128
UN_ASM, UN_CORNER, UN_FIRST, UN_SECOND, UN_PACK, UN_UNPACK, UN_STEP, UN_FIN = 4, 4, 16, 1, 8, 4, 16, 16
META = 15

Z_S0, Z_S1, Z_V, Z_META, Z_ROWS = 0, 128, 256, 304, 312
A0, E0, A1, E1, FACE, NUMBERS, ROWS = 0, 256, 512, 640, 768, 960, 968
C_LOW, C_HIGH, C_A1, C_E1, C_META, C_ROWS = 0, 512, 1024, 1152, 1280, 1296
R_E, R_ROWS = 512, 640


def lanes(rows=8):
    return lax.broadcasted_iota(jnp.int32, (rows, L), 1)


def subs():
    return lax.broadcasted_iota(jnp.int32, (8, L), 0)


def roll(x, amount):
    amount = amount % L
    return x if amount == 0 else pltpu.roll(x, amount, 1)


def block_numbers(meta, row, step, ix, iy):
    at = ((step * 2 + ix) * 2 + iy) * META
    shift = [meta[row, at + d].astype(jnp.int32) for d in range(3)]
    weights = [[meta[row, at + 3 + 4 * d + t] for t in range(4)] for d in range(3)]
    return shift, weights


def loop(count, body, unroll=1):
    def step(i, _):
        body(i)
        return 0

    lax.fori_loop(0, count, step, 0, unroll=unroll)


def inside(axis):
    i, n = lax.axis_index(axis), lax.axis_size(axis)
    return jnp.where(i > 0, 1.0, 0.0).astype(F32), jnp.where(i < n - 1, 1.0, 0.0).astype(F32)


def sources_kernel(v_hbm, g_hbm, sx_hbm, sy_hbm, sz_hbm, fr_hbm, s0, s1, up, down, v, g, sx, sy, sz, fr, sem, small_sem):
    copies = []
    for q in range(4):
        part = pl.ds(4 * q, 4)
        copies.append(pltpu.make_async_copy(v_hbm.at[:, part], v.at[:, part], sem.at[2 * q]))
        copies.append(pltpu.make_async_copy(g_hbm.at[:, :, part], g.at[:, :, part], sem.at[2 * q + 1]))
    small = [
        pltpu.make_async_copy(a, b, small_sem.at[n])
        for n, (a, b) in enumerate(((sx_hbm, sx), (sy_hbm, sy), (sz_hbm, sz), (fr_hbm, fr)))
    ]
    for copy in copies + small:
        copy.start()
    lane = lanes(T)
    for x in range(T):
        if x % 4 == 0:
            copies[x // 2].wait()
            copies[x // 2 + 1].wait()
        vel = [v[c, x] for c in range(3)]
        for k, s in ((0, s0), (1, s1)):
            total = g[k, 0, x].astype(F32) * vel[0]
            for c in (1, 2):
                total = total + g[k, c, x].astype(F32) * vel[c]
            s[x] = STEP_SIZE * total
    upper = lane >= 64
    for start, s in ((Z_S0, s0), (Z_S1, s1)):
        for x in range(8):
            rows = pl.ds(start + x * T, T)
            a, b = s[x], roll(s[x + 8], 64)
            up[rows] = jnp.where(upper, a, b)
            down[rows] = jnp.where(upper, b, a)
    piece = lane // 8
    for c in range(3):
        u, d = v[c, 0], v[c, 0]
        for x in range(1, T):
            r = roll(v[c, x], 8 * x)
            u = jnp.where(piece == (15 + x) % 16, r, u)
            d = jnp.where(piece == x, r, d)
        up[pl.ds(Z_V + c * T, T)] = u
        down[pl.ds(Z_V + c * T, T)] = d
    lane = lanes()
    for copy in small:
        copy.wait()
    shifts, eighths = jnp.zeros((8, L), jnp.int32), jnp.zeros((8, L), jnp.int32)
    for k in range(2):
        for ix in range(2):
            for iy in range(2):
                at = ((k * 2 + ix) * 2 + iy) * META
                for n, ref in enumerate((sx, sy, sz)):
                    shifts = jnp.where(lane == at + n, ref[k, ix, 0, iy], shifts)
                    first = at + 3 + 4 * n
                    eighths = jnp.where((lane >= first) & (lane < first + 4), fr[k, ix, iy, 0, n], eighths)
    e = eighths.astype(F32) / 8.0
    e2 = e * e
    e3 = e2 * e
    weights = [
        0.5 * (2.0 * e2 - e3 - e),
        0.5 * (3.0 * e3 - 5.0 * e2 + 2.0),
        0.5 * (4.0 * e2 - 3.0 * e3 + e),
        0.5 * (e3 - e2),
    ]
    place = lane % META
    tap = (place - 3) % 4
    row = jnp.where(tap == 0, weights[0], jnp.where(tap == 1, weights[1], jnp.where(tap == 2, weights[2], weights[3])))
    row = jnp.where(place < 3, shifts.astype(F32), row)
    up[pl.ds(Z_META, 8)] = row
    down[pl.ds(Z_META, 8)] = row


def tile_messages_kernel(s0, s1, v, own, low, high, yup, ydown, xup, xdown):
    low_in, high_in = inside("gz")
    upper = lanes(T) >= 64
    outs = (yup, ydown, xup, xdown)
    for start, to, s in ((Z_S0, 0, s0), (Z_S1, 1, s1)):
        for j in range(8):
            a, b = low_in * low[pl.ds(start + j * T, T)], high_in * high[pl.ds(start + j * T, T)]
            edges = (jnp.where(upper, a, b), roll(jnp.where(upper, b, a), 64))
            for h in range(2):
                x = j + 8 * h
                for at, value in ((0, s[x]), (1, edges[h])):
                    if to == 0:
                        for out in outs:
                            out[pl.ds((A0, E0)[at] + x * T, T)] = value
                    else:
                        yup[pl.ds((A1, E1)[at] + x * 8, 8)] = value[8:16]
                        ydown[pl.ds((A1, E1)[at] + x * 8, 8)] = value[0:8]
                        (xdown, xup)[h][pl.ds((A1, E1)[at] + j * T, T)] = value
    first_half = subs() < 4
    for c in range(3):
        for x in range(8):
            rows = pl.ds(FACE + (c * 8 + x) * 8, 8)
            yup[rows] = jnp.where(first_half, pltpu.roll(v[c, x + 8, 8:16], 4, 0), v[c, x, 8:16])
            ydown[rows] = jnp.where(first_half, v[c, x, 0:8], pltpu.roll(v[c, x + 8, 0:8], 4, 0))
        for i in range(4):
            xup[pl.ds(FACE + (c * 4 + i) * T, T)] = v[c, 12 + i]
            xdown[pl.ds(FACE + (c * 4 + i) * T, T)] = v[c, i]
    sub = subs()
    meta = [ref[pl.ds(Z_META, 8)] for ref in (low, own, high)]
    row = jnp.where(sub == 0, low_in * meta[0], jnp.where(sub == 1, meta[1], high_in * meta[2]))
    for out in outs:
        out[pl.ds(NUMBERS, 8)] = row


def corner_message_kernel(low, high, xlow, xhigh, up, down):
    del xlow, xhigh
    for y, (ref, keep, to) in enumerate(zip((low, high), inside("gy"), (C_LOW, C_HIGH))):
        for x in range(2 * T):
            value = keep * ref[pl.ds(A0 + x * T, T)]
            up[pl.ds(to + x * T, T)] = value
            down[pl.ds(to + x * T, T)] = value
        for start, place in ((A1, C_A1), (E1, C_E1)):
            for x in range(8):
                down[pl.ds(place + x * T + 8 * y, 8)] = keep * ref[pl.ds(start + x * 8, 8)]
                up[pl.ds(place + x * T + 8 * y, 8)] = keep * ref[pl.ds(start + (8 + x) * 8, 8)]
        value = keep * ref[pl.ds(NUMBERS, 8)]
        up[pl.ds(C_META + 8 * y, 8)] = value
        down[pl.ds(C_META + 8 * y, 8)] = value


def put(low, high, rows, upper, a, e):
    low[rows] = jnp.where(upper, e, a)
    high[rows] = jnp.where(upper, a, e)


def assemble_kernel(own_up, own_down, xlow, xhigh, ylow, yhigh, c_low, c_high, d_low, d_high):
    (xl, xh), (yl, yh) = inside("gx"), inside("gy")
    upper, upper8 = lanes(T) >= 64, lanes(8) >= 64

    def first(x):
        at = pl.multiple_of(x * T, 8)
        for ref, keep, dx, dy in ((own_up, None, 16, 16), (xlow, xl, 0, 16), (xhigh, xh, 32, 16), (ylow, yl, 16, 0), (yhigh, yh, 16, 32)):
            a, e = ref[pl.ds(A0 + at, T)], ref[pl.ds(E0 + at, T)]
            if keep is not None:
                a, e = keep * a, keep * e
            put(c_low, c_high, pl.ds(pl.multiple_of((dx + x) * 48 + dy, 8), T), upper, a, e)

    loop(T, first, UN_ASM)

    def second(x):
        at = pl.multiple_of(x * T, 8)
        for ref, keep, dx in ((own_down, None, 8), (own_up, None, 16), (xlow, xl, 0), (xhigh, xh, 24)):
            a, e = ref[pl.ds(A1 + at, T)], ref[pl.ds(E1 + at, T)]
            if keep is not None:
                a, e = keep * a, keep * e
            put(d_low, d_high, pl.ds(pl.multiple_of((dx + x) * 32 + 8, 8), T), upper, a, e)
        for h in range(2):
            at = pl.multiple_of((8 * h + x) * 8, 8)
            for ref, keep, dy in ((ylow, yl, 0), (yhigh, yh, 24)):
                a, e = keep * ref[pl.ds(A1 + at, 8)], keep * ref[pl.ds(E1 + at, 8)]
                put(d_low, d_high, pl.ds(pl.multiple_of((8 + 8 * h + x) * 32 + dy, 8), 8), upper8, a, e)

    loop(8, second, UN_ASM)


def gather_xy(ref, width, x0, y0, wx, wy):
    base = x0 * width + y0
    planes = []
    for i in range(11):
        plane = wy[0] * ref[pl.ds(base + i * width, 8), :]
        for t in range(1, 4):
            plane = plane + wy[t] * ref[pl.ds(base + (i * width + t), 8), :]
        planes.append(plane)
    out = []
    for i in range(8):
        value = wx[0] * planes[i]
        for t in range(1, 4):
            value = value + wx[t] * planes[i + t]
        out.append(value)
    return out


def scatter_xy(ref, width, vals, x0, y0, wx, wy):
    sub = subs()
    base = x0 * width + y0
    places = [pl.ds(base + (p * width + 8 * half), 8) for p in range(11) for half in range(2)]
    low_w = [jnp.where(sub >= t, wy[t], 0.0) for t in range(4)]
    high_w = [jnp.where(sub < t, wy[t], 0.0) for t in range(4)]
    pairs = []
    for value in vals:
        first, second = wy[0] * value, None
        for t in range(1, 4):
            turned = pltpu.roll(value, t, 0)
            first = first + low_w[t] * turned
            second = high_w[t] * turned if second is None else second + high_w[t] * turned
        pairs.append((first, second))
    sums = []
    for p in range(11):
        for half in range(2):
            total = ref[places[len(sums)], :]
            for t in range(4):
                if 0 <= p - t < 8:
                    total = total + wx[t] * pairs[p - t][half]
            sums.append(total)
    for place, total in zip(places, sums):
        ref[place, :] = total


def block_of(b):
    return (b + 1) // 2, (b + 1) % 2


def steps_kernel(
    own, xlow, xhigh, ylow, yhigh, corner_low, corner_high, c_low_in, c_high_in, d_low_in, d_high_in,
    up, down, numbers, c_low, c_high, d_low, d_high, r_low, r_high, meta, sem,
):
    (xl, xh), (yl, yh) = inside("gx"), inside("gy")
    lane = lanes()
    upper = lane >= 64
    tiles = (
        (0, xl * corner_low[pl.ds(C_META, 8)]),
        (8, xl * xlow[pl.ds(NUMBERS, 8)]),
        (16, xl * corner_low[pl.ds(C_META + 8, 8)]),
        (24, yl * ylow[pl.ds(NUMBERS, 8)]),
        (32, own[pl.ds(NUMBERS, 8)]),
        (40, yh * yhigh[pl.ds(NUMBERS, 8)]),
        (48, xh * corner_high[pl.ds(C_META, 8)]),
        (56, xh * xhigh[pl.ds(NUMBERS, 8)]),
        (64, xh * corner_high[pl.ds(C_META + 8, 8)]),
    )
    for at, value in tiles:
        numbers[pl.ds(at, 8)] = value
    copy = pltpu.make_async_copy(numbers, meta, sem)
    copy.start()
    upper16 = lanes(T) >= 64

    def corners(x):
        at = pl.multiple_of(x * T, 8)
        for ref, keep, dx in ((corner_low, xl, 0), (corner_high, xh, 32)):
            for start, dy in ((C_LOW, 0), (C_HIGH, 32)):
                a, e = keep * ref[pl.ds(start + at, T)], keep * ref[pl.ds(start + 256 + at, T)]
                put(c_low, c_high, pl.ds(pl.multiple_of((dx + x) * 48 + dy, 8), T), upper16, a, e)

    loop(T, corners, UN_CORNER)

    def corners_second(x):
        at = pl.multiple_of(x * T, 8)
        for ref, keep, dx in ((corner_low, xl, 0), (corner_high, xh, 24)):
            for half, dy in ((0, 0), (8, 24)):
                a, e = keep * ref[pl.ds(C_A1 + half + at, 8)], keep * ref[pl.ds(C_E1 + half + at, 8)]
                put(d_low, d_high, pl.ds(pl.multiple_of((dx + x) * 32 + dy, 8), 8), upper, a, e)

    loop(8, corners_second, UN_CORNER)

    def clear(i):
        rows = pl.ds(pl.multiple_of(i * 128, 8), 128)
        r_low[rows] = jnp.zeros((128, L), F32)
        r_high[rows] = jnp.zeros((128, L), F32)

    loop(10, clear)
    copy.wait()

    def apply(low, high, width, row, step, ix, iy, bx, by):
        places = []
        values = []
        for n in (1, 0, 2):
            (a, b, c), (wx, wy, wz) = block_numbers(meta, row + n, step, ix, iy)
            x0, y0 = bx * 8 + 7 + a, by * 8 + 7 + b
            turns = [(1 - c - t) & 127 for t in range(4)]
            places.append((x0, y0, c, wx, wy, wz))
            if n == 1:
                masks = [jnp.logical_xor(((lane - (c + t - 1)) & -128) == 0, upper) for t in range(4)]
                lows = gather_xy(low, width, x0, y0, wx, wy)
                highs = gather_xy(high, width, x0, y0, wx, wy)
                values.append(
                    [
                        sum(wz[t] * pltpu.roll(jnp.where(masks[t], lows[p], highs[p]), turns[t], 1) for t in range(4))
                        for p in range(8)
                    ]
                )
            else:
                ins = gather_xy(low if n == 0 else high, width, x0, y0, wx, wy)
                values.append([sum(wz[t] * pltpu.roll(value, turns[t], 1) for t in range(4)) for value in ins])
        return places, values

    def first_step(i):
        bx, by = i // 4, i % 4
        (slot_x, ix), (slot_y, iy) = block_of(bx), block_of(by)
        _, (own_z, below, above) = apply(c_low, c_high, 48, slot_x * 24 + slot_y * 8, 0, ix, iy, bx, by)
        for p in range(8):
            rows = pl.ds(pl.multiple_of(bx * 256 + by * 8, 8) + p * 32, 8)
            d_low[rows, :] = d_low[rows, :] + jnp.where(upper, below[p], own_z[p])
            d_high[rows, :] = d_high[rows, :] + jnp.where(upper, own_z[p], above[p])

    loop(16, first_step, UN_FIRST)

    def second_step(i):
        ix, iy = i // 2, i % 2
        places, (own_z, below, above) = apply(d_low, d_high, 32, 32, 1, ix, iy, ix, iy)
        below = [jnp.where(lane >= 96, value, 0.0) for value in below]
        above = [jnp.where(lane < 32, value, 0.0) for value in above]
        x0, y0, c, wx, wy, wz = places[0]
        back = [(c + t - 1) & 127 for t in range(4)]
        masks = [jnp.logical_xor(((lane - (c + t - 1)) & -128) == 0, upper) for t in range(4)]
        low_w = [jnp.where(masks[t], wz[t], 0.0) for t in range(4)]
        high_w = [jnp.where(masks[t], 0.0, wz[t]) for t in range(4)]
        to_low, to_high = [], []
        for value in own_z:
            turned = [pltpu.roll(value, back[t], 1) for t in range(4)]
            to_low.append(sum(low_w[t] * turned[t] for t in range(4)))
            to_high.append(sum(high_w[t] * turned[t] for t in range(4)))
        scatter_xy(r_low, 40, to_low, x0, y0, wx, wy)
        scatter_xy(r_high, 40, to_high, x0, y0, wx, wy)
        for (x0, y0, c, wx, wy, wz), values, ref in ((places[1], below, r_low), (places[2], above, r_high)):
            back = [(c + t - 1) & 127 for t in range(4)]
            moved = [sum(wz[t] * pltpu.roll(value, back[t], 1) for t in range(4)) for value in values]
            scatter_xy(ref, 40, moved, x0, y0, wx, wy)

    loop(4, second_step, UN_SECOND)

    wide = lanes(32)
    wide_upper = wide >= 64
    quarter = ((wide + 16) & 127) // 32

    def pack(i):
        packed = None
        for g in range(4):
            at = 16 * (i // 4) + 4 * g + i % 4
            rows = pl.ds(pl.multiple_of(at * 40, 8), 32)
            low, high = r_low[rows], r_high[rows]
            a = jnp.where(wide_upper, high, low)
            e = roll(jnp.where(wide_upper, low, high), 32 * g)
            packed = e if g == 0 else jnp.where(quarter == g, e, packed)
            down[pl.ds(pl.multiple_of(at * T, 8), T)] = a[0:16]
            up[pl.ds(pl.multiple_of(at * T, 8), T)] = a[16:32]
        down[pl.ds(pl.multiple_of(R_E + i * T, 8), T)] = packed[0:16]
        up[pl.ds(pl.multiple_of(R_E + i * T, 8), T)] = packed[16:32]

    loop(8, pack, UN_PACK)


def sum_y_kernel(own_up, own_down, low, high, up, down):
    low_in, high_in = inside("gy")
    for h, out in ((0, down), (1, up)):
        for start, planes in ((0, 16), (R_E, 4)):
            for x in range(planes):
                rows = pl.ds(start + (h * planes + x) * T, T)
                out[pl.ds(start + x * 32, T)] = own_down[rows] + low_in * low[rows]
                out[pl.ds(start + x * 32 + T, T)] = own_up[rows] + high_in * high[rows]


def last_step_kernel(own_up, own_down, low, high, numbers, g, reg, out, a1, e1, acc, meta, sem):
    copy = pltpu.make_async_copy(numbers, meta, sem)
    copy.start()
    low_in, high_in = inside("gx")
    wide = lanes(32)
    valid = (wide < 16) | (wide >= 112)
    for h, (mine, other, keep) in enumerate(((own_down, low, low_in), (own_up, high, high_in))):

        def unpack(x, h=h, mine=mine, other=other, keep=keep):
            rows = pl.ds(pl.multiple_of(R_E + x * 32, 8), 32)
            packed = mine[rows] + keep * other[rows]
            for q in range(4):
                at = pl.multiple_of((4 * q + x) * 32, 8)
                e1[pl.ds(512 * h + at, 32)] = jnp.where(valid, roll(packed, -32 * q), 0.0)
                a1[pl.ds(512 * h + at, 32)] = mine[pl.ds(at, 32)] + keep * other[pl.ds(at, 32)]

        loop(4, unpack, UN_UNPACK)

    def clear(i):
        acc[pl.ds(pl.multiple_of(i * 168, 8), 168)] = jnp.zeros((168, L), F32)

    loop(16, clear)
    copy.wait()
    lane = lanes()
    upper = lane >= 64

    def step(i):
        bx, by = i // 4, i % 4
        (slot_x, ix), (slot_y, iy) = block_of(bx), block_of(by)
        row = slot_x * 24 + slot_y * 8
        rows = [pl.ds(pl.multiple_of(bx * 256 + by * 8, 8) + p * 32, 8) for p in range(8)]
        inner = [a1[r, :] for r in rows]
        outer = [e1[r, :] for r in rows]
        for n in range(3):
            (a, b, c), (wx, wy, wz) = block_numbers(meta, row + n, 0, ix, iy)
            back = [(c + t - 1) & 127 for t in range(4)]
            if n == 1:
                w = [jnp.where(((lane - (c + t - 1)) & -128) == 0, wz[t], 0.0) for t in range(4)]
                values = inner
            else:
                lands = upper if n == 2 else jnp.logical_not(upper)
                w = [jnp.where(lands, wz[t], 0.0) for t in range(4)]
                values = [jnp.where(upper if n == 0 else jnp.logical_not(upper), value, 0.0) for value in outer]
            moved = [sum(w[t] * pltpu.roll(value, back[t], 1) for t in range(4)) for value in values]
            scatter_xy(acc, 56, moved, bx * 8 + 7 + a, by * 8 + 7 + b, wx, wy)

    loop(16, step, UN_STEP)

    def finish(x):
        first, second = acc[pl.ds(pl.multiple_of((16 + x) * 56 + 16, 8), 16)], a1[pl.ds(pl.multiple_of((8 + x) * 32 + 8, 8), 16)]
        for c in range(3):
            out[c, x] = reg[c, x] + STEP_SIZE * (g[1, c, x].astype(F32) * second + g[0, c, x].astype(F32) * first)

    loop(T, finish, UN_FIN)


def laplace_kernel(v, zlow, zhigh, ylow, yhigh, xlow, xhigh, out, w):
    lane = lanes(T)
    half = (lane & 4) == 0
    (x_low, x_high), (y_low, y_high), (z_low, z_high) = inside("gx"), inside("gy"), inside("gz")
    sides = [-REG_WEIGHT * t for t in LAPLACE_TAPS]
    for c in range(3):
        rows = pl.ds(Z_V + c * T, T)
        faces = jnp.where(half, z_high * zhigh[rows], z_low * zlow[rows])
        for i in range(4):
            rows = pl.ds(FACE + (c * 4 + i) * T, T)
            w[i, 8:24] = x_low * xlow[rows]
            w[20 + i, 8:24] = x_high * xhigh[rows]
        for x in range(8):
            rows = pl.ds(FACE + (c * 8 + x) * 8, 8)
            a, b = y_low * ylow[rows], y_high * yhigh[rows]
            w[4 + x, 0:8] = a
            w[12 + x, 0:8] = pltpu.roll(a, 4, 0)
            w[4 + x, 24:32] = b
            w[12 + x, 24:32] = pltpu.roll(b, 4, 0)
        for x in range(T):
            w[4 + x, 8:24] = v[c, x]
        for x in range(T):
            here = v[c, x]
            edge = roll(faces, -8 * x)
            total = 3.0 * sides[0] * here
            for k in range(1, 5):
                near = roll(jnp.where(lane < k, edge, here), -k) + roll(jnp.where(lane >= L - k, edge, here), k)
                near = near + w[4 + x - k, 8:24] + w[4 + x + k, 8:24]
                near = near + w[4 + x, 8 - k : 24 - k] + w[4 + x, 8 + k : 24 + k]
                total = total + sides[k] * near
            out[c, x] = total


VMEM = pl.BlockSpec(memory_space=pltpu.VMEM)
HBM = pl.BlockSpec(memory_space=pltpu.HBM)


def call(kernel, args, outs, scratch=(), hbm=(), cost=20000, alias=None):
    specs = [HBM if i in hbm else VMEM for i in range(len(args))]
    shapes = [jax.ShapeDtypeStruct(s, F32) for s in outs]
    return pl.pallas_call(
        kernel,
        out_shape=shapes,
        in_specs=specs,
        out_specs=[VMEM] * len(shapes),
        input_output_aliases=alias or {},
        scratch_shapes=list(scratch),
        compiler_params=pltpu.CompilerParams(vmem_limit_bytes=24 * 1024 * 1024),
        cost_estimate=pl.CostEstimate(flops=cost, bytes_accessed=cost, transcendentals=0),
    )(*args)


def exchange(up, down, axis):
    n = lax.axis_size(axis)
    rise = [(i, (i + 1) % n) for i in range(n)]
    fall = [(j, i) for i, j in rise]
    return lax.ppermute(up, axis, rise), lax.ppermute(down, axis, fall)


def body(velocity, gradients, shift_x, shift_y, shift_z, fractions):
    v, g = velocity, gradients
    tile = (T, T, L)
    vm = lambda *s: pltpu.VMEM(s, F32)
    shifts = [s.transpose(0, 1, 3, 2) for s in (shift_x, shift_y, shift_z)]
    s0, s1, zup, zdown = call(
        sources_kernel,
        [pltpu.with_memory_space_constraint(a, pltpu.HBM) for a in (v, g, *shifts, fractions.transpose(0, 2, 3, 4, 1))],
        [tile, tile, (Z_ROWS, L), (Z_ROWS, L)],
        scratch=[vm(*v.shape), pltpu.VMEM(g.shape, g.dtype)]
        + [pltpu.SMEM((2, 2, 1, 2), jnp.int32)] * 3
        + [pltpu.SMEM((2, 2, 2, 1, 3), jnp.int32), pltpu.SemaphoreType.DMA((8,)), pltpu.SemaphoreType.DMA((4,))],
        hbm=range(6),
    )
    zlow, zhigh = exchange(zup, zdown, "gz")
    yup, ydown, xup, xdown = call(tile_messages_kernel, (s0, s1, v, zup, zlow, zhigh), [(ROWS, L)] * 4)
    ylow, yhigh = exchange(yup, ydown, "gy")
    xlow, xhigh = exchange(xup, xdown, "gx")
    up, down = call(corner_message_kernel, (ylow, yhigh, xlow, xhigh), [(C_ROWS, L)] * 2)
    corner_low, corner_high = exchange(up, down, "gx")
    fields = [(48 * 48, L)] * 2 + [(32 * 32, L)] * 2
    filled = call(assemble_kernel, (xup, xdown, xlow, xhigh, ylow, yhigh), fields)
    meta = [pltpu.SMEM((72, L), F32), pltpu.SemaphoreType.DMA]
    up, down, numbers, *_ = call(
        steps_kernel,
        (xup, xlow, xhigh, ylow, yhigh, corner_low, corner_high, *filled),
        [(R_ROWS, L), (R_ROWS, L), (72, L)] + fields,
        scratch=[vm(32 * 40, L), vm(32 * 40, L)] + meta,
        alias={7: 3, 8: 4, 9: 5, 10: 6},
    )
    (reg,) = call(
        laplace_kernel, (v, zlow, zhigh, ylow, yhigh, xlow, xhigh), [v.shape], scratch=[vm(24, 32, L)], cost=4000000
    )
    low, high = exchange(up, down, "gy")
    up, down = call(sum_y_kernel, (up, down, low, high), [(R_ROWS, L)] * 2)
    low, high = exchange(up, down, "gx")
    (out,) = call(
        last_step_kernel,
        (up, down, low, high, numbers, g, reg),
        [v.shape],
        scratch=[vm(32 * 32, L), vm(32 * 32, L), vm(48 * 56, L)] + meta,
    )
    return out


def solution(mesh):
    in_specs = (
        P(None, "gx", "gy", "gz"),
        P(None, None, "gx", "gy", "gz"),
        P(None, "gx", "gy", "gz"),
        P(None, "gx", "gy", "gz"),
        P(None, "gx", "gy", "gz"),
        P(None, None, "gx", "gy", "gz"),
    )
    out_specs = P(None, "gx", "gy", "gz")
    return jax.shard_map(body, mesh=mesh, in_specs=in_specs, out_specs=out_specs, check_vma=False)
```

time: 72 us -> 70 us (0.972)
  starting transfers between devices: 24.9 us -> 20 us
  waiting for transfers between devices: 32.1 us -> 33.9 us
  local copies, waits for them, and re-layouts: 0.01 us -> 1.01 us
    ppermute x12, starting transfers between devices: 24.9 us -> 20 us  [exchange(): return (lax.ppermute(up, axis, rise), lax.ppermute(down, axis, fall))]
    ppermute x12, waiting for transfers between devices: 32.1 us -> 33.9 us  [exchange(): return (lax.ppermute(up, axis, rise), lax.ppermute(down, axis, fall))]
    unnamed x4 -> x6, local copies, waits for them, and re-layouts: 0.01 us -> 1.01 us
  transfers between devices with their start and end apart: 12 -> 12, of which waited for: 8 -> 9; matrix products, arithmetic and copies ran while one was open for 0% -> 0% of each run, Pallas kernels for 5% -> 5%
where the time goes in v4:
time: 70 us; the launch traced here: 69.9 us
  waiting for transfers between devices  33.9 us (48%)
  starting transfers between devices  20 us (29%)
  Pallas kernels  14.9 us (21%)
  local copies, waits for them, and re-layouts  1.01 us (1%)
    ppermute x12, waiting for transfers between devices, exchange(): return (lax.ppermute(up, axis, rise), lax.ppermute(down, axis, fall))  33.9 us
    ppermute x12, starting transfers between devices, exchange(): return (lax.ppermute(up, axis, rise), lax.ppermute(down, axis, fall))  20 us
    pallas_call x8, Pallas kernels, call(): pl.pallas_call(kernel, out_shape=shapes, in_specs=specs, out_specs=[VMEM]...  14.9 us
  transfers between devices with their start and end apart: 12, of which 9 were waited for; matrix products, arithmetic and copies ran while one was open for 0% of the time, Pallas kernels for 5%

profile of v4, /device:TPU:1, one launch (start us, length us, event | category | flops | bytes accessed | tf_op | source)
XLA Modules:
  0.0 69.9 jit_solution(13560319162276465983)
XLA Ops:
  0.0 1.6 %shard_map.64 = (f32[16,16,128]{2,1,0:T(8,128)S(1)}, f32[16,16,128]{2,1,0:T(8,128)S(1)}, f32[312,128]{1,0:T(8,128)S(1)}, f32[312,128]{1,0:T(8,128)S(1)}) custom-call(f32[3,16,16,128]{3,2,1,0:T(8,128)} %v.3, bf16[2,3,16,16,128]{4,3,2,1,0:T(8,128)(2,1)} %g.1, s32[2,2,1,2]{3,2,1,0:T(1,128)} %bitcast.11, s32[2,2,1,2]{3,2,1,0:T(1,128)} %bitcast.12, ...), custom_call_target="tpu_custom_call" | custom-call | flops 20000 | bytes 20000 | tf_op jit(solution)/shard_map/pallas_call | solution.py:491
  1.6 2.5 %collective-permute-start = (f32[312,128]{1,0:T(8,128)S(1)}, f32[312,128]{1,0:T(8,128)S(1)}, u32[]{:S(2)}, u32[]{:S(2)}) collective-permute-start(f32[312,128]{1,0:T(8,128)S(1)} %get-tuple-element.26.own), channel_id=1, source_target_pairs={{0,1},{1,2},{2,3},{3,4},{4,5},{5,6},{6,7},{7,0},{8,9},{9,10},{10,1... | collective-permute-start | bytes 479240 | tf_op jit(solution)/shard_map/ppermute | solution.py:507
  4.1 4.0 %collective-permute-start.1 = (f32[312,128]{1,0:T(8,128)S(1)}, f32[312,128]{1,0:T(8,128)S(1)}, u32[]{:S(2)}, u32[]{:S(2)}) collective-permute-start(f32[312,128]{1,0:T(8,128)S(1)} %get-tuple-element.27), channel_id=1, source_target_pairs={{1,0},{2,1},{3,2},{4,3},{5,4},{6,5},{7,6},{0,7},{9,8},{10,9},{11,1... | collective-permute-start | bytes 479240 | tf_op jit(solution)/shard_map/ppermute | solution.py:507
  8.2 3.7 %collective-permute-done.low.zlow = f32[312,128]{1,0:T(8,128)S(1)} collective-permute-done((f32[312,128]{1,0:T(8,128)S(1)}, f32[312,128]{1,0:T(8,128)S(1)}, u32[]{:S(2)}, u32[]{:S(2)}) %collective-permute-start) | collective-permute-done | bytes 159776 | tf_op jit(solution)/shard_map/ppermute | solution.py:507
  11.9 0.0 collective-permute-done.1.high.zhigh
  11.9 0.0 copy-start
  11.9 1.0 %copy-done = f32[3,16,16,128]{3,2,1,0:T(8,128)S(1)} copy-done((f32[3,16,16,128]{3,2,1,0:T(8,128)S(1)}, f32[3,16,16,128]{3,2,1,0:T(8,128)}, u32[]{:S(2)}) %copy-start) | copy-done | bytes 393240
  12.9 0.1 shard_map.65
  13.1 2.3 %collective-permute-start.2 = (f32[968,128]{1,0:T(8,128)S(1)}, f32[968,128]{1,0:T(8,128)S(1)}, u32[]{:S(2)}, u32[]{:S(2)}) collective-permute-start(f32[968,128]{1,0:T(8,128)S(1)} %get-tuple-element.28.own_up.own), channel_id=1, source_target_pairs={{0,32},{32,64},{64,96},{96,128},{128,160},{160,192},{192,224},{224... | collective-permute-start | bytes 1486856 | tf_op jit(solution)/shard_map/ppermute | solution.py:507
  15.4 0.0 collective-permute-start.3
  15.4 1.3 %collective-permute-start.4 = (f32[968,128]{1,0:T(8,128)S(1)}, f32[968,128]{1,0:T(8,128)S(1)}, u32[]{:S(2)}, u32[]{:S(2)}) collective-permute-start(f32[968,128]{1,0:T(8,128)S(1)} %get-tuple-element.30), channel_id=1, source_target_pairs={{0,8},{8,16},{16,24},{24,0},{1,9},{9,17},{17,25},{25,1},{2,10},{10... | collective-permute-start | bytes 1486856 | tf_op jit(solution)/shard_map/ppermute | solution.py:507
  16.7 1.4 %collective-permute-start.5 = (f32[968,128]{1,0:T(8,128)S(1)}, f32[968,128]{1,0:T(8,128)S(1)}, u32[]{:S(2)}, u32[]{:S(2)}) collective-permute-start(f32[968,128]{1,0:T(8,128)S(1)} %get-tuple-element.31), channel_id=1, source_target_pairs={{8,0},{16,8},{24,16},{0,24},{9,1},{17,9},{25,17},{1,25},{10,2},{18... | collective-permute-start | bytes 1486856 | tf_op jit(solution)/shard_map/ppermute | solution.py:507
  18.1 3.1 %collective-permute-done.2.xlow = f32[968,128]{1,0:T(8,128)S(1)} collective-permute-done((f32[968,128]{1,0:T(8,128)S(1)}, f32[968,128]{1,0:T(8,128)S(1)}, u32[]{:S(2)}, u32[]{:S(2)}) %collective-permute-start.2) | collective-permute-done | bytes 495648 | tf_op jit(solution)/shard_map/ppermute | solution.py:507
  21.2 2.8 %collective-permute-done.3.xhigh = f32[968,128]{1,0:T(8,128)S(1)} collective-permute-done((f32[968,128]{1,0:T(8,128)S(1)}, f32[968,128]{1,0:T(8,128)S(1)}, u32[]{:S(2)}, u32[]{:S(2)}) %collective-permute-start.3) | collective-permute-done | bytes 495648 | tf_op jit(solution)/shard_map/ppermute | solution.py:507
  24.0 3.7 %collective-permute-done.4.low.ylow = f32[968,128]{1,0:T(8,128)S(1)} collective-permute-done((f32[968,128]{1,0:T(8,128)S(1)}, f32[968,128]{1,0:T(8,128)S(1)}, u32[]{:S(2)}, u32[]{:S(2)}) %collective-permute-start.4) | collective-permute-done | bytes 495648 | tf_op jit(solution)/shard_map/ppermute | solution.py:507
  27.7 0.0 collective-permute-done.5.high.yhigh
  27.7 0.1 shard_map.66
  27.8 3.8 %collective-permute-start.6 = (f32[1296,128]{1,0:T(8,128)S(1)}, f32[1296,128]{1,0:T(8,128)S(1)}, u32[]{:S(2)}, u32[]{:S(2)}) collective-permute-start(f32[1296,128]{1,0:T(8,128)S(1)} %get-tuple-element.32), channel_id=1, source_target_pairs={{0,32},{32,64},{64,96},{96,128},{128,160},{160,192},{192,224},{224... | collective-permute-start | bytes 1990664 | tf_op jit(solution)/shard_map/ppermute | solution.py:507
  31.6 0.0 collective-permute-start.7
  31.6 0.2 shard_map.67
  31.9 7.4 %collective-permute-done.6.corner_low = f32[1296,128]{1,0:T(8,128)S(1)} collective-permute-done((f32[1296,128]{1,0:T(8,128)S(1)}, f32[1296,128]{1,0:T(8,128)S(1)}, u32[]{:S(2)}, u32[]{:S(2)}) %collective-permute-start.6) | collective-permute-done | bytes 663584 | tf_op jit(solution)/shard_map/ppermute | solution.py:507
  39.3 2.5 %collective-permute-done.7.corner_high = f32[1296,128]{1,0:T(8,128)S(1)} collective-permute-done((f32[1296,128]{1,0:T(8,128)S(1)}, f32[1296,128]{1,0:T(8,128)S(1)}, u32[]{:S(2)}, u32[]{:S(2)}) %collective-permute-start.7) | collective-permute-done | bytes 663584 | tf_op jit(solution)/shard_map/ppermute | solution.py:507
  41.7 4.8 %shard_map.68 = (f32[640,128]{1,0:T(8,128)S(1)}, f32[640,128]{1,0:T(8,128)S(1)}, f32[72,128]{1,0:T(8,128)S(1)}, f32[2304,128]{1,0:T(8,128)S(1)}, f32[2304,128]{1...) custom-call(f32[968,128]{1,0:T(8,128)S(1)} %get-tuple-element.28.own, ...), custom_call_target="tpu_custom_call", output_to_operand_aliasing={{3}: (7, {}), {4}: (8, {}), {5}: (9, {}), {6}: (10, {})} | custom-call | flops 20000 | bytes 20000 | tf_op jit(solution)/shard_map/pallas_call | solution.py:491
  46.5 0.0 copy-start.1
  46.5 1.4 %collective-permute-start.8 = (f32[640,128]{1,0:T(8,128)S(1)}, f32[640,128]{1,0:T(8,128)S(1)}, u32[]{:S(2)}, u32[]{:S(2)}) collective-permute-start(f32[640,128]{1,0:T(8,128)S(1)} %get-tuple-element.38.own_up), channel_id=1, source_target_pairs={{0,8},{8,16},{16,24},{24,0},{1,9},{9,17},{17,25},{25,1},{2,10},{10... | collective-permute-start | bytes 983048 | tf_op jit(solution)/shard_map/ppermute | solution.py:507
  47.9 1.4 %collective-permute-start.9 = (f32[640,128]{1,0:T(8,128)S(1)}, f32[640,128]{1,0:T(8,128)S(1)}, u32[]{:S(2)}, u32[]{:S(2)}) collective-permute-start(f32[640,128]{1,0:T(8,128)S(1)} %get-tuple-element.39.own_down), channel_id=1, source_target_pairs={{8,0},{16,8},{24,16},{0,24},{9,1},{17,9},{25,17},{1,25},{10,2},{18... | collective-permute-start | bytes 983048 | tf_op jit(solution)/shard_map/ppermute | solution.py:507
  49.4 7.6 %collective-permute-done.8.low = f32[640,128]{1,0:T(8,128)S(1)} collective-permute-done((f32[640,128]{1,0:T(8,128)S(1)}, f32[640,128]{1,0:T(8,128)S(1)}, u32[]{:S(2)}, u32[]{:S(2)}) %collective-permute-start.8) | collective-permute-done | bytes 327712 | tf_op jit(solution)/shard_map/ppermute | solution.py:507
  57.0 0.0 collective-permute-done.9.high
  57.0 0.1 shard_map.69
  57.1 1.7 %collective-permute-start.10 = (f32[640,128]{1,0:T(8,128)S(1)}, f32[640,128]{1,0:T(8,128)S(1)}, u32[]{:S(2)}, u32[]{:S(2)}) collective-permute-start(f32[640,128]{1,0:T(8,128)S(1)} %get-tuple-element.40.own_up), channel_id=1, source_target_pairs={{0,32},{32,64},{64,96},{96,128},{128,160},{160,192},{192,224},{224... | collective-permute-start | bytes 983048 | tf_op jit(solution)/shard_map/ppermute | solution.py:507
  58.8 0.0 copy-start.2
  58.8 0.0 collective-permute-start.11
  58.8 0.0 copy-done.1
  58.8 3.6 %shard_map.70.reg = f32[3,16,16,128]{3,2,1,0:T(8,128)S(1)} custom-call(f32[3,16,16,128]{3,2,1,0:T(8,128)S(1)} %copy-done.1, f32[312,128]{1,0:T(8,128)S(1)} %collective-permute-done.low.zlow, f32[312,128]{1,0:T(8,128)S(1)} %collective-permute-done.1.high.zhigh, f32[968,128]{1,0:T(8,128)S(1)} %collective-permute-done.4.low.ylow, ...), custom_call_target="tpu_custom_call" | custom-call | flops 4000000 | bytes 4000000 | tf_op jit(solution)/shard_map/pallas_call | solution.py:491
  62.4 0.4 collective-permute-done.10.low
  62.9 2.6 %collective-permute-done.11.high = f32[640,128]{1,0:T(8,128)S(1)} collective-permute-done((f32[640,128]{1,0:T(8,128)S(1)}, f32[640,128]{1,0:T(8,128)S(1)}, u32[]{:S(2)}, u32[]{:S(2)}) %collective-permute-start.11) | collective-permute-done | bytes 327712 | tf_op jit(solution)/shard_map/ppermute | solution.py:507
  65.5 0.0 copy-done.2
  65.5 4.4 %shard_map.71 = f32[3,16,16,128]{3,2,1,0:T(8,128)} custom-call(f32[640,128]{1,0:T(8,128)S(1)} %get-tuple-element.40.own_up, f32[640,128]{1,0:T(8,128)S(1)} %get-tuple-element.41.own_down, f32[640,128]{1,0:T(8,128)S(1)} %collective-permute-done.10.low, f32[640,128]{1,0:T(8,128)S(1)} %collective-permute-done.11.high, f32[72,128]{1,0:T(8,128)S(1)} %get-tuple-element.42.numbers, ...), custom_call_target="tpu_custom_call" | custom-call | flops 20000 | bytes 20000 | tf_op jit(solution)/shard_map/pallas_call | solution.py:491
Async XLA Ops:
  1.6 10.3 %collective-permute-start = (f32[312,128]{1,0:T(8,128)S(1)}, f32[312,128]{1,0:T(8,128)S(1)}, u32[]{:S(2)}, u32[]{:S(2)}) collective-permute-start(f32[312,128]{1,0:T(8,128)S(1)} %get-tuple-element.26.own), channel_id=1, source_target_pairs={{0,1},{1,2},{2,3},{3,4},{4,5},{5,6},{6,7},{7,0},{8,9},{9,10},{10,1... | collective-permute-start | bytes 479240 | tf_op jit(solution)/shard_map/ppermute | solution.py:507
  4.1 7.8 %collective-permute-start.1 = (f32[312,128]{1,0:T(8,128)S(1)}, f32[312,128]{1,0:T(8,128)S(1)}, u32[]{:S(2)}, u32[]{:S(2)}) collective-permute-start(f32[312,128]{1,0:T(8,128)S(1)} %get-tuple-element.27), channel_id=1, source_target_pairs={{1,0},{2,1},{3,2},{4,3},{5,4},{6,5},{7,6},{0,7},{9,8},{10,9},{11,1... | collective-permute-start | bytes 479240 | tf_op jit(solution)/shard_map/ppermute | solution.py:507
  11.9 1.0 %copy-start = (f32[3,16,16,128]{3,2,1,0:T(8,128)S(1)}, f32[3,16,16,128]{3,2,1,0:T(8,128)}, u32[]{:S(2)}) copy-start(f32[3,16,16,128]{3,2,1,0:T(8,128)} %v.3) | copy-start | bytes 1179652
  13.1 8.2 %collective-permute-start.2 = (f32[968,128]{1,0:T(8,128)S(1)}, f32[968,128]{1,0:T(8,128)S(1)}, u32[]{:S(2)}, u32[]{:S(2)}) collective-permute-start(f32[968,128]{1,0:T(8,128)S(1)} %get-tuple-element.28.own_up.own), channel_id=1, source_target_pairs={{0,32},{32,64},{64,96},{96,128},{128,160},{160,192},{192,224},{224... | collective-permute-start | bytes 1486856 | tf_op jit(solution)/shard_map/ppermute | solution.py:507
  15.4 8.6 %collective-permute-start.3 = (f32[968,128]{1,0:T(8,128)S(1)}, f32[968,128]{1,0:T(8,128)S(1)}, u32[]{:S(2)}, u32[]{:S(2)}) collective-permute-start(f32[968,128]{1,0:T(8,128)S(1)} %get-tuple-element.29.own_down), channel_id=1, source_target_pairs={{32,0},{64,32},{96,64},{128,96},{160,128},{192,160},{224,192},{0,2... | collective-permute-start | bytes 1486856 | tf_op jit(solution)/shard_map/ppermute | solution.py:507
  15.4 12.3 %collective-permute-start.4 = (f32[968,128]{1,0:T(8,128)S(1)}, f32[968,128]{1,0:T(8,128)S(1)}, u32[]{:S(2)}, u32[]{:S(2)}) collective-permute-start(f32[968,128]{1,0:T(8,128)S(1)} %get-tuple-element.30), channel_id=1, source_target_pairs={{0,8},{8,16},{16,24},{24,0},{1,9},{9,17},{17,25},{25,1},{2,10},{10... | collective-permute-start | bytes 1486856 | tf_op jit(solution)/shard_map/ppermute | solution.py:507
  16.7 11.0 %collective-permute-start.5 = (f32[968,128]{1,0:T(8,128)S(1)}, f32[968,128]{1,0:T(8,128)S(1)}, u32[]{:S(2)}, u32[]{:S(2)}) collective-permute-start(f32[968,128]{1,0:T(8,128)S(1)} %get-tuple-element.31), channel_id=1, source_target_pairs={{8,0},{16,8},{24,16},{0,24},{9,1},{17,9},{25,17},{1,25},{10,2},{18... | collective-permute-start | bytes 1486856 | tf_op jit(solution)/shard_map/ppermute | solution.py:507
  27.8 11.5 %collective-permute-start.6 = (f32[1296,128]{1,0:T(8,128)S(1)}, f32[1296,128]{1,0:T(8,128)S(1)}, u32[]{:S(2)}, u32[]{:S(2)}) collective-permute-start(f32[1296,128]{1,0:T(8,128)S(1)} %get-tuple-element.32), channel_id=1, source_target_pairs={{0,32},{32,64},{64,96},{96,128},{128,160},{160,192},{192,224},{224... | collective-permute-start | bytes 1990664 | tf_op jit(solution)/shard_map/ppermute | solution.py:507
  31.6 10.1 %collective-permute-start.7 = (f32[1296,128]{1,0:T(8,128)S(1)}, f32[1296,128]{1,0:T(8,128)S(1)}, u32[]{:S(2)}, u32[]{:S(2)}) collective-permute-start(f32[1296,128]{1,0:T(8,128)S(1)} %get-tuple-element.33), channel_id=1, source_target_pairs={{32,0},{64,32},{96,64},{128,96},{160,128},{192,160},{224,192},{0,2... | collective-permute-start | bytes 1990664 | tf_op jit(solution)/shard_map/ppermute | solution.py:507
  46.5 12.3 %copy-start.1 = (f32[3,16,16,128]{3,2,1,0:T(8,128)S(1)}, f32[3,16,16,128]{3,2,1,0:T(8,128)}, u32[]{:S(2)}) copy-start(f32[3,16,16,128]{3,2,1,0:T(8,128)} %v.3) | copy-start | bytes 1179652
  46.5 10.5 %collective-permute-start.8 = (f32[640,128]{1,0:T(8,128)S(1)}, f32[640,128]{1,0:T(8,128)S(1)}, u32[]{:S(2)}, u32[]{:S(2)}) collective-permute-start(f32[640,128]{1,0:T(8,128)S(1)} %get-tuple-element.38.own_up), channel_id=1, source_target_pairs={{0,8},{8,16},{16,24},{24,0},{1,9},{9,17},{17,25},{25,1},{2,10},{10... | collective-permute-start | bytes 983048 | tf_op jit(solution)/shard_map/ppermute | solution.py:507
  47.9 9.1 %collective-permute-start.9 = (f32[640,128]{1,0:T(8,128)S(1)}, f32[640,128]{1,0:T(8,128)S(1)}, u32[]{:S(2)}, u32[]{:S(2)}) collective-permute-start(f32[640,128]{1,0:T(8,128)S(1)} %get-tuple-element.39.own_down), channel_id=1, source_target_pairs={{8,0},{16,8},{24,16},{0,24},{9,1},{17,9},{25,17},{1,25},{10,2},{18... | collective-permute-start | bytes 983048 | tf_op jit(solution)/shard_map/ppermute | solution.py:507
  57.1 5.7 %collective-permute-start.10 = (f32[640,128]{1,0:T(8,128)S(1)}, f32[640,128]{1,0:T(8,128)S(1)}, u32[]{:S(2)}, u32[]{:S(2)}) collective-permute-start(f32[640,128]{1,0:T(8,128)S(1)} %get-tuple-element.40.own_up), channel_id=1, source_target_pairs={{0,32},{32,64},{64,96},{96,128},{128,160},{160,192},{192,224},{224... | collective-permute-start | bytes 983048 | tf_op jit(solution)/shard_map/ppermute | solution.py:507
  58.8 6.7 %copy-start.2 = (bf16[2,3,16,16,128]{4,3,2,1,0:T(8,128)(2,1)S(1)}, bf16[2,3,16,16,128]{4,3,2,1,0:T(8,128)(2,1)}, u32[]{:S(2)}) copy-start(bf16[2,3,16,16,128]{4,3,2,1,0:T(8,128)(2,1)} %g.1) | copy-start | bytes 1179652
  58.8 6.7 %collective-permute-start.11 = (f32[640,128]{1,0:T(8,128)S(1)}, f32[640,128]{1,0:T(8,128)S(1)}, u32[]{:S(2)}, u32[]{:S(2)}) collective-permute-start(f32[640,128]{1,0:T(8,128)S(1)} %get-tuple-element.41.own_down), channel_id=1, source_target_pairs={{32,0},{64,32},{96,64},{128,96},{160,128},{192,160},{224,192},{0,2... | collective-permute-start | bytes 983048 | tf_op jit(solution)/shard_map/ppermute | solution.py:507

commit v5 on v4

--- a/solution.py
+++ b/solution.py
@@ -15,6 +15,8 @@
 META = 15
 
 Z_S0, Z_S1, Z_V, Z_META, Z_ROWS = 0, 128, 256, 304, 312
+Y_S0, Y_S1, Y_FACE, Y_ROWS = 0, 256, 384, 576
+Y_E0, Y_E1, Y_META, Y_EROWS = 0, 256, 384, 392
 A0, E0, A1, E1, FACE, NUMBERS, ROWS = 0, 256, 512, 640, 768, 960, 968
 C_LOW, C_HIGH, C_A1, C_E1, C_META, C_ROWS = 0, 512, 1024, 1152, 1280, 1296
 R_E, R_ROWS = 512, 640
@@ -53,7 +55,9 @@
     return jnp.where(i > 0, 1.0, 0.0).astype(F32), jnp.where(i < n - 1, 1.0, 0.0).astype(F32)
 
 
-def sources_kernel(v_hbm, g_hbm, sx_hbm, sy_hbm, sz_hbm, fr_hbm, s0, s1, up, down, v, g, sx, sy, sz, fr, sem, small_sem):
+def sources_kernel(
+    v_hbm, g_hbm, sx_hbm, sy_hbm, sz_hbm, fr_hbm, v, s0, s1, up, down, yup, ydown, g, sx, sy, sz, fr, sem, small_sem
+):
     copies = []
     for q in range(4):
         part = pl.ds(4 * q, 4)
@@ -75,7 +79,20 @@
             total = g[k, 0, x].astype(F32) * vel[0]
             for c in (1, 2):
                 total = total + g[k, c, x].astype(F32) * vel[c]
-            s[x] = STEP_SIZE * total
+            value = STEP_SIZE * total
+            s[x] = value
+            if k == 0:
+                yup[pl.ds(Y_S0 + x * T, T)] = value
+                ydown[pl.ds(Y_S0 + x * T, T)] = value
+            else:
+                yup[pl.ds(Y_S1 + x * 8, 8)] = value[8:16]
+                ydown[pl.ds(Y_S1 + x * 8, 8)] = value[0:8]
+    first_half = subs() < 4
+    for c in range(3):
+        for x in range(8):
+            rows = pl.ds(Y_FACE + (c * 8 + x) * 8, 8)
+            yup[rows] = jnp.where(first_half, pltpu.roll(v[c, x + 8, 8:16], 4, 0), v[c, x, 8:16])
+            ydown[rows] = jnp.where(first_half, v[c, x, 0:8], pltpu.roll(v[c, x + 8, 0:8], 4, 0))
     upper = lane >= 64
     for start, s in ((Z_S0, s0), (Z_S1, s1)):
         for x in range(8):
@@ -121,52 +138,53 @@
     down[pl.ds(Z_META, 8)] = row
 
 
-def tile_messages_kernel(s0, s1, v, own, low, high, yup, ydown, xup, xdown):
+def tile_messages_kernel(s0, s1, v, own, low, high, ylow, yhigh, yup, ydown, xup, xdown):
+    del ylow, yhigh
     low_in, high_in = inside("gz")
     upper = lanes(T) >= 64
-    outs = (yup, ydown, xup, xdown)
-    for start, to, s in ((Z_S0, 0, s0), (Z_S1, 1, s1)):
+    for start, s in ((Z_S0, s0), (Z_S1, s1)):
         for j in range(8):
             a, b = low_in * low[pl.ds(start + j * T, T)], high_in * high[pl.ds(start + j * T, T)]
             edges = (jnp.where(upper, a, b), roll(jnp.where(upper, b, a), 64))
-            for h in range(2):
+            for h, edge in enumerate(edges):
                 x = j + 8 * h
-                for at, value in ((0, s[x]), (1, edges[h])):
-                    if to == 0:
-                        for out in outs:
-                            out[pl.ds((A0, E0)[at] + x * T, T)] = value
-                    else:
-                        yup[pl.ds((A1, E1)[at] + x * 8, 8)] = value[8:16]
-                        ydown[pl.ds((A1, E1)[at] + x * 8, 8)] = value[0:8]
-                        (xdown, xup)[h][pl.ds((A1, E1)[at] + j * T, T)] = value
-    first_half = subs() < 4
+                if start == Z_S0:
+                    for out in (xup, xdown):
+                        out[pl.ds(A0 + x * T, T)] = s[x]
+                        out[pl.ds(E0 + x * T, T)] = edge
+                    for out in (yup, ydown):
+                        out[pl.ds(Y_E0 + x * T, T)] = edge
+                else:
+                    yup[pl.ds(Y_E1 + x * 8, 8)] = edge[8:16]
+                    ydown[pl.ds(Y_E1 + x * 8, 8)] = edge[0:8]
+                    out = (xdown, xup)[h]
+                    out[pl.ds(A1 + j * T, T)] = s[x]
+                    out[pl.ds(E1 + j * T, T)] = edge
     for c in range(3):
-        for x in range(8):
-            rows = pl.ds(FACE + (c * 8 + x) * 8, 8)
-            yup[rows] = jnp.where(first_half, pltpu.roll(v[c, x + 8, 8:16], 4, 0), v[c, x, 8:16])
-            ydown[rows] = jnp.where(first_half, v[c, x, 0:8], pltpu.roll(v[c, x + 8, 0:8], 4, 0))
         for i in range(4):
             xup[pl.ds(FACE + (c * 4 + i) * T, T)] = v[c, 12 + i]
             xdown[pl.ds(FACE + (c * 4 + i) * T, T)] = v[c, i]
     sub = subs()
     meta = [ref[pl.ds(Z_META, 8)] for ref in (low, own, high)]
     row = jnp.where(sub == 0, low_in * meta[0], jnp.where(sub == 1, meta[1], high_in * meta[2]))
-    for out in outs:
-        out[pl.ds(NUMBERS, 8)] = row
-
-
-def corner_message_kernel(low, high, xlow, xhigh, up, down):
+    for out, at in ((yup, Y_META), (ydown, Y_META), (xup, NUMBERS), (xdown, NUMBERS)):
+        out[pl.ds(at, 8)] = row
+
+
+def corner_message_kernel(low, high, elow, ehigh, xlow, xhigh, up, down):
     del xlow, xhigh
-    for y, (ref, keep, to) in enumerate(zip((low, high), inside("gy"), (C_LOW, C_HIGH))):
-        for x in range(2 * T):
-            value = keep * ref[pl.ds(A0 + x * T, T)]
-            up[pl.ds(to + x * T, T)] = value
-            down[pl.ds(to + x * T, T)] = value
-        for start, place in ((A1, C_A1), (E1, C_E1)):
+    sides = ((low, elow, C_LOW), (high, ehigh, C_HIGH))
+    for y, ((a, e, to), keep) in enumerate(zip(sides, inside("gy"))):
+        for x in range(T):
+            for at, value in ((0, a[pl.ds(Y_S0 + x * T, T)]), (256, e[pl.ds(Y_E0 + x * T, T)])):
+                value = keep * value
+                up[pl.ds(to + at + x * T, T)] = value
+                down[pl.ds(to + at + x * T, T)] = value
+        for ref, start, place in ((a, Y_S1, C_A1), (e, Y_E1, C_E1)):
             for x in range(8):
                 down[pl.ds(place + x * T + 8 * y, 8)] = keep * ref[pl.ds(start + x * 8, 8)]
                 up[pl.ds(place + x * T + 8 * y, 8)] = keep * ref[pl.ds(start + (8 + x) * 8, 8)]
-        value = keep * ref[pl.ds(NUMBERS, 8)]
+        value = keep * e[pl.ds(Y_META, 8)]
         up[pl.ds(C_META + 8 * y, 8)] = value
         down[pl.ds(C_META + 8 * y, 8)] = value
 
@@ -176,17 +194,20 @@
     high[rows] = jnp.where(upper, a, e)
 
 
-def assemble_kernel(own_up, own_down, xlow, xhigh, ylow, yhigh, c_low, c_high, d_low, d_high):
+def assemble_kernel(own_up, own_down, xlow, xhigh, ylow, yhigh, elow, ehigh, c_low, c_high, d_low, d_high):
     (xl, xh), (yl, yh) = inside("gx"), inside("gy")
     upper, upper8 = lanes(T) >= 64, lanes(8) >= 64
 
     def first(x):
         at = pl.multiple_of(x * T, 8)
-        for ref, keep, dx, dy in ((own_up, None, 16, 16), (xlow, xl, 0, 16), (xhigh, xh, 32, 16), (ylow, yl, 16, 0), (yhigh, yh, 16, 32)):
+        for ref, keep, dx in ((own_up, None, 16), (xlow, xl, 0), (xhigh, xh, 32)):
             a, e = ref[pl.ds(A0 + at, T)], ref[pl.ds(E0 + at, T)]
             if keep is not None:
                 a, e = keep * a, keep * e
-            put(c_low, c_high, pl.ds(pl.multiple_of((dx + x) * 48 + dy, 8), T), upper, a, e)
+            put(c_low, c_high, pl.ds(pl.multiple_of((dx + x) * 48 + 16, 8), T), upper, a, e)
+        for ref, eref, keep, dy in ((ylow, elow, yl, 0), (yhigh, ehigh, yh, 32)):
+            a, e = keep * ref[pl.ds(Y_S0 + at, T)], keep * eref[pl.ds(Y_E0 + at, T)]
+            put(c_low, c_high, pl.ds(pl.multiple_of((16 + x) * 48 + dy, 8), T), upper, a, e)
 
     loop(T, first, UN_ASM)
 
@@ -199,8 +220,8 @@
             put(d_low, d_high, pl.ds(pl.multiple_of((dx + x) * 32 + 8, 8), T), upper, a, e)
         for h in range(2):
             at = pl.multiple_of((8 * h + x) * 8, 8)
-            for ref, keep, dy in ((ylow, yl, 0), (yhigh, yh, 24)):
-                a, e = keep * ref[pl.ds(A1 + at, 8)], keep * ref[pl.ds(E1 + at, 8)]
+            for ref, eref, keep, dy in ((ylow, elow, yl, 0), (yhigh, ehigh, yh, 24)):
+                a, e = keep * ref[pl.ds(Y_S1 + at, 8)], keep * eref[pl.ds(Y_E1 + at, 8)]
                 put(d_low, d_high, pl.ds(pl.multiple_of((8 + 8 * h + x) * 32 + dy, 8), 8), upper8, a, e)
 
     loop(8, second, UN_ASM)
@@ -264,9 +285,9 @@
         (0, xl * corner_low[pl.ds(C_META, 8)]),
         (8, xl * xlow[pl.ds(NUMBERS, 8)]),
         (16, xl * corner_low[pl.ds(C_META + 8, 8)]),
-        (24, yl * ylow[pl.ds(NUMBERS, 8)]),
+        (24, yl * ylow[pl.ds(Y_META, 8)]),
         (32, own[pl.ds(NUMBERS, 8)]),
-        (40, yh * yhigh[pl.ds(NUMBERS, 8)]),
+        (40, yh * yhigh[pl.ds(Y_META, 8)]),
         (48, xh * corner_high[pl.ds(C_META, 8)]),
         (56, xh * xhigh[pl.ds(NUMBERS, 8)]),
         (64, xh * corner_high[pl.ds(C_META + 8, 8)]),
@@ -461,7 +482,7 @@
             w[i, 8:24] = x_low * xlow[rows]
             w[20 + i, 8:24] = x_high * xhigh[rows]
         for x in range(8):
-            rows = pl.ds(FACE + (c * 8 + x) * 8, 8)
+            rows = pl.ds(Y_FACE + (c * 8 + x) * 8, 8)
             a, b = y_low * ylow[rows], y_high * yhigh[rows]
             w[4 + x, 0:8] = a
             w[12 + x, 0:8] = pltpu.roll(a, 4, 0)
@@ -512,27 +533,31 @@
     tile = (T, T, L)
     vm = lambda *s: pltpu.VMEM(s, F32)
     shifts = [s.transpose(0, 1, 3, 2) for s in (shift_x, shift_y, shift_z)]
-    s0, s1, zup, zdown = call(
+    inputs = [v, g, *shifts, fractions.transpose(0, 2, 3, 4, 1)]
+    v, s0, s1, zup, zdown, yup, ydown = call(
         sources_kernel,
-        [pltpu.with_memory_space_constraint(a, pltpu.HBM) for a in (v, g, *shifts, fractions.transpose(0, 2, 3, 4, 1))],
-        [tile, tile, (Z_ROWS, L), (Z_ROWS, L)],
-        scratch=[vm(*v.shape), pltpu.VMEM(g.shape, g.dtype)]
+        [pltpu.with_memory_space_constraint(a, pltpu.HBM) for a in inputs],
+        [v.shape, tile, tile, (Z_ROWS, L), (Z_ROWS, L), (Y_ROWS, L), (Y_ROWS, L)],
+        scratch=[pltpu.VMEM(g.shape, g.dtype)]
         + [pltpu.SMEM((2, 2, 1, 2), jnp.int32)] * 3
         + [pltpu.SMEM((2, 2, 2, 1, 3), jnp.int32), pltpu.SemaphoreType.DMA((8,)), pltpu.SemaphoreType.DMA((4,))],
         hbm=range(6),
     )
     zlow, zhigh = exchange(zup, zdown, "gz")
-    yup, ydown, xup, xdown = call(tile_messages_kernel, (s0, s1, v, zup, zlow, zhigh), [(ROWS, L)] * 4)
     ylow, yhigh = exchange(yup, ydown, "gy")
+    yup, ydown, xup, xdown = call(
+        tile_messages_kernel, (s0, s1, v, zup, zlow, zhigh, ylow, yhigh), [(Y_EROWS, L)] * 2 + [(ROWS, L)] * 2
+    )
+    elow, ehigh = exchange(yup, ydown, "gy")
     xlow, xhigh = exchange(xup, xdown, "gx")
-    up, down = call(corner_message_kernel, (ylow, yhigh, xlow, xhigh), [(C_ROWS, L)] * 2)
+    up, down = call(corner_message_kernel, (ylow, yhigh, elow, ehigh, xlow, xhigh), [(C_ROWS, L)] * 2)
     corner_low, corner_high = exchange(up, down, "gx")
     fields = [(48 * 48, L)] * 2 + [(32 * 32, L)] * 2
-    filled = call(assemble_kernel, (xup, xdown, xlow, xhigh, ylow, yhigh), fields)
+    filled = call(assemble_kernel, (xup, xdown, xlow, xhigh, ylow, yhigh, elow, ehigh), fields)
     meta = [pltpu.SMEM((72, L), F32), pltpu.SemaphoreType.DMA]
     up, down, numbers, *_ = call(
         steps_kernel,
-        (xup, xlow, xhigh, ylow, yhigh, corner_low, corner_high, *filled),
+        (xup, xlow, xhigh, elow, ehigh, corner_low, corner_high, *filled),
         [(R_ROWS, L), (R_ROWS, L), (72, L)] + fields,
         scratch=[vm(32 * 40, L), vm(32 * 40, L)] + meta,
         alias={7: 3, 8: 4, 9: 5, 10: 6},

time: 70 us -> 68.2 us (0.974); the launches traced: 69.9 us -> 67.3 us
  waiting for transfers between devices: 33.9 us -> 30.9 us
  starting transfers between devices: 20 us -> 21.3 us
  local copies, waits for them, and re-layouts: 1.01 us -> 0.01 us
    ppermute x12 -> x14, waiting for transfers between devices: 33.9 us -> 30.9 us  [exchange(): return (lax.ppermute(up, axis, rise), lax.ppermute(down, axis, fall))]
    ppermute x12 -> x14, starting transfers between devices: 20 us -> 21.3 us  [exchange(): return (lax.ppermute(up, axis, rise), lax.ppermute(down, axis, fall))]
    unnamed x6 -> x2, local copies, waits for them, and re-layouts: 1.01 us -> 0.01 us
  transfers between devices with their start and end apart: 12 -> 14, of which waited for: 9 -> 8; matrix products, arithmetic and copies ran while one was open for 0% -> 0% of each run, Pallas kernels for 5% -> 6%
where the time goes in v5:
time: 68.2 us; the launch traced here: 67.3 us
  waiting for transfers between devices  30.9 us (45%)
  starting transfers between devices  21.3 us (31%)
  Pallas kernels  14.9 us (22%)
    ppermute x14, waiting for transfers between devices, exchange(): return (lax.ppermute(up, axis, rise), lax.ppermute(down, axis, fall))  30.9 us
    ppermute x14, starting transfers between devices, exchange(): return (lax.ppermute(up, axis, rise), lax.ppermute(down, axis, fall))  21.3 us
    pallas_call x8, Pallas kernels, call(): pl.pallas_call(kernel, out_shape=shapes, in_specs=specs, out_specs=[VMEM]...  14.9 us
  transfers between devices with their start and end apart: 14, of which 8 were waited for; matrix products, arithmetic and copies ran while one was open for 0% of the time, Pallas kernels for 6%

profile of v5, /device:TPU:1, one launch (start us, length us, event | category | flops | bytes accessed | tf_op | source)
XLA Modules:
  0.0 67.3 jit_solution(5780052424751005812)
XLA Ops:
  0.0 1.6 %shard_map.64 = (f32[3,16,16,128]{3,2,1,0:T(8,128)S(1)}, f32[16,16,128]{2,1,0:T(8,128)S(1)}, f32[16,16,128]{2,1,0:T(8,128)S(1)}, f32[312,128]{1,0:T(8,128)S(1)},...) custom-call(f32[3,16,16,128]{3,2,1,0:T(8,128)} %v_hbm.1, bf16[2,3,16,16,128]{4,3,2,1,0:T(8,128)(2,1)} %g.1, ...), custom_call_target="tpu_custom_call" | custom-call | flops 20000 | bytes 20000 | tf_op jit(solution)/shard_map/pallas_call | solution.py:512
  1.6 2.2 %collective-permute-start.2 = (f32[576,128]{1,0:T(8,128)S(1)}, f32[576,128]{1,0:T(8,128)S(1)}, u32[]{:S(2)}, u32[]{:S(2)}) collective-permute-start(f32[576,128]{1,0:T(8,128)S(1)} %get-tuple-element.32), channel_id=1, source_target_pairs={{0,8},{8,16},{16,24},{24,0},{1,9},{9,17},{17,25},{25,1},{2,10},{10... | collective-permute-start | bytes 884744 | tf_op jit(solution)/shard_map/ppermute | solution.py:528
  3.8 1.5 %collective-permute-start.3 = (f32[576,128]{1,0:T(8,128)S(1)}, f32[576,128]{1,0:T(8,128)S(1)}, u32[]{:S(2)}, u32[]{:S(2)}) collective-permute-start(f32[576,128]{1,0:T(8,128)S(1)} %get-tuple-element.33), channel_id=1, source_target_pairs={{8,0},{16,8},{24,16},{0,24},{9,1},{17,9},{25,17},{1,25},{10,2},{18... | collective-permute-start | bytes 884744 | tf_op jit(solution)/shard_map/ppermute | solution.py:528
  5.4 5.6 %collective-permute-start.1 = (f32[312,128]{1,0:T(8,128)S(1)}, f32[312,128]{1,0:T(8,128)S(1)}, u32[]{:S(2)}, u32[]{:S(2)}) collective-permute-start(f32[312,128]{1,0:T(8,128)S(1)} %get-tuple-element.31), channel_id=1, source_target_pairs={{1,0},{2,1},{3,2},{4,3},{5,4},{6,5},{7,6},{0,7},{9,8},{10,9},{11,1... | collective-permute-start | bytes 479240 | tf_op jit(solution)/shard_map/ppermute | solution.py:528
  10.9 0.0 collective-permute-start
  10.9 2.2 %collective-permute-done.1.high.zhigh = f32[312,128]{1,0:T(8,128)S(1)} collective-permute-done((f32[312,128]{1,0:T(8,128)S(1)}, f32[312,128]{1,0:T(8,128)S(1)}, u32[]{:S(2)}, u32[]{:S(2)}) %collective-permute-start.1) | collective-permute-done | bytes 159776 | tf_op jit(solution)/shard_map/ppermute | solution.py:528
  13.1 3.1 %collective-permute-done.low.zlow = f32[312,128]{1,0:T(8,128)S(1)} collective-permute-done((f32[312,128]{1,0:T(8,128)S(1)}, f32[312,128]{1,0:T(8,128)S(1)}, u32[]{:S(2)}, u32[]{:S(2)}) %collective-permute-start) | collective-permute-done | bytes 159776 | tf_op jit(solution)/shard_map/ppermute | solution.py:528
  16.3 0.0 collective-permute-done.2.ylow.low
  16.3 0.0 collective-permute-done.3.yhigh.high
  16.3 0.1 shard_map.65
  16.4 2.5 %collective-permute-start.5 = (f32[968,128]{1,0:T(8,128)S(1)}, f32[968,128]{1,0:T(8,128)S(1)}, u32[]{:S(2)}, u32[]{:S(2)}) collective-permute-start(f32[968,128]{1,0:T(8,128)S(1)} %get-tuple-element.35.own_down), channel_id=1, source_target_pairs={{32,0},{64,32},{96,64},{128,96},{160,128},{192,160},{224,192},{0,2... | collective-permute-start | bytes 1486856 | tf_op jit(solution)/shard_map/ppermute | solution.py:528
  18.9 1.1 %collective-permute-start.4 = (f32[968,128]{1,0:T(8,128)S(1)}, f32[968,128]{1,0:T(8,128)S(1)}, u32[]{:S(2)}, u32[]{:S(2)}) collective-permute-start(f32[968,128]{1,0:T(8,128)S(1)} %get-tuple-element.34.own_up.own), channel_id=1, source_target_pairs={{0,32},{32,64},{64,96},{96,128},{128,160},{160,192},{192,224},{224... | collective-permute-start | bytes 1486856 | tf_op jit(solution)/shard_map/ppermute | solution.py:528
  20.0 0.1 collective-permute-start.6
  20.1 2.6 %collective-permute-start.7 = (f32[392,128]{1,0:T(8,128)S(1)}, f32[392,128]{1,0:T(8,128)S(1)}, u32[]{:S(2)}, u32[]{:S(2)}) collective-permute-start(f32[392,128]{1,0:T(8,128)S(1)} %get-tuple-element.37), channel_id=1, source_target_pairs={{8,0},{16,8},{24,16},{0,24},{9,1},{17,9},{25,17},{1,25},{10,2},{18... | collective-permute-start | bytes 602120 | tf_op jit(solution)/shard_map/ppermute | solution.py:528
  22.7 5.4 %collective-permute-done.6.elow.ylow = f32[392,128]{1,0:T(8,128)S(1)} collective-permute-done((f32[392,128]{1,0:T(8,128)S(1)}, f32[392,128]{1,0:T(8,128)S(1)}, u32[]{:S(2)}, u32[]{:S(2)}) %collective-permute-start.6) | collective-permute-done | bytes 200736 | tf_op jit(solution)/shard_map/ppermute | solution.py:528
  28.1 0.0 collective-permute-done.7.ehigh.yhigh
  28.1 0.0 collective-permute-done.5.xhigh
  28.1 0.0 collective-permute-done.4.xlow
  28.1 0.1 shard_map.66
  28.2 1.3 %collective-permute-start.8 = (f32[1296,128]{1,0:T(8,128)S(1)}, f32[1296,128]{1,0:T(8,128)S(1)}, u32[]{:S(2)}, u32[]{:S(2)}) collective-permute-start(f32[1296,128]{1,0:T(8,128)S(1)} %get-tuple-element.38), channel_id=1, source_target_pairs={{0,32},{32,64},{64,96},{96,128},{128,160},{160,192},{192,224},{224... | collective-permute-start | bytes 1990664 | tf_op jit(solution)/shard_map/ppermute | solution.py:528
  29.6 0.0 collective-permute-start.9
  29.6 0.2 shard_map.67
  29.8 7.4 %collective-permute-done.8.corner_low = f32[1296,128]{1,0:T(8,128)S(1)} collective-permute-done((f32[1296,128]{1,0:T(8,128)S(1)}, f32[1296,128]{1,0:T(8,128)S(1)}, u32[]{:S(2)}, u32[]{:S(2)}) %collective-permute-start.8) | collective-permute-done | bytes 663584 | tf_op jit(solution)/shard_map/ppermute | solution.py:528
  37.2 2.6 %collective-permute-done.9.corner_high = f32[1296,128]{1,0:T(8,128)S(1)} collective-permute-done((f32[1296,128]{1,0:T(8,128)S(1)}, f32[1296,128]{1,0:T(8,128)S(1)}, u32[]{:S(2)}, u32[]{:S(2)}) %collective-permute-start.9) | collective-permute-done | bytes 663584 | tf_op jit(solution)/shard_map/ppermute | solution.py:528
  39.8 4.8 %shard_map.68 = (f32[640,128]{1,0:T(8,128)S(1)}, f32[640,128]{1,0:T(8,128)S(1)}, f32[72,128]{1,0:T(8,128)S(1)}, f32[2304,128]{1,0:T(8,128)S(1)}, f32[2304,128]{1...) custom-call(f32[968,128]{1,0:T(8,128)S(1)} %get-tuple-element.34.own, ...), custom_call_target="tpu_custom_call", output_to_operand_aliasing={{3}: (7, {}), {4}: (8, {}), {5}: (9, {}), {6}: (10, {})} | custom-call | flops 20000 | bytes 20000 | tf_op jit(solution)/shard_map/pallas_call | solution.py:512
  44.6 0.4 collective-permute-start.10
  45.0 2.8 %collective-permute-start.11 = (f32[640,128]{1,0:T(8,128)S(1)}, f32[640,128]{1,0:T(8,128)S(1)}, u32[]{:S(2)}, u32[]{:S(2)}) collective-permute-start(f32[640,128]{1,0:T(8,128)S(1)} %get-tuple-element.45.own_down), channel_id=1, source_target_pairs={{8,0},{16,8},{24,16},{0,24},{9,1},{17,9},{25,17},{1,25},{10,2},{18... | collective-permute-start | bytes 983048 | tf_op jit(solution)/shard_map/ppermute | solution.py:528
  47.8 7.3 %collective-permute-done.10.low = f32[640,128]{1,0:T(8,128)S(1)} collective-permute-done((f32[640,128]{1,0:T(8,128)S(1)}, f32[640,128]{1,0:T(8,128)S(1)}, u32[]{:S(2)}, u32[]{:S(2)}) %collective-permute-start.10) | collective-permute-done | bytes 327712 | tf_op jit(solution)/shard_map/ppermute | solution.py:528
  55.1 0.0 collective-permute-done.11.high
  55.1 0.1 shard_map.69
  55.2 0.7 %collective-permute-start.12 = (f32[640,128]{1,0:T(8,128)S(1)}, f32[640,128]{1,0:T(8,128)S(1)}, u32[]{:S(2)}, u32[]{:S(2)}) collective-permute-start(f32[640,128]{1,0:T(8,128)S(1)} %get-tuple-element.46.own_up), channel_id=1, source_target_pairs={{0,32},{32,64},{64,96},{96,128},{128,160},{160,192},{192,224},{224... | collective-permute-start | bytes 983048 | tf_op jit(solution)/shard_map/ppermute | solution.py:528
  56.0 0.0 copy-start
  56.0 0.4 collective-permute-start.13
  56.3 3.6 %shard_map.70.reg = f32[3,16,16,128]{3,2,1,0:T(8,128)S(1)} custom-call(f32[3,16,16,128]{3,2,1,0:T(8,128)S(1)} %get-tuple-element.29.v, f32[312,128]{1,0:T(8,128)S(1)} %collective-permute-done.low.zlow, f32[312,128]{1,0:T(8,128)S(1)} %collective-permute-done.1.high.zhigh, f32[576,128]{1,0:T(8,128)S(1)} %collective-permute-done.2.ylow.low, ...), custom_call_target="tpu_custom_call" | custom-call | flops 4000000 | bytes 4000000 | tf_op jit(solution)/shard_map/pallas_call | solution.py:512
  59.9 0.1 collective-permute-done.12.low
  60.0 2.8 %collective-permute-done.13.high = f32[640,128]{1,0:T(8,128)S(1)} collective-permute-done((f32[640,128]{1,0:T(8,128)S(1)}, f32[640,128]{1,0:T(8,128)S(1)}, u32[]{:S(2)}, u32[]{:S(2)}) %collective-permute-start.13) | collective-permute-done | bytes 327712 | tf_op jit(solution)/shard_map/ppermute | solution.py:528
  62.7 0.0 copy-done
  62.8 4.4 %shard_map.71 = f32[3,16,16,128]{3,2,1,0:T(8,128)} custom-call(f32[640,128]{1,0:T(8,128)S(1)} %get-tuple-element.46.own_up, f32[640,128]{1,0:T(8,128)S(1)} %get-tuple-element.47.own_down, f32[640,128]{1,0:T(8,128)S(1)} %collective-permute-done.12.low, f32[640,128]{1,0:T(8,128)S(1)} %collective-permute-done.13.high, f32[72,128]{1,0:T(8,128)S(1)} %get-tuple-element.48.numbers, ...), custom_call_target="tpu_custom_call" | custom-call | flops 20000 | bytes 20000 | tf_op jit(solution)/shard_map/pallas_call | solution.py:512
Async XLA Ops:
  1.6 14.6 %collective-permute-start.2 = (f32[576,128]{1,0:T(8,128)S(1)}, f32[576,128]{1,0:T(8,128)S(1)}, u32[]{:S(2)}, u32[]{:S(2)}) collective-permute-start(f32[576,128]{1,0:T(8,128)S(1)} %get-tuple-element.32), channel_id=1, source_target_pairs={{0,8},{8,16},{16,24},{24,0},{1,9},{9,17},{17,25},{25,1},{2,10},{10... | collective-permute-start | bytes 884744 | tf_op jit(solution)/shard_map/ppermute | solution.py:528
  3.8 12.4 %collective-permute-start.3 = (f32[576,128]{1,0:T(8,128)S(1)}, f32[576,128]{1,0:T(8,128)S(1)}, u32[]{:S(2)}, u32[]{:S(2)}) collective-permute-start(f32[576,128]{1,0:T(8,128)S(1)} %get-tuple-element.33), channel_id=1, source_target_pairs={{8,0},{16,8},{24,16},{0,24},{9,1},{17,9},{25,17},{1,25},{10,2},{18... | collective-permute-start | bytes 884744 | tf_op jit(solution)/shard_map/ppermute | solution.py:528
  5.4 7.8 %collective-permute-start.1 = (f32[312,128]{1,0:T(8,128)S(1)}, f32[312,128]{1,0:T(8,128)S(1)}, u32[]{:S(2)}, u32[]{:S(2)}) collective-permute-start(f32[312,128]{1,0:T(8,128)S(1)} %get-tuple-element.31), channel_id=1, source_target_pairs={{1,0},{2,1},{3,2},{4,3},{5,4},{6,5},{7,6},{0,7},{9,8},{10,9},{11,1... | collective-permute-start | bytes 479240 | tf_op jit(solution)/shard_map/ppermute | solution.py:528
  10.9 5.3 %collective-permute-start = (f32[312,128]{1,0:T(8,128)S(1)}, f32[312,128]{1,0:T(8,128)S(1)}, u32[]{:S(2)}, u32[]{:S(2)}) collective-permute-start(f32[312,128]{1,0:T(8,128)S(1)} %get-tuple-element.30.own), channel_id=1, source_target_pairs={{0,1},{1,2},{2,3},{3,4},{4,5},{5,6},{6,7},{7,0},{8,9},{9,10},{10,1... | collective-permute-start | bytes 479240 | tf_op jit(solution)/shard_map/ppermute | solution.py:528
  16.4 11.7 %collective-permute-start.5 = (f32[968,128]{1,0:T(8,128)S(1)}, f32[968,128]{1,0:T(8,128)S(1)}, u32[]{:S(2)}, u32[]{:S(2)}) collective-permute-start(f32[968,128]{1,0:T(8,128)S(1)} %get-tuple-element.35.own_down), channel_id=1, source_target_pairs={{32,0},{64,32},{96,64},{128,96},{160,128},{192,160},{224,192},{0,2... | collective-permute-start | bytes 1486856 | tf_op jit(solution)/shard_map/ppermute | solution.py:528
  18.9 9.2 %collective-permute-start.4 = (f32[968,128]{1,0:T(8,128)S(1)}, f32[968,128]{1,0:T(8,128)S(1)}, u32[]{:S(2)}, u32[]{:S(2)}) collective-permute-start(f32[968,128]{1,0:T(8,128)S(1)} %get-tuple-element.34.own_up.own), channel_id=1, source_target_pairs={{0,32},{32,64},{64,96},{96,128},{128,160},{160,192},{192,224},{224... | collective-permute-start | bytes 1486856 | tf_op jit(solution)/shard_map/ppermute | solution.py:528
  20.0 8.1 %collective-permute-start.6 = (f32[392,128]{1,0:T(8,128)S(1)}, f32[392,128]{1,0:T(8,128)S(1)}, u32[]{:S(2)}, u32[]{:S(2)}) collective-permute-start(f32[392,128]{1,0:T(8,128)S(1)} %get-tuple-element.36), channel_id=1, source_target_pairs={{0,8},{8,16},{16,24},{24,0},{1,9},{9,17},{17,25},{25,1},{2,10},{10... | collective-permute-start | bytes 602120 | tf_op jit(solution)/shard_map/ppermute | solution.py:528
  20.1 8.0 %collective-permute-start.7 = (f32[392,128]{1,0:T(8,128)S(1)}, f32[392,128]{1,0:T(8,128)S(1)}, u32[]{:S(2)}, u32[]{:S(2)}) collective-permute-start(f32[392,128]{1,0:T(8,128)S(1)} %get-tuple-element.37), channel_id=1, source_target_pairs={{8,0},{16,8},{24,16},{0,24},{9,1},{17,9},{25,17},{1,25},{10,2},{18... | collective-permute-start | bytes 602120 | tf_op jit(solution)/shard_map/ppermute | solution.py:528
  28.2 9.0 %collective-permute-start.8 = (f32[1296,128]{1,0:T(8,128)S(1)}, f32[1296,128]{1,0:T(8,128)S(1)}, u32[]{:S(2)}, u32[]{:S(2)}) collective-permute-start(f32[1296,128]{1,0:T(8,128)S(1)} %get-tuple-element.38), channel_id=1, source_target_pairs={{0,32},{32,64},{64,96},{96,128},{128,160},{160,192},{192,224},{224... | collective-permute-start | bytes 1990664 | tf_op jit(solution)/shard_map/ppermute | solution.py:528
  29.6 10.2 %collective-permute-start.9 = (f32[1296,128]{1,0:T(8,128)S(1)}, f32[1296,128]{1,0:T(8,128)S(1)}, u32[]{:S(2)}, u32[]{:S(2)}) collective-permute-start(f32[1296,128]{1,0:T(8,128)S(1)} %get-tuple-element.39), channel_id=1, source_target_pairs={{32,0},{64,32},{96,64},{128,96},{160,128},{192,160},{224,192},{0,2... | collective-permute-start | bytes 1990664 | tf_op jit(solution)/shard_map/ppermute | solution.py:528
  44.6 10.5 %collective-permute-start.10 = (f32[640,128]{1,0:T(8,128)S(1)}, f32[640,128]{1,0:T(8,128)S(1)}, u32[]{:S(2)}, u32[]{:S(2)}) collective-permute-start(f32[640,128]{1,0:T(8,128)S(1)} %get-tuple-element.44.own_up), channel_id=1, source_target_pairs={{0,8},{8,16},{16,24},{24,0},{1,9},{9,17},{17,25},{25,1},{2,10},{10... | collective-permute-start | bytes 983048 | tf_op jit(solution)/shard_map/ppermute | solution.py:528
  45.0 10.1 %collective-permute-start.11 = (f32[640,128]{1,0:T(8,128)S(1)}, f32[640,128]{1,0:T(8,128)S(1)}, u32[]{:S(2)}, u32[]{:S(2)}) collective-permute-start(f32[640,128]{1,0:T(8,128)S(1)} %get-tuple-element.45.own_down), channel_id=1, source_target_pairs={{8,0},{16,8},{24,16},{0,24},{9,1},{17,9},{25,17},{1,25},{10,2},{18... | collective-permute-start | bytes 983048 | tf_op jit(solution)/shard_map/ppermute | solution.py:528
  55.2 4.7 %collective-permute-start.12 = (f32[640,128]{1,0:T(8,128)S(1)}, f32[640,128]{1,0:T(8,128)S(1)}, u32[]{:S(2)}, u32[]{:S(2)}) collective-permute-start(f32[640,128]{1,0:T(8,128)S(1)} %get-tuple-element.46.own_up), channel_id=1, source_target_pairs={{0,32},{32,64},{64,96},{96,128},{128,160},{160,192},{192,224},{224... | collective-permute-start | bytes 983048 | tf_op jit(solution)/shard_map/ppermute | solution.py:528
  56.0 6.8 %copy-start = (bf16[2,3,16,16,128]{4,3,2,1,0:T(8,128)(2,1)S(1)}, bf16[2,3,16,16,128]{4,3,2,1,0:T(8,128)(2,1)}, u32[]{:S(2)}) copy-start(bf16[2,3,16,16,128]{4,3,2,1,0:T(8,128)(2,1)} %g.1) | copy-start | bytes 1179652
  56.0 6.8 %collective-permute-start.13 = (f32[640,128]{1,0:T(8,128)S(1)}, f32[640,128]{1,0:T(8,128)S(1)}, u32[]{:S(2)}, u32[]{:S(2)}) collective-permute-start(f32[640,128]{1,0:T(8,128)S(1)} %get-tuple-element.47.own_down), channel_id=1, source_target_pairs={{32,0},{64,32},{96,64},{128,96},{160,128},{192,160},{224,192},{0,2... | collective-permute-start | bytes 983048 | tf_op jit(solution)/shard_map/ppermute | solution.py:528

commit v6 on v5

--- a/solution.py
+++ b/solution.py
@@ -11,7 +11,7 @@
 REG_WEIGHT = 0.1
 T = 16
 L = 128
-UN_ASM, UN_CORNER, UN_FIRST, UN_SECOND, UN_PACK, UN_UNPACK, UN_STEP, UN_FIN = 4, 4, 16, 1, 8, 4, 16, 16
+UN_ASM, UN_CORNER, UN_FIRST, UN_SECOND, UN_PACK, UN_UNPACK = 8, 16, 16, 4, 8, 4
 META = 15
 
 Z_S0, Z_S1, Z_V, Z_META, Z_ROWS = 0, 128, 256, 304, 312
@@ -413,7 +413,7 @@
                 out[pl.ds(start + x * 32 + T, T)] = own_up[rows] + high_in * high[rows]
 
 
-def last_step_kernel(own_up, own_down, low, high, numbers, g, reg, out, a1, e1, acc, meta, sem):
+def last_step_kernel(own_up, own_down, low, high, numbers, g, reg, result, a1, e1, acc, out, meta, sem, out_sem):
     copy = pltpu.make_async_copy(numbers, meta, sem)
     copy.start()
     low_in, high_in = inside("gx")
@@ -459,14 +459,22 @@
             moved = [sum(w[t] * pltpu.roll(value, back[t], 1) for t in range(4)) for value in values]
             scatter_xy(acc, 56, moved, bx * 8 + 7 + a, by * 8 + 7 + b, wx, wy)
 
-    loop(16, step, UN_STEP)
 
     def finish(x):
         first, second = acc[pl.ds(pl.multiple_of((16 + x) * 56 + 16, 8), 16)], a1[pl.ds(pl.multiple_of((8 + x) * 32 + 8, 8), 16)]
         for c in range(3):
             out[c, x] = reg[c, x] + STEP_SIZE * (g[1, c, x].astype(F32) * second + g[0, c, x].astype(F32) * first)
 
-    loop(T, finish, UN_FIN)
+    copies = []
+    for h, (first_block, blocks) in enumerate(((0, 12), (12, 4))):
+        loop(blocks, lambda i, first_block=first_block: step(first_block + i), blocks)
+        loop(8, lambda x, h=h: finish(8 * h + x), 8)
+        half = pl.ds(8 * h, 8)
+        done = pltpu.make_async_copy(out.at[:, half], result.at[:, half], out_sem.at[h])
+        done.start()
+        copies.append(done)
+    for done in copies:
+        done.wait()
 
 
 def laplace_kernel(v, zlow, zhigh, ylow, yhigh, xlow, xhigh, out, w):
@@ -506,14 +514,14 @@
 HBM = pl.BlockSpec(memory_space=pltpu.HBM)
 
 
-def call(kernel, args, outs, scratch=(), hbm=(), cost=20000, alias=None):
+def call(kernel, args, outs, scratch=(), hbm=(), cost=20000, alias=None, out_space=None):
     specs = [HBM if i in hbm else VMEM for i in range(len(args))]
     shapes = [jax.ShapeDtypeStruct(s, F32) for s in outs]
     return pl.pallas_call(
         kernel,
         out_shape=shapes,
         in_specs=specs,
-        out_specs=[VMEM] * len(shapes),
+        out_specs=[out_space or VMEM] * len(shapes),
         input_output_aliases=alias or {},
         scratch_shapes=list(scratch),
         compiler_params=pltpu.CompilerParams(vmem_limit_bytes=24 * 1024 * 1024),
@@ -526,6 +534,12 @@
     rise = [(i, (i + 1) % n) for i in range(n)]
     fall = [(j, i) for i, j in rise]
     return lax.ppermute(up, axis, rise), lax.ppermute(down, axis, fall)
+
+
+def last_call(args, vm, meta):
+    shape = args[-1].shape
+    scratch = [vm(32 * 32, L), vm(32 * 32, L), vm(48 * 56, L), vm(*shape)] + meta + [pltpu.SemaphoreType.DMA((2,))]
+    return call(last_step_kernel, args, [shape], scratch=scratch, out_space=HBM)
 
 
 def body(velocity, gradients, shift_x, shift_y, shift_z, fractions):
@@ -548,8 +562,8 @@
     yup, ydown, xup, xdown = call(
         tile_messages_kernel, (s0, s1, v, zup, zlow, zhigh, ylow, yhigh), [(Y_EROWS, L)] * 2 + [(ROWS, L)] * 2
     )
+    xlow, xhigh = exchange(xup, xdown, "gx")
     elow, ehigh = exchange(yup, ydown, "gy")
-    xlow, xhigh = exchange(xup, xdown, "gx")
     up, down = call(corner_message_kernel, (ylow, yhigh, elow, ehigh, xlow, xhigh), [(C_ROWS, L)] * 2)
     corner_low, corner_high = exchange(up, down, "gx")
     fields = [(48 * 48, L)] * 2 + [(32 * 32, L)] * 2
@@ -568,12 +582,7 @@
     low, high = exchange(up, down, "gy")
     up, down = call(sum_y_kernel, (up, down, low, high), [(R_ROWS, L)] * 2)
     low, high = exchange(up, down, "gx")
-    (out,) = call(
-        last_step_kernel,
-        (up, down, low, high, numbers, g, reg),
-        [v.shape],
-        scratch=[vm(32 * 32, L), vm(32 * 32, L), vm(48 * 56, L)] + meta,
-    )
+    (out,) = last_call((up, down, low, high, numbers, g, reg), vm, meta)
     return out
 
 

time: 68.2 us -> 67.8 us (level)
  no operation moved by 1% of the time
where the time goes in v6:
time: 67.8 us; the launch traced here: 66.9 us
  waiting for transfers between devices  31 us (46%)
  starting transfers between devices  21.3 us (31%)
  Pallas kernels  14.5 us (21%)
    ppermute x14, waiting for transfers between devices, exchange(): return (lax.ppermute(up, axis, rise), lax.ppermute(down, axis, fall))  31 us
    ppermute x14, starting transfers between devices, exchange(): return (lax.ppermute(up, axis, rise), lax.ppermute(down, axis, fall))  21.3 us
    pallas_call x8, Pallas kernels, call(): pl.pallas_call(kernel, out_shape=shapes, in_specs=specs, out_specs=[out_s...  14.5 us
  transfers between devices with their start and end apart: 14, of which 8 were waited for; matrix products, arithmetic and copies ran while one was open for 0% of the time, Pallas kernels for 6%

profile of v6, /device:TPU:1, one launch (start us, length us, event | category | flops | bytes accessed | tf_op | source)
XLA Modules:
  0.0 66.9 jit_solution(4502439212616680622)
XLA Ops:
  0.0 1.6 %shard_map.64 = (f32[3,16,16,128]{3,2,1,0:T(8,128)S(1)}, f32[16,16,128]{2,1,0:T(8,128)S(1)}, f32[16,16,128]{2,1,0:T(8,128)S(1)}, f32[312,128]{1,0:T(8,128)S(1)},...) custom-call(f32[3,16,16,128]{3,2,1,0:T(8,128)} %v_hbm.1, bf16[2,3,16,16,128]{4,3,2,1,0:T(8,128)(2,1)} %g.1, ...), custom_call_target="tpu_custom_call" | custom-call | flops 20000 | bytes 20000 | tf_op jit(solution)/shard_map/pallas_call | solution.py:520
  1.6 2.2 %collective-permute-start.2 = (f32[576,128]{1,0:T(8,128)S(1)}, f32[576,128]{1,0:T(8,128)S(1)}, u32[]{:S(2)}, u32[]{:S(2)}) collective-permute-start(f32[576,128]{1,0:T(8,128)S(1)} %get-tuple-element.32), channel_id=1, source_target_pairs={{0,8},{8,16},{16,24},{24,0},{1,9},{9,17},{17,25},{25,1},{2,10},{10... | collective-permute-start | bytes 884744 | tf_op jit(solution)/shard_map/ppermute | solution.py:536
  3.8 1.5 %collective-permute-start.3 = (f32[576,128]{1,0:T(8,128)S(1)}, f32[576,128]{1,0:T(8,128)S(1)}, u32[]{:S(2)}, u32[]{:S(2)}) collective-permute-start(f32[576,128]{1,0:T(8,128)S(1)} %get-tuple-element.33), channel_id=1, source_target_pairs={{8,0},{16,8},{24,16},{0,24},{9,1},{17,9},{25,17},{1,25},{10,2},{18... | collective-permute-start | bytes 884744 | tf_op jit(solution)/shard_map/ppermute | solution.py:536
  5.4 5.6 %collective-permute-start.1 = (f32[312,128]{1,0:T(8,128)S(1)}, f32[312,128]{1,0:T(8,128)S(1)}, u32[]{:S(2)}, u32[]{:S(2)}) collective-permute-start(f32[312,128]{1,0:T(8,128)S(1)} %get-tuple-element.31), channel_id=1, source_target_pairs={{1,0},{2,1},{3,2},{4,3},{5,4},{6,5},{7,6},{0,7},{9,8},{10,9},{11,1... | collective-permute-start | bytes 479240 | tf_op jit(solution)/shard_map/ppermute | solution.py:536
  10.9 0.0 collective-permute-start
  10.9 2.2 %collective-permute-done.1.high.zhigh = f32[312,128]{1,0:T(8,128)S(1)} collective-permute-done((f32[312,128]{1,0:T(8,128)S(1)}, f32[312,128]{1,0:T(8,128)S(1)}, u32[]{:S(2)}, u32[]{:S(2)}) %collective-permute-start.1) | collective-permute-done | bytes 159776 | tf_op jit(solution)/shard_map/ppermute | solution.py:536
  13.1 3.1 %collective-permute-done.low.zlow = f32[312,128]{1,0:T(8,128)S(1)} collective-permute-done((f32[312,128]{1,0:T(8,128)S(1)}, f32[312,128]{1,0:T(8,128)S(1)}, u32[]{:S(2)}, u32[]{:S(2)}) %collective-permute-start) | collective-permute-done | bytes 159776 | tf_op jit(solution)/shard_map/ppermute | solution.py:536
  16.3 0.0 collective-permute-done.2.ylow.low
  16.3 0.0 collective-permute-done.3.yhigh.high
  16.3 0.1 shard_map.65
  16.4 2.5 %collective-permute-start.5 = (f32[968,128]{1,0:T(8,128)S(1)}, f32[968,128]{1,0:T(8,128)S(1)}, u32[]{:S(2)}, u32[]{:S(2)}) collective-permute-start(f32[968,128]{1,0:T(8,128)S(1)} %get-tuple-element.35.own_down), channel_id=1, source_target_pairs={{32,0},{64,32},{96,64},{128,96},{160,128},{192,160},{224,192},{0,2... | collective-permute-start | bytes 1486856 | tf_op jit(solution)/shard_map/ppermute | solution.py:536
  18.9 1.1 %collective-permute-start.4 = (f32[968,128]{1,0:T(8,128)S(1)}, f32[968,128]{1,0:T(8,128)S(1)}, u32[]{:S(2)}, u32[]{:S(2)}) collective-permute-start(f32[968,128]{1,0:T(8,128)S(1)} %get-tuple-element.34.own_up.own), channel_id=1, source_target_pairs={{0,32},{32,64},{64,96},{96,128},{128,160},{160,192},{192,224},{224... | collective-permute-start | bytes 1486856 | tf_op jit(solution)/shard_map/ppermute | solution.py:536
  20.0 0.1 collective-permute-start.6
  20.1 2.6 %collective-permute-start.7 = (f32[392,128]{1,0:T(8,128)S(1)}, f32[392,128]{1,0:T(8,128)S(1)}, u32[]{:S(2)}, u32[]{:S(2)}) collective-permute-start(f32[392,128]{1,0:T(8,128)S(1)} %get-tuple-element.37), channel_id=1, source_target_pairs={{8,0},{16,8},{24,16},{0,24},{9,1},{17,9},{25,17},{1,25},{10,2},{18... | collective-permute-start | bytes 602120 | tf_op jit(solution)/shard_map/ppermute | solution.py:536
  22.7 5.4 %collective-permute-done.6.elow.ylow = f32[392,128]{1,0:T(8,128)S(1)} collective-permute-done((f32[392,128]{1,0:T(8,128)S(1)}, f32[392,128]{1,0:T(8,128)S(1)}, u32[]{:S(2)}, u32[]{:S(2)}) %collective-permute-start.6) | collective-permute-done | bytes 200736 | tf_op jit(solution)/shard_map/ppermute | solution.py:536
  28.1 0.0 collective-permute-done.7.ehigh.yhigh
  28.1 0.0 collective-permute-done.5.xhigh
  28.1 0.0 collective-permute-done.4.xlow
  28.1 0.1 shard_map.66
  28.2 1.3 %collective-permute-start.8 = (f32[1296,128]{1,0:T(8,128)S(1)}, f32[1296,128]{1,0:T(8,128)S(1)}, u32[]{:S(2)}, u32[]{:S(2)}) collective-permute-start(f32[1296,128]{1,0:T(8,128)S(1)} %get-tuple-element.38), channel_id=1, source_target_pairs={{0,32},{32,64},{64,96},{96,128},{128,160},{160,192},{192,224},{224... | collective-permute-start | bytes 1990664 | tf_op jit(solution)/shard_map/ppermute | solution.py:536
  29.6 0.0 collective-permute-start.9
  29.6 0.2 shard_map.67
  29.8 7.4 %collective-permute-done.8.corner_low = f32[1296,128]{1,0:T(8,128)S(1)} collective-permute-done((f32[1296,128]{1,0:T(8,128)S(1)}, f32[1296,128]{1,0:T(8,128)S(1)}, u32[]{:S(2)}, u32[]{:S(2)}) %collective-permute-start.8) | collective-permute-done | bytes 663584 | tf_op jit(solution)/shard_map/ppermute | solution.py:536
  37.2 2.6 %collective-permute-done.9.corner_high = f32[1296,128]{1,0:T(8,128)S(1)} collective-permute-done((f32[1296,128]{1,0:T(8,128)S(1)}, f32[1296,128]{1,0:T(8,128)S(1)}, u32[]{:S(2)}, u32[]{:S(2)}) %collective-permute-start.9) | collective-permute-done | bytes 663584 | tf_op jit(solution)/shard_map/ppermute | solution.py:536
  39.8 4.5 %shard_map.68 = (f32[640,128]{1,0:T(8,128)S(1)}, f32[640,128]{1,0:T(8,128)S(1)}, f32[72,128]{1,0:T(8,128)S(1)}, f32[2304,128]{1,0:T(8,128)S(1)}, f32[2304,128]{1...) custom-call(f32[968,128]{1,0:T(8,128)S(1)} %get-tuple-element.34.own, ...), custom_call_target="tpu_custom_call", output_to_operand_aliasing={{3}: (7, {}), {4}: (8, {}), {5}: (9, {}), {6}: (10, {})} | custom-call | flops 20000 | bytes 20000 | tf_op jit(solution)/shard_map/pallas_call | solution.py:520
  44.3 0.4 collective-permute-start.10
  44.7 2.8 %collective-permute-start.11 = (f32[640,128]{1,0:T(8,128)S(1)}, f32[640,128]{1,0:T(8,128)S(1)}, u32[]{:S(2)}, u32[]{:S(2)}) collective-permute-start(f32[640,128]{1,0:T(8,128)S(1)} %get-tuple-element.45.own_down), channel_id=1, source_target_pairs={{8,0},{16,8},{24,16},{0,24},{9,1},{17,9},{25,17},{1,25},{10,2},{18... | collective-permute-start | bytes 983048 | tf_op jit(solution)/shard_map/ppermute | solution.py:536
  47.5 7.4 %collective-permute-done.10.low = f32[640,128]{1,0:T(8,128)S(1)} collective-permute-done((f32[640,128]{1,0:T(8,128)S(1)}, f32[640,128]{1,0:T(8,128)S(1)}, u32[]{:S(2)}, u32[]{:S(2)}) %collective-permute-start.10) | collective-permute-done | bytes 327712 | tf_op jit(solution)/shard_map/ppermute | solution.py:536
  54.8 0.0 collective-permute-done.11.high
  54.8 0.1 shard_map.69
  54.9 0.7 %collective-permute-start.12 = (f32[640,128]{1,0:T(8,128)S(1)}, f32[640,128]{1,0:T(8,128)S(1)}, u32[]{:S(2)}, u32[]{:S(2)}) collective-permute-start(f32[640,128]{1,0:T(8,128)S(1)} %get-tuple-element.46.own_up), channel_id=1, source_target_pairs={{0,32},{32,64},{64,96},{96,128},{128,160},{160,192},{192,224},{224... | collective-permute-start | bytes 983048 | tf_op jit(solution)/shard_map/ppermute | solution.py:536
  55.6 0.0 copy-start
  55.6 0.4 collective-permute-start.13
  56.0 3.6 %shard_map.70.reg = f32[3,16,16,128]{3,2,1,0:T(8,128)S(1)} custom-call(f32[3,16,16,128]{3,2,1,0:T(8,128)S(1)} %get-tuple-element.29.v, f32[312,128]{1,0:T(8,128)S(1)} %collective-permute-done.low.zlow, f32[312,128]{1,0:T(8,128)S(1)} %collective-permute-done.1.high.zhigh, f32[576,128]{1,0:T(8,128)S(1)} %collective-permute-done.2.ylow.low, ...), custom_call_target="tpu_custom_call" | custom-call | flops 4000000 | bytes 4000000 | tf_op jit(solution)/shard_map/pallas_call | solution.py:520
  59.6 0.1 collective-permute-done.12.low
  59.6 2.8 %collective-permute-done.13.high = f32[640,128]{1,0:T(8,128)S(1)} collective-permute-done((f32[640,128]{1,0:T(8,128)S(1)}, f32[640,128]{1,0:T(8,128)S(1)}, u32[]{:S(2)}, u32[]{:S(2)}) %collective-permute-start.13) | collective-permute-done | bytes 327712 | tf_op jit(solution)/shard_map/ppermute | solution.py:536
  62.4 0.0 copy-done
  62.4 4.4 %shard_map.71 = f32[3,16,16,128]{3,2,1,0:T(8,128)} custom-call(f32[640,128]{1,0:T(8,128)S(1)} %get-tuple-element.46.own_up, f32[640,128]{1,0:T(8,128)S(1)} %get-tuple-element.47.own_down, f32[640,128]{1,0:T(8,128)S(1)} %collective-permute-done.12.low, f32[640,128]{1,0:T(8,128)S(1)} %collective-permute-done.13.high, f32[72,128]{1,0:T(8,128)S(1)} %get-tuple-element.48.numbers, ...), custom_call_target="tpu_custom_call" | custom-call | flops 20000 | bytes 20000 | tf_op jit(solution)/shard_map/pallas_call | solution.py:520
Async XLA Ops:
  1.6 14.6 %collective-permute-start.2 = (f32[576,128]{1,0:T(8,128)S(1)}, f32[576,128]{1,0:T(8,128)S(1)}, u32[]{:S(2)}, u32[]{:S(2)}) collective-permute-start(f32[576,128]{1,0:T(8,128)S(1)} %get-tuple-element.32), channel_id=1, source_target_pairs={{0,8},{8,16},{16,24},{24,0},{1,9},{9,17},{17,25},{25,1},{2,10},{10... | collective-permute-start | bytes 884744 | tf_op jit(solution)/shard_map/ppermute | solution.py:536
  3.8 12.4 %collective-permute-start.3 = (f32[576,128]{1,0:T(8,128)S(1)}, f32[576,128]{1,0:T(8,128)S(1)}, u32[]{:S(2)}, u32[]{:S(2)}) collective-permute-start(f32[576,128]{1,0:T(8,128)S(1)} %get-tuple-element.33), channel_id=1, source_target_pairs={{8,0},{16,8},{24,16},{0,24},{9,1},{17,9},{25,17},{1,25},{10,2},{18... | collective-permute-start | bytes 884744 | tf_op jit(solution)/shard_map/ppermute | solution.py:536
  5.4 7.8 %collective-permute-start.1 = (f32[312,128]{1,0:T(8,128)S(1)}, f32[312,128]{1,0:T(8,128)S(1)}, u32[]{:S(2)}, u32[]{:S(2)}) collective-permute-start(f32[312,128]{1,0:T(8,128)S(1)} %get-tuple-element.31), channel_id=1, source_target_pairs={{1,0},{2,1},{3,2},{4,3},{5,4},{6,5},{7,6},{0,7},{9,8},{10,9},{11,1... | collective-permute-start | bytes 479240 | tf_op jit(solution)/shard_map/ppermute | solution.py:536
  10.9 5.3 %collective-permute-start = (f32[312,128]{1,0:T(8,128)S(1)}, f32[312,128]{1,0:T(8,128)S(1)}, u32[]{:S(2)}, u32[]{:S(2)}) collective-permute-start(f32[312,128]{1,0:T(8,128)S(1)} %get-tuple-element.30.own), channel_id=1, source_target_pairs={{0,1},{1,2},{2,3},{3,4},{4,5},{5,6},{6,7},{7,0},{8,9},{9,10},{10,1... | collective-permute-start | bytes 479240 | tf_op jit(solution)/shard_map/ppermute | solution.py:536
  16.4 11.7 %collective-permute-start.5 = (f32[968,128]{1,0:T(8,128)S(1)}, f32[968,128]{1,0:T(8,128)S(1)}, u32[]{:S(2)}, u32[]{:S(2)}) collective-permute-start(f32[968,128]{1,0:T(8,128)S(1)} %get-tuple-element.35.own_down), channel_id=1, source_target_pairs={{32,0},{64,32},{96,64},{128,96},{160,128},{192,160},{224,192},{0,2... | collective-permute-start | bytes 1486856 | tf_op jit(solution)/shard_map/ppermute | solution.py:536
  18.9 9.2 %collective-permute-start.4 = (f32[968,128]{1,0:T(8,128)S(1)}, f32[968,128]{1,0:T(8,128)S(1)}, u32[]{:S(2)}, u32[]{:S(2)}) collective-permute-start(f32[968,128]{1,0:T(8,128)S(1)} %get-tuple-element.34.own_up.own), channel_id=1, source_target_pairs={{0,32},{32,64},{64,96},{96,128},{128,160},{160,192},{192,224},{224... | collective-permute-start | bytes 1486856 | tf_op jit(solution)/shard_map/ppermute | solution.py:536
  20.0 8.1 %collective-permute-start.6 = (f32[392,128]{1,0:T(8,128)S(1)}, f32[392,128]{1,0:T(8,128)S(1)}, u32[]{:S(2)}, u32[]{:S(2)}) collective-permute-start(f32[392,128]{1,0:T(8,128)S(1)} %get-tuple-element.36), channel_id=1, source_target_pairs={{0,8},{8,16},{16,24},{24,0},{1,9},{9,17},{17,25},{25,1},{2,10},{10... | collective-permute-start | bytes 602120 | tf_op jit(solution)/shard_map/ppermute | solution.py:536
  20.1 8.0 %collective-permute-start.7 = (f32[392,128]{1,0:T(8,128)S(1)}, f32[392,128]{1,0:T(8,128)S(1)}, u32[]{:S(2)}, u32[]{:S(2)}) collective-permute-start(f32[392,128]{1,0:T(8,128)S(1)} %get-tuple-element.37), channel_id=1, source_target_pairs={{8,0},{16,8},{24,16},{0,24},{9,1},{17,9},{25,17},{1,25},{10,2},{18... | collective-permute-start | bytes 602120 | tf_op jit(solution)/shard_map/ppermute | solution.py:536
  28.2 9.0 %collective-permute-start.8 = (f32[1296,128]{1,0:T(8,128)S(1)}, f32[1296,128]{1,0:T(8,128)S(1)}, u32[]{:S(2)}, u32[]{:S(2)}) collective-permute-start(f32[1296,128]{1,0:T(8,128)S(1)} %get-tuple-element.38), channel_id=1, source_target_pairs={{0,32},{32,64},{64,96},{96,128},{128,160},{160,192},{192,224},{224... | collective-permute-start | bytes 1990664 | tf_op jit(solution)/shard_map/ppermute | solution.py:536
  29.6 10.2 %collective-permute-start.9 = (f32[1296,128]{1,0:T(8,128)S(1)}, f32[1296,128]{1,0:T(8,128)S(1)}, u32[]{:S(2)}, u32[]{:S(2)}) collective-permute-start(f32[1296,128]{1,0:T(8,128)S(1)} %get-tuple-element.39), channel_id=1, source_target_pairs={{32,0},{64,32},{96,64},{128,96},{160,128},{192,160},{224,192},{0,2... | collective-permute-start | bytes 1990664 | tf_op jit(solution)/shard_map/ppermute | solution.py:536
  44.3 10.6 %collective-permute-start.10 = (f32[640,128]{1,0:T(8,128)S(1)}, f32[640,128]{1,0:T(8,128)S(1)}, u32[]{:S(2)}, u32[]{:S(2)}) collective-permute-start(f32[640,128]{1,0:T(8,128)S(1)} %get-tuple-element.44.own_up), channel_id=1, source_target_pairs={{0,8},{8,16},{16,24},{24,0},{1,9},{9,17},{17,25},{25,1},{2,10},{10... | collective-permute-start | bytes 983048 | tf_op jit(solution)/shard_map/ppermute | solution.py:536
  44.7 10.2 %collective-permute-start.11 = (f32[640,128]{1,0:T(8,128)S(1)}, f32[640,128]{1,0:T(8,128)S(1)}, u32[]{:S(2)}, u32[]{:S(2)}) collective-permute-start(f32[640,128]{1,0:T(8,128)S(1)} %get-tuple-element.45.own_down), channel_id=1, source_target_pairs={{8,0},{16,8},{24,16},{0,24},{9,1},{17,9},{25,17},{1,25},{10,2},{18... | collective-permute-start | bytes 983048 | tf_op jit(solution)/shard_map/ppermute | solution.py:536
  54.9 4.7 %collective-permute-start.12 = (f32[640,128]{1,0:T(8,128)S(1)}, f32[640,128]{1,0:T(8,128)S(1)}, u32[]{:S(2)}, u32[]{:S(2)}) collective-permute-start(f32[640,128]{1,0:T(8,128)S(1)} %get-tuple-element.46.own_up), channel_id=1, source_target_pairs={{0,32},{32,64},{64,96},{96,128},{128,160},{160,192},{192,224},{224... | collective-permute-start | bytes 983048 | tf_op jit(solution)/shard_map/ppermute | solution.py:536
  55.6 6.8 %copy-start = (bf16[2,3,16,16,128]{4,3,2,1,0:T(8,128)(2,1)S(1)}, bf16[2,3,16,16,128]{4,3,2,1,0:T(8,128)(2,1)}, u32[]{:S(2)}) copy-start(bf16[2,3,16,16,128]{4,3,2,1,0:T(8,128)(2,1)} %g.1) | copy-start | bytes 1179652
  55.6 6.8 %collective-permute-start.13 = (f32[640,128]{1,0:T(8,128)S(1)}, f32[640,128]{1,0:T(8,128)S(1)}, u32[]{:S(2)}, u32[]{:S(2)}) collective-permute-start(f32[640,128]{1,0:T(8,128)S(1)} %get-tuple-element.47.own_down), channel_id=1, source_target_pairs={{32,0},{64,32},{96,64},{128,96},{160,128},{192,160},{224,192},{0,2... | collective-permute-start | bytes 983048 | tf_op jit(solution)/shard_map/ppermute | solution.py:536

commit v7 on v6

--- a/solution.py
+++ b/solution.py
@@ -55,8 +55,12 @@
     return jnp.where(i > 0, 1.0, 0.0).astype(F32), jnp.where(i < n - 1, 1.0, 0.0).astype(F32)
 
 
+def is_even(axis):
+    return lax.axis_index(axis) % 2 == 0
+
+
 def sources_kernel(
-    v_hbm, g_hbm, sx_hbm, sy_hbm, sz_hbm, fr_hbm, v, s0, s1, up, down, yup, ydown, g, sx, sy, sz, fr, sem, small_sem
+    v_hbm, g_hbm, sx_hbm, sy_hbm, sz_hbm, fr_hbm, v, s0, s1, swap0, swap1, yup, ydown, g, sx, sy, sz, fr, sem, small_sem
 ):
     copies = []
     for q in range(4):
@@ -93,13 +97,15 @@
             rows = pl.ds(Y_FACE + (c * 8 + x) * 8, 8)
             yup[rows] = jnp.where(first_half, pltpu.roll(v[c, x + 8, 8:16], 4, 0), v[c, x, 8:16])
             ydown[rows] = jnp.where(first_half, v[c, x, 0:8], pltpu.roll(v[c, x + 8, 0:8], 4, 0))
+    even = is_even("gz")
     upper = lane >= 64
     for start, s in ((Z_S0, s0), (Z_S1, s1)):
         for x in range(8):
             rows = pl.ds(start + x * T, T)
             a, b = s[x], roll(s[x + 8], 64)
-            up[rows] = jnp.where(upper, a, b)
-            down[rows] = jnp.where(upper, b, a)
+            u, d = jnp.where(upper, a, b), jnp.where(upper, b, a)
+            swap0[rows] = jnp.where(even, u, d)
+            swap1[rows] = jnp.where(even, d, u)
     piece = lane // 8
     for c in range(3):
         u, d = v[c, 0], v[c, 0]
@@ -107,8 +113,8 @@
             r = roll(v[c, x], 8 * x)
             u = jnp.where(piece == (15 + x) % 16, r, u)
             d = jnp.where(piece == x, r, d)
-        up[pl.ds(Z_V + c * T, T)] = u
-        down[pl.ds(Z_V + c * T, T)] = d
+        swap0[pl.ds(Z_V + c * T, T)] = jnp.where(even, u, d)
+        swap1[pl.ds(Z_V + c * T, T)] = jnp.where(even, d, u)
     lane = lanes()
     for copy in small:
         copy.wait()
@@ -134,17 +140,19 @@
     tap = (place - 3) % 4
     row = jnp.where(tap == 0, weights[0], jnp.where(tap == 1, weights[1], jnp.where(tap == 2, weights[2], weights[3])))
     row = jnp.where(place < 3, shifts.astype(F32), row)
-    up[pl.ds(Z_META, 8)] = row
-    down[pl.ds(Z_META, 8)] = row
-
-
-def tile_messages_kernel(s0, s1, v, own, low, high, ylow, yhigh, yup, ydown, xup, xdown):
+    swap0[pl.ds(Z_META, 8)] = row
+    swap1[pl.ds(Z_META, 8)] = row
+
+
+def tile_messages_kernel(s0, s1, v, own, swap0, swap1, ylow, yhigh, yup, ydown, xup, xdown):
     del ylow, yhigh
     low_in, high_in = inside("gz")
+    even = is_even("gz")
     upper = lanes(T) >= 64
     for start, s in ((Z_S0, s0), (Z_S1, s1)):
         for j in range(8):
-            a, b = low_in * low[pl.ds(start + j * T, T)], high_in * high[pl.ds(start + j * T, T)]
+            a, b = swap0[pl.ds(start + j * T, T)], swap1[pl.ds(start + j * T, T)]
+            a, b = low_in * jnp.where(even, b, a), high_in * jnp.where(even, a, b)
             edges = (jnp.where(upper, a, b), roll(jnp.where(upper, b, a), 64))
             for h, edge in enumerate(edges):
                 x = j + 8 * h
@@ -165,8 +173,9 @@
             xup[pl.ds(FACE + (c * 4 + i) * T, T)] = v[c, 12 + i]
             xdown[pl.ds(FACE + (c * 4 + i) * T, T)] = v[c, i]
     sub = subs()
-    meta = [ref[pl.ds(Z_META, 8)] for ref in (low, own, high)]
-    row = jnp.where(sub == 0, low_in * meta[0], jnp.where(sub == 1, meta[1], high_in * meta[2]))
+    a, b = swap0[pl.ds(Z_META, 8)], swap1[pl.ds(Z_META, 8)]
+    a, b = low_in * jnp.where(even, b, a), high_in * jnp.where(even, a, b)
+    row = jnp.where(sub == 0, a, jnp.where(sub == 1, own[pl.ds(Z_META, 8)], b))
     for out, at in ((yup, Y_META), (ydown, Y_META), (xup, NUMBERS), (xdown, NUMBERS)):
         out[pl.ds(at, 8)] = row
 
@@ -477,14 +486,16 @@
         done.wait()
 
 
-def laplace_kernel(v, zlow, zhigh, ylow, yhigh, xlow, xhigh, out, w):
+def laplace_kernel(v, swap0, swap1, ylow, yhigh, xlow, xhigh, out, w):
     lane = lanes(T)
     half = (lane & 4) == 0
+    even = is_even("gz")
     (x_low, x_high), (y_low, y_high), (z_low, z_high) = inside("gx"), inside("gy"), inside("gz")
     sides = [-REG_WEIGHT * t for t in LAPLACE_TAPS]
     for c in range(3):
         rows = pl.ds(Z_V + c * T, T)
-        faces = jnp.where(half, z_high * zhigh[rows], z_low * zlow[rows])
+        a, b = swap0[rows], swap1[rows]
+        faces = jnp.where(half, z_high * jnp.where(even, a, b), z_low * jnp.where(even, b, a))
         for i in range(4):
             rows = pl.ds(FACE + (c * 4 + i) * T, T)
             w[i, 8:24] = x_low * xlow[rows]
@@ -542,13 +553,20 @@
     return call(last_step_kernel, args, [shape], scratch=scratch, out_space=HBM)
 
 
+def swap(first, second, axis):
+    n = lax.axis_size(axis)
+    pairs = [(i, i + 1 if i % 2 == 0 else i - 1) for i in range(n)]
+    others = [(i, i if i in (0, n - 1) else i - 1 if i % 2 == 0 else i + 1) for i in range(n)]
+    return lax.ppermute(first, axis, pairs), lax.ppermute(second, axis, others)
+
+
 def body(velocity, gradients, shift_x, shift_y, shift_z, fractions):
     v, g = velocity, gradients
     tile = (T, T, L)
     vm = lambda *s: pltpu.VMEM(s, F32)
     shifts = [s.transpose(0, 1, 3, 2) for s in (shift_x, shift_y, shift_z)]
     inputs = [v, g, *shifts, fractions.transpose(0, 2, 3, 4, 1)]
-    v, s0, s1, zup, zdown, yup, ydown = call(
+    v, s0, s1, first, second, yup, ydown = call(
         sources_kernel,
         [pltpu.with_memory_space_constraint(a, pltpu.HBM) for a in inputs],
         [v.shape, tile, tile, (Z_ROWS, L), (Z_ROWS, L), (Y_ROWS, L), (Y_ROWS, L)],
@@ -557,10 +575,10 @@
         + [pltpu.SMEM((2, 2, 2, 1, 3), jnp.int32), pltpu.SemaphoreType.DMA((8,)), pltpu.SemaphoreType.DMA((4,))],
         hbm=range(6),
     )
-    zlow, zhigh = exchange(zup, zdown, "gz")
+    swap0, swap1 = swap(first, second, "gz")
     ylow, yhigh = exchange(yup, ydown, "gy")
     yup, ydown, xup, xdown = call(
-        tile_messages_kernel, (s0, s1, v, zup, zlow, zhigh, ylow, yhigh), [(Y_EROWS, L)] * 2 + [(ROWS, L)] * 2
+        tile_messages_kernel, (s0, s1, v, first, swap0, swap1, ylow, yhigh), [(Y_EROWS, L)] * 2 + [(ROWS, L)] * 2
     )
     xlow, xhigh = exchange(xup, xdown, "gx")
     elow, ehigh = exchange(yup, ydown, "gy")
@@ -577,7 +595,7 @@
         alias={7: 3, 8: 4, 9: 5, 10: 6},
     )
     (reg,) = call(
-        laplace_kernel, (v, zlow, zhigh, ylow, yhigh, xlow, xhigh), [v.shape], scratch=[vm(24, 32, L)], cost=4000000
+        laplace_kernel, (v, swap0, swap1, ylow, yhigh, xlow, xhigh), [v.shape], scratch=[vm(24, 32, L)], cost=4000000
     )
     low, high = exchange(up, down, "gy")
     up, down = call(sum_y_kernel, (up, down, low, high), [(R_ROWS, L)] * 2)

time: 67.8 us -> 65.9 us (0.972)
  the two profiles are of different devices: /device:TPU:1 before, /device:TPU:95 now
where the time goes in v7:
time: 65.9 us; the launch traced here: 65.8 us
  waiting for transfers between devices  34.3 us (52%)
  starting transfers between devices  16.8 us (25%)
  Pallas kernels  14.5 us (22%)
    ppermute x12, waiting for transfers between devices, exchange(): return (lax.ppermute(up, axis, rise), lax.ppermute(down, axis, fall))  31.7 us
    pallas_call x8, Pallas kernels, call(): pl.pallas_call(kernel, out_shape=shapes, in_specs=specs, out_specs=[out_s...  14.5 us
    ppermute x12, starting transfers between devices, exchange(): return (lax.ppermute(up, axis, rise), lax.ppermute(down, axis, fall))  10.3 us
    ppermute x1, starting transfers between devices, swap(): lax.ppermute(first, axis, pairs)  4.56 us
    ppermute x1, waiting for transfers between devices, swap(): lax.ppermute(first, axis, pairs)  2.66 us
    ppermute x1, starting transfers between devices, swap(): lax.ppermute(second, axis, others)  1.91 us
  transfers between devices with their start and end apart: 14, of which 9 were waited for; matrix products, arithmetic and copies ran while one was open for 0% of the time, Pallas kernels for 6%

profile of v7, /device:TPU:95, one launch (start us, length us, event | category | flops | bytes accessed | tf_op | source)
XLA Modules:
  0.0 65.8 jit_solution(11583215589208477420)
XLA Ops:
  0.0 1.6 %shard_map.64 = (f32[3,16,16,128]{3,2,1,0:T(8,128)S(1)}, f32[16,16,128]{2,1,0:T(8,128)S(1)}, f32[16,16,128]{2,1,0:T(8,128)S(1)}, f32[312,128]{1,0:T(8,128)S(1)},...) custom-call(f32[3,16,16,128]{3,2,1,0:T(8,128)} %v_hbm.1, bf16[2,3,16,16,128]{4,3,2,1,0:T(8,128)(2,1)} %g.1, ...), custom_call_target="tpu_custom_call" | custom-call | flops 20000 | bytes 20000 | tf_op jit(solution)/shard_map/pallas_call | solution.py:531
  1.6 0.1 collective-permute-start.2
  1.7 1.5 %collective-permute-start.3 = (f32[576,128]{1,0:T(8,128)S(1)}, f32[576,128]{1,0:T(8,128)S(1)}, u32[]{:S(2)}, u32[]{:S(2)}) collective-permute-start(f32[576,128]{1,0:T(8,128)S(1)} %get-tuple-element.33), channel_id=1, source_target_pairs={{8,0},{16,8},{24,16},{0,24},{9,1},{17,9},{25,17},{1,25},{10,2},{18... | collective-permute-start | bytes 884744 | tf_op jit(solution)/shard_map/ppermute | solution.py:547
  3.2 1.9 %collective-permute-start.1 = (f32[312,128]{1,0:T(8,128)S(1)}, f32[312,128]{1,0:T(8,128)S(1)}, u32[]{:S(2)}, u32[]{:S(2)}) collective-permute-start(f32[312,128]{1,0:T(8,128)S(1)} %get-tuple-element.31), channel_id=1, source_target_pairs={{0,0},{1,2},{2,1},{3,4},{4,3},{5,6},{6,5},{7,7},{8,8},{9,10},{10,9... | collective-permute-start | bytes 479240 | tf_op jit(solution)/shard_map/ppermute | solution.py:560
  5.1 4.6 %collective-permute-start = (f32[312,128]{1,0:T(8,128)S(1)}, f32[312,128]{1,0:T(8,128)S(1)}, u32[]{:S(2)}, u32[]{:S(2)}) collective-permute-start(f32[312,128]{1,0:T(8,128)S(1)} %get-tuple-element.30.own), channel_id=1, source_target_pairs={{0,1},{1,0},{2,3},{3,2},{4,5},{5,4},{6,7},{7,6},{8,9},{9,8},{10,11... | collective-permute-start | bytes 479240 | tf_op jit(solution)/shard_map/ppermute | solution.py:560
  9.6 0.0 collective-permute-done.1.swap1
  9.6 2.7 %collective-permute-done.swap0 = f32[312,128]{1,0:T(8,128)S(1)} collective-permute-done((f32[312,128]{1,0:T(8,128)S(1)}, f32[312,128]{1,0:T(8,128)S(1)}, u32[]{:S(2)}, u32[]{:S(2)}) %collective-permute-start) | collective-permute-done | bytes 159776 | tf_op jit(solution)/shard_map/ppermute | solution.py:560
  12.3 0.0 collective-permute-done.2.ylow.low
  12.3 0.0 collective-permute-done.3.yhigh.high
  12.3 0.1 shard_map.65
  12.4 2.4 %collective-permute-start.5 = (f32[968,128]{1,0:T(8,128)S(1)}, f32[968,128]{1,0:T(8,128)S(1)}, u32[]{:S(2)}, u32[]{:S(2)}) collective-permute-start(f32[968,128]{1,0:T(8,128)S(1)} %get-tuple-element.35.own_down), channel_id=1, source_target_pairs={{32,0},{64,32},{96,64},{128,96},{160,128},{192,160},{224,192},{0,2... | collective-permute-start | bytes 1486856 | tf_op jit(solution)/shard_map/ppermute | solution.py:547
  14.8 0.6 collective-permute-start.4
  15.4 1.7 %collective-permute-start.6 = (f32[392,128]{1,0:T(8,128)S(1)}, f32[392,128]{1,0:T(8,128)S(1)}, u32[]{:S(2)}, u32[]{:S(2)}) collective-permute-start(f32[392,128]{1,0:T(8,128)S(1)} %get-tuple-element.36), channel_id=1, source_target_pairs={{0,8},{8,16},{16,24},{24,0},{1,9},{9,17},{17,25},{25,1},{2,10},{10... | collective-permute-start | bytes 602120 | tf_op jit(solution)/shard_map/ppermute | solution.py:547
  17.1 0.0 collective-permute-start.7
  17.1 5.0 %collective-permute-done.6.elow.ylow = f32[392,128]{1,0:T(8,128)S(1)} collective-permute-done((f32[392,128]{1,0:T(8,128)S(1)}, f32[392,128]{1,0:T(8,128)S(1)}, u32[]{:S(2)}, u32[]{:S(2)}) %collective-permute-start.6) | collective-permute-done | bytes 200736 | tf_op jit(solution)/shard_map/ppermute | solution.py:547
  22.1 2.9 %collective-permute-done.7.ehigh.yhigh = f32[392,128]{1,0:T(8,128)S(1)} collective-permute-done((f32[392,128]{1,0:T(8,128)S(1)}, f32[392,128]{1,0:T(8,128)S(1)}, u32[]{:S(2)}, u32[]{:S(2)}) %collective-permute-start.7) | collective-permute-done | bytes 200736 | tf_op jit(solution)/shard_map/ppermute | solution.py:547
  25.0 0.0 collective-permute-done.5.xhigh
  25.0 0.0 collective-permute-done.4.xlow
  25.0 0.1 shard_map.66
  25.1 1.0 %collective-permute-start.8 = (f32[1296,128]{1,0:T(8,128)S(1)}, f32[1296,128]{1,0:T(8,128)S(1)}, u32[]{:S(2)}, u32[]{:S(2)}) collective-permute-start(f32[1296,128]{1,0:T(8,128)S(1)} %get-tuple-element.38), channel_id=1, source_target_pairs={{0,32},{32,64},{64,96},{96,128},{128,160},{160,192},{192,224},{224... | collective-permute-start | bytes 1990664 | tf_op jit(solution)/shard_map/ppermute | solution.py:547
  26.1 0.0 collective-permute-start.9
  26.1 0.2 shard_map.67
  26.3 7.4 %collective-permute-done.8.corner_low = f32[1296,128]{1,0:T(8,128)S(1)} collective-permute-done((f32[1296,128]{1,0:T(8,128)S(1)}, f32[1296,128]{1,0:T(8,128)S(1)}, u32[]{:S(2)}, u32[]{:S(2)}) %collective-permute-start.8) | collective-permute-done | bytes 663584 | tf_op jit(solution)/shard_map/ppermute | solution.py:547
  33.7 3.7 %collective-permute-done.9.corner_high = f32[1296,128]{1,0:T(8,128)S(1)} collective-permute-done((f32[1296,128]{1,0:T(8,128)S(1)}, f32[1296,128]{1,0:T(8,128)S(1)}, u32[]{:S(2)}, u32[]{:S(2)}) %collective-permute-start.9) | collective-permute-done | bytes 663584 | tf_op jit(solution)/shard_map/ppermute | solution.py:547
  37.4 4.4 %shard_map.68 = (f32[640,128]{1,0:T(8,128)S(1)}, f32[640,128]{1,0:T(8,128)S(1)}, f32[72,128]{1,0:T(8,128)S(1)}, f32[2304,128]{1,0:T(8,128)S(1)}, f32[2304,128]{1...) custom-call(f32[968,128]{1,0:T(8,128)S(1)} %get-tuple-element.34.own, ...), custom_call_target="tpu_custom_call", output_to_operand_aliasing={{3}: (7, {}), {4}: (8, {}), {5}: (9, {}), {6}: (10, {})} | custom-call | flops 20000 | bytes 20000 | tf_op jit(solution)/shard_map/pallas_call | solution.py:531
  41.9 0.7 %collective-permute-start.10 = (f32[640,128]{1,0:T(8,128)S(1)}, f32[640,128]{1,0:T(8,128)S(1)}, u32[]{:S(2)}, u32[]{:S(2)}) collective-permute-start(f32[640,128]{1,0:T(8,128)S(1)} %get-tuple-element.44.own_up), channel_id=1, source_target_pairs={{0,8},{8,16},{16,24},{24,0},{1,9},{9,17},{17,25},{25,1},{2,10},{10... | collective-permute-start | bytes 983048 | tf_op jit(solution)/shard_map/ppermute | solution.py:547
  42.6 0.8 %collective-permute-start.11 = (f32[640,128]{1,0:T(8,128)S(1)}, f32[640,128]{1,0:T(8,128)S(1)}, u32[]{:S(2)}, u32[]{:S(2)}) collective-permute-start(f32[640,128]{1,0:T(8,128)S(1)} %get-tuple-element.45.own_down), channel_id=1, source_target_pairs={{8,0},{16,8},{24,16},{0,24},{9,1},{17,9},{25,17},{1,25},{10,2},{18... | collective-permute-start | bytes 983048 | tf_op jit(solution)/shard_map/ppermute | solution.py:547
  43.4 7.3 %collective-permute-done.10.low = f32[640,128]{1,0:T(8,128)S(1)} collective-permute-done((f32[640,128]{1,0:T(8,128)S(1)}, f32[640,128]{1,0:T(8,128)S(1)}, u32[]{:S(2)}, u32[]{:S(2)}) %collective-permute-start.10) | collective-permute-done | bytes 327712 | tf_op jit(solution)/shard_map/ppermute | solution.py:547
  50.7 1.2 %collective-permute-done.11.high = f32[640,128]{1,0:T(8,128)S(1)} collective-permute-done((f32[640,128]{1,0:T(8,128)S(1)}, f32[640,128]{1,0:T(8,128)S(1)}, u32[]{:S(2)}, u32[]{:S(2)}) %collective-permute-start.11) | collective-permute-done | bytes 327712 | tf_op jit(solution)/shard_map/ppermute | solution.py:547
  51.9 0.1 shard_map.69
  52.0 1.6 %collective-permute-start.12 = (f32[640,128]{1,0:T(8,128)S(1)}, f32[640,128]{1,0:T(8,128)S(1)}, u32[]{:S(2)}, u32[]{:S(2)}) collective-permute-start(f32[640,128]{1,0:T(8,128)S(1)} %get-tuple-element.46.own_up), channel_id=1, source_target_pairs={{0,32},{32,64},{64,96},{96,128},{128,160},{160,192},{192,224},{224... | collective-permute-start | bytes 983048 | tf_op jit(solution)/shard_map/ppermute | solution.py:547
  53.5 0.0 copy-start
  53.5 0.0 collective-permute-start.13
  53.5 3.6 %shard_map.70.reg = f32[3,16,16,128]{3,2,1,0:T(8,128)S(1)} custom-call(f32[3,16,16,128]{3,2,1,0:T(8,128)S(1)} %get-tuple-element.29.v, f32[312,128]{1,0:T(8,128)S(1)} %collective-permute-done.swap0, f32[312,128]{1,0:T(8,128)S(1)} %collective-permute-done.1.swap1, f32[576,128]{1,0:T(8,128)S(1)} %collective-permute-done.2.ylow.low, ...), custom_call_target="tpu_custom_call" | custom-call | flops 4000000 | bytes 4000000 | tf_op jit(solution)/shard_map/pallas_call | solution.py:531
  57.1 0.4 collective-permute-done.12.low
  57.6 3.7 %collective-permute-done.13.high = f32[640,128]{1,0:T(8,128)S(1)} collective-permute-done((f32[640,128]{1,0:T(8,128)S(1)}, f32[640,128]{1,0:T(8,128)S(1)}, u32[]{:S(2)}, u32[]{:S(2)}) %collective-permute-start.13) | collective-permute-done | bytes 327712 | tf_op jit(solution)/shard_map/ppermute | solution.py:547
  61.3 0.0 copy-done
  61.3 4.4 %shard_map.71 = f32[3,16,16,128]{3,2,1,0:T(8,128)} custom-call(f32[640,128]{1,0:T(8,128)S(1)} %get-tuple-element.46.own_up, f32[640,128]{1,0:T(8,128)S(1)} %get-tuple-element.47.own_down, f32[640,128]{1,0:T(8,128)S(1)} %collective-permute-done.12.low, f32[640,128]{1,0:T(8,128)S(1)} %collective-permute-done.13.high, f32[72,128]{1,0:T(8,128)S(1)} %get-tuple-element.48.numbers, ...), custom_call_target="tpu_custom_call" | custom-call | flops 20000 | bytes 20000 | tf_op jit(solution)/shard_map/pallas_call | solution.py:531
Async XLA Ops:
  1.6 10.7 %collective-permute-start.2 = (f32[576,128]{1,0:T(8,128)S(1)}, f32[576,128]{1,0:T(8,128)S(1)}, u32[]{:S(2)}, u32[]{:S(2)}) collective-permute-start(f32[576,128]{1,0:T(8,128)S(1)} %get-tuple-element.32), channel_id=1, source_target_pairs={{0,8},{8,16},{16,24},{24,0},{1,9},{9,17},{17,25},{25,1},{2,10},{10... | collective-permute-start | bytes 884744 | tf_op jit(solution)/shard_map/ppermute | solution.py:547
  1.7 10.6 %collective-permute-start.3 = (f32[576,128]{1,0:T(8,128)S(1)}, f32[576,128]{1,0:T(8,128)S(1)}, u32[]{:S(2)}, u32[]{:S(2)}) collective-permute-start(f32[576,128]{1,0:T(8,128)S(1)} %get-tuple-element.33), channel_id=1, source_target_pairs={{8,0},{16,8},{24,16},{0,24},{9,1},{17,9},{25,17},{1,25},{10,2},{18... | collective-permute-start | bytes 884744 | tf_op jit(solution)/shard_map/ppermute | solution.py:547
  3.2 6.5 %collective-permute-start.1 = (f32[312,128]{1,0:T(8,128)S(1)}, f32[312,128]{1,0:T(8,128)S(1)}, u32[]{:S(2)}, u32[]{:S(2)}) collective-permute-start(f32[312,128]{1,0:T(8,128)S(1)} %get-tuple-element.31), channel_id=1, source_target_pairs={{0,0},{1,2},{2,1},{3,4},{4,3},{5,6},{6,5},{7,7},{8,8},{9,10},{10,9... | collective-permute-start | bytes 479240 | tf_op jit(solution)/shard_map/ppermute | solution.py:560
  5.1 7.2 %collective-permute-start = (f32[312,128]{1,0:T(8,128)S(1)}, f32[312,128]{1,0:T(8,128)S(1)}, u32[]{:S(2)}, u32[]{:S(2)}) collective-permute-start(f32[312,128]{1,0:T(8,128)S(1)} %get-tuple-element.30.own), channel_id=1, source_target_pairs={{0,1},{1,0},{2,3},{3,2},{4,5},{5,4},{6,7},{7,6},{8,9},{9,8},{10,11... | collective-permute-start | bytes 479240 | tf_op jit(solution)/shard_map/ppermute | solution.py:560
  12.4 12.6 %collective-permute-start.5 = (f32[968,128]{1,0:T(8,128)S(1)}, f32[968,128]{1,0:T(8,128)S(1)}, u32[]{:S(2)}, u32[]{:S(2)}) collective-permute-start(f32[968,128]{1,0:T(8,128)S(1)} %get-tuple-element.35.own_down), channel_id=1, source_target_pairs={{32,0},{64,32},{96,64},{128,96},{160,128},{192,160},{224,192},{0,2... | collective-permute-start | bytes 1486856 | tf_op jit(solution)/shard_map/ppermute | solution.py:547
  14.8 10.2 %collective-permute-start.4 = (f32[968,128]{1,0:T(8,128)S(1)}, f32[968,128]{1,0:T(8,128)S(1)}, u32[]{:S(2)}, u32[]{:S(2)}) collective-permute-start(f32[968,128]{1,0:T(8,128)S(1)} %get-tuple-element.34.own_up.own), channel_id=1, source_target_pairs={{0,32},{32,64},{64,96},{96,128},{128,160},{160,192},{192,224},{224... | collective-permute-start | bytes 1486856 | tf_op jit(solution)/shard_map/ppermute | solution.py:547
  15.4 6.7 %collective-permute-start.6 = (f32[392,128]{1,0:T(8,128)S(1)}, f32[392,128]{1,0:T(8,128)S(1)}, u32[]{:S(2)}, u32[]{:S(2)}) collective-permute-start(f32[392,128]{1,0:T(8,128)S(1)} %get-tuple-element.36), channel_id=1, source_target_pairs={{0,8},{8,16},{16,24},{24,0},{1,9},{9,17},{17,25},{25,1},{2,10},{10... | collective-permute-start | bytes 602120 | tf_op jit(solution)/shard_map/ppermute | solution.py:547
  17.1 7.9 %collective-permute-start.7 = (f32[392,128]{1,0:T(8,128)S(1)}, f32[392,128]{1,0:T(8,128)S(1)}, u32[]{:S(2)}, u32[]{:S(2)}) collective-permute-start(f32[392,128]{1,0:T(8,128)S(1)} %get-tuple-element.37), channel_id=1, source_target_pairs={{8,0},{16,8},{24,16},{0,24},{9,1},{17,9},{25,17},{1,25},{10,2},{18... | collective-permute-start | bytes 602120 | tf_op jit(solution)/shard_map/ppermute | solution.py:547
  25.1 8.6 %collective-permute-start.8 = (f32[1296,128]{1,0:T(8,128)S(1)}, f32[1296,128]{1,0:T(8,128)S(1)}, u32[]{:S(2)}, u32[]{:S(2)}) collective-permute-start(f32[1296,128]{1,0:T(8,128)S(1)} %get-tuple-element.38), channel_id=1, source_target_pairs={{0,32},{32,64},{64,96},{96,128},{128,160},{160,192},{192,224},{224... | collective-permute-start | bytes 1990664 | tf_op jit(solution)/shard_map/ppermute | solution.py:547
  26.1 11.3 %collective-permute-start.9 = (f32[1296,128]{1,0:T(8,128)S(1)}, f32[1296,128]{1,0:T(8,128)S(1)}, u32[]{:S(2)}, u32[]{:S(2)}) collective-permute-start(f32[1296,128]{1,0:T(8,128)S(1)} %get-tuple-element.39), channel_id=1, source_target_pairs={{32,0},{64,32},{96,64},{128,96},{160,128},{192,160},{224,192},{0,2... | collective-permute-start | bytes 1990664 | tf_op jit(solution)/shard_map/ppermute | solution.py:547
  41.9 8.8 %collective-permute-start.10 = (f32[640,128]{1,0:T(8,128)S(1)}, f32[640,128]{1,0:T(8,128)S(1)}, u32[]{:S(2)}, u32[]{:S(2)}) collective-permute-start(f32[640,128]{1,0:T(8,128)S(1)} %get-tuple-element.44.own_up), channel_id=1, source_target_pairs={{0,8},{8,16},{16,24},{24,0},{1,9},{9,17},{17,25},{25,1},{2,10},{10... | collective-permute-start | bytes 983048 | tf_op jit(solution)/shard_map/ppermute | solution.py:547
  42.6 9.3 %collective-permute-start.11 = (f32[640,128]{1,0:T(8,128)S(1)}, f32[640,128]{1,0:T(8,128)S(1)}, u32[]{:S(2)}, u32[]{:S(2)}) collective-permute-start(f32[640,128]{1,0:T(8,128)S(1)} %get-tuple-element.45.own_down), channel_id=1, source_target_pairs={{8,0},{16,8},{24,16},{0,24},{9,1},{17,9},{25,17},{1,25},{10,2},{18... | collective-permute-start | bytes 983048 | tf_op jit(solution)/shard_map/ppermute | solution.py:547
  52.0 5.6 %collective-permute-start.12 = (f32[640,128]{1,0:T(8,128)S(1)}, f32[640,128]{1,0:T(8,128)S(1)}, u32[]{:S(2)}, u32[]{:S(2)}) collective-permute-start(f32[640,128]{1,0:T(8,128)S(1)} %get-tuple-element.46.own_up), channel_id=1, source_target_pairs={{0,32},{32,64},{64,96},{96,128},{128,160},{160,192},{192,224},{224... | collective-permute-start | bytes 983048 | tf_op jit(solution)/shard_map/ppermute | solution.py:547
  53.5 7.7 %copy-start = (bf16[2,3,16,16,128]{4,3,2,1,0:T(8,128)(2,1)S(1)}, bf16[2,3,16,16,128]{4,3,2,1,0:T(8,128)(2,1)}, u32[]{:S(2)}) copy-start(bf16[2,3,16,16,128]{4,3,2,1,0:T(8,128)(2,1)} %g.1) | copy-start | bytes 1179652
  53.5 7.7 %collective-permute-start.13 = (f32[640,128]{1,0:T(8,128)S(1)}, f32[640,128]{1,0:T(8,128)S(1)}, u32[]{:S(2)}, u32[]{:S(2)}) collective-permute-start(f32[640,128]{1,0:T(8,128)S(1)} %get-tuple-element.47.own_down), channel_id=1, source_target_pairs={{32,0},{64,32},{96,64},{128,96},{160,128},{192,160},{224,192},{0,2... | collective-permute-start | bytes 983048 | tf_op jit(solution)/shard_map/ppermute | solution.py:547

commit v8 on v7

--- a/solution.py
+++ b/solution.py
@@ -59,8 +59,33 @@
     return lax.axis_index(axis) % 2 == 0
 
 
+class Side:
+    def __init__(self, axis, refs, up):
+        self.even, self.refs = is_even(axis), refs if up else refs[::-1]
+
+    def __getitem__(self, rows):
+        return jnp.where(self.even, self.refs[0][rows], self.refs[1][rows])
+
+
+def sides(axis, refs):
+    return Side(axis, refs, False), Side(axis, refs, True)
+
+
+class Swap:
+    def __init__(self, axis, refs):
+        self.even, self.refs = is_even(axis), refs
+
+    def write(self, rows, up, down):
+        if up is down:
+            self.refs[0][rows] = up
+            self.refs[1][rows] = up
+        else:
+            self.refs[0][rows] = jnp.where(self.even, up, down)
+            self.refs[1][rows] = jnp.where(self.even, down, up)
+
+
 def sources_kernel(
-    v_hbm, g_hbm, sx_hbm, sy_hbm, sz_hbm, fr_hbm, v, s0, s1, swap0, swap1, yup, ydown, g, sx, sy, sz, fr, sem, small_sem
+    v_hbm, g_hbm, sx_hbm, sy_hbm, sz_hbm, fr_hbm, v, s0, s1, swap0, swap1, y0, y1, g, sx, sy, sz, fr, sem, small_sem
 ):
     copies = []
     for q in range(4):
@@ -73,6 +98,7 @@
     ]
     for copy in copies + small:
         copy.start()
+    y_swap = Swap("gy", (y0, y1))
     lane = lanes(T)
     for x in range(T):
         if x % 4 == 0:
@@ -86,17 +112,16 @@
             value = STEP_SIZE * total
             s[x] = value
             if k == 0:
-                yup[pl.ds(Y_S0 + x * T, T)] = value
-                ydown[pl.ds(Y_S0 + x * T, T)] = value
+                y_swap.write(pl.ds(Y_S0 + x * T, T), value, value)
             else:
-                yup[pl.ds(Y_S1 + x * 8, 8)] = value[8:16]
-                ydown[pl.ds(Y_S1 + x * 8, 8)] = value[0:8]
+                y_swap.write(pl.ds(Y_S1 + x * 8, 8), value[8:16], value[0:8])
     first_half = subs() < 4
     for c in range(3):
         for x in range(8):
             rows = pl.ds(Y_FACE + (c * 8 + x) * 8, 8)
-            yup[rows] = jnp.where(first_half, pltpu.roll(v[c, x + 8, 8:16], 4, 0), v[c, x, 8:16])
-            ydown[rows] = jnp.where(first_half, v[c, x, 0:8], pltpu.roll(v[c, x + 8, 0:8], 4, 0))
+            u = jnp.where(first_half, pltpu.roll(v[c, x + 8, 8:16], 4, 0), v[c, x, 8:16])
+            d = jnp.where(first_half, v[c, x, 0:8], pltpu.roll(v[c, x + 8, 0:8], 4, 0))
+            y_swap.write(rows, u, d)
     even = is_even("gz")
     upper = lane >= 64
     for start, s in ((Z_S0, s0), (Z_S1, s1)):
@@ -144,8 +169,9 @@
     swap1[pl.ds(Z_META, 8)] = row
 
 
-def tile_messages_kernel(s0, s1, v, own, swap0, swap1, ylow, yhigh, yup, ydown, xup, xdown):
+def tile_messages_kernel(s0, s1, v, own, swap0, swap1, ylow, yhigh, y0, y1, x0, x1):
     del ylow, yhigh
+    y_swap, x_swap = Swap("gy", (y0, y1)), Swap("gx", (x0, x1))
     low_in, high_in = inside("gz")
     even = is_even("gz")
     upper = lanes(T) >= 64
@@ -157,45 +183,41 @@
             for h, edge in enumerate(edges):
                 x = j + 8 * h
                 if start == Z_S0:
-                    for out in (xup, xdown):
-                        out[pl.ds(A0 + x * T, T)] = s[x]
-                        out[pl.ds(E0 + x * T, T)] = edge
-                    for out in (yup, ydown):
-                        out[pl.ds(Y_E0 + x * T, T)] = edge
+                    inner = s[x]
+                    x_swap.write(pl.ds(A0 + x * T, T), inner, inner)
+                    x_swap.write(pl.ds(E0 + x * T, T), edge, edge)
+                    y_swap.write(pl.ds(Y_E0 + x * T, T), edge, edge)
                 else:
-                    yup[pl.ds(Y_E1 + x * 8, 8)] = edge[8:16]
-                    ydown[pl.ds(Y_E1 + x * 8, 8)] = edge[0:8]
-                    out = (xdown, xup)[h]
-                    out[pl.ds(A1 + j * T, T)] = s[x]
-                    out[pl.ds(E1 + j * T, T)] = edge
+                    y_swap.write(pl.ds(Y_E1 + x * 8, 8), edge[8:16], edge[0:8])
+            if start == Z_S1:
+                x_swap.write(pl.ds(A1 + j * T, T), s[j + 8], s[j])
+                x_swap.write(pl.ds(E1 + j * T, T), edges[1], edges[0])
     for c in range(3):
         for i in range(4):
-            xup[pl.ds(FACE + (c * 4 + i) * T, T)] = v[c, 12 + i]
-            xdown[pl.ds(FACE + (c * 4 + i) * T, T)] = v[c, i]
+            x_swap.write(pl.ds(FACE + (c * 4 + i) * T, T), v[c, 12 + i], v[c, i])
     sub = subs()
     a, b = swap0[pl.ds(Z_META, 8)], swap1[pl.ds(Z_META, 8)]
     a, b = low_in * jnp.where(even, b, a), high_in * jnp.where(even, a, b)
     row = jnp.where(sub == 0, a, jnp.where(sub == 1, own[pl.ds(Z_META, 8)], b))
-    for out, at in ((yup, Y_META), (ydown, Y_META), (xup, NUMBERS), (xdown, NUMBERS)):
-        out[pl.ds(at, 8)] = row
-
-
-def corner_message_kernel(low, high, elow, ehigh, xlow, xhigh, up, down):
-    del xlow, xhigh
-    sides = ((low, elow, C_LOW), (high, ehigh, C_HIGH))
-    for y, ((a, e, to), keep) in enumerate(zip(sides, inside("gy"))):
+    y_swap.write(pl.ds(Y_META, 8), row, row)
+    x_swap.write(pl.ds(NUMBERS, 8), row, row)
+
+
+def corner_message_kernel(y0, y1, e0, e1, from_x0, from_x1, x0, x1):
+    del from_x0, from_x1
+    x_swap = Swap("gx", (x0, x1))
+    places = zip(sides("gy", (y0, y1)), sides("gy", (e0, e1)), inside("gy"), (C_LOW, C_HIGH))
+    for y, (a, e, keep, to) in enumerate(places):
         for x in range(T):
             for at, value in ((0, a[pl.ds(Y_S0 + x * T, T)]), (256, e[pl.ds(Y_E0 + x * T, T)])):
                 value = keep * value
-                up[pl.ds(to + at + x * T, T)] = value
-                down[pl.ds(to + at + x * T, T)] = value
+                x_swap.write(pl.ds(to + at + x * T, T), value, value)
         for ref, start, place in ((a, Y_S1, C_A1), (e, Y_E1, C_E1)):
             for x in range(8):
-                down[pl.ds(place + x * T + 8 * y, 8)] = keep * ref[pl.ds(start + x * 8, 8)]
-                up[pl.ds(place + x * T + 8 * y, 8)] = keep * ref[pl.ds(start + (8 + x) * 8, 8)]
+                u, d = keep * ref[pl.ds(start + (8 + x) * 8, 8)], keep * ref[pl.ds(start + x * 8, 8)]
+                x_swap.write(pl.ds(place + x * T + 8 * y, 8), u, d)
         value = keep * e[pl.ds(Y_META, 8)]
-        up[pl.ds(C_META + 8 * y, 8)] = value
-        down[pl.ds(C_META + 8 * y, 8)] = value
+        x_swap.write(pl.ds(C_META + 8 * y, 8), value, value)
 
 
 def put(low, high, rows, upper, a, e):
@@ -203,13 +225,15 @@
     high[rows] = jnp.where(upper, a, e)
 
 
-def assemble_kernel(own_up, own_down, xlow, xhigh, ylow, yhigh, elow, ehigh, c_low, c_high, d_low, d_high):
+def assemble_kernel(own0, own1, x0, x1, y0, y1, e0, e1, c_low, c_high, d_low, d_high):
+    own_down, own_up = sides("gx", (own0, own1))
+    (xlow, xhigh), (ylow, yhigh), (elow, ehigh) = sides("gx", (x0, x1)), sides("gy", (y0, y1)), sides("gy", (e0, e1))
     (xl, xh), (yl, yh) = inside("gx"), inside("gy")
     upper, upper8 = lanes(T) >= 64, lanes(8) >= 64
 
     def first(x):
         at = pl.multiple_of(x * T, 8)
-        for ref, keep, dx in ((own_up, None, 16), (xlow, xl, 0), (xhigh, xh, 32)):
+        for ref, keep, dx in ((own0, None, 16), (xlow, xl, 0), (xhigh, xh, 32)):
             a, e = ref[pl.ds(A0 + at, T)], ref[pl.ds(E0 + at, T)]
             if keep is not None:
                 a, e = keep * a, keep * e
@@ -284,10 +308,13 @@
 
 
 def steps_kernel(
-    own, xlow, xhigh, ylow, yhigh, corner_low, corner_high, c_low_in, c_high_in, d_low_in, d_high_in,
-    up, down, numbers, c_low, c_high, d_low, d_high, r_low, r_high, meta, sem,
+    own, x0, x1, e0, e1, corner0, corner1, c_low_in, c_high_in, d_low_in, d_high_in,
+    out0, out1, numbers, c_low, c_high, d_low, d_high, r_low, r_high, meta, sem,
 ):
     (xl, xh), (yl, yh) = inside("gx"), inside("gy")
+    (xlow, xhigh), (ylow, yhigh) = sides("gx", (x0, x1)), sides("gy", (e0, e1))
+    corner_low, corner_high = sides("gx", (corner0, corner1))
+    y_swap = Swap("gy", (out0, out1))
     lane = lanes()
     upper = lane >= 64
     tiles = (
@@ -404,28 +431,30 @@
             a = jnp.where(wide_upper, high, low)
             e = roll(jnp.where(wide_upper, low, high), 32 * g)
             packed = e if g == 0 else jnp.where(quarter == g, e, packed)
-            down[pl.ds(pl.multiple_of(at * T, 8), T)] = a[0:16]
-            up[pl.ds(pl.multiple_of(at * T, 8), T)] = a[16:32]
-        down[pl.ds(pl.multiple_of(R_E + i * T, 8), T)] = packed[0:16]
-        up[pl.ds(pl.multiple_of(R_E + i * T, 8), T)] = packed[16:32]
+            y_swap.write(pl.ds(pl.multiple_of(at * T, 8), T), a[16:32], a[0:16])
+        y_swap.write(pl.ds(pl.multiple_of(R_E + i * T, 8), T), packed[16:32], packed[0:16])
 
     loop(8, pack, UN_PACK)
 
 
-def sum_y_kernel(own_up, own_down, low, high, up, down):
+def sum_y_kernel(own0, own1, y0, y1, x0, x1):
     low_in, high_in = inside("gy")
-    for h, out in ((0, down), (1, up)):
-        for start, planes in ((0, 16), (R_E, 4)):
-            for x in range(planes):
-                rows = pl.ds(start + (h * planes + x) * T, T)
-                out[pl.ds(start + x * 32, T)] = own_down[rows] + low_in * low[rows]
-                out[pl.ds(start + x * 32 + T, T)] = own_up[rows] + high_in * high[rows]
-
-
-def last_step_kernel(own_up, own_down, low, high, numbers, g, reg, result, a1, e1, acc, out, meta, sem, out_sem):
+    (own_down, own_up), (low, high) = sides("gy", (own0, own1)), sides("gy", (y0, y1))
+    x_swap = Swap("gx", (x0, x1))
+    for start, planes in ((0, 16), (R_E, 4)):
+        for x in range(planes):
+            rows = [pl.ds(start + (h * planes + x) * T, T) for h in range(2)]
+            lows = [own_down[r] + low_in * low[r] for r in rows]
+            highs = [own_up[r] + high_in * high[r] for r in rows]
+            x_swap.write(pl.ds(start + x * 32, T), lows[1], lows[0])
+            x_swap.write(pl.ds(start + x * 32 + T, T), highs[1], highs[0])
+
+
+def last_step_kernel(own0, own1, x0, x1, numbers, g, reg, result, a1, e1, acc, out, meta, sem, out_sem):
     copy = pltpu.make_async_copy(numbers, meta, sem)
     copy.start()
     low_in, high_in = inside("gx")
+    (own_down, own_up), (low, high) = sides("gx", (own0, own1)), sides("gx", (x0, x1))
     wide = lanes(32)
     valid = (wide < 16) | (wide >= 112)
     for h, (mine, other, keep) in enumerate(((own_down, low, low_in), (own_up, high, high_in))):
@@ -486,12 +515,13 @@
         done.wait()
 
 
-def laplace_kernel(v, swap0, swap1, ylow, yhigh, xlow, xhigh, out, w):
+def laplace_kernel(v, swap0, swap1, y0, y1, x0, x1, out, w):
+    (ylow, yhigh), (xlow, xhigh) = sides("gy", (y0, y1)), sides("gx", (x0, x1))
     lane = lanes(T)
     half = (lane & 4) == 0
     even = is_even("gz")
     (x_low, x_high), (y_low, y_high), (z_low, z_high) = inside("gx"), inside("gy"), inside("gz")
-    sides = [-REG_WEIGHT * t for t in LAPLACE_TAPS]
+    taps = [-REG_WEIGHT * t for t in LAPLACE_TAPS]
     for c in range(3):
         rows = pl.ds(Z_V + c * T, T)
         a, b = swap0[rows], swap1[rows]
@@ -512,12 +542,12 @@
         for x in range(T):
             here = v[c, x]
             edge = roll(faces, -8 * x)
-            total = 3.0 * sides[0] * here
+            total = 3.0 * taps[0] * here
             for k in range(1, 5):
                 near = roll(jnp.where(lane < k, edge, here), -k) + roll(jnp.where(lane >= L - k, edge, here), k)
                 near = near + w[4 + x - k, 8:24] + w[4 + x + k, 8:24]
                 near = near + w[4 + x, 8 - k : 24 - k] + w[4 + x, 8 + k : 24 + k]
-                total = total + sides[k] * near
+                total = total + taps[k] * near
             out[c, x] = total
 
 
@@ -540,13 +570,6 @@
     )(*args)
 
 
-def exchange(up, down, axis):
-    n = lax.axis_size(axis)
-    rise = [(i, (i + 1) % n) for i in range(n)]
-    fall = [(j, i) for i, j in rise]
-    return lax.ppermute(up, axis, rise), lax.ppermute(down, axis, fall)
-
-
 def last_call(args, vm, meta):
     shape = args[-1].shape
     scratch = [vm(32 * 32, L), vm(32 * 32, L), vm(48 * 56, L), vm(*shape)] + meta + [pltpu.SemaphoreType.DMA((2,))]
@@ -566,7 +589,7 @@
     vm = lambda *s: pltpu.VMEM(s, F32)
     shifts = [s.transpose(0, 1, 3, 2) for s in (shift_x, shift_y, shift_z)]
     inputs = [v, g, *shifts, fractions.transpose(0, 2, 3, 4, 1)]
-    v, s0, s1, first, second, yup, ydown = call(
+    v, s0, s1, z0, z1, *ys = call(
         sources_kernel,
         [pltpu.with_memory_space_constraint(a, pltpu.HBM) for a in inputs],
         [v.shape, tile, tile, (Z_ROWS, L), (Z_ROWS, L), (Y_ROWS, L), (Y_ROWS, L)],
@@ -575,32 +598,32 @@
         + [pltpu.SMEM((2, 2, 2, 1, 3), jnp.int32), pltpu.SemaphoreType.DMA((8,)), pltpu.SemaphoreType.DMA((4,))],
         hbm=range(6),
     )
-    swap0, swap1 = swap(first, second, "gz")
-    ylow, yhigh = exchange(yup, ydown, "gy")
-    yup, ydown, xup, xdown = call(
-        tile_messages_kernel, (s0, s1, v, first, swap0, swap1, ylow, yhigh), [(Y_EROWS, L)] * 2 + [(ROWS, L)] * 2
+    zs = swap(z0, z1, "gz")
+    from_y = swap(*ys, "gy")
+    *es, x0, x1 = call(
+        tile_messages_kernel, (s0, s1, v, z0, *zs, *from_y), [(Y_EROWS, L)] * 2 + [(ROWS, L)] * 2
     )
-    xlow, xhigh = exchange(xup, xdown, "gx")
-    elow, ehigh = exchange(yup, ydown, "gy")
-    up, down = call(corner_message_kernel, (ylow, yhigh, elow, ehigh, xlow, xhigh), [(C_ROWS, L)] * 2)
-    corner_low, corner_high = exchange(up, down, "gx")
+    from_x = swap(x0, x1, "gx")
+    from_e = swap(*es, "gy")
+    corners = call(corner_message_kernel, (*from_y, *from_e, *from_x), [(C_ROWS, L)] * 2)
+    from_corner = swap(*corners, "gx")
     fields = [(48 * 48, L)] * 2 + [(32 * 32, L)] * 2
-    filled = call(assemble_kernel, (xup, xdown, xlow, xhigh, ylow, yhigh, elow, ehigh), fields)
+    filled = call(assemble_kernel, (x0, x1, *from_x, *from_y, *from_e), fields)
     meta = [pltpu.SMEM((72, L), F32), pltpu.SemaphoreType.DMA]
-    up, down, numbers, *_ = call(
+    sum0, sum1, numbers, *_ = call(
         steps_kernel,
-        (xup, xlow, xhigh, elow, ehigh, corner_low, corner_high, *filled),
+        (x0, *from_x, *from_e, *from_corner, *filled),
         [(R_ROWS, L), (R_ROWS, L), (72, L)] + fields,
         scratch=[vm(32 * 40, L), vm(32 * 40, L)] + meta,
         alias={7: 3, 8: 4, 9: 5, 10: 6},
     )
     (reg,) = call(
-        laplace_kernel, (v, swap0, swap1, ylow, yhigh, xlow, xhigh), [v.shape], scratch=[vm(24, 32, L)], cost=4000000
+        laplace_kernel, (v, *zs, *from_y, *from_x), [v.shape], scratch=[vm(24, 32, L)], cost=4000000
     )
-    low, high = exchange(up, down, "gy")
-    up, down = call(sum_y_kernel, (up, down, low, high), [(R_ROWS, L)] * 2)
-    low, high = exchange(up, down, "gx")
-    (out,) = last_call((up, down, low, high, numbers, g, reg), vm, meta)
+    from_y = swap(sum0, sum1, "gy")
+    sums = call(sum_y_kernel, (sum0, sum1, *from_y), [(R_ROWS, L)] * 2)
+    from_x = swap(*sums, "gx")
+    (out,) = last_call((*sums, *from_x, numbers, g, reg), vm, meta)
     return out
 
 

time: 65.9 us -> 72.6 us (1.10)
  the two profiles are of different devices: /device:TPU:95 before, /device:TPU:107 now
where the time goes in v8:
time: 72.6 us; the launch traced here: 72.3 us
  waiting for transfers between devices  30.7 us (42%)
  starting transfers between devices  26.6 us (37%)
  Pallas kernels  14.7 us (20%)
    ppermute x7, starting transfers between devices, swap(): lax.ppermute(second, axis, others)  23.8 us
    ppermute x7, waiting for transfers between devices, swap(): lax.ppermute(second, axis, others)  17.7 us
    pallas_call x8, Pallas kernels, call(): pl.pallas_call(kernel, out_shape=shapes, in_specs=specs, out_specs=[out_s...  14.7 us
    ppermute x7, waiting for transfers between devices, swap(): lax.ppermute(first, axis, pairs)  13 us
    ppermute x7, starting transfers between devices, swap(): lax.ppermute(first, axis, pairs)  2.83 us
  transfers between devices with their start and end apart: 14, of which 8 were waited for; matrix products, arithmetic and copies ran while one was open for 0% of the time, Pallas kernels for 5%

profile of v8, /device:TPU:107, one launch (start us, length us, event | category | flops | bytes accessed | tf_op | source)
XLA Modules:
  0.0 72.3 jit_solution(16125546664256524545)
XLA Ops:
  0.0 1.6 %shard_map.64 = (f32[3,16,16,128]{3,2,1,0:T(8,128)S(1)}, f32[16,16,128]{2,1,0:T(8,128)S(1)}, f32[16,16,128]{2,1,0:T(8,128)S(1)}, f32[312,128]{1,0:T(8,128)S(1)},...) custom-call(f32[3,16,16,128]{3,2,1,0:T(8,128)} %v_hbm.1, bf16[2,3,16,16,128]{4,3,2,1,0:T(8,128)(2,1)} %g.1, ...), custom_call_target="tpu_custom_call" | custom-call | flops 20000 | bytes 20000 | tf_op jit(solution)/shard_map/pallas_call | solution.py:561
  1.6 0.3 collective-permute-start.2
  1.9 4.0 %collective-permute-start.3 = (f32[576,128]{1,0:T(8,128)S(1)}, f32[576,128]{1,0:T(8,128)S(1)}, u32[]{:S(2)}, u32[]{:S(2)}) collective-permute-start(f32[576,128]{1,0:T(8,128)S(1)} %get-tuple-element.33), channel_id=1, source_target_pairs={{0,0},{8,16},{16,8},{24,24},{1,1},{9,17},{17,9},{25,25},{2,2},{10,... | collective-permute-start | bytes 884744 | tf_op jit(solution)/shard_map/ppermute | solution.py:583
  5.9 4.8 %collective-permute-start.1 = (f32[312,128]{1,0:T(8,128)S(1)}, f32[312,128]{1,0:T(8,128)S(1)}, u32[]{:S(2)}, u32[]{:S(2)}) collective-permute-start(f32[312,128]{1,0:T(8,128)S(1)} %get-tuple-element.31), channel_id=1, source_target_pairs={{0,0},{1,2},{2,1},{3,4},{4,3},{5,6},{6,5},{7,7},{8,8},{9,10},{10,9... | collective-permute-start | bytes 479240 | tf_op jit(solution)/shard_map/ppermute | solution.py:583
  10.7 0.1 collective-permute-start
  10.8 3.0 %collective-permute-done.1.swap1 = f32[312,128]{1,0:T(8,128)S(1)} collective-permute-done((f32[312,128]{1,0:T(8,128)S(1)}, f32[312,128]{1,0:T(8,128)S(1)}, u32[]{:S(2)}, u32[]{:S(2)}) %collective-permute-start.1) | collective-permute-done | bytes 159776 | tf_op jit(solution)/shard_map/ppermute | solution.py:583
  13.8 1.4 %collective-permute-done.swap0 = f32[312,128]{1,0:T(8,128)S(1)} collective-permute-done((f32[312,128]{1,0:T(8,128)S(1)}, f32[312,128]{1,0:T(8,128)S(1)}, u32[]{:S(2)}, u32[]{:S(2)}) %collective-permute-start) | collective-permute-done | bytes 159776 | tf_op jit(solution)/shard_map/ppermute | solution.py:583
  15.2 0.0 collective-permute-done.2.ylow.y0
  15.2 0.0 collective-permute-done.3.yhigh.y1
  15.2 0.1 shard_map.65
  15.3 5.4 %collective-permute-start.5 = (f32[968,128]{1,0:T(8,128)S(1)}, f32[968,128]{1,0:T(8,128)S(1)}, u32[]{:S(2)}, u32[]{:S(2)}) collective-permute-start(f32[968,128]{1,0:T(8,128)S(1)} %get-tuple-element.35.own1), channel_id=1, source_target_pairs={{0,0},{32,64},{64,32},{96,128},{128,96},{160,192},{192,160},{224,2... | collective-permute-start | bytes 1486856 | tf_op jit(solution)/shard_map/ppermute | solution.py:583
  20.7 0.1 collective-permute-start.4
  20.8 0.1 collective-permute-start.6
  20.9 1.9 %collective-permute-start.7 = (f32[392,128]{1,0:T(8,128)S(1)}, f32[392,128]{1,0:T(8,128)S(1)}, u32[]{:S(2)}, u32[]{:S(2)}) collective-permute-start(f32[392,128]{1,0:T(8,128)S(1)} %get-tuple-element.37), channel_id=1, source_target_pairs={{0,0},{8,16},{16,8},{24,24},{1,1},{9,17},{17,9},{25,25},{2,2},{10,... | collective-permute-start | bytes 602120 | tf_op jit(solution)/shard_map/ppermute | solution.py:583
  22.8 4.2 %collective-permute-done.6.e0 = f32[392,128]{1,0:T(8,128)S(1)} collective-permute-done((f32[392,128]{1,0:T(8,128)S(1)}, f32[392,128]{1,0:T(8,128)S(1)}, u32[]{:S(2)}, u32[]{:S(2)}) %collective-permute-start.6) | collective-permute-done | bytes 200736 | tf_op jit(solution)/shard_map/ppermute | solution.py:583
  27.0 1.9 %collective-permute-done.7.e1 = f32[392,128]{1,0:T(8,128)S(1)} collective-permute-done((f32[392,128]{1,0:T(8,128)S(1)}, f32[392,128]{1,0:T(8,128)S(1)}, u32[]{:S(2)}, u32[]{:S(2)}) %collective-permute-start.7) | collective-permute-done | bytes 200736 | tf_op jit(solution)/shard_map/ppermute | solution.py:583
  29.0 0.0 collective-permute-done.5.from_x1.x1
  29.0 0.0 collective-permute-done.4.from_x0.x0
  29.0 0.1 shard_map.66
  29.1 1.3 %collective-permute-start.8 = (f32[1296,128]{1,0:T(8,128)S(1)}, f32[1296,128]{1,0:T(8,128)S(1)}, u32[]{:S(2)}, u32[]{:S(2)}) collective-permute-start(f32[1296,128]{1,0:T(8,128)S(1)} %get-tuple-element.38), channel_id=1, source_target_pairs={{0,32},{32,0},{64,96},{96,64},{128,160},{160,128},{192,224},{224,1... | collective-permute-start | bytes 1990664 | tf_op jit(solution)/shard_map/ppermute | solution.py:583
  30.4 2.7 %collective-permute-start.9 = (f32[1296,128]{1,0:T(8,128)S(1)}, f32[1296,128]{1,0:T(8,128)S(1)}, u32[]{:S(2)}, u32[]{:S(2)}) collective-permute-start(f32[1296,128]{1,0:T(8,128)S(1)} %get-tuple-element.39), channel_id=1, source_target_pairs={{0,0},{32,64},{64,32},{96,128},{128,96},{160,192},{192,160},{224,2... | collective-permute-start | bytes 1990664 | tf_op jit(solution)/shard_map/ppermute | solution.py:583
  33.1 0.3 shard_map.67
  33.4 0.0 collective-permute-done.8.corner0
  33.4 9.0 %collective-permute-done.9.corner1 = f32[1296,128]{1,0:T(8,128)S(1)} collective-permute-done((f32[1296,128]{1,0:T(8,128)S(1)}, f32[1296,128]{1,0:T(8,128)S(1)}, u32[]{:S(2)}, u32[]{:S(2)}) %collective-permute-start.9) | collective-permute-done | bytes 663584 | tf_op jit(solution)/shard_map/ppermute | solution.py:583
  42.4 4.5 %shard_map.68 = (f32[640,128]{1,0:T(8,128)S(1)}, f32[640,128]{1,0:T(8,128)S(1)}, f32[72,128]{1,0:T(8,128)S(1)}, f32[2304,128]{1,0:T(8,128)S(1)}, f32[2304,128]{1...) custom-call(f32[968,128]{1,0:T(8,128)S(1)} %get-tuple-element.34.own, ...), custom_call_target="tpu_custom_call", output_to_operand_aliasing={{3}: (7, {}), {4}: (8, {}), {5}: (9, {}), {6}: (10, {})} | custom-call | flops 20000 | bytes 20000 | tf_op jit(solution)/shard_map/pallas_call | solution.py:561
  46.9 0.1 collective-permute-start.10
  47.0 1.9 %collective-permute-start.11 = (f32[640,128]{1,0:T(8,128)S(1)}, f32[640,128]{1,0:T(8,128)S(1)}, u32[]{:S(2)}, u32[]{:S(2)}) collective-permute-start(f32[640,128]{1,0:T(8,128)S(1)} %get-tuple-element.45.own1), channel_id=1, source_target_pairs={{0,0},{8,16},{16,8},{24,24},{1,1},{9,17},{17,9},{25,25},{2,2},{10,... | collective-permute-start | bytes 983048 | tf_op jit(solution)/shard_map/ppermute | solution.py:583
  48.9 7.4 %collective-permute-done.10.y0 = f32[640,128]{1,0:T(8,128)S(1)} collective-permute-done((f32[640,128]{1,0:T(8,128)S(1)}, f32[640,128]{1,0:T(8,128)S(1)}, u32[]{:S(2)}, u32[]{:S(2)}) %collective-permute-start.10) | collective-permute-done | bytes 327712 | tf_op jit(solution)/shard_map/ppermute | solution.py:583
  56.3 1.9 %collective-permute-done.11.y1 = f32[640,128]{1,0:T(8,128)S(1)} collective-permute-done((f32[640,128]{1,0:T(8,128)S(1)}, f32[640,128]{1,0:T(8,128)S(1)}, u32[]{:S(2)}, u32[]{:S(2)}) %collective-permute-start.11) | collective-permute-done | bytes 327712 | tf_op jit(solution)/shard_map/ppermute | solution.py:583
  58.2 0.1 shard_map.69
  58.3 0.9 %collective-permute-start.12 = (f32[640,128]{1,0:T(8,128)S(1)}, f32[640,128]{1,0:T(8,128)S(1)}, u32[]{:S(2)}, u32[]{:S(2)}) collective-permute-start(f32[640,128]{1,0:T(8,128)S(1)} %get-tuple-element.46.own0), channel_id=1, source_target_pairs={{0,32},{32,0},{64,96},{96,64},{128,160},{160,128},{192,224},{224,1... | collective-permute-start | bytes 983048 | tf_op jit(solution)/shard_map/ppermute | solution.py:583
  59.2 0.0 copy-start
  59.2 3.0 %collective-permute-start.13 = (f32[640,128]{1,0:T(8,128)S(1)}, f32[640,128]{1,0:T(8,128)S(1)}, u32[]{:S(2)}, u32[]{:S(2)}) collective-permute-start(f32[640,128]{1,0:T(8,128)S(1)} %get-tuple-element.47.own1), channel_id=1, source_target_pairs={{0,0},{32,64},{64,32},{96,128},{128,96},{160,192},{192,160},{224,2... | collective-permute-start | bytes 983048 | tf_op jit(solution)/shard_map/ppermute | solution.py:583
  62.2 3.6 %shard_map.70.reg = f32[3,16,16,128]{3,2,1,0:T(8,128)S(1)} custom-call(f32[3,16,16,128]{3,2,1,0:T(8,128)S(1)} %get-tuple-element.29.v, f32[312,128]{1,0:T(8,128)S(1)} %collective-permute-done.swap0, f32[312,128]{1,0:T(8,128)S(1)} %collective-permute-done.1.swap1, f32[576,128]{1,0:T(8,128)S(1)} %collective-permute-done.2.ylow.y0, ...), custom_call_target="tpu_custom_call" | custom-call | flops 4000000 | bytes 4000000 | tf_op jit(solution)/shard_map/pallas_call | solution.py:561
  65.8 0.0 collective-permute-done.12.x0
  65.8 1.9 %collective-permute-done.13.x1 = f32[640,128]{1,0:T(8,128)S(1)} collective-permute-done((f32[640,128]{1,0:T(8,128)S(1)}, f32[640,128]{1,0:T(8,128)S(1)}, u32[]{:S(2)}, u32[]{:S(2)}) %collective-permute-start.13) | collective-permute-done | bytes 327712 | tf_op jit(solution)/shard_map/ppermute | solution.py:583
  67.7 0.0 copy-done
  67.7 4.4 %shard_map.71 = f32[3,16,16,128]{3,2,1,0:T(8,128)} custom-call(f32[640,128]{1,0:T(8,128)S(1)} %get-tuple-element.46.own0, f32[640,128]{1,0:T(8,128)S(1)} %get-tuple-element.47.own1, f32[640,128]{1,0:T(8,128)S(1)} %collective-permute-done.12.x0, f32[640,128]{1,0:T(8,128)S(1)} %collective-permute-done.13.x1, f32[72,128]{1,0:T(8,128)S(1)} %get-tuple-element.48.numbers, ...), custom_call_target="tpu_custom_call" | custom-call | flops 20000 | bytes 20000 | tf_op jit(solution)/shard_map/pallas_call | solution.py:561
Async XLA Ops:
  1.6 13.6 %collective-permute-start.2 = (f32[576,128]{1,0:T(8,128)S(1)}, f32[576,128]{1,0:T(8,128)S(1)}, u32[]{:S(2)}, u32[]{:S(2)}) collective-permute-start(f32[576,128]{1,0:T(8,128)S(1)} %get-tuple-element.32), channel_id=1, source_target_pairs={{0,8},{8,0},{16,24},{24,16},{1,9},{9,1},{17,25},{25,17},{2,10},{10... | collective-permute-start | bytes 884744 | tf_op jit(solution)/shard_map/ppermute | solution.py:583
  1.9 13.3 %collective-permute-start.3 = (f32[576,128]{1,0:T(8,128)S(1)}, f32[576,128]{1,0:T(8,128)S(1)}, u32[]{:S(2)}, u32[]{:S(2)}) collective-permute-start(f32[576,128]{1,0:T(8,128)S(1)} %get-tuple-element.33), channel_id=1, source_target_pairs={{0,0},{8,16},{16,8},{24,24},{1,1},{9,17},{17,9},{25,25},{2,2},{10,... | collective-permute-start | bytes 884744 | tf_op jit(solution)/shard_map/ppermute | solution.py:583
  5.9 7.8 %collective-permute-start.1 = (f32[312,128]{1,0:T(8,128)S(1)}, f32[312,128]{1,0:T(8,128)S(1)}, u32[]{:S(2)}, u32[]{:S(2)}) collective-permute-start(f32[312,128]{1,0:T(8,128)S(1)} %get-tuple-element.31), channel_id=1, source_target_pairs={{0,0},{1,2},{2,1},{3,4},{4,3},{5,6},{6,5},{7,7},{8,8},{9,10},{10,9... | collective-permute-start | bytes 479240 | tf_op jit(solution)/shard_map/ppermute | solution.py:583
  10.7 4.5 %collective-permute-start = (f32[312,128]{1,0:T(8,128)S(1)}, f32[312,128]{1,0:T(8,128)S(1)}, u32[]{:S(2)}, u32[]{:S(2)}) collective-permute-start(f32[312,128]{1,0:T(8,128)S(1)} %get-tuple-element.30.own), channel_id=1, source_target_pairs={{0,1},{1,0},{2,3},{3,2},{4,5},{5,4},{6,7},{7,6},{8,9},{9,8},{10,11... | collective-permute-start | bytes 479240 | tf_op jit(solution)/shard_map/ppermute | solution.py:583
  15.3 13.7 %collective-permute-start.5 = (f32[968,128]{1,0:T(8,128)S(1)}, f32[968,128]{1,0:T(8,128)S(1)}, u32[]{:S(2)}, u32[]{:S(2)}) collective-permute-start(f32[968,128]{1,0:T(8,128)S(1)} %get-tuple-element.35.own1), channel_id=1, source_target_pairs={{0,0},{32,64},{64,32},{96,128},{128,96},{160,192},{192,160},{224,2... | collective-permute-start | bytes 1486856 | tf_op jit(solution)/shard_map/ppermute | solution.py:583
  20.7 8.3 %collective-permute-start.4 = (f32[968,128]{1,0:T(8,128)S(1)}, f32[968,128]{1,0:T(8,128)S(1)}, u32[]{:S(2)}, u32[]{:S(2)}) collective-permute-start(f32[968,128]{1,0:T(8,128)S(1)} %get-tuple-element.34.own0.own), channel_id=1, source_target_pairs={{0,32},{32,0},{64,96},{96,64},{128,160},{160,128},{192,224},{224,1... | collective-permute-start | bytes 1486856 | tf_op jit(solution)/shard_map/ppermute | solution.py:583
  20.8 6.2 %collective-permute-start.6 = (f32[392,128]{1,0:T(8,128)S(1)}, f32[392,128]{1,0:T(8,128)S(1)}, u32[]{:S(2)}, u32[]{:S(2)}) collective-permute-start(f32[392,128]{1,0:T(8,128)S(1)} %get-tuple-element.36), channel_id=1, source_target_pairs={{0,8},{8,0},{16,24},{24,16},{1,9},{9,1},{17,25},{25,17},{2,10},{10... | collective-permute-start | bytes 602120 | tf_op jit(solution)/shard_map/ppermute | solution.py:583
  20.9 8.1 %collective-permute-start.7 = (f32[392,128]{1,0:T(8,128)S(1)}, f32[392,128]{1,0:T(8,128)S(1)}, u32[]{:S(2)}, u32[]{:S(2)}) collective-permute-start(f32[392,128]{1,0:T(8,128)S(1)} %get-tuple-element.37), channel_id=1, source_target_pairs={{0,0},{8,16},{16,8},{24,24},{1,1},{9,17},{17,9},{25,25},{2,2},{10,... | collective-permute-start | bytes 602120 | tf_op jit(solution)/shard_map/ppermute | solution.py:583
  29.1 4.3 %collective-permute-start.8 = (f32[1296,128]{1,0:T(8,128)S(1)}, f32[1296,128]{1,0:T(8,128)S(1)}, u32[]{:S(2)}, u32[]{:S(2)}) collective-permute-start(f32[1296,128]{1,0:T(8,128)S(1)} %get-tuple-element.38), channel_id=1, source_target_pairs={{0,32},{32,0},{64,96},{96,64},{128,160},{160,128},{192,224},{224,1... | collective-permute-start | bytes 1990664 | tf_op jit(solution)/shard_map/ppermute | solution.py:583
  30.4 12.0 %collective-permute-start.9 = (f32[1296,128]{1,0:T(8,128)S(1)}, f32[1296,128]{1,0:T(8,128)S(1)}, u32[]{:S(2)}, u32[]{:S(2)}) collective-permute-start(f32[1296,128]{1,0:T(8,128)S(1)} %get-tuple-element.39), channel_id=1, source_target_pairs={{0,0},{32,64},{64,32},{96,128},{128,96},{160,192},{192,160},{224,2... | collective-permute-start | bytes 1990664 | tf_op jit(solution)/shard_map/ppermute | solution.py:583
  46.9 9.4 %collective-permute-start.10 = (f32[640,128]{1,0:T(8,128)S(1)}, f32[640,128]{1,0:T(8,128)S(1)}, u32[]{:S(2)}, u32[]{:S(2)}) collective-permute-start(f32[640,128]{1,0:T(8,128)S(1)} %get-tuple-element.44.own0), channel_id=1, source_target_pairs={{0,8},{8,0},{16,24},{24,16},{1,9},{9,1},{17,25},{25,17},{2,10},{10... | collective-permute-start | bytes 983048 | tf_op jit(solution)/shard_map/ppermute | solution.py:583
  47.0 11.2 %collective-permute-start.11 = (f32[640,128]{1,0:T(8,128)S(1)}, f32[640,128]{1,0:T(8,128)S(1)}, u32[]{:S(2)}, u32[]{:S(2)}) collective-permute-start(f32[640,128]{1,0:T(8,128)S(1)} %get-tuple-element.45.own1), channel_id=1, source_target_pairs={{0,0},{8,16},{16,8},{24,24},{1,1},{9,17},{17,9},{25,25},{2,2},{10,... | collective-permute-start | bytes 983048 | tf_op jit(solution)/shard_map/ppermute | solution.py:583
  58.3 7.5 %collective-permute-start.12 = (f32[640,128]{1,0:T(8,128)S(1)}, f32[640,128]{1,0:T(8,128)S(1)}, u32[]{:S(2)}, u32[]{:S(2)}) collective-permute-start(f32[640,128]{1,0:T(8,128)S(1)} %get-tuple-element.46.own0), channel_id=1, source_target_pairs={{0,32},{32,0},{64,96},{96,64},{128,160},{160,128},{192,224},{224,1... | collective-permute-start | bytes 983048 | tf_op jit(solution)/shard_map/ppermute | solution.py:583
  59.2 8.5 %copy-start = (bf16[2,3,16,16,128]{4,3,2,1,0:T(8,128)(2,1)S(1)}, bf16[2,3,16,16,128]{4,3,2,1,0:T(8,128)(2,1)}, u32[]{:S(2)}) copy-start(bf16[2,3,16,16,128]{4,3,2,1,0:T(8,128)(2,1)} %g.1) | copy-start | bytes 1179652
  59.2 8.5 %collective-permute-start.13 = (f32[640,128]{1,0:T(8,128)S(1)}, f32[640,128]{1,0:T(8,128)S(1)}, u32[]{:S(2)}, u32[]{:S(2)}) collective-permute-start(f32[640,128]{1,0:T(8,128)S(1)} %get-tuple-element.47.own1), channel_id=1, source_target_pairs={{0,0},{32,64},{64,32},{96,128},{128,96},{160,192},{192,160},{224,2... | collective-permute-start | bytes 983048 | tf_op jit(solution)/shard_map/ppermute | solution.py:583

commit v9 on v7

--- a/solution.py
+++ b/solution.py
@@ -395,50 +395,50 @@
     wide_upper = wide >= 64
     quarter = ((wide + 16) & 127) // 32
 
-    def pack(i):
-        packed = None
-        for g in range(4):
-            at = 16 * (i // 4) + 4 * g + i % 4
-            rows = pl.ds(pl.multiple_of(at * 40, 8), 32)
-            low, high = r_low[rows], r_high[rows]
-            a = jnp.where(wide_upper, high, low)
-            e = roll(jnp.where(wide_upper, low, high), 32 * g)
-            packed = e if g == 0 else jnp.where(quarter == g, e, packed)
-            down[pl.ds(pl.multiple_of(at * T, 8), T)] = a[0:16]
-            up[pl.ds(pl.multiple_of(at * T, 8), T)] = a[16:32]
-        down[pl.ds(pl.multiple_of(R_E + i * T, 8), T)] = packed[0:16]
-        up[pl.ds(pl.multiple_of(R_E + i * T, 8), T)] = packed[16:32]
-
-    loop(8, pack, UN_PACK)
-
-
-def sum_y_kernel(own_up, own_down, low, high, up, down):
-    low_in, high_in = inside("gy")
     for h, out in ((0, down), (1, up)):
+
+        def pack(x, h=h, out=out):
+            packed = None
+            for g in range(4):
+                rows = pl.ds(pl.multiple_of((16 * h + 4 * g + x) * 40, 8), 32)
+                low, high = r_low[rows], r_high[rows]
+                e = roll(jnp.where(wide_upper, low, high), 32 * g)
+                packed = e if g == 0 else jnp.where(quarter == g, e, packed)
+                out[pl.ds(pl.multiple_of((4 * g + x) * 32, 8), 32)] = jnp.where(wide_upper, high, low)
+            out[pl.ds(pl.multiple_of(R_E + x * 32, 8), 32)] = packed
+
+        loop(4, pack, UN_PACK)
+
+
+def sum_x_kernel(own_up, own_down, low, high, up, down):
+    low_in, high_in = inside("gx")
+    for h, (mine, other, keep) in enumerate(((own_down, low, low_in), (own_up, high, high_in))):
         for start, planes in ((0, 16), (R_E, 4)):
             for x in range(planes):
+                value = mine[pl.ds(start + x * 32, 32)] + keep * other[pl.ds(start + x * 32, 32)]
                 rows = pl.ds(start + (h * planes + x) * T, T)
-                out[pl.ds(start + x * 32, T)] = own_down[rows] + low_in * low[rows]
-                out[pl.ds(start + x * 32 + T, T)] = own_up[rows] + high_in * high[rows]
+                down[rows] = value[0:16]
+                up[rows] = value[16:32]
 
 
 def last_step_kernel(own_up, own_down, low, high, numbers, g, reg, result, a1, e1, acc, out, meta, sem, out_sem):
     copy = pltpu.make_async_copy(numbers, meta, sem)
     copy.start()
-    low_in, high_in = inside("gx")
-    wide = lanes(32)
+    low_in, high_in = inside("gy")
+    wide = lanes(T)
     valid = (wide < 16) | (wide >= 112)
-    for h, (mine, other, keep) in enumerate(((own_down, low, low_in), (own_up, high, high_in))):
-
-        def unpack(x, h=h, mine=mine, other=other, keep=keep):
-            rows = pl.ds(pl.multiple_of(R_E + x * 32, 8), 32)
+
+    def unpack(i):
+        for mine, other, keep, y in ((own_down, low, low_in, 0), (own_up, high, high_in, T)):
+            rows = pl.ds(pl.multiple_of(R_E + i * T, 8), T)
             packed = mine[rows] + keep * other[rows]
             for q in range(4):
-                at = pl.multiple_of((4 * q + x) * 32, 8)
-                e1[pl.ds(512 * h + at, 32)] = jnp.where(valid, roll(packed, -32 * q), 0.0)
-                a1[pl.ds(512 * h + at, 32)] = mine[pl.ds(at, 32)] + keep * other[pl.ds(at, 32)]
-
-        loop(4, unpack, UN_UNPACK)
+                x = 16 * (i // 4) + 4 * q + i % 4
+                rows, to = pl.ds(pl.multiple_of(x * T, 8), T), pl.ds(pl.multiple_of(x * 32 + y, 8), T)
+                e1[to] = jnp.where(valid, roll(packed, -32 * q), 0.0)
+                a1[to] = mine[rows] + keep * other[rows]
+
+    loop(8, unpack, 2 * UN_UNPACK)
 
     def clear(i):
         acc[pl.ds(pl.multiple_of(i * 168, 8), 168)] = jnp.zeros((168, L), F32)
@@ -597,9 +597,9 @@
     (reg,) = call(
         laplace_kernel, (v, swap0, swap1, ylow, yhigh, xlow, xhigh), [v.shape], scratch=[vm(24, 32, L)], cost=4000000
     )
+    low, high = exchange(up, down, "gx")
+    up, down = call(sum_x_kernel, (up, down, low, high), [(R_ROWS, L)] * 2)
     low, high = exchange(up, down, "gy")
-    up, down = call(sum_y_kernel, (up, down, low, high), [(R_ROWS, L)] * 2)
-    low, high = exchange(up, down, "gx")
     (out,) = last_call((up, down, low, high, numbers, g, reg), vm, meta)
     return out
 

time: 65.9 us -> 64.8 us (0.983)
  the two profiles are of different devices: /device:TPU:95 before, /device:TPU:88 now
where the time goes in v9:
time: 64.8 us; the launch traced here: 64.6 us
  waiting for transfers between devices  29.7 us (46%)
  starting transfers between devices  19.7 us (30%)
  Pallas kernels  15 us (23%)
    ppermute x12, waiting for transfers between devices, exchange(): return (lax.ppermute(up, axis, rise), lax.ppermute(down, axis, fall))  26.4 us
    pallas_call x8, Pallas kernels, call(): pl.pallas_call(kernel, out_shape=shapes, in_specs=specs, out_specs=[out_s...  15 us
    ppermute x12, starting transfers between devices, exchange(): return (lax.ppermute(up, axis, rise), lax.ppermute(down, axis, fall))  12.7 us
    ppermute x1, starting transfers between devices, swap(): lax.ppermute(first, axis, pairs)  5.02 us
    ppermute x1, waiting for transfers between devices, swap(): lax.ppermute(first, axis, pairs)  3.13 us
    ppermute x1, starting transfers between devices, swap(): lax.ppermute(second, axis, others)  2 us
  transfers between devices with their start and end apart: 14, of which 8 were waited for; matrix products, arithmetic and copies ran while one was open for 0% of the time, Pallas kernels for 6%

profile of v9, /device:TPU:88, one launch (start us, length us, event | category | flops | bytes accessed | tf_op | source)
XLA Modules:
  0.0 64.6 jit_solution(2329054159016962147)
XLA Ops:
  0.0 1.6 %shard_map.64 = (f32[3,16,16,128]{3,2,1,0:T(8,128)S(1)}, f32[16,16,128]{2,1,0:T(8,128)S(1)}, f32[16,16,128]{2,1,0:T(8,128)S(1)}, f32[312,128]{1,0:T(8,128)S(1)},...) custom-call(f32[3,16,16,128]{3,2,1,0:T(8,128)} %v_hbm.1, bf16[2,3,16,16,128]{4,3,2,1,0:T(8,128)(2,1)} %g.1, ...), custom_call_target="tpu_custom_call" | custom-call | flops 20000 | bytes 20000 | tf_op jit(solution)/shard_map/pallas_call | solution.py:531
  1.6 0.3 collective-permute-start.2
  1.9 1.8 %collective-permute-start.3 = (f32[576,128]{1,0:T(8,128)S(1)}, f32[576,128]{1,0:T(8,128)S(1)}, u32[]{:S(2)}, u32[]{:S(2)}) collective-permute-start(f32[576,128]{1,0:T(8,128)S(1)} %get-tuple-element.33), channel_id=1, source_target_pairs={{8,0},{16,8},{24,16},{0,24},{9,1},{17,9},{25,17},{1,25},{10,2},{18... | collective-permute-start | bytes 884744 | tf_op jit(solution)/shard_map/ppermute | solution.py:547
  3.7 2.0 %collective-permute-start.1 = (f32[312,128]{1,0:T(8,128)S(1)}, f32[312,128]{1,0:T(8,128)S(1)}, u32[]{:S(2)}, u32[]{:S(2)}) collective-permute-start(f32[312,128]{1,0:T(8,128)S(1)} %get-tuple-element.31), channel_id=1, source_target_pairs={{0,0},{1,2},{2,1},{3,4},{4,3},{5,6},{6,5},{7,7},{8,8},{9,10},{10,9... | collective-permute-start | bytes 479240 | tf_op jit(solution)/shard_map/ppermute | solution.py:560
  5.7 5.0 %collective-permute-start = (f32[312,128]{1,0:T(8,128)S(1)}, f32[312,128]{1,0:T(8,128)S(1)}, u32[]{:S(2)}, u32[]{:S(2)}) collective-permute-start(f32[312,128]{1,0:T(8,128)S(1)} %get-tuple-element.30.own), channel_id=1, source_target_pairs={{0,1},{1,0},{2,3},{3,2},{4,5},{5,4},{6,7},{7,6},{8,9},{9,8},{10,11... | collective-permute-start | bytes 479240 | tf_op jit(solution)/shard_map/ppermute | solution.py:560
  10.8 0.1 collective-permute-done.1.swap1
  10.9 3.1 %collective-permute-done.swap0 = f32[312,128]{1,0:T(8,128)S(1)} collective-permute-done((f32[312,128]{1,0:T(8,128)S(1)}, f32[312,128]{1,0:T(8,128)S(1)}, u32[]{:S(2)}, u32[]{:S(2)}) %collective-permute-start) | collective-permute-done | bytes 159776 | tf_op jit(solution)/shard_map/ppermute | solution.py:560
  14.0 0.0 collective-permute-done.2.ylow.low
  14.0 0.0 collective-permute-done.3.yhigh.high
  14.0 0.1 shard_map.65
  14.2 0.5 collective-permute-start.5
  14.6 0.0 collective-permute-start.4
  14.7 1.9 %collective-permute-start.6 = (f32[392,128]{1,0:T(8,128)S(1)}, f32[392,128]{1,0:T(8,128)S(1)}, u32[]{:S(2)}, u32[]{:S(2)}) collective-permute-start(f32[392,128]{1,0:T(8,128)S(1)} %get-tuple-element.36), channel_id=1, source_target_pairs={{0,8},{8,16},{16,24},{24,0},{1,9},{9,17},{17,25},{25,1},{2,10},{10... | collective-permute-start | bytes 602120 | tf_op jit(solution)/shard_map/ppermute | solution.py:547
  16.6 0.1 collective-permute-start.7
  16.7 5.7 %collective-permute-done.6.elow.ylow = f32[392,128]{1,0:T(8,128)S(1)} collective-permute-done((f32[392,128]{1,0:T(8,128)S(1)}, f32[392,128]{1,0:T(8,128)S(1)}, u32[]{:S(2)}, u32[]{:S(2)}) %collective-permute-start.6) | collective-permute-done | bytes 200736 | tf_op jit(solution)/shard_map/ppermute | solution.py:547
  22.4 2.8 %collective-permute-done.7.ehigh.yhigh = f32[392,128]{1,0:T(8,128)S(1)} collective-permute-done((f32[392,128]{1,0:T(8,128)S(1)}, f32[392,128]{1,0:T(8,128)S(1)}, u32[]{:S(2)}, u32[]{:S(2)}) %collective-permute-start.7) | collective-permute-done | bytes 200736 | tf_op jit(solution)/shard_map/ppermute | solution.py:547
  25.2 0.0 collective-permute-done.5.xhigh
  25.2 0.0 collective-permute-done.4.xlow
  25.2 0.1 shard_map.66
  25.3 0.0 collective-permute-start.8
  25.3 2.9 %collective-permute-start.9 = (f32[1296,128]{1,0:T(8,128)S(1)}, f32[1296,128]{1,0:T(8,128)S(1)}, u32[]{:S(2)}, u32[]{:S(2)}) collective-permute-start(f32[1296,128]{1,0:T(8,128)S(1)} %get-tuple-element.39), channel_id=1, source_target_pairs={{32,0},{64,32},{96,64},{128,96},{160,128},{192,160},{224,192},{0,2... | collective-permute-start | bytes 1990664 | tf_op jit(solution)/shard_map/ppermute | solution.py:547
  28.3 0.2 shard_map.67
  28.5 8.2 %collective-permute-done.8.corner_low = f32[1296,128]{1,0:T(8,128)S(1)} collective-permute-done((f32[1296,128]{1,0:T(8,128)S(1)}, f32[1296,128]{1,0:T(8,128)S(1)}, u32[]{:S(2)}, u32[]{:S(2)}) %collective-permute-start.8) | collective-permute-done | bytes 663584 | tf_op jit(solution)/shard_map/ppermute | solution.py:547
  36.6 0.0 collective-permute-done.9.corner_high
  36.6 4.9 %shard_map.68 = (f32[640,128]{1,0:T(8,128)S(1)}, f32[640,128]{1,0:T(8,128)S(1)}, f32[72,128]{1,0:T(8,128)S(1)}, f32[2304,128]{1,0:T(8,128)S(1)}, f32[2304,128]{1...) custom-call(f32[968,128]{1,0:T(8,128)S(1)} %get-tuple-element.34.own, ...), custom_call_target="tpu_custom_call", output_to_operand_aliasing={{3}: (7, {}), {4}: (8, {}), {5}: (9, {}), {6}: (10, {})} | custom-call | flops 20000 | bytes 20000 | tf_op jit(solution)/shard_map/pallas_call | solution.py:531
  41.6 0.4 collective-permute-start.10
  42.0 2.6 %collective-permute-start.11 = (f32[640,128]{1,0:T(8,128)S(1)}, f32[640,128]{1,0:T(8,128)S(1)}, u32[]{:S(2)}, u32[]{:S(2)}) collective-permute-start(f32[640,128]{1,0:T(8,128)S(1)} %get-tuple-element.45.own_down), channel_id=1, source_target_pairs={{32,0},{64,32},{96,64},{128,96},{160,128},{192,160},{224,192},{0,2... | collective-permute-start | bytes 983048 | tf_op jit(solution)/shard_map/ppermute | solution.py:547
  44.6 4.7 %collective-permute-done.10.low = f32[640,128]{1,0:T(8,128)S(1)} collective-permute-done((f32[640,128]{1,0:T(8,128)S(1)}, f32[640,128]{1,0:T(8,128)S(1)}, u32[]{:S(2)}, u32[]{:S(2)}) %collective-permute-start.10) | collective-permute-done | bytes 327712 | tf_op jit(solution)/shard_map/ppermute | solution.py:547
  49.3 0.0 collective-permute-done.11.high
  49.3 0.1 shard_map.69
  49.4 1.0 %collective-permute-start.12 = (f32[640,128]{1,0:T(8,128)S(1)}, f32[640,128]{1,0:T(8,128)S(1)}, u32[]{:S(2)}, u32[]{:S(2)}) collective-permute-start(f32[640,128]{1,0:T(8,128)S(1)} %get-tuple-element.46.own_up), channel_id=1, source_target_pairs={{0,8},{8,16},{16,24},{24,0},{1,9},{9,17},{17,25},{25,1},{2,10},{10... | collective-permute-start | bytes 983048 | tf_op jit(solution)/shard_map/ppermute | solution.py:547
  50.4 0.0 copy-start
  50.4 1.1 %collective-permute-start.13 = (f32[640,128]{1,0:T(8,128)S(1)}, f32[640,128]{1,0:T(8,128)S(1)}, u32[]{:S(2)}, u32[]{:S(2)}) collective-permute-start(f32[640,128]{1,0:T(8,128)S(1)} %get-tuple-element.47.own_down), channel_id=1, source_target_pairs={{8,0},{16,8},{24,16},{0,24},{9,1},{17,9},{25,17},{1,25},{10,2},{18... | collective-permute-start | bytes 983048 | tf_op jit(solution)/shard_map/ppermute | solution.py:547
  51.5 3.6 %shard_map.70.reg = f32[3,16,16,128]{3,2,1,0:T(8,128)S(1)} custom-call(f32[3,16,16,128]{3,2,1,0:T(8,128)S(1)} %get-tuple-element.29.v, f32[312,128]{1,0:T(8,128)S(1)} %collective-permute-done.swap0, f32[312,128]{1,0:T(8,128)S(1)} %collective-permute-done.1.swap1, f32[576,128]{1,0:T(8,128)S(1)} %collective-permute-done.2.ylow.low, ...), custom_call_target="tpu_custom_call" | custom-call | flops 4000000 | bytes 4000000 | tf_op jit(solution)/shard_map/pallas_call | solution.py:531
  55.1 3.5 %collective-permute-done.12.low = f32[640,128]{1,0:T(8,128)S(1)} collective-permute-done((f32[640,128]{1,0:T(8,128)S(1)}, f32[640,128]{1,0:T(8,128)S(1)}, u32[]{:S(2)}, u32[]{:S(2)}) %collective-permute-start.12) | collective-permute-done | bytes 327712 | tf_op jit(solution)/shard_map/ppermute | solution.py:547
  58.6 1.5 %collective-permute-done.13.high = f32[640,128]{1,0:T(8,128)S(1)} collective-permute-done((f32[640,128]{1,0:T(8,128)S(1)}, f32[640,128]{1,0:T(8,128)S(1)}, u32[]{:S(2)}, u32[]{:S(2)}) %collective-permute-start.13) | collective-permute-done | bytes 327712 | tf_op jit(solution)/shard_map/ppermute | solution.py:547
  60.1 0.0 copy-done
  60.1 4.4 %shard_map.71 = f32[3,16,16,128]{3,2,1,0:T(8,128)} custom-call(f32[640,128]{1,0:T(8,128)S(1)} %get-tuple-element.46.own_up, f32[640,128]{1,0:T(8,128)S(1)} %get-tuple-element.47.own_down, f32[640,128]{1,0:T(8,128)S(1)} %collective-permute-done.12.low, f32[640,128]{1,0:T(8,128)S(1)} %collective-permute-done.13.high, f32[72,128]{1,0:T(8,128)S(1)} %get-tuple-element.48.numbers, ...), custom_call_target="tpu_custom_call" | custom-call | flops 20000 | bytes 20000 | tf_op jit(solution)/shard_map/pallas_call | solution.py:531
Async XLA Ops:
  1.6 12.4 %collective-permute-start.2 = (f32[576,128]{1,0:T(8,128)S(1)}, f32[576,128]{1,0:T(8,128)S(1)}, u32[]{:S(2)}, u32[]{:S(2)}) collective-permute-start(f32[576,128]{1,0:T(8,128)S(1)} %get-tuple-element.32), channel_id=1, source_target_pairs={{0,8},{8,16},{16,24},{24,0},{1,9},{9,17},{17,25},{25,1},{2,10},{10... | collective-permute-start | bytes 884744 | tf_op jit(solution)/shard_map/ppermute | solution.py:547
  1.9 12.1 %collective-permute-start.3 = (f32[576,128]{1,0:T(8,128)S(1)}, f32[576,128]{1,0:T(8,128)S(1)}, u32[]{:S(2)}, u32[]{:S(2)}) collective-permute-start(f32[576,128]{1,0:T(8,128)S(1)} %get-tuple-element.33), channel_id=1, source_target_pairs={{8,0},{16,8},{24,16},{0,24},{9,1},{17,9},{25,17},{1,25},{10,2},{18... | collective-permute-start | bytes 884744 | tf_op jit(solution)/shard_map/ppermute | solution.py:547
  3.7 7.2 %collective-permute-start.1 = (f32[312,128]{1,0:T(8,128)S(1)}, f32[312,128]{1,0:T(8,128)S(1)}, u32[]{:S(2)}, u32[]{:S(2)}) collective-permute-start(f32[312,128]{1,0:T(8,128)S(1)} %get-tuple-element.31), channel_id=1, source_target_pairs={{0,0},{1,2},{2,1},{3,4},{4,3},{5,6},{6,5},{7,7},{8,8},{9,10},{10,9... | collective-permute-start | bytes 479240 | tf_op jit(solution)/shard_map/ppermute | solution.py:560
  5.7 8.3 %collective-permute-start = (f32[312,128]{1,0:T(8,128)S(1)}, f32[312,128]{1,0:T(8,128)S(1)}, u32[]{:S(2)}, u32[]{:S(2)}) collective-permute-start(f32[312,128]{1,0:T(8,128)S(1)} %get-tuple-element.30.own), channel_id=1, source_target_pairs={{0,1},{1,0},{2,3},{3,2},{4,5},{5,4},{6,7},{7,6},{8,9},{9,8},{10,11... | collective-permute-start | bytes 479240 | tf_op jit(solution)/shard_map/ppermute | solution.py:560
  14.2 11.1 %collective-permute-start.5 = (f32[968,128]{1,0:T(8,128)S(1)}, f32[968,128]{1,0:T(8,128)S(1)}, u32[]{:S(2)}, u32[]{:S(2)}) collective-permute-start(f32[968,128]{1,0:T(8,128)S(1)} %get-tuple-element.35.own_down), channel_id=1, source_target_pairs={{32,0},{64,32},{96,64},{128,96},{160,128},{192,160},{224,192},{0,2... | collective-permute-start | bytes 1486856 | tf_op jit(solution)/shard_map/ppermute | solution.py:547
  14.6 10.6 %collective-permute-start.4 = (f32[968,128]{1,0:T(8,128)S(1)}, f32[968,128]{1,0:T(8,128)S(1)}, u32[]{:S(2)}, u32[]{:S(2)}) collective-permute-start(f32[968,128]{1,0:T(8,128)S(1)} %get-tuple-element.34.own_up.own), channel_id=1, source_target_pairs={{0,32},{32,64},{64,96},{96,128},{128,160},{160,192},{192,224},{224... | collective-permute-start | bytes 1486856 | tf_op jit(solution)/shard_map/ppermute | solution.py:547
  14.7 7.7 %collective-permute-start.6 = (f32[392,128]{1,0:T(8,128)S(1)}, f32[392,128]{1,0:T(8,128)S(1)}, u32[]{:S(2)}, u32[]{:S(2)}) collective-permute-start(f32[392,128]{1,0:T(8,128)S(1)} %get-tuple-element.36), channel_id=1, source_target_pairs={{0,8},{8,16},{16,24},{24,0},{1,9},{9,17},{17,25},{25,1},{2,10},{10... | collective-permute-start | bytes 602120 | tf_op jit(solution)/shard_map/ppermute | solution.py:547
  16.6 8.6 %collective-permute-start.7 = (f32[392,128]{1,0:T(8,128)S(1)}, f32[392,128]{1,0:T(8,128)S(1)}, u32[]{:S(2)}, u32[]{:S(2)}) collective-permute-start(f32[392,128]{1,0:T(8,128)S(1)} %get-tuple-element.37), channel_id=1, source_target_pairs={{8,0},{16,8},{24,16},{0,24},{9,1},{17,9},{25,17},{1,25},{10,2},{18... | collective-permute-start | bytes 602120 | tf_op jit(solution)/shard_map/ppermute | solution.py:547
  25.3 11.3 %collective-permute-start.8 = (f32[1296,128]{1,0:T(8,128)S(1)}, f32[1296,128]{1,0:T(8,128)S(1)}, u32[]{:S(2)}, u32[]{:S(2)}) collective-permute-start(f32[1296,128]{1,0:T(8,128)S(1)} %get-tuple-element.38), channel_id=1, source_target_pairs={{0,32},{32,64},{64,96},{96,128},{128,160},{160,192},{192,224},{224... | collective-permute-start | bytes 1990664 | tf_op jit(solution)/shard_map/ppermute | solution.py:547
  25.3 11.3 %collective-permute-start.9 = (f32[1296,128]{1,0:T(8,128)S(1)}, f32[1296,128]{1,0:T(8,128)S(1)}, u32[]{:S(2)}, u32[]{:S(2)}) collective-permute-start(f32[1296,128]{1,0:T(8,128)S(1)} %get-tuple-element.39), channel_id=1, source_target_pairs={{32,0},{64,32},{96,64},{128,96},{160,128},{192,160},{224,192},{0,2... | collective-permute-start | bytes 1990664 | tf_op jit(solution)/shard_map/ppermute | solution.py:547
  41.6 7.7 %collective-permute-start.10 = (f32[640,128]{1,0:T(8,128)S(1)}, f32[640,128]{1,0:T(8,128)S(1)}, u32[]{:S(2)}, u32[]{:S(2)}) collective-permute-start(f32[640,128]{1,0:T(8,128)S(1)} %get-tuple-element.44.own_up), channel_id=1, source_target_pairs={{0,32},{32,64},{64,96},{96,128},{128,160},{160,192},{192,224},{224... | collective-permute-start | bytes 983048 | tf_op jit(solution)/shard_map/ppermute | solution.py:547
  42.0 7.3 %collective-permute-start.11 = (f32[640,128]{1,0:T(8,128)S(1)}, f32[640,128]{1,0:T(8,128)S(1)}, u32[]{:S(2)}, u32[]{:S(2)}) collective-permute-start(f32[640,128]{1,0:T(8,128)S(1)} %get-tuple-element.45.own_down), channel_id=1, source_target_pairs={{32,0},{64,32},{96,64},{128,96},{160,128},{192,160},{224,192},{0,2... | collective-permute-start | bytes 983048 | tf_op jit(solution)/shard_map/ppermute | solution.py:547
  49.4 9.2 %collective-permute-start.12 = (f32[640,128]{1,0:T(8,128)S(1)}, f32[640,128]{1,0:T(8,128)S(1)}, u32[]{:S(2)}, u32[]{:S(2)}) collective-permute-start(f32[640,128]{1,0:T(8,128)S(1)} %get-tuple-element.46.own_up), channel_id=1, source_target_pairs={{0,8},{8,16},{16,24},{24,0},{1,9},{9,17},{17,25},{25,1},{2,10},{10... | collective-permute-start | bytes 983048 | tf_op jit(solution)/shard_map/ppermute | solution.py:547
  50.4 9.7 %copy-start = (bf16[2,3,16,16,128]{4,3,2,1,0:T(8,128)(2,1)S(1)}, bf16[2,3,16,16,128]{4,3,2,1,0:T(8,128)(2,1)}, u32[]{:S(2)}) copy-start(bf16[2,3,16,16,128]{4,3,2,1,0:T(8,128)(2,1)} %g.1) | copy-start | bytes 1179652
  50.4 9.7 %collective-permute-start.13 = (f32[640,128]{1,0:T(8,128)S(1)}, f32[640,128]{1,0:T(8,128)S(1)}, u32[]{:S(2)}, u32[]{:S(2)}) collective-permute-start(f32[640,128]{1,0:T(8,128)S(1)} %get-tuple-element.47.own_down), channel_id=1, source_target_pairs={{8,0},{16,8},{24,16},{0,24},{9,1},{17,9},{25,17},{1,25},{10,2},{18... | collective-permute-start | bytes 983048 | tf_op jit(solution)/shard_map/ppermute | solution.py:547

commit v10 on v9

--- a/solution.py
+++ b/solution.py
@@ -11,7 +11,7 @@
 REG_WEIGHT = 0.1
 T = 16
 L = 128
-UN_ASM, UN_CORNER, UN_FIRST, UN_SECOND, UN_PACK, UN_UNPACK = 8, 16, 16, 4, 8, 4
+UN_ASM, UN_CORNER, UN_FIRST, UN_SECOND, UN_PACK, UN_UNPACK = 8, 4, 16, 4, 4, 2
 META = 15
 
 Z_S0, Z_S1, Z_V, Z_META, Z_ROWS = 0, 128, 256, 304, 312
@@ -557,7 +557,8 @@
     n = lax.axis_size(axis)
     pairs = [(i, i + 1 if i % 2 == 0 else i - 1) for i in range(n)]
     others = [(i, i if i in (0, n - 1) else i - 1 if i % 2 == 0 else i + 1) for i in range(n)]
-    return lax.ppermute(first, axis, pairs), lax.ppermute(second, axis, others)
+    from_other = lax.ppermute(second, axis, others)
+    return lax.ppermute(first, axis, pairs), from_other
 
 
 def body(velocity, gradients, shift_x, shift_y, shift_z, fractions):

time: 64.8 us -> 64.1 us (0.989)
  Pallas kernels: 15 us -> 14.3 us
    pallas_call x8, Pallas kernels: 15 us -> 14.3 us  [call(): pl.pallas_call(kernel, out_shape=shapes, in_specs=specs, out_specs=[out_s...]
where the time goes in v10:
time: 64.1 us; the launch traced here: 64 us
  waiting for transfers between devices  29.7 us (46%)
  starting transfers between devices  19.7 us (31%)
  Pallas kernels  14.3 us (22%)
    ppermute x12, waiting for transfers between devices, exchange(): return (lax.ppermute(up, axis, rise), lax.ppermute(down, axis, fall))  26.4 us
    pallas_call x8, Pallas kernels, call(): pl.pallas_call(kernel, out_shape=shapes, in_specs=specs, out_specs=[out_s...  14.3 us
    ppermute x12, starting transfers between devices, exchange(): return (lax.ppermute(up, axis, rise), lax.ppermute(down, axis, fall))  12.7 us
    ppermute x1, starting transfers between devices, swap(): return (lax.ppermute(first, axis, pairs), from_other)  5.02 us
    ppermute x1, waiting for transfers between devices, swap(): return (lax.ppermute(first, axis, pairs), from_other)  3.13 us
    ppermute x1, starting transfers between devices, swap(): from_other = lax.ppermute(second, axis, others)  2 us
  transfers between devices with their start and end apart: 14, of which 8 were waited for; matrix products, arithmetic and copies ran while one was open for 0% of the time, Pallas kernels for 6%

profile of v10, /device:TPU:88, one launch (start us, length us, event | category | flops | bytes accessed | tf_op | source)
XLA Modules:
  0.0 64.0 jit_solution(6484956785774326034)
XLA Ops:
  0.0 1.6 %shard_map.64 = (f32[3,16,16,128]{3,2,1,0:T(8,128)S(1)}, f32[16,16,128]{2,1,0:T(8,128)S(1)}, f32[16,16,128]{2,1,0:T(8,128)S(1)}, f32[312,128]{1,0:T(8,128)S(1)},...) custom-call(f32[3,16,16,128]{3,2,1,0:T(8,128)} %v_hbm.1, bf16[2,3,16,16,128]{4,3,2,1,0:T(8,128)(2,1)} %g.1, ...), custom_call_target="tpu_custom_call" | custom-call | flops 20000 | bytes 20000 | tf_op jit(solution)/shard_map/pallas_call | solution.py:531
  1.6 0.3 collective-permute-start.2
  1.9 1.8 %collective-permute-start.3 = (f32[576,128]{1,0:T(8,128)S(1)}, f32[576,128]{1,0:T(8,128)S(1)}, u32[]{:S(2)}, u32[]{:S(2)}) collective-permute-start(f32[576,128]{1,0:T(8,128)S(1)} %get-tuple-element.33), channel_id=1, source_target_pairs={{8,0},{16,8},{24,16},{0,24},{9,1},{17,9},{25,17},{1,25},{10,2},{18... | collective-permute-start | bytes 884744 | tf_op jit(solution)/shard_map/ppermute | solution.py:547
  3.7 2.0 %collective-permute-start.1 = (f32[312,128]{1,0:T(8,128)S(1)}, f32[312,128]{1,0:T(8,128)S(1)}, u32[]{:S(2)}, u32[]{:S(2)}) collective-permute-start(f32[312,128]{1,0:T(8,128)S(1)} %get-tuple-element.31), channel_id=1, source_target_pairs={{0,0},{1,2},{2,1},{3,4},{4,3},{5,6},{6,5},{7,7},{8,8},{9,10},{10,9... | collective-permute-start | bytes 479240 | tf_op jit(solution)/shard_map/ppermute | solution.py:560
  5.7 5.0 %collective-permute-start = (f32[312,128]{1,0:T(8,128)S(1)}, f32[312,128]{1,0:T(8,128)S(1)}, u32[]{:S(2)}, u32[]{:S(2)}) collective-permute-start(f32[312,128]{1,0:T(8,128)S(1)} %get-tuple-element.30.own), channel_id=1, source_target_pairs={{0,1},{1,0},{2,3},{3,2},{4,5},{5,4},{6,7},{7,6},{8,9},{9,8},{10,11... | collective-permute-start | bytes 479240 | tf_op jit(solution)/shard_map/ppermute | solution.py:561
  10.8 0.1 collective-permute-done.1.swap1
  10.9 3.1 %collective-permute-done.swap0 = f32[312,128]{1,0:T(8,128)S(1)} collective-permute-done((f32[312,128]{1,0:T(8,128)S(1)}, f32[312,128]{1,0:T(8,128)S(1)}, u32[]{:S(2)}, u32[]{:S(2)}) %collective-permute-start) | collective-permute-done | bytes 159776 | tf_op jit(solution)/shard_map/ppermute | solution.py:561
  14.0 0.0 collective-permute-done.2.ylow.low
  14.0 0.0 collective-permute-done.3.yhigh.high
  14.0 0.1 shard_map.65
  14.2 0.5 collective-permute-start.5
  14.6 0.0 collective-permute-start.4
  14.7 1.9 %collective-permute-start.6 = (f32[392,128]{1,0:T(8,128)S(1)}, f32[392,128]{1,0:T(8,128)S(1)}, u32[]{:S(2)}, u32[]{:S(2)}) collective-permute-start(f32[392,128]{1,0:T(8,128)S(1)} %get-tuple-element.36), channel_id=1, source_target_pairs={{0,8},{8,16},{16,24},{24,0},{1,9},{9,17},{17,25},{25,1},{2,10},{10... | collective-permute-start | bytes 602120 | tf_op jit(solution)/shard_map/ppermute | solution.py:547
  16.6 0.1 collective-permute-start.7
  16.7 5.7 %collective-permute-done.6.elow.ylow = f32[392,128]{1,0:T(8,128)S(1)} collective-permute-done((f32[392,128]{1,0:T(8,128)S(1)}, f32[392,128]{1,0:T(8,128)S(1)}, u32[]{:S(2)}, u32[]{:S(2)}) %collective-permute-start.6) | collective-permute-done | bytes 200736 | tf_op jit(solution)/shard_map/ppermute | solution.py:547
  22.4 2.8 %collective-permute-done.7.ehigh.yhigh = f32[392,128]{1,0:T(8,128)S(1)} collective-permute-done((f32[392,128]{1,0:T(8,128)S(1)}, f32[392,128]{1,0:T(8,128)S(1)}, u32[]{:S(2)}, u32[]{:S(2)}) %collective-permute-start.7) | collective-permute-done | bytes 200736 | tf_op jit(solution)/shard_map/ppermute | solution.py:547
  25.2 0.0 collective-permute-done.5.xhigh
  25.2 0.0 collective-permute-done.4.xlow
  25.2 0.1 shard_map.66
  25.3 0.0 collective-permute-start.8
  25.3 2.9 %collective-permute-start.9 = (f32[1296,128]{1,0:T(8,128)S(1)}, f32[1296,128]{1,0:T(8,128)S(1)}, u32[]{:S(2)}, u32[]{:S(2)}) collective-permute-start(f32[1296,128]{1,0:T(8,128)S(1)} %get-tuple-element.39), channel_id=1, source_target_pairs={{32,0},{64,32},{96,64},{128,96},{160,128},{192,160},{224,192},{0,2... | collective-permute-start | bytes 1990664 | tf_op jit(solution)/shard_map/ppermute | solution.py:547
  28.3 0.2 shard_map.67
  28.5 8.2 %collective-permute-done.8.corner_low = f32[1296,128]{1,0:T(8,128)S(1)} collective-permute-done((f32[1296,128]{1,0:T(8,128)S(1)}, f32[1296,128]{1,0:T(8,128)S(1)}, u32[]{:S(2)}, u32[]{:S(2)}) %collective-permute-start.8) | collective-permute-done | bytes 663584 | tf_op jit(solution)/shard_map/ppermute | solution.py:547
  36.6 0.0 collective-permute-done.9.corner_high
  36.6 4.5 %shard_map.68 = (f32[640,128]{1,0:T(8,128)S(1)}, f32[640,128]{1,0:T(8,128)S(1)}, f32[72,128]{1,0:T(8,128)S(1)}, f32[2304,128]{1,0:T(8,128)S(1)}, f32[2304,128]{1...) custom-call(f32[968,128]{1,0:T(8,128)S(1)} %get-tuple-element.34.own, ...), custom_call_target="tpu_custom_call", output_to_operand_aliasing={{3}: (7, {}), {4}: (8, {}), {5}: (9, {}), {6}: (10, {})} | custom-call | flops 20000 | bytes 20000 | tf_op jit(solution)/shard_map/pallas_call | solution.py:531
  41.1 0.4 collective-permute-start.10
  41.5 2.6 %collective-permute-start.11 = (f32[640,128]{1,0:T(8,128)S(1)}, f32[640,128]{1,0:T(8,128)S(1)}, u32[]{:S(2)}, u32[]{:S(2)}) collective-permute-start(f32[640,128]{1,0:T(8,128)S(1)} %get-tuple-element.45.own_down), channel_id=1, source_target_pairs={{32,0},{64,32},{96,64},{128,96},{160,128},{192,160},{224,192},{0,2... | collective-permute-start | bytes 983048 | tf_op jit(solution)/shard_map/ppermute | solution.py:547
  44.1 4.7 %collective-permute-done.10.low = f32[640,128]{1,0:T(8,128)S(1)} collective-permute-done((f32[640,128]{1,0:T(8,128)S(1)}, f32[640,128]{1,0:T(8,128)S(1)}, u32[]{:S(2)}, u32[]{:S(2)}) %collective-permute-start.10) | collective-permute-done | bytes 327712 | tf_op jit(solution)/shard_map/ppermute | solution.py:547
  48.8 0.0 collective-permute-done.11.high
  48.8 0.1 shard_map.69
  48.9 1.0 %collective-permute-start.12 = (f32[640,128]{1,0:T(8,128)S(1)}, f32[640,128]{1,0:T(8,128)S(1)}, u32[]{:S(2)}, u32[]{:S(2)}) collective-permute-start(f32[640,128]{1,0:T(8,128)S(1)} %get-tuple-element.46.own_up), channel_id=1, source_target_pairs={{0,8},{8,16},{16,24},{24,0},{1,9},{9,17},{17,25},{25,1},{2,10},{10... | collective-permute-start | bytes 983048 | tf_op jit(solution)/shard_map/ppermute | solution.py:547
  49.9 0.0 copy-start
  49.9 1.1 %collective-permute-start.13 = (f32[640,128]{1,0:T(8,128)S(1)}, f32[640,128]{1,0:T(8,128)S(1)}, u32[]{:S(2)}, u32[]{:S(2)}) collective-permute-start(f32[640,128]{1,0:T(8,128)S(1)} %get-tuple-element.47.own_down), channel_id=1, source_target_pairs={{8,0},{16,8},{24,16},{0,24},{9,1},{17,9},{25,17},{1,25},{10,2},{18... | collective-permute-start | bytes 983048 | tf_op jit(solution)/shard_map/ppermute | solution.py:547
  51.0 3.6 %shard_map.70.reg = f32[3,16,16,128]{3,2,1,0:T(8,128)S(1)} custom-call(f32[3,16,16,128]{3,2,1,0:T(8,128)S(1)} %get-tuple-element.29.v, f32[312,128]{1,0:T(8,128)S(1)} %collective-permute-done.swap0, f32[312,128]{1,0:T(8,128)S(1)} %collective-permute-done.1.swap1, f32[576,128]{1,0:T(8,128)S(1)} %collective-permute-done.2.ylow.low, ...), custom_call_target="tpu_custom_call" | custom-call | flops 4000000 | bytes 4000000 | tf_op jit(solution)/shard_map/pallas_call | solution.py:531
  54.6 3.5 %collective-permute-done.12.low = f32[640,128]{1,0:T(8,128)S(1)} collective-permute-done((f32[640,128]{1,0:T(8,128)S(1)}, f32[640,128]{1,0:T(8,128)S(1)}, u32[]{:S(2)}, u32[]{:S(2)}) %collective-permute-start.12) | collective-permute-done | bytes 327712 | tf_op jit(solution)/shard_map/ppermute | solution.py:547
  58.1 1.5 %collective-permute-done.13.high = f32[640,128]{1,0:T(8,128)S(1)} collective-permute-done((f32[640,128]{1,0:T(8,128)S(1)}, f32[640,128]{1,0:T(8,128)S(1)}, u32[]{:S(2)}, u32[]{:S(2)}) %collective-permute-start.13) | collective-permute-done | bytes 327712 | tf_op jit(solution)/shard_map/ppermute | solution.py:547
  59.6 0.0 copy-done
  59.6 4.2 %shard_map.71 = f32[3,16,16,128]{3,2,1,0:T(8,128)} custom-call(f32[640,128]{1,0:T(8,128)S(1)} %get-tuple-element.46.own_up, f32[640,128]{1,0:T(8,128)S(1)} %get-tuple-element.47.own_down, f32[640,128]{1,0:T(8,128)S(1)} %collective-permute-done.12.low, f32[640,128]{1,0:T(8,128)S(1)} %collective-permute-done.13.high, f32[72,128]{1,0:T(8,128)S(1)} %get-tuple-element.48.numbers, ...), custom_call_target="tpu_custom_call" | custom-call | flops 20000 | bytes 20000 | tf_op jit(solution)/shard_map/pallas_call | solution.py:531
Async XLA Ops:
  1.6 12.4 %collective-permute-start.2 = (f32[576,128]{1,0:T(8,128)S(1)}, f32[576,128]{1,0:T(8,128)S(1)}, u32[]{:S(2)}, u32[]{:S(2)}) collective-permute-start(f32[576,128]{1,0:T(8,128)S(1)} %get-tuple-element.32), channel_id=1, source_target_pairs={{0,8},{8,16},{16,24},{24,0},{1,9},{9,17},{17,25},{25,1},{2,10},{10... | collective-permute-start | bytes 884744 | tf_op jit(solution)/shard_map/ppermute | solution.py:547
  1.9 12.1 %collective-permute-start.3 = (f32[576,128]{1,0:T(8,128)S(1)}, f32[576,128]{1,0:T(8,128)S(1)}, u32[]{:S(2)}, u32[]{:S(2)}) collective-permute-start(f32[576,128]{1,0:T(8,128)S(1)} %get-tuple-element.33), channel_id=1, source_target_pairs={{8,0},{16,8},{24,16},{0,24},{9,1},{17,9},{25,17},{1,25},{10,2},{18... | collective-permute-start | bytes 884744 | tf_op jit(solution)/shard_map/ppermute | solution.py:547
  3.7 7.2 %collective-permute-start.1 = (f32[312,128]{1,0:T(8,128)S(1)}, f32[312,128]{1,0:T(8,128)S(1)}, u32[]{:S(2)}, u32[]{:S(2)}) collective-permute-start(f32[312,128]{1,0:T(8,128)S(1)} %get-tuple-element.31), channel_id=1, source_target_pairs={{0,0},{1,2},{2,1},{3,4},{4,3},{5,6},{6,5},{7,7},{8,8},{9,10},{10,9... | collective-permute-start | bytes 479240 | tf_op jit(solution)/shard_map/ppermute | solution.py:560
  5.7 8.3 %collective-permute-start = (f32[312,128]{1,0:T(8,128)S(1)}, f32[312,128]{1,0:T(8,128)S(1)}, u32[]{:S(2)}, u32[]{:S(2)}) collective-permute-start(f32[312,128]{1,0:T(8,128)S(1)} %get-tuple-element.30.own), channel_id=1, source_target_pairs={{0,1},{1,0},{2,3},{3,2},{4,5},{5,4},{6,7},{7,6},{8,9},{9,8},{10,11... | collective-permute-start | bytes 479240 | tf_op jit(solution)/shard_map/ppermute | solution.py:561
  14.2 11.1 %collective-permute-start.5 = (f32[968,128]{1,0:T(8,128)S(1)}, f32[968,128]{1,0:T(8,128)S(1)}, u32[]{:S(2)}, u32[]{:S(2)}) collective-permute-start(f32[968,128]{1,0:T(8,128)S(1)} %get-tuple-element.35.own_down), channel_id=1, source_target_pairs={{32,0},{64,32},{96,64},{128,96},{160,128},{192,160},{224,192},{0,2... | collective-permute-start | bytes 1486856 | tf_op jit(solution)/shard_map/ppermute | solution.py:547
  14.6 10.6 %collective-permute-start.4 = (f32[968,128]{1,0:T(8,128)S(1)}, f32[968,128]{1,0:T(8,128)S(1)}, u32[]{:S(2)}, u32[]{:S(2)}) collective-permute-start(f32[968,128]{1,0:T(8,128)S(1)} %get-tuple-element.34.own_up.own), channel_id=1, source_target_pairs={{0,32},{32,64},{64,96},{96,128},{128,160},{160,192},{192,224},{224... | collective-permute-start | bytes 1486856 | tf_op jit(solution)/shard_map/ppermute | solution.py:547
  14.7 7.7 %collective-permute-start.6 = (f32[392,128]{1,0:T(8,128)S(1)}, f32[392,128]{1,0:T(8,128)S(1)}, u32[]{:S(2)}, u32[]{:S(2)}) collective-permute-start(f32[392,128]{1,0:T(8,128)S(1)} %get-tuple-element.36), channel_id=1, source_target_pairs={{0,8},{8,16},{16,24},{24,0},{1,9},{9,17},{17,25},{25,1},{2,10},{10... | collective-permute-start | bytes 602120 | tf_op jit(solution)/shard_map/ppermute | solution.py:547
  16.6 8.6 %collective-permute-start.7 = (f32[392,128]{1,0:T(8,128)S(1)}, f32[392,128]{1,0:T(8,128)S(1)}, u32[]{:S(2)}, u32[]{:S(2)}) collective-permute-start(f32[392,128]{1,0:T(8,128)S(1)} %get-tuple-element.37), channel_id=1, source_target_pairs={{8,0},{16,8},{24,16},{0,24},{9,1},{17,9},{25,17},{1,25},{10,2},{18... | collective-permute-start | bytes 602120 | tf_op jit(solution)/shard_map/ppermute | solution.py:547
  25.3 11.3 %collective-permute-start.8 = (f32[1296,128]{1,0:T(8,128)S(1)}, f32[1296,128]{1,0:T(8,128)S(1)}, u32[]{:S(2)}, u32[]{:S(2)}) collective-permute-start(f32[1296,128]{1,0:T(8,128)S(1)} %get-tuple-element.38), channel_id=1, source_target_pairs={{0,32},{32,64},{64,96},{96,128},{128,160},{160,192},{192,224},{224... | collective-permute-start | bytes 1990664 | tf_op jit(solution)/shard_map/ppermute | solution.py:547
  25.3 11.3 %collective-permute-start.9 = (f32[1296,128]{1,0:T(8,128)S(1)}, f32[1296,128]{1,0:T(8,128)S(1)}, u32[]{:S(2)}, u32[]{:S(2)}) collective-permute-start(f32[1296,128]{1,0:T(8,128)S(1)} %get-tuple-element.39), channel_id=1, source_target_pairs={{32,0},{64,32},{96,64},{128,96},{160,128},{192,160},{224,192},{0,2... | collective-permute-start | bytes 1990664 | tf_op jit(solution)/shard_map/ppermute | solution.py:547
  41.1 7.7 %collective-permute-start.10 = (f32[640,128]{1,0:T(8,128)S(1)}, f32[640,128]{1,0:T(8,128)S(1)}, u32[]{:S(2)}, u32[]{:S(2)}) collective-permute-start(f32[640,128]{1,0:T(8,128)S(1)} %get-tuple-element.44.own_up), channel_id=1, source_target_pairs={{0,32},{32,64},{64,96},{96,128},{128,160},{160,192},{192,224},{224... | collective-permute-start | bytes 983048 | tf_op jit(solution)/shard_map/ppermute | solution.py:547
  41.5 7.3 %collective-permute-start.11 = (f32[640,128]{1,0:T(8,128)S(1)}, f32[640,128]{1,0:T(8,128)S(1)}, u32[]{:S(2)}, u32[]{:S(2)}) collective-permute-start(f32[640,128]{1,0:T(8,128)S(1)} %get-tuple-element.45.own_down), channel_id=1, source_target_pairs={{32,0},{64,32},{96,64},{128,96},{160,128},{192,160},{224,192},{0,2... | collective-permute-start | bytes 983048 | tf_op jit(solution)/shard_map/ppermute | solution.py:547
  48.9 9.2 %collective-permute-start.12 = (f32[640,128]{1,0:T(8,128)S(1)}, f32[640,128]{1,0:T(8,128)S(1)}, u32[]{:S(2)}, u32[]{:S(2)}) collective-permute-start(f32[640,128]{1,0:T(8,128)S(1)} %get-tuple-element.46.own_up), channel_id=1, source_target_pairs={{0,8},{8,16},{16,24},{24,0},{1,9},{9,17},{17,25},{25,1},{2,10},{10... | collective-permute-start | bytes 983048 | tf_op jit(solution)/shard_map/ppermute | solution.py:547
  49.9 9.7 %copy-start = (bf16[2,3,16,16,128]{4,3,2,1,0:T(8,128)(2,1)S(1)}, bf16[2,3,16,16,128]{4,3,2,1,0:T(8,128)(2,1)}, u32[]{:S(2)}) copy-start(bf16[2,3,16,16,128]{4,3,2,1,0:T(8,128)(2,1)} %g.1) | copy-start | bytes 1179652
  49.9 9.7 %collective-permute-start.13 = (f32[640,128]{1,0:T(8,128)S(1)}, f32[640,128]{1,0:T(8,128)S(1)}, u32[]{:S(2)}, u32[]{:S(2)}) collective-permute-start(f32[640,128]{1,0:T(8,128)S(1)} %get-tuple-element.47.own_down), channel_id=1, source_target_pairs={{8,0},{16,8},{24,16},{0,24},{9,1},{17,9},{25,17},{1,25},{10,2},{18... | collective-permute-start | bytes 983048 | tf_op jit(solution)/shard_map/ppermute | solution.py:547
